TPU v7x, 32 devices: a whole 2x2x4 slice. The times are simulated.
32 devices in a mesh: seq: 4 (over y, core), fsdp: 8 (over z, x).
Axes of the slice: x: 2, y: 2, z: 4, core: 2. Of those that a mesh axis runs over, the one named last changes fastest.
Arguments:
- hidden_in: bfloat16 [8, 512, 1024], P('fsdp', 'seq'), may hold values from -6 to 6
- memory: bfloat16 [8, 64, 1024], P('fsdp', 'seq'), may hold values from -6 to 6
- out_grad: bfloat16 [8, 512, 1024], P('fsdp', 'seq'), may hold values from -6 to 6
- segment_ids: int32 [8, 512], P('fsdp', 'seq'), may hold values from 0 to 7, as said below
- memory_segments: int32 [8, 64], P('fsdp', 'seq'), may hold values from 1 to 7, as said below
- deal: int32 [8], replicated, may hold values from 0 to 7, as said below
- attn_in: float32 [2, 3, 1024, 1024], P(None, None, 'fsdp'), may hold values from -0.1875 to 0.1875
- attn_out: float32 [2, 1024, 1024], P(None, 'fsdp'), may hold values from -0.5 to 0.5
- fc1: float32 [1024, 8192], P('fsdp'), may hold values from -0.1875 to 0.1875
- fc2: float32 [8192, 1024], P('fsdp'), may hold values from -0.0625 to 0.0625
- proj_bias: float32 [7, 1024], P(None, 'fsdp'), may hold values from -4 to 4
- fc1_bias: float32 [8192], P('fsdp'), may hold values from -4 to 4
- norm_gain: float32 [3, 1024], P(None, 'fsdp'), may hold values from 0.1 to 1.9
- norm_bias: float32 [3, 1024], P(None, 'fsdp'), may hold values from -3 to 3
Outputs:
- out: bfloat16 [8, 512, 1024], P('fsdp', 'seq')
- grad_hidden: float32 [8, 512, 1024], P('fsdp', 'seq')
- grad_memory: float32 [8, 64, 1024], P('fsdp', 'seq')
- grad_attn_in: float32 [2, 3, 1024, 1024], P(None, None, ('seq', 'fsdp'))
- grad_attn_out: float32 [2, 1024, 1024], P(None, ('seq', 'fsdp'))
- grad_fc1: float32 [1024, 8192], P(('seq', 'fsdp'))
- grad_fc2: float32 [8192, 1024], P(('seq', 'fsdp'))
- grad_proj_bias: float32 [7, 1024], P(None, ('seq', 'fsdp'))
- grad_fc1_bias: float32 [8192], P(('seq', 'fsdp'))
- grad_norm_gain: float32 [3, 1024], P(None, ('seq', 'fsdp'))
- grad_norm_bias: float32 [3, 1024], P(None, ('seq', 'fsdp'))
Inputs may be any that keep to these rules, and one draw needn't show every extreme that they name: `deal`: entry i names the block of 64 consecutive positions stored i-th; entries 2 * d and 2 * d + 1 sum to 7. `segment_ids`: 0 marks padding; in position order the tokens of one nonzero id form one run. `memory_segments`: ids never fall along a row.
All inputs are finite; a program needn't handle non-finite values.
Results may differ from a plain program's by a relative error of at most 0.018.
Values may be sent and summed in bfloat16 or wider, within the bound.
No kernel may reach another device: no remote copies, remote signals or barrier semaphores. Data moves between devices by JAX's collectives and lax.ppermute only.
A program may use at most 384 MiB of HBM per device.

v0:
```python
import math

import jax
import jax.numpy as jnp
from jax import lax
from jax.sharding import PartitionSpec as P

HEADS = 16


EPSILON = 1e-05
NEGATIVE = -1e30


def layer_norm(values, gain, shift):
    centre = jnp.mean(values, axis=-1, keepdims=True)
    centred = values - centre
    spread = jnp.mean(centred * centred, axis=-1, keepdims=True)
    return centred * lax.rsqrt(spread + EPSILON) * gain + shift


def matmul(left, right):
    return jnp.dot(left, right, preferred_element_type=jnp.float32)


def contract_rows(left, right):
    return lax.dot_general(
        left, right, (((0,), (0,)), ((), ())), preferred_element_type=jnp.float32
    )


def times_transpose(left, right):
    return lax.dot_general(
        left, right, (((1,), (1,)), ((), ())), preferred_element_type=jnp.float32
    )


def column_sums(values):
    return jnp.sum(values.astype(jnp.float32), axis=0)


def split_heads(values):
    return values.reshape(values.shape[0], HEADS, values.shape[1] // HEADS)


def stacked_blocks(values, block_size):
    return values.reshape((values.shape[0] // block_size, block_size) + values.shape[1:])


def attention_setup(queries, key_all, value_all, key_pos, key_seg):
    block_size = math.gcd(key_all.shape[0], 512)
    score_scale = 1.0 / math.sqrt(queries.shape[1] // HEADS)
    pieces = (
        stacked_blocks(key_all, block_size),
        stacked_blocks(value_all, block_size),
        stacked_blocks(key_pos, block_size),
        stacked_blocks(key_seg, block_size),
    )
    return (score_scale, pieces)


def scored_piece(query_heads, query_pos, query_seg, causal, score_scale, piece):
    key_piece, value_piece, pos_piece, seg_piece = piece
    allowed = (query_seg[:, None] == seg_piece[None, :]) & (query_seg[:, None] != 0)
    if causal:
        allowed = allowed & (pos_piece[None, :] <= query_pos[:, None])
    allowed = allowed[None]
    scores = (
        jnp.einsum(
            "qhd,khd->hqk", query_heads, split_heads(key_piece), preferred_element_type=jnp.float32
        )
        * score_scale
    )
    return (allowed, jnp.where(allowed, scores, NEGATIVE))


def chance_of(allowed, scores, row_top, divisor):
    return jnp.where(allowed, jnp.exp(scores - row_top[..., None]), 0.0) / divisor[..., None]


def attention_forward(queries, key_all, value_all, query_pos, query_seg, key_pos, key_seg, causal):
    score_scale, pieces = attention_setup(queries, key_all, value_all, key_pos, key_seg)
    query_heads = split_heads(queries)
    row_count = queries.shape[0]

    def stats_step(running, piece):
        row_top, row_total = running
        allowed, scores = scored_piece(
            query_heads, query_pos, query_seg, causal, score_scale, piece
        )
        new_top = jnp.maximum(row_top, jnp.max(scores, axis=-1))
        raised = jnp.where(allowed, jnp.exp(scores - new_top[..., None]), 0.0)
        row_total = row_total * jnp.exp(row_top - new_top) + jnp.sum(raised, axis=-1)
        return ((new_top, row_total), None)

    start = (
        jnp.full((HEADS, row_count), NEGATIVE, jnp.float32),
        jnp.zeros((HEADS, row_count), jnp.float32),
    )
    (row_top, row_total), _ = lax.scan(stats_step, start, pieces)
    divisor = jnp.maximum(row_total, 1.0)

    def value_step(running, piece):
        high_sum, rest_sum = running
        allowed, scores = scored_piece(
            query_heads, query_pos, query_seg, causal, score_scale, piece
        )
        chance = chance_of(allowed, scores, row_top, divisor)
        high_part = chance.astype(jnp.bfloat16)
        rest_part = (chance - high_part.astype(jnp.float32)).astype(jnp.bfloat16)
        value_heads = split_heads(piece[1])
        high_sum = high_sum + jnp.einsum(
            "hqk,khd->qhd", high_part, value_heads, preferred_element_type=jnp.float32
        )
        rest_sum = rest_sum + jnp.einsum(
            "hqk,khd->qhd", rest_part, value_heads, preferred_element_type=jnp.float32
        )
        return ((high_sum, rest_sum), None)

    zeros = jnp.zeros(query_heads.shape, jnp.float32)
    (high_sum, rest_sum), _ = lax.scan(value_step, (zeros, zeros), pieces)
    return (
        high_sum.reshape(row_count, -1),
        (high_sum + rest_sum).reshape(row_count, -1),
        row_top,
        divisor,
    )


def attention_backward(
    queries,
    key_all,
    value_all,
    query_pos,
    query_seg,
    key_pos,
    key_seg,
    causal,
    grad_out,
    unrounded,
    row_top,
    divisor,
):
    score_scale, pieces = attention_setup(queries, key_all, value_all, key_pos, key_seg)
    query_heads = split_heads(queries)
    grad_heads = split_heads(grad_out)
    row_count = queries.shape[0]
    model_width = queries.shape[1]
    delta = jnp.einsum("qhd,qhd->hq", grad_heads.astype(jnp.float32), split_heads(unrounded))

    def grad_step(query_grad, piece):
        allowed, scores = scored_piece(
            query_heads, query_pos, query_seg, causal, score_scale, piece
        )
        chance = chance_of(allowed, scores, row_top, divisor)
        key_heads = split_heads(piece[0])
        value_heads = split_heads(piece[1])
        chance_grad = jnp.einsum(
            "qhd,khd->hqk", grad_heads, value_heads, preferred_element_type=jnp.float32
        )
        score_grad = (chance * (chance_grad - delta[..., None])).astype(jnp.bfloat16)
        query_grad = (
            query_grad
            + jnp.einsum("hqk,khd->qhd", score_grad, key_heads, preferred_element_type=jnp.float32)
            * score_scale
        )
        key_grad = (
            jnp.einsum("hqk,qhd->khd", score_grad, query_heads, preferred_element_type=jnp.float32)
            * score_scale
        )
        value_grad = jnp.einsum(
            "hqk,qhd->khd",
            chance.astype(jnp.bfloat16),
            grad_heads,
            preferred_element_type=jnp.float32,
        )
        piece_rows = key_heads.shape[0]
        return (
            query_grad,
            (
                key_grad.reshape(piece_rows, model_width),
                value_grad.reshape(piece_rows, model_width),
            ),
        )

    start = jnp.zeros(query_heads.shape, jnp.float32)
    query_grad, (key_grads, value_grads) = lax.scan(grad_step, start, pieces)
    return (
        query_grad.reshape(row_count, model_width),
        key_grads.reshape(-1, model_width),
        value_grads.reshape(-1, model_width),
    )


def unpack(gathered):
    w_in, w_out, w_up, w_down, biases, up_bias, gains, shifts = gathered
    return (
        w_in,
        w_out,
        w_up,
        w_down,
        biases.astype(jnp.float32),
        up_bias.astype(jnp.float32),
        gains.astype(jnp.float32),
        shifts.astype(jnp.float32),
    )


def body(
    hidden_in,
    memory,
    out_grad,
    segment_ids,
    memory_segments,
    deal,
    attn_in,
    attn_out,
    fc1,
    fc2,
    proj_bias,
    fc1_bias,
    norm_gain,
    norm_bias,
):
    gathered = (
        lax.all_gather(attn_in.astype(jnp.bfloat16), "fsdp", axis=2, tiled=True),
        lax.all_gather(attn_out.astype(jnp.bfloat16), "fsdp", axis=1, tiled=True),
        lax.all_gather(fc1.astype(jnp.bfloat16), "fsdp", axis=0, tiled=True),
        lax.all_gather(fc2.astype(jnp.bfloat16), "fsdp", axis=0, tiled=True),
        lax.all_gather(proj_bias.astype(jnp.bfloat16), "fsdp", axis=1, tiled=True),
        lax.all_gather(fc1_bias.astype(jnp.bfloat16), "fsdp", axis=0, tiled=True),
        lax.all_gather(norm_gain.astype(jnp.bfloat16), "fsdp", axis=1, tiled=True),
        lax.all_gather(norm_bias.astype(jnp.bfloat16), "fsdp", axis=1, tiled=True),
    )
    w_in, w_out, w_up, w_down, biases, up_bias, gains, shifts = unpack(gathered)
    tokens = hidden_in.shape[1]
    half_rows = tokens // 2
    device_place = lax.axis_index("seq")
    offsets = jnp.arange(half_rows, dtype=jnp.int32)
    block_ids = lax.dynamic_slice_in_dim(deal, 2 * device_place, 2)
    query_pos = (block_ids[:, None] * half_rows + offsets[None, :]).reshape(tokens)
    key_pos = (deal[:, None] * half_rows + offsets[None, :]).reshape(-1)
    seg_all, source_seg_all = (
        lax.all_gather(segment_ids, "seq", axis=1, tiled=True),
        lax.all_gather(memory_segments, "seq", axis=1, tiled=True),
    )
    query_seg = segment_ids[0]
    key_seg = seg_all[0]
    source_seg = source_seg_all[0]
    source_pos = jnp.zeros(source_seg.shape, jnp.int32)
    inputs = hidden_in[0].astype(jnp.float32)
    sources = memory[0]
    normed_one = layer_norm(inputs, gains[0], shifts[0]).astype(jnp.bfloat16)
    query_self = (matmul(normed_one, w_in[0, 0]) + biases[0]).astype(jnp.bfloat16)
    key_self = matmul(normed_one, w_in[0, 1]).astype(jnp.bfloat16)
    value_self = (matmul(normed_one, w_in[0, 2]) + biases[1]).astype(jnp.bfloat16)
    key_all, value_all = (
        lax.all_gather(key_self, "seq", axis=0, tiled=True),
        lax.all_gather(value_self, "seq", axis=0, tiled=True),
    )
    self_mixed, self_unrounded, self_top, self_divisor = attention_forward(
        query_self, key_all, value_all, query_pos, query_seg, key_pos, key_seg, True
    )
    self_out = self_mixed.astype(jnp.bfloat16)
    after_self = inputs + matmul(self_out, w_out[0]) + biases[2]
    local_keys = matmul(sources, w_in[1, 1]).astype(jnp.bfloat16)
    local_values = (matmul(sources, w_in[1, 2]) + biases[4]).astype(jnp.bfloat16)
    cross_key_all, cross_value_all = (
        lax.all_gather(local_keys, "seq", axis=0, tiled=True),
        lax.all_gather(local_values, "seq", axis=0, tiled=True),
    )
    normed_two = layer_norm(after_self, gains[1], shifts[1]).astype(jnp.bfloat16)
    query_cross = (matmul(normed_two, w_in[1, 0]) + biases[3]).astype(jnp.bfloat16)
    cross_mixed, cross_unrounded, cross_top, cross_divisor = attention_forward(
        query_cross,
        cross_key_all,
        cross_value_all,
        query_pos,
        query_seg,
        source_pos,
        source_seg,
        False,
    )
    cross_out = cross_mixed.astype(jnp.bfloat16)
    after_cross = after_self + matmul(cross_out, w_out[1]) + biases[5]
    normed_three = layer_norm(after_cross, gains[2], shifts[2]).astype(jnp.bfloat16)
    pre_act = matmul(normed_three, w_up) + up_bias
    activated = jax.nn.gelu(pre_act, approximate=True).astype(jnp.bfloat16)
    result = after_cross + matmul(activated, w_down) + biases[6]
    result_grad = out_grad[0].astype(jnp.float32)
    down_grad = result_grad.astype(jnp.bfloat16)
    bias_down = column_sums(down_grad)
    act_grad = times_transpose(down_grad, w_down)
    _, gelu_back = jax.vjp(lambda value: jax.nn.gelu(value, approximate=True), pre_act)
    pre_grad = gelu_back(act_grad)[0].astype(jnp.bfloat16)
    seq_count = lax.axis_size("seq")
    width_rows = normed_three.shape[1] // seq_count
    hidden_rows = activated.shape[1] // seq_count
    piece_normed = lax.all_gather(normed_three, "seq", axis=0, tiled=True)
    piece_pre = lax.all_gather(pre_grad, "seq", axis=0, tiled=True)
    piece_act = lax.all_gather(activated, "seq", axis=0, tiled=True)
    piece_down = lax.all_gather(down_grad, "seq", axis=0, tiled=True)
    normed_part = lax.dynamic_slice_in_dim(piece_normed, device_place * width_rows, width_rows, 1)
    act_part = lax.dynamic_slice_in_dim(piece_act, device_place * hidden_rows, hidden_rows, 1)
    pre_part = lax.dynamic_slice_in_dim(piece_pre, device_place * hidden_rows, hidden_rows, 1)
    mlp_sums = (
        lax.psum_scatter(
            contract_rows(normed_part, piece_pre).astype(jnp.bfloat16),
            "fsdp",
            scatter_dimension=0,
            tiled=True,
        ).astype(jnp.float32),
        lax.psum_scatter(
            contract_rows(act_part, piece_down).astype(jnp.bfloat16),
            "fsdp",
            scatter_dimension=0,
            tiled=True,
        ).astype(jnp.float32),
        lax.psum_scatter(
            column_sums(pre_part).astype(jnp.bfloat16), "fsdp", scatter_dimension=0, tiled=True
        ).astype(jnp.float32),
    )
    _, norm_back = jax.vjp(layer_norm, after_cross, gains[2], shifts[2])
    cross_part, gain_three, shift_three = norm_back(times_transpose(pre_grad, w_up))
    after_grad = result_grad + cross_part
    cross_branch = after_grad.astype(jnp.bfloat16)
    grad_cross_out = contract_rows(cross_out, cross_branch)
    bias_cross_out = column_sums(cross_branch)
    cross_head_grad = times_transpose(cross_branch, w_out[1]).astype(jnp.bfloat16)
    query_cross_grad, key_cross_terms, value_cross_terms = attention_backward(
        query_cross,
        cross_key_all,
        cross_value_all,
        query_pos,
        query_seg,
        source_pos,
        source_seg,
        False,
        cross_head_grad,
        cross_unrounded,
        cross_top,
        cross_divisor,
    )
    key_cross_sum, value_cross_sum = (
        lax.psum_scatter(
            key_cross_terms.astype(jnp.bfloat16), "seq", scatter_dimension=0, tiled=True
        ).astype(jnp.float32),
        lax.psum_scatter(
            value_cross_terms.astype(jnp.bfloat16), "seq", scatter_dimension=0, tiled=True
        ).astype(jnp.float32),
    )
    key_cross_grad = key_cross_sum.astype(jnp.bfloat16)
    value_cross_grad = value_cross_sum.astype(jnp.bfloat16)
    query_cross_grad = query_cross_grad.astype(jnp.bfloat16)
    grad_cross_key = contract_rows(sources, key_cross_grad)
    grad_cross_value = contract_rows(sources, value_cross_grad)
    grad_cross_query = contract_rows(normed_two, query_cross_grad)
    grad_memory = times_transpose(key_cross_grad, w_in[1, 1]) + times_transpose(
        value_cross_grad, w_in[1, 2]
    )
    _, norm_back = jax.vjp(layer_norm, after_self, gains[1], shifts[1])
    self_part, gain_two, shift_two = norm_back(times_transpose(query_cross_grad, w_in[1, 0]))
    self_grad = after_grad + self_part
    self_branch = self_grad.astype(jnp.bfloat16)
    grad_self_out = contract_rows(self_out, self_branch)
    bias_self_out = column_sums(self_branch)
    self_head_grad = times_transpose(self_branch, w_out[0]).astype(jnp.bfloat16)
    query_self_grad, key_self_terms, value_self_terms = attention_backward(
        query_self,
        key_all,
        value_all,
        query_pos,
        query_seg,
        key_pos,
        key_seg,
        True,
        self_head_grad,
        self_unrounded,
        self_top,
        self_divisor,
    )
    key_self_sum, value_self_sum = (
        lax.psum_scatter(
            key_self_terms.astype(jnp.bfloat16), "seq", scatter_dimension=0, tiled=True
        ).astype(jnp.float32),
        lax.psum_scatter(
            value_self_terms.astype(jnp.bfloat16), "seq", scatter_dimension=0, tiled=True
        ).astype(jnp.float32),
    )
    key_self_grad = key_self_sum.astype(jnp.bfloat16)
    value_self_grad = value_self_sum.astype(jnp.bfloat16)
    query_self_grad = query_self_grad.astype(jnp.bfloat16)
    grad_self_query = contract_rows(normed_one, query_self_grad)
    grad_self_key = contract_rows(normed_one, key_self_grad)
    grad_self_value = contract_rows(normed_one, value_self_grad)
    normed_grad = (
        times_transpose(query_self_grad, w_in[0, 0])
        + times_transpose(key_self_grad, w_in[0, 1])
        + times_transpose(value_self_grad, w_in[0, 2])
    )
    _, norm_back = jax.vjp(layer_norm, inputs, gains[0], shifts[0])
    input_part, gain_one, shift_one = norm_back(normed_grad)
    grad_hidden = self_grad + input_part
    grad_biases = jnp.stack(
        [
            column_sums(query_self_grad),
            column_sums(value_self_grad),
            bias_self_out,
            column_sums(query_cross_grad),
            column_sums(value_cross_grad),
            bias_cross_out,
            bias_down,
        ]
    )
    grad_gains = jnp.stack([gain_one, gain_two, gain_three])
    grad_shifts = jnp.stack([shift_one, shift_two, shift_three])
    shares = (
        lax.psum_scatter(grad_self_query, ("seq", "fsdp"), scatter_dimension=0, tiled=True),
        lax.psum_scatter(grad_self_key, ("seq", "fsdp"), scatter_dimension=0, tiled=True),
        lax.psum_scatter(grad_self_value, ("seq", "fsdp"), scatter_dimension=0, tiled=True),
        lax.psum_scatter(grad_cross_query, ("seq", "fsdp"), scatter_dimension=0, tiled=True),
        lax.psum_scatter(grad_cross_key, ("seq", "fsdp"), scatter_dimension=0, tiled=True),
        lax.psum_scatter(grad_cross_value, ("seq", "fsdp"), scatter_dimension=0, tiled=True),
        lax.psum_scatter(grad_self_out, ("seq", "fsdp"), scatter_dimension=0, tiled=True),
        lax.psum_scatter(grad_cross_out, ("seq", "fsdp"), scatter_dimension=0, tiled=True),
        lax.psum_scatter(grad_biases, ("seq", "fsdp"), scatter_dimension=1, tiled=True),
        lax.psum_scatter(grad_gains, ("seq", "fsdp"), scatter_dimension=1, tiled=True),
        lax.psum_scatter(grad_shifts, ("seq", "fsdp"), scatter_dimension=1, tiled=True),
    )
    grad_in_proj = jnp.stack(
        [jnp.stack([shares[0], shares[1], shares[2]]), jnp.stack([shares[3], shares[4], shares[5]])]
    )
    grad_out_proj = jnp.stack([shares[6], shares[7]])
    return (
        result.astype(jnp.bfloat16)[None],
        grad_hidden[None],
        grad_memory[None],
        grad_in_proj,
        grad_out_proj,
        mlp_sums[0],
        mlp_sums[1],
        shares[8],
        mlp_sums[2],
        shares[9],
        shares[10],
    )


def solution(mesh):
    placed = (
        P("fsdp", "seq", None),
        P("fsdp", "seq", None),
        P("fsdp", "seq", None),
        P("fsdp", "seq"),
        P("fsdp", "seq"),
        P(),
        P(None, None, "fsdp", None),
        P(None, "fsdp", None),
        P("fsdp", None),
        P("fsdp", None),
        P(None, "fsdp"),
        P("fsdp"),
        P(None, "fsdp"),
        P(None, "fsdp"),
    )
    return jax.shard_map(
        body,
        mesh=mesh,
        in_specs=placed,
        out_specs=(
            P("fsdp", "seq", None),
            P("fsdp", "seq", None),
            P("fsdp", "seq", None),
            P(None, None, ("seq", "fsdp"), None),
            P(None, ("seq", "fsdp"), None),
            P(("seq", "fsdp"), None),
            P(("seq", "fsdp"), None),
            P(None, ("seq", "fsdp")),
            P(("seq", "fsdp")),
            P(None, ("seq", "fsdp")),
            P(None, ("seq", "fsdp")),
        ),
        check_vma=False,
    )
```

profile of v0, /device:TPU:4, one launch (start us, length us, event | category | flops | bytes accessed | tf_op | source)
XLA Modules:
  0.0 2806.0 jit_solution(1418109932052115753)
XLA Ops:
  7.3 3.4 convert_element_type.279
  10.8 21.0 all_gather.58
  31.8 16.6 all_gather.59
  49.3 139.1 %all-gather.12.cloned.1.call-done = bf16[2,3,1024,1024]{3,2,1,0:T(8,128)(2,1)} async-done(((bf16[2,3,128,1024]{3,2,1,0:T(8,128)(2,1)}), bf16[2,3,1024,1024]{3,2,1,0:T(8,128)(2,1)}) %all-gather.12.cloned.1.call-update) | async-done | bytes 12582928 | tf_op jit(solution)/shard_map/all_gather | solution.py:226
  188.5 2.8 fusion.49
  191.4 26.0 all_gather.61
  218.0 2.8 fusion.52
  221.8 3.7 convert_element_type.299
  225.7 3.9 convert_element_type.303
  230.1 26.1 all_gather.72
  258.2 4.3 all-reduce
  262.5 5.0 all_gather.63
  272.1 5.4 all_gather.70
  279.7 5.9 all_gather.67
  293.3 2.5 fusion.150
  295.9 15.1 all-gather.18.cloned.1.call-done
  322.0 216.9 %all-gather.20.cloned.1.call-done = bf16[1024,8192]{1,0:T(8,128)(2,1)} async-done(((bf16[128,8192]{1,0:T(8,128)(2,1)}), bf16[1024,8192]{1,0:T(8,128)(2,1)}) %all-gather.20.cloned.1.call-update) | async-done | bytes 16777232 | tf_op jit(solution)/shard_map/all_gather | solution.py:228
  538.9 12.5 multiply_convert_fusion.1
  551.4 215.3 %all-gather.22.cloned.1.call-done = bf16[8192,1024]{1,0:T(8,128)(2,1)} async-done(((bf16[1024,1024]{1,0:T(8,128)(2,1)}), bf16[8192,1024]{1,0:T(8,128)(2,1)}) %all-gather.22.cloned.1.call-update) | async-done | bytes 16777232 | tf_op jit(solution)/shard_map/all_gather | solution.py:229
  766.7 12.2 fusion.6
  779.0 13.5 multiply_reduce_fusion
  795.0 3.2 fusion.47
  802.1 2.5 fusion.57
  806.9 3.7 multiply_reduce_fusion.1
  814.2 4.8 convolution_convert_fusion.2
  821.4 4.6 fusion.56
  837.8 2.5 convert_reduce_fusion.7
  840.5 3.3 fusion.14
  844.9 13.3 reduce-scatter.54.cloned.1.call-done
  858.2 3.3 fusion.12
  861.5 24.7 reduce-scatter.52.cloned.1.call-done
  886.3 2.9 fusion.143
  893.8 2.6 fusion.155
  896.6 2.7 fusion.118
  899.5 2.8 fusion.132
  902.6 5.5 reduce-scatter.56.cloned.1.call-done
  908.1 3.4 convolution_bitcast_fusion.1
  911.7 2.7 convolution_bitcast_fusion
  914.5 2.8 fusion.135
  917.4 2.8 fusion.129
  920.3 2.8 fusion.127
  923.2 4.0 all-gather.24.cloned.1.call-done
  927.2 59.7 %all-gather.26.cloned.1.call-done = bf16[512,8192]{1,0:T(8,128)(2,1)} async-done(((bf16[128,8192]{1,0:T(8,128)(2,1)}), bf16[512,8192]{1,0:T(8,128)(2,1)}) %all-gather.26.cloned.1.call-update) | async-done | bytes 8388624 | tf_op jit(solution)/shard_map/all_gather | solution.py:300
  986.9 7.8 convolution_convert_fusion
  995.1 10.1 all-gather.30.cloned.1.call-done
  1005.2 59.7 %all-gather.28.cloned.1.call-done = bf16[512,8192]{1,0:T(8,128)(2,1)} async-done(((bf16[128,8192]{1,0:T(8,128)(2,1)}), bf16[512,8192]{1,0:T(8,128)(2,1)}) %all-gather.28.cloned.1.call-update) | async-done | bytes 8388624 | tf_op jit(solution)/shard_map/all_gather | solution.py:301
  1065.0 6.2 convolution_convert_fusion.1
  1073.1 8.8 fusion.58
  1082.0 2.3 fusion.20
  1084.3 2.9 fusion.60
  1088.3 113.6 %reduce-scatter.64.cloned.1.call-done = f32[32,3]{1,0:T(8,128)} async-done(((f32[1024,3]{1,0:T(8,128)}), f32[32,3]{1,0:T(8,128)}) %reduce-scatter.64.cloned.1.call-update) | async-done | bytes 400
  1203.3 131.4 %reduce-scatter.62.cloned.1.call-done = f32[32,3]{1,0:T(8,128)} async-done(((f32[1024,3]{1,0:T(8,128)}), f32[32,3]{1,0:T(8,128)}) %reduce-scatter.62.cloned.1.call-update) | async-done | bytes 400
  1336.1 131.3 %reduce-scatter.60.cloned.1.call-done = f32[32,7]{1,0:T(8,128)} async-done(((f32[1024,7]{1,0:T(8,128)}), f32[32,7]{1,0:T(8,128)}) %reduce-scatter.60.cloned.1.call-update) | async-done | bytes 912
  1468.7 140.1 %reduce-scatter.46.cloned.1.call-done = f32[32,1024]{1,0:T(8,128)} async-done(((f32[1024,1024]{1,0:T(8,128)}), f32[32,1024]{1,0:T(8,128)}) %reduce-scatter.46.cloned.1.call-update) | async-done | bytes 131088 | tf_op jit(solution)/shard_map/reduce_scatter | solution.py:425
  1608.8 143.6 %reduce-scatter.44.cloned.1.call-done = f32[32,1024]{1,0:T(8,128)} async-done(((f32[1024,1024]{1,0:T(8,128)}), f32[32,1024]{1,0:T(8,128)}) %reduce-scatter.44.cloned.1.call-update) | async-done | bytes 131088 | tf_op jit(solution)/shard_map/reduce_scatter | solution.py:424
  1754.1 141.3 %reduce-scatter.38.cloned.1.call-done = f32[32,1024]{1,0:T(8,128)} async-done(((f32[1024,1024]{1,0:T(8,128)}), f32[32,1024]{1,0:T(8,128)}) %reduce-scatter.38.cloned.1.call-update) | async-done | bytes 131088 | tf_op jit(solution)/shard_map/reduce_scatter | solution.py:421
  1895.4 144.2 %reduce-scatter.40.cloned.1.call-done = f32[32,1024]{1,0:T(8,128)} async-done(((f32[1024,1024]{1,0:T(8,128)}), f32[32,1024]{1,0:T(8,128)}) %reduce-scatter.40.cloned.1.call-update) | async-done | bytes 131088 | tf_op jit(solution)/shard_map/reduce_scatter | solution.py:422
  2039.5 143.3 %reduce-scatter.42.cloned.1.call-done = f32[32,1024]{1,0:T(8,128)} async-done(((f32[1024,1024]{1,0:T(8,128)}), f32[32,1024]{1,0:T(8,128)}) %reduce-scatter.42.cloned.1.call-update) | async-done | bytes 131088 | tf_op jit(solution)/shard_map/reduce_scatter | solution.py:423
  2183.9 142.4 %reduce-scatter.32.cloned.1.call-done = f32[32,1024]{1,0:T(8,128)} async-done(((f32[1024,1024]{1,0:T(8,128)}), f32[32,1024]{1,0:T(8,128)}) %reduce-scatter.32.cloned.1.call-update) | async-done | bytes 131088 | tf_op jit(solution)/shard_map/reduce_scatter | solution.py:418
  2326.3 143.6 %reduce-scatter.34.cloned.1.call-done = f32[32,1024]{1,0:T(8,128)} async-done(((f32[1024,1024]{1,0:T(8,128)}), f32[32,1024]{1,0:T(8,128)}) %reduce-scatter.34.cloned.1.call-update) | async-done | bytes 131088 | tf_op jit(solution)/shard_map/reduce_scatter | solution.py:419
  2469.9 144.3 %reduce-scatter.36.cloned.1.call-done = f32[32,1024]{1,0:T(8,128)} async-done(((f32[1024,1024]{1,0:T(8,128)}), f32[32,1024]{1,0:T(8,128)}) %reduce-scatter.36.cloned.1.call-update) | async-done | bytes 131088 | tf_op jit(solution)/shard_map/reduce_scatter | solution.py:420
  2618.2 17.7 all-reduce.1
  2636.5 68.8 %reduce-scatter.48.cloned.1.call-done = bf16[32,8192]{1,0:T(8,128)(2,1)} async-done(((bf16[256,8192]{1,0:T(8,128)(2,1)}), bf16[32,8192]{1,0:T(8,128)(2,1)}) %reduce-scatter.48.cloned.1.call-update) | async-done | bytes 524304 | tf_op jit(solution)/shard_map/reduce_scatter | solution.py:307
  2707.4 89.1 %reduce-scatter.50.cloned.1.call-done = bf16[256,1024]{1,0:T(8,128)(2,1)} async-done(((bf16[2048,1024]{1,0:T(8,128)(2,1)}), bf16[256,1024]{1,0:T(8,128)(2,1)}) %reduce-scatter.50.cloned.1.call-update) | async-done | bytes 524304 | tf_op jit(solution)/shard_map/reduce_scatter | solution.py:313
  (321 shorter events, 80.9 us)
Async XLA Ops:
  7.2 262.9 %copy-start = (bf16[1,16,1024]{2,1,0:T(8,128)(2,1)S(1)}, bf16[1,16,1024]{2,1,0:T(8,128)(2,1)}, u32[]{:S(2)}) copy-start(bf16[1,16,1024]{2,1,0:T(8,128)(2,1)} %param.15) | copy-start | bytes 98308
  7.2 41.1 %copy-start.1 = (bf16[1,128,1024]{2,1,0:T(8,128)(2,1)S(1)}, bf16[1,128,1024]{2,1,0:T(8,128)(2,1)}, u32[]{:S(2)}) copy-start(bf16[1,128,1024]{2,1,0:T(8,128)(2,1)} %param.14) | copy-start | bytes 786436
  7.2 181.2 %all-gather.12.cloned.1.call-start = ((), (), s32[]{:S(2)}) async-start(), calls=%async_computation.17 | async-start | bytes 14155776 | tf_op jit(solution)/shard_map/all_gather | solution.py:226
  10.6 180.7 %copy-start.59 = (f32[7,128]{1,0:T(8,128)S(1)}, f32[7,128]{1,0:T(8,128)}, u32[]{:S(2)}) copy-start(f32[7,128]{1,0:T(8,128)} %param.24) | copy-start | bytes 10756
  10.7 275.9 %all-gather.16.cloned.1.call-start = ((), (), s32[]{:S(2)}) async-start(), calls=%async_computation.19 | async-start | bytes 1310720 | tf_op jit(solution)/shard_map/all_gather | solution.py:258
  48.4 172.4 %copy-start.22 = (f32[2,128,1024]{2,1,0:T(8,128)S(1)}, f32[2,128,1024]{2,1,0:T(8,128)}, u32[]{:S(2)}) copy-start(f32[2,128,1024]{2,1,0:T(8,128)} %param.21) | copy-start | bytes 3145732
  48.7 142.7 %copy-start.70 = (f32[128]{0:T(128)}, f32[128]{0:T(128)S(1)}, u32[]{:S(2)}) copy-start(f32[128]{0:T(128)S(1)} %fusion.77) | copy-start | bytes 1540
  48.7 219.1 %copy-start.42 = (f32[128]{0:T(128)}, f32[128]{0:T(128)S(1)}, u32[]{:S(2)}) copy-start(f32[128]{0:T(128)S(1)} %fusion.109) | copy-start | bytes 1540
  49.3 264.6 %copy-start.39 = (f32[1,1024]{1,0:T(1,128)}, f32[1,1024]{1,0:T(1,128)S(1)}, u32[]{:S(2)}) copy-start(f32[1,1024]{1,0:T(1,128)S(1)} %get-tuple-element.209) | copy-start | bytes 12292
  191.3 96.8 %all-gather.14.cloned.1.call-start = ((), (), s32[]{:S(2)}) async-start(), calls=%async_computation.18 | async-start | bytes 1310720 | tf_op jit(solution)/shard_map/all_gather | solution.py:259
  220.8 90.2 %all-gather.18.cloned.1.call-start = ((), (), s32[]{:S(2)}) async-start(), calls=%async_computation.20 | async-start | bytes 4718592 | tf_op jit(solution)/shard_map/all_gather | solution.py:227
  221.8 317.1 %all-gather.20.cloned.1.call-start = ((), (), s32[]{:S(2)}) async-start(), calls=%async_computation.21 | async-start | bytes 18874368 | tf_op jit(solution)/shard_map/all_gather | solution.py:228
  225.6 31.2 %copy-start.80 = (u32[32]{0:T(128)S(1)}, u32[32]{0:T(128)}, u32[]{:S(2)}) copy-start(u32[32]{0:T(128)} %constant.175) | copy-start | bytes 388
  225.6 32.5 %copy-start.78 = (s32[1,16]{1,0:T(1,128)S(1)}, s32[1,16]{1,0:T(1,128)}, u32[]{:S(2)}) copy-start(s32[1,16]{1,0:T(1,128)} %param.18) | copy-start | bytes 196
  225.6 36.8 %copy-start.53 = (s32[1,128]{1,0:T(1,128)S(1)}, s32[1,128]{1,0:T(1,128)}, u32[]{:S(2)}) copy-start(s32[1,128]{1,0:T(1,128)} %param.17) | copy-start | bytes 1540
  225.7 541.0 %all-gather.22.cloned.1.call-start = ((), (), s32[]{:S(2)}) async-start(), calls=%async_computation.22 | async-start | bytes 18874368 | tf_op jit(solution)/shard_map/all_gather | solution.py:229
  229.7 614.2 %reduce-scatter.58.cloned.1.call-start = ((), (), s32[]{:S(2)}) async-start(), calls=%async_computation.40 | async-start | bytes 163840
  270.1 20.3 copy-start.14
  295.9 18.1 copy-start.27
  316.6 234.8 %copy-start.16 = (f32[16,128,64]{1,2,0:T(8,128)}, f32[16,128,64]{1,2,0:T(8,128)S(1)}, u32[]{:S(2)}) copy-start(f32[16,128,64]{1,2,0:T(8,128)S(1)} %get-tuple-element.218) | copy-start | bytes 1572868
  322.0 444.7 %copy-start.10 = (bf16[1,128,1024]{2,1,0:T(8,128)(2,1)S(1)}, bf16[1,128,1024]{2,1,0:T(8,128)(2,1)}, u32[]{:S(2)}) copy-start(bf16[1,128,1024]{2,1,0:T(8,128)(2,1)} %param.16) | copy-start | bytes 786436
  766.7 12.2 copy-start.46
  766.7 12.2 copy-start.52
  778.9 13.5 copy-start.76
  795.0 9.6 copy-start.35
  804.6 6.0 copy-start.74
  804.6 6.0 copy-start.55
  804.6 6.0 copy-start.68
  804.6 6.3 copy-start.11
  804.6 6.3 copy-start.64
  813.9 44.3 %reduce-scatter.54.cloned.1.call-start = ((), (), s32[]{:S(2)}) async-start(), calls=%async_computation.38 | async-start | bytes 1310720
  814.2 7.2 copy-start.48
  821.3 64.9 %reduce-scatter.52.cloned.1.call-start = ((), (), s32[]{:S(2)}) async-start(), calls=%async_computation.37 | async-start | bytes 1310720
  833.1 75.1 %reduce-scatter.56.cloned.1.call-start = ((), (), s32[]{:S(2)}) async-start(), calls=%async_computation.39 | async-start | bytes 163840
  835.1 92.0 %all-gather.24.cloned.1.call-start = ((), (), s32[]{:S(2)}) async-start(), calls=%async_computation.31 | async-start | bytes 1310720 | tf_op jit(solution)/shard_map/all_gather | solution.py:299
  835.9 151.0 %all-gather.26.cloned.1.call-start = ((), (), s32[]{:S(2)}) async-start(), calls=%async_computation.32 | async-start | bytes 10485760 | tf_op jit(solution)/shard_map/all_gather | solution.py:300
  836.5 168.8 %all-gather.30.cloned.1.call-start = ((), (), s32[]{:S(2)}) async-start(), calls=%async_computation.36 | async-start | bytes 1310720 | tf_op jit(solution)/shard_map/all_gather | solution.py:302
  837.2 227.8 %all-gather.28.cloned.1.call-start = ((), (), s32[]{:S(2)}) async-start(), calls=%async_computation.34 | async-start | bytes 10485760 | tf_op jit(solution)/shard_map/all_gather | solution.py:301
  837.8 364.1 %reduce-scatter.64.cloned.1.call-start = ((), (), s32[]{:S(2)}) async-start(), calls=%async_computation.43 | async-start | bytes 540672
  840.3 48.8 %copy-start.31 = (bf16[16,64,128]{2,1,0:T(8,128)(2,1)}, bf16[16,64,128]{2,1,0:T(8,128)(2,1)S(1)}, u32[]{:S(2)}) copy-start(bf16[16,64,128]{2,1,0:T(8,128)(2,1)S(1)} %get-tuple-element.244) | copy-start | bytes 786436
  843.8 45.3 %copy-start.37 = (f32[1024]{0:T(1024)S(1)}, f32[1024]{0:T(1024)}, u32[]{:S(2)}) copy-start(f32[1024]{0:T(1024)} %get-tuple-element.162) | copy-start | bytes 12292
  843.8 45.3 %copy-start.58 = (f32[1024]{0:T(1024)S(1)}, f32[1024]{0:T(1024)}, u32[]{:S(2)}) copy-start(f32[1024]{0:T(1024)} %get-tuple-element.161) | copy-start | bytes 12292
  843.8 46.4 %copy-start.71 = (f32[128]{0:T(128)S(1)}, f32[128]{0:T(128)}, u32[]{:S(2)}) copy-start(f32[128]{0:T(128)} %copy-done.70) | copy-start | bytes 1540
  844.9 45.4 %copy-start.43 = (f32[128]{0:T(128)S(1)}, f32[128]{0:T(128)}, u32[]{:S(2)}) copy-start(f32[128]{0:T(128)} %copy-done.42) | copy-start | bytes 1540
  844.9 46.2 %copy-start.57 = (f32[1024]{0:T(1024)S(1)}, f32[1024]{0:T(1024)}, u32[]{:S(2)}) copy-start(f32[1024]{0:T(1024)} %get-tuple-element.153) | copy-start | bytes 12292
  861.5 30.8 %copy-start.30 = (bf16[128,1024]{1,0:T(8,128)(2,1)S(1)}, bf16[128,1024]{1,0:T(8,128)(2,1)}, u32[]{:S(2)}) copy-start(bf16[128,1024]{1,0:T(8,128)(2,1)} %reduce-scatter.54.cloned.1.call-done) | copy-start | bytes 786436
  861.5 32.3 %copy-start.18 = (bf16[16,64,128]{2,1,0:T(8,128)(2,1)S(1)}, bf16[16,64,128]{2,1,0:T(8,128)(2,1)}, u32[]{:S(2)}) copy-start(bf16[16,64,128]{2,1,0:T(8,128)(2,1)} %copy-done.17) | copy-start | bytes 786436
  861.5 32.3 %copy-start.26 = (bf16[128,1024]{1,0:T(8,128)(2,1)S(1)}, bf16[128,1024]{1,0:T(8,128)(2,1)}, u32[]{:S(2)}) copy-start(bf16[128,1024]{1,0:T(8,128)(2,1)} %copy-done.25) | copy-start | bytes 786436
  889.1 7.3 copy-start.6
  890.2 6.2 copy-start.61
  890.3 444.4 %reduce-scatter.62.cloned.1.call-start = ((), (), s32[]{:S(2)}) async-start(), calls=%async_computation.42 | async-start | bytes 540672
  892.2 575.1 %reduce-scatter.60.cloned.1.call-start = ((), (), s32[]{:S(2)}) async-start(), calls=%async_computation.41 | async-start | bytes 540672
  893.8 715.1 %reduce-scatter.46.cloned.1.call-start = ((), (), s32[]{:S(2)}) async-start(), calls=%async_computation.30 | async-start | bytes 4325376 | tf_op jit(solution)/shard_map/reduce_scatter | solution.py:425
  896.5 855.9 %reduce-scatter.44.cloned.1.call-start = ((), (), s32[]{:S(2)}) async-start(), calls=%async_computation.29 | async-start | bytes 4325376 | tf_op jit(solution)/shard_map/reduce_scatter | solution.py:424
  899.4 996.0 %reduce-scatter.38.cloned.1.call-start = ((), (), s32[]{:S(2)}) async-start(), calls=%async_computation.26 | async-start | bytes 4325376 | tf_op jit(solution)/shard_map/reduce_scatter | solution.py:421
  902.3 9.4 copy-start.33
  902.3 1137.2 %reduce-scatter.40.cloned.1.call-start = ((), (), s32[]{:S(2)}) async-start(), calls=%async_computation.27 | async-start | bytes 4325376 | tf_op jit(solution)/shard_map/reduce_scatter | solution.py:422
  911.6 1271.2 %reduce-scatter.42.cloned.1.call-start = ((), (), s32[]{:S(2)}) async-start(), calls=%async_computation.28 | async-start | bytes 4325376 | tf_op jit(solution)/shard_map/reduce_scatter | solution.py:423
  914.5 1411.8 %reduce-scatter.32.cloned.1.call-start = ((), (), s32[]{:S(2)}) async-start(), calls=%async_computation.23 | async-start | bytes 4325376 | tf_op jit(solution)/shard_map/reduce_scatter | solution.py:418
  917.3 1552.6 %reduce-scatter.34.cloned.1.call-start = ((), (), s32[]{:S(2)}) async-start(), calls=%async_computation.24 | async-start | bytes 4325376 | tf_op jit(solution)/shard_map/reduce_scatter | solution.py:419
  920.3 1694.0 %reduce-scatter.36.cloned.1.call-start = ((), (), s32[]{:S(2)}) async-start(), calls=%async_computation.25 | async-start | bytes 4325376 | tf_op jit(solution)/shard_map/reduce_scatter | solution.py:420
  923.2 1782.2 %reduce-scatter.48.cloned.1.call-start = ((), (), s32[]{:S(2)}) async-start(), calls=%async_computation.33 | async-start | bytes 4718592 | tf_op jit(solution)/shard_map/reduce_scatter | solution.py:307
  994.8 1801.7 %reduce-scatter.50.cloned.1.call-start = ((), (), s32[]{:S(2)}) async-start(), calls=%async_computation.35 | async-start | bytes 4718592 | tf_op jit(solution)/shard_map/reduce_scatter | solution.py:313
  1073.1 11.2 copy-start.36
  (44 other events, 132.1 us)
Sparse Core Ops, SparseCore 0:
  10.8 177.6 all-gather.11
  191.4 13.7 all-gather.15
  221.0 12.7 all-gather.13
  236.4 74.5 all-gather.17
  313.0 225.8 all-gather.19
  540.9 225.7 all-gather.21
  814.0 16.4 reduce-scatter.57
  833.2 24.9 reduce-scatter.53
  861.3 24.8 reduce-scatter.51
  888.7 19.4 reduce-scatter.55
  910.3 16.8 all-gather.23
  928.6 58.2 all-gather.25
  988.5 16.7 all-gather.29
  1006.7 58.2 all-gather.27
  1067.6 134.2 reduce-scatter.63
  1204.6 130.0 reduce-scatter.61
  1337.4 129.9 reduce-scatter.59
  1469.6 139.2 reduce-scatter.45
  1611.2 141.1 reduce-scatter.43
  1754.6 140.6 reduce-scatter.37
  1897.8 141.7 reduce-scatter.39
  2041.9 140.8 reduce-scatter.41
  2185.2 141.0 reduce-scatter.31
  2328.5 141.3 reduce-scatter.33
  2472.3 141.8 reduce-scatter.35
  2618.1 87.1 reduce-scatter.47
  2708.8 87.6 reduce-scatter.49
where the time goes:
time: 2810 us
  waiting for transfers between devices  2440 us (87%)
  matrix products  151 us (5%)
  blocking collectives  128 us (5%)
  local copies, waits for them, and re-layouts  32.7 us (1%)
  other arithmetic  31.8 us (1%)
    unnamed x34, waiting for transfers between devices  423 us
    all_gather x1, waiting for transfers between devices, body(): lax.all_gather(fc1.astype(jnp.bfloat16), 'fsdp', axis=0, tiled=True)  217 us
    all_gather x1, waiting for transfers between devices, body(): lax.all_gather(fc2.astype(jnp.bfloat16), 'fsdp', axis=0, tiled=True)  215 us
    reduce_scatter x1, waiting for transfers between devices, body(): lax.psum_scatter(grad_self_value, ('seq', 'fsdp'), scatter_dimension=0, t...  144 us
    reduce_scatter x1, waiting for transfers between devices, body(): lax.psum_scatter(grad_cross_key, ('seq', 'fsdp'), scatter_dimension=0, ti...  144 us
    reduce_scatter x1, waiting for transfers between devices, body(): lax.psum_scatter(grad_self_key, ('seq', 'fsdp'), scatter_dimension=0, til...  144 us
    reduce_scatter x1, waiting for transfers between devices, body(): lax.psum_scatter(grad_self_out, ('seq', 'fsdp'), scatter_dimension=0, til...  144 us
    reduce_scatter x1, waiting for transfers between devices, body(): lax.psum_scatter(grad_cross_value, ('seq', 'fsdp'), scatter_dimension=0,...  143 us
  transfers between devices with their start and end apart: 27, of which 24 were waited for; matrix products, arithmetic and copies ran while one was open for 5% of the time, Pallas kernels for 0%

commit v1 on v0

v1 whole, which is shorter than its diff:
```python
import math

import jax
import jax.numpy as jnp
from jax import lax
from jax.sharding import Mesh
from jax.sharding import PartitionSpec as P

HEADS = 16
EPSILON = 1e-05
NEGATIVE = -1e30
GELU_IN = math.sqrt(2.0 / math.pi)
GELU_CUBE = 0.044715
SEQ = ("y", "core")
FSDP = ("z", "x")
PLANE = ("y", "core", "x")
ALL = ("y", "core", "z", "x")
BF = jnp.bfloat16
F32 = jnp.float32


def matmul(left, right):
    return jnp.dot(left, right, preferred_element_type=F32)


def contract_rows(left, right):
    return lax.dot_general(left, right, (((0,), (0,)), ((), ())), preferred_element_type=F32)


def times_transpose(left, right):
    return lax.dot_general(left, right, (((1,), (1,)), ((), ())), preferred_element_type=F32)


def column_sums(values):
    return jnp.sum(values.astype(F32), axis=0)


def swap(value, axis, step):
    return lax.ppermute(value, axis, [(i, i ^ step) for i in range(lax.axis_size(axis))])


def norm_parts(values):
    centred = values - jnp.mean(values, axis=-1, keepdims=True)
    scale = lax.rsqrt(jnp.mean(centred * centred, axis=-1, keepdims=True) + EPSILON)
    return centred * scale, scale


def norm_back(normed, scale, gain, grad):
    inner = grad * gain
    means = jnp.mean(inner, axis=-1, keepdims=True)
    along = jnp.mean(inner * normed, axis=-1, keepdims=True)
    return (
        scale * (inner - means - normed * along),
        jnp.sum(grad * normed, axis=0),
        jnp.sum(grad, axis=0),
    )


def heads_first(values):
    return values.reshape(values.shape[0], HEADS, -1).transpose(1, 0, 2)


def heads_last(values):
    return values.transpose(1, 0, 2).reshape(values.shape[1], -1)


def batched(left, right, left_dim, right_dim):
    return lax.dot_general(
        left, right, (((left_dim,), (right_dim,)), ((0,), (0,))), preferred_element_type=F32
    )


def attend(queries, keys, values, allowed):
    score_scale = 1.0 / math.sqrt(queries.shape[2])
    scores = jnp.where(allowed[None], batched(queries, keys, 2, 2) * score_scale, NEGATIVE)
    top = jnp.max(scores, axis=-1, keepdims=True)
    raised = jnp.where(allowed[None], jnp.exp(scores - top), 0.0)
    chance = raised / jnp.maximum(jnp.sum(raised, axis=-1, keepdims=True), 1.0)
    return batched(chance.astype(BF), values, 2, 1), chance


def attend_back(queries, keys, values, chance, grad):
    score_scale = 1.0 / math.sqrt(queries.shape[2])
    chance_grad = batched(grad, values, 2, 2)
    delta = jnp.sum(chance * chance_grad, axis=-1, keepdims=True)
    score_grad = (chance * (chance_grad - delta)).astype(BF)
    return (
        batched(score_grad, keys, 2, 1) * score_scale,
        batched(score_grad, queries, 1, 1) * score_scale,
        batched(chance.astype(BF), grad, 1, 1),
    )


def body(
    hidden_in,
    memory,
    out_grad,
    segment_ids,
    memory_segments,
    deal,
    attn_in,
    attn_out,
    fc1,
    fc2,
    proj_bias,
    fc1_bias,
    norm_gain,
    norm_bias,
):
    y_size, z_size, x_size = lax.axis_size("y"), lax.axis_size("z"), lax.axis_size("x")
    s_size, f_size = y_size * 2, z_size * x_size
    y_place, core_place = lax.axis_index("y"), lax.axis_index("core")
    z_place = lax.axis_index("z")
    s_place = y_place * 2 + core_place
    f_place = z_place * x_size + lax.axis_index("x")
    place = s_place * f_size + f_place
    count = s_size * f_size
    tokens, width = hidden_in.shape[1:]
    sources_len = memory.shape[1]
    held = attn_in.shape[2]
    share = held // s_size

    wi_share = lax.dynamic_slice_in_dim(attn_in, s_place * share, share, 2).astype(BF)
    wo_share = lax.dynamic_slice_in_dim(attn_out, s_place * share, share, 1).astype(BF)
    small = jnp.concatenate(
        [
            proj_bias.reshape(-1).astype(BF),
            norm_gain.reshape(-1).astype(BF),
            norm_bias.reshape(-1).astype(BF),
            fc1_bias.astype(BF),
            segment_ids.reshape(-1).astype(BF),
            memory_segments.reshape(-1).astype(BF),
        ]
    )
    small_rows = -(-small.shape[0] // (16 * width)) * 16
    small = jnp.pad(small, (0, small_rows * width - small.shape[0])).reshape(small_rows, width)
    first = jnp.concatenate([wi_share[0].reshape(3 * share, width), small])
    second = jnp.concatenate([wi_share[1].reshape(3 * share, width), wo_share.reshape(2 * share, width)])
    first = lax.all_gather(first, ALL)
    second = lax.all_gather(second, ALL)

    def in_order(gathered, number):
        parts = gathered.reshape(s_size, f_size, number, share, width)
        return parts.transpose(2, 1, 0, 3, 4).reshape(number, width, width)

    w_self = in_order(first[:, : 3 * share], 3)
    w_rest = in_order(second, 5)
    small = first[:, 3 * share :].reshape(s_size, f_size, small_rows * width)
    by_fsdp = small[0]
    lane = width // f_size

    def columns(start, number):
        part = by_fsdp[:, start : start + number * lane].reshape(f_size, number, lane)
        return part.transpose(1, 0, 2).reshape(number, width).astype(F32)

    biases = columns(0, 7)
    gains = columns(7 * lane, 3)
    shifts = columns(10 * lane, 3)
    up_bias = by_fsdp[:, 13 * lane : 13 * lane + fc1_bias.shape[0]].reshape(-1).astype(F32)
    seg_start = 13 * lane + fc1_bias.shape[0]
    segs = lax.dynamic_index_in_dim(
        small[:, :, seg_start : seg_start + tokens + sources_len], f_place, 1, keepdims=False
    ).astype(jnp.int32)

    unit = fc2.shape[0] // s_size
    down_share = lax.dynamic_slice_in_dim(fc2, s_place * unit, unit, 0).astype(BF)
    down_share = lax.ppermute(
        down_share,
        ALL,
        [(s * f_size + f, f * s_size + s) for s in range(s_size) for f in range(f_size)],
    )
    w_down = lax.all_gather(down_share, PLANE, axis=0, tiled=True)
    up_share = lax.dynamic_slice_in_dim(fc1, s_place * share, share, 0).astype(BF)
    up_share = up_share.reshape(share, s_size, z_size, x_size, unit).transpose(2, 0, 1, 3, 4)
    hidden = s_size * x_size * unit
    up_share = up_share.reshape(z_size, share, hidden)
    up_parts = jnp.stack(
        [
            swap(lax.dynamic_index_in_dim(up_share, z_place ^ k, 0, keepdims=False), "z", k)
            if k
            else lax.dynamic_index_in_dim(up_share, z_place, 0, keepdims=False)
            for k in range(z_size)
        ]
    )
    up_parts = jnp.stack(
        [
            lax.dynamic_index_in_dim(up_parts, z_place ^ j, 0, keepdims=False)
            for j in range(z_size)
        ]
    )
    w_up = lax.all_gather(up_parts, PLANE).reshape(s_size, x_size, z_size, share, hidden)
    w_up = w_up.transpose(2, 1, 0, 3, 4).reshape(width, hidden)
    up_bias = lax.dynamic_index_in_dim(
        up_bias.reshape(s_size, z_size, x_size * unit), z_place, 1, keepdims=False
    ).reshape(hidden)

    down_grad = out_grad[0]
    down_all = jnp.concatenate([down_grad] + [swap(down_grad, "z", k) for k in range(1, z_size)])

    half_rows = tokens // 2
    offsets = jnp.arange(half_rows, dtype=jnp.int32)
    owners = jnp.stack([(y_place ^ k) * 2 + (core_place ^ c) for k in range(y_size) for c in range(2)])
    deal_pairs = deal.reshape(s_size, 2)
    key_pos = (deal_pairs[owners][:, :, None] * half_rows + offsets).reshape(-1)
    key_seg = segs[owners][:, :tokens].reshape(-1)
    query_pos = key_pos[:tokens]
    query_seg = segment_ids[0]
    source_seg = segs[:, tokens:].reshape(-1)
    real = query_seg[:, None] != 0
    self_allowed = (
        (query_seg[:, None] == key_seg[None]) & real & (key_pos[None] <= query_pos[:, None])
    )
    cross_allowed = (query_seg[:, None] == source_seg[None]) & real

    inputs = hidden_in[0].astype(F32)
    sources = memory[0]
    unit_one, scale_one = norm_parts(inputs)
    normed_one = (unit_one * gains[0] + shifts[0]).astype(BF)
    query_self = (matmul(normed_one, w_self[0]) + biases[0]).astype(BF)
    pair = jnp.concatenate(
        [
            matmul(normed_one, w_self[1]).astype(BF),
            (matmul(normed_one, w_self[2]) + biases[1]).astype(BF),
        ],
        axis=1,
    )
    pairs = []
    for k in range(y_size):
        mine = swap(pair, "y", k) if k else pair
        pairs += [mine, swap(mine, "core", 1)]
    pair_all = jnp.concatenate(pairs)
    query_heads = heads_first(query_self)
    key_heads = heads_first(pair_all[:, :width])
    value_heads = heads_first(pair_all[:, width:])
    self_mixed, self_chance = attend(query_heads, key_heads, value_heads, self_allowed)
    self_out = heads_last(self_mixed).astype(BF)
    after_self = inputs + matmul(self_out, w_rest[3]) + biases[2]

    source_pair = jnp.concatenate(
        [
            matmul(sources, w_rest[1]).astype(BF),
            (matmul(sources, w_rest[2]) + biases[4]).astype(BF),
        ],
        axis=1,
    )
    source_all = lax.all_gather(source_pair, SEQ, axis=0, tiled=True)
    unit_two, scale_two = norm_parts(after_self)
    normed_two = (unit_two * gains[1] + shifts[1]).astype(BF)
    query_cross = (matmul(normed_two, w_rest[0]) + biases[3]).astype(BF)
    query_cross_heads = heads_first(query_cross)
    source_key_heads = heads_first(source_all[:, :width])
    source_value_heads = heads_first(source_all[:, width:])
    cross_mixed, cross_chance = attend(
        query_cross_heads, source_key_heads, source_value_heads, cross_allowed
    )
    cross_out = heads_last(cross_mixed).astype(BF)
    after_cross = after_self + matmul(cross_out, w_rest[4]) + biases[5]

    unit_three, scale_three = norm_parts(after_cross)
    normed_three = (unit_three * gains[2] + shifts[2]).astype(BF)
    normed_all = jnp.concatenate(
        [normed_three] + [swap(normed_three, "z", k) for k in range(1, z_size)]
    )
    pre_act = matmul(normed_all, w_up) + up_bias
    bent = jnp.tanh(GELU_IN * (pre_act + GELU_CUBE * pre_act * pre_act * pre_act))
    activated = (0.5 * pre_act * (1.0 + bent)).astype(BF)
    slope = 0.5 * (1.0 + bent) + 0.5 * pre_act * (1.0 - bent * bent) * GELU_IN * (
        1.0 + 3.0 * GELU_CUBE * pre_act * pre_act
    )
    pre_grad = (times_transpose(down_all, w_down) * slope).astype(BF)

    def to_owners(partial):
        parts = partial.reshape(z_size, tokens, width)
        total = parts[0]
        for k in range(1, z_size):
            total = total + swap(parts[k].astype(BF), "z", k).astype(F32)
        return total

    normed_grad_three = to_owners(times_transpose(pre_grad, w_up))
    result = after_cross + to_owners(matmul(activated, w_down)) + biases[6]
    grad_up = contract_rows(normed_all, pre_grad).astype(BF)
    grad_down = contract_rows(activated, down_all).astype(BF)
    up_rows = width // count
    grad_up = grad_up.reshape(s_size, z_size, x_size, up_rows, hidden).transpose(0, 2, 1, 3, 4)
    grad_up = lax.psum_scatter(
        grad_up.reshape(s_size * x_size, z_size, up_rows, hidden), PLANE, scatter_dimension=0
    )
    grad_down = lax.psum_scatter(grad_down, PLANE, scatter_dimension=0, tiled=True).astype(F32)
    grad_up = jnp.stack(
        [
            swap(lax.dynamic_index_in_dim(grad_up, z_place ^ k, 0, keepdims=False), "z", k)
            if k
            else lax.dynamic_index_in_dim(grad_up, z_place, 0, keepdims=False)
            for k in range(z_size)
        ]
    )
    grad_up = jnp.stack(
        [lax.dynamic_index_in_dim(grad_up, z_place ^ j, 0, keepdims=False) for j in range(z_size)]
    )
    grad_up = grad_up.reshape(z_size, up_rows, s_size, x_size, unit).transpose(1, 2, 0, 3, 4)
    grad_up = grad_up.reshape(up_rows, -1).astype(F32)
    grad_up_bias = column_sums(pre_grad)

    result_grad = down_grad.astype(F32)
    moved, gain_three, shift_three = norm_back(unit_three, scale_three, gains[2], normed_grad_three)
    after_grad = result_grad + moved
    cross_branch = after_grad.astype(BF)
    cross_head_grad = times_transpose(cross_branch, w_rest[4]).astype(BF)
    query_cross_grad, source_key_grad, source_value_grad = attend_back(
        query_cross_heads,
        source_key_heads,
        source_value_heads,
        cross_chance,
        heads_first(cross_head_grad),
    )
    query_cross_grad = heads_last(query_cross_grad).astype(BF)
    source_grad = jnp.concatenate([heads_last(source_key_grad), heads_last(source_value_grad)], axis=1)
    source_grad = lax.psum_scatter(source_grad.astype(BF), SEQ, scatter_dimension=0, tiled=True)
    grad_memory = times_transpose(source_grad[:, :width], w_rest[1]) + times_transpose(
        source_grad[:, width:], w_rest[2]
    )
    normed_grad_two = times_transpose(query_cross_grad, w_rest[0])
    moved, gain_two, shift_two = norm_back(unit_two, scale_two, gains[1], normed_grad_two)
    self_grad = after_grad + moved

    def to_shares(grads):
        parts = [g.astype(BF).reshape(s_size, z_size, x_size, up_rows, width) for g in grads]
        parts = jnp.stack(parts, axis=3).transpose(0, 2, 1, 3, 4, 5)
        parts = parts.reshape(s_size * x_size, z_size, len(grads) * up_rows, width)
        parts = lax.psum_scatter(parts, PLANE, scatter_dimension=0)
        parts = lax.psum_scatter(parts, "z", scatter_dimension=0)
        return parts.reshape(len(grads), up_rows, width).astype(F32)

    cross_shares = to_shares(
        [
            contract_rows(normed_two, query_cross_grad),
            contract_rows(sources, source_grad[:, :width]),
            contract_rows(sources, source_grad[:, width:]),
            contract_rows(cross_out, cross_branch),
        ]
    )

    self_branch = self_grad.astype(BF)
    self_head_grad = times_transpose(self_branch, w_rest[3]).astype(BF)
    query_self_grad, key_grad, value_grad = attend_back(
        query_heads, key_heads, value_heads, self_chance, heads_first(self_head_grad)
    )
    query_self_grad = heads_last(query_self_grad).astype(BF)
    pair_grad = jnp.concatenate([heads_last(key_grad), heads_last(value_grad)], axis=1).astype(BF)
    pair_grad = pair_grad.reshape(y_size, 2, tokens, 2 * width)
    pair_grad = pair_grad[:, 0].astype(F32) + swap(pair_grad[:, 1], "core", 1).astype(F32)
    pair_sum = pair_grad[0]
    for k in range(1, y_size):
        pair_sum = pair_sum + swap(pair_grad[k].astype(BF), "y", k).astype(F32)
    key_self_grad = pair_sum[:, :width].astype(BF)
    value_self_grad = pair_sum[:, width:].astype(BF)
    self_shares = to_shares(
        [
            contract_rows(normed_one, query_self_grad),
            contract_rows(normed_one, key_self_grad),
            contract_rows(normed_one, value_self_grad),
            contract_rows(self_out, self_branch),
        ]
    )
    normed_grad_one = (
        times_transpose(query_self_grad, w_self[0])
        + times_transpose(key_self_grad, w_self[1])
        + times_transpose(value_self_grad, w_self[2])
    )
    moved, gain_one, shift_one = norm_back(unit_one, scale_one, gains[0], normed_grad_one)
    grad_hidden = self_grad + moved

    rows = [
        column_sums(query_self_grad),
        column_sums(value_self_grad),
        column_sums(self_branch),
        column_sums(query_cross_grad),
        column_sums(source_grad[:, width:]),
        column_sums(cross_branch),
        column_sums(down_grad),
        gain_one,
        gain_two,
        gain_three,
        shift_one,
        shift_two,
        shift_three,
    ]
    spread = jnp.zeros((s_size, z_size, x_size * unit), F32)
    spread = lax.dynamic_update_slice_in_dim(
        spread, grad_up_bias.reshape(s_size, 1, x_size * unit), z_place, 1
    )
    vector = lax.psum(jnp.concatenate(rows + [spread.reshape(-1)]), ALL)
    table = lax.dynamic_index_in_dim(
        vector[: len(rows) * width].reshape(len(rows), count, up_rows), place, 1, keepdims=False
    )
    grad_up_bias = lax.dynamic_slice_in_dim(vector[len(rows) * width :], place * unit, unit)
    return (
        result.astype(BF)[None],
        grad_hidden[None],
        grad_memory[None],
        jnp.stack([self_shares[:3], cross_shares[:3]]),
        jnp.stack([self_shares[3], cross_shares[3]]),
        grad_up,
        grad_down,
        table[:7],
        grad_up_bias,
        table[7:10],
        table[10:13],
    )


def solution(mesh):
    seq, fsdp = mesh.shape["seq"], mesh.shape["fsdp"]
    split = Mesh(mesh.devices.reshape(seq // 2, 2, 4, fsdp // 4), ALL)
    placed = (
        P(FSDP, SEQ, None),
        P(FSDP, SEQ, None),
        P(FSDP, SEQ, None),
        P(FSDP, SEQ),
        P(FSDP, SEQ),
        P(),
        P(None, None, FSDP, None),
        P(None, FSDP, None),
        P(FSDP, None),
        P(FSDP, None),
        P(None, FSDP),
        P(FSDP),
        P(None, FSDP),
        P(None, FSDP),
    )
    return jax.shard_map(
        body,
        mesh=split,
        in_specs=placed,
        out_specs=(
            P(FSDP, SEQ, None),
            P(FSDP, SEQ, None),
            P(FSDP, SEQ, None),
            P(None, None, ALL, None),
            P(None, ALL, None),
            P(ALL, None),
            P(ALL, None),
            P(None, ALL),
            P(ALL),
            P(None, ALL),
            P(None, ALL),
        ),
        check_vma=False,
    )
```

time: 2810 us -> 917 us (0.33)
  waiting for transfers between devices: 2440 us -> 613 us
  blocking collectives: 128 us -> 6.18 us
  local copies, waits for them, and re-layouts: 32.7 us -> 113 us
  matrix products: 151 us -> 85.7 us
  starting transfers between devices: 1.87 us -> 39.9 us
    reduce_scatter x10 -> x7, waiting for transfers between devices: 1300 us -> 226 us  [the longest x2 60.5 us: to_shares(): parts = lax.psum_scatter(parts, PLANE, scatter_dimension=0)]
    all_gather x10 -> x4, waiting for transfers between devices: 720 us -> 136 us  [the longest x1 79.2 us: body(): first = lax.all_gather(first, ALL)]
    unnamed x34 -> x12, waiting for transfers between devices: 423 us -> 0.83 us
    ppermute x0 -> x24, waiting for transfers between devices: none -> 128 us  [the longest x23 100 us: swap(): lax.ppermute(value, axis, [(i, i ^ step) for i in range(lax.axis_size(axi...]
    psum x0 -> x1, waiting for transfers between devices: none -> 123 us  [body(): vector = lax.psum(jnp.concatenate(rows + [spread.reshape(-1)]), ALL)]
    all_gather x7 -> x1, blocking collectives: 106 us -> 6.18 us  [body(): source_all = lax.all_gather(source_pair, SEQ, axis=0, tiled=True)]
    ppermute x0 -> x24, starting transfers between devices: none -> 38.9 us  [the longest x23 35.1 us: swap(): lax.ppermute(value, axis, [(i, i ^ step) for i in range(lax.axis_size(axi...]
    slice x3 -> x30, local copies, waits for them, and re-layouts: 1.23 us -> 33.2 us  [the longest x2 10.3 us: body(): after_cross = after_self + matmul(cross_out, w_rest[4]) + biases[5]]
  transfers between devices with their start and end apart: 27 -> 36, of which waited for: 24 -> 23; matrix products, arithmetic and copies ran while one was open for 5% -> 18% of each run, Pallas kernels for 0% -> 0%
where the time goes in v1:
time: 917 us; the launch traced here: 907 us
  waiting for transfers between devices  613 us (67%)
  local copies, waits for them, and re-layouts  113 us (12%)
  matrix products  85.7 us (9%)
  starting transfers between devices  39.9 us (4%)
  other arithmetic  32.8 us (4%)
  between operations  16.2 us (2%)
    psum x1, waiting for transfers between devices, body(): vector = lax.psum(jnp.concatenate(rows + [spread.reshape(-1)]), ALL)  123 us
    ppermute x23, waiting for transfers between devices, swap(): lax.ppermute(value, axis, [(i, i ^ step) for i in range(lax.axis_size(axi...  100 us
    all_gather x1, waiting for transfers between devices, body(): first = lax.all_gather(first, ALL)  79.2 us
    reduce_scatter x2, waiting for transfers between devices, to_shares(): parts = lax.psum_scatter(parts, PLANE, scatter_dimension=0)  60.5 us
    reduce_scatter x1, waiting for transfers between devices, body(): lax.psum_scatter(grad_up.reshape(s_size * x_size, z_size, up_rows, hidden...  56 us
    all_gather x1, waiting for transfers between devices, body(): second = lax.all_gather(second, ALL)  48 us
    reduce_scatter x2, waiting for transfers between devices, to_shares(): parts = lax.psum_scatter(parts, 'z', scatter_dimension=0)  47.1 us
    reduce_scatter x1, waiting for transfers between devices, body(): lax.psum_scatter(grad_down, PLANE, scatter_dimension=0, tiled=True)  45.8 us
  transfers between devices with their start and end apart: 36, of which 23 were waited for; matrix products, arithmetic and copies ran while one was open for 18% of the time, Pallas kernels for 0%

profile of v1, /device:TPU:4, one launch (start us, length us, event | category | flops | bytes accessed | tf_op | source)
XLA Modules:
  0.0 907.3 jit_solution(6491080370000628320)
XLA Ops:
  7.3 2.2 dynamic-slice_convert_fusion.1
  9.5 2.2 reshape.761
  11.7 2.2 copy.172
  13.9 2.2 reshape.762
  19.0 2.6 collective-permute-start.7
  21.8 2.4 collective-permute-done.6
  24.2 7.7 collective-permute-done.7
  41.7 3.8 collective-permute-start.9
  46.9 28.0 %collective-permute-done.9 = bf16[256,1024]{1,0:T(8,128)(2,1)S(1)} collective-permute-done((bf16[256,1024]{1,0:T(8,128)(2,1)S(1)}, bf16[256,1024]{1,0:T(8,128)(2,1)S(1)}, u32[]{:S(2)}, u32[]{:S(2)}) %collective-permute-start.9) | collective-permute-done | bytes 524320 | tf_op jit(solution)/shard_map/ppermute | solution.py:167
  75.8 8.4 all-gather.14.cloned.1.call-done
  84.2 4.8 copy.132
  88.9 79.2 %all-gather.10.cloned.1.call-done = bf16[3584,1024]{1,0:T(8,128)(2,1)} async-done(((bf16[112,1024]{1,0:T(8,128)(2,1)}), bf16[3584,1024]{1,0:T(8,128)(2,1)}) %all-gather.10.cloned.1.call-update) | async-done | bytes 7340048 | tf_op jit(solution)/shard_map/all_gather | solution.py:139
  169.3 3.6 slice.345
  172.9 2.1 fusion.112
  183.8 10.2 %collective-permute-done.1 = bf16[128,2048]{1,0:T(8,128)(2,1)} collective-permute-done((bf16[128,2048]{1,0:T(8,128)(2,1)}, bf16[128,2048]{1,0:T(8,128)(2,1)}, u32[]{:S(2)}, u32[]{:S(2)}) %collective-permute-start.1) | collective-permute-done | bytes 524320 | tf_op jit(solution)/shard_map/ppermute | solution.py:39
  196.3 3.0 pad_maximum_fusion
  203.8 3.8 fusion.118
  207.6 3.1 convolution_convert_fusion.15
  210.7 48.0 %all-gather.12.cloned.1.call-done = bf16[5120,1024]{1,0:T(8,128)(2,1)} async-done(((bf16[160,1024]{1,0:T(8,128)(2,1)}), bf16[5120,1024]{1,0:T(8,128)(2,1)}) %all-gather.12.cloned.1.call-update) | async-done | bytes 10485776 | tf_op jit(solution)/shard_map/all_gather | solution.py:140
  258.7 7.1 fusion.111
  272.8 6.2 all_gather.28
  282.7 3.2 copy.130
  289.4 2.1 fusion.121
  298.4 8.6 collective-permute-done.3
  308.7 13.1 %collective-permute-done.4 = bf16[128,1024]{1,0:T(8,128)(2,1)} collective-permute-done((bf16[128,1024]{1,0:T(8,128)(2,1)}, bf16[128,1024]{1,0:T(8,128)(2,1)}, u32[]{:S(2)}, u32[]{:S(2)}) %collective-permute-start.4) | collective-permute-done | bytes 262176 | tf_op jit(solution)/shard_map/ppermute | solution.py:39
  321.8 6.9 fusion.79
  328.8 8.4 convert_reduce_fusion
  337.3 2.4 fusion.122
  339.7 6.2 collective-permute-start.16
  348.4 3.0 fusion.123
  354.1 3.4 collective-permute-done.16
  357.4 2.8 collective-permute-start.12
  360.3 7.1 collective-permute-done.17
  369.6 20.0 %collective-permute-done.11 = bf16[128,1024]{1,0:T(8,128)(2,1)S(1)} collective-permute-done((bf16[128,1024]{1,0:T(8,128)(2,1)S(1)}, bf16[128,1024]{1,0:T(8,128)(2,1)S(1)}, u32[]{:S(2)}, u32[]{:S(2)}) %collective-permute-start.11) | collective-permute-done | bytes 262176 | tf_op jit(solution)/shard_map/ppermute | solution.py:39
  397.1 2.3 fusion.28
  407.5 2.2 convolution_convert_fusion.5
  409.6 16.2 %reduce-scatter.8.cloned.1.call-done = bf16[16,2048]{1,0:T(8,128)(2,1)} async-done(((bf16[64,2048]{1,0:T(8,128)(2,1)}), bf16[16,2048]{1,0:T(8,128)(2,1)}) %reduce-scatter.8.cloned.1.call-update) | async-done | bytes 65552 | tf_op jit(solution)/shard_map/reduce_scatter | solution.py:318
  429.0 3.8 maximum_bitcast_fusion.1
  432.8 8.5 copy.142
  444.4 3.5 multiply_reduce_fusion
  450.3 2.3 concatenate.67
  452.6 3.8 copy.137
  456.4 4.3 fusion.13
  460.7 2.1 concatenate.68
  462.8 3.7 copy.138
  471.0 2.1 collective-permute-start.20
  474.7 22.2 %collective-permute-done.20 = bf16[128,2048]{1,0:T(8,128)(2,1)S(1)} collective-permute-done((bf16[128,2048]{1,0:T(8,128)(2,1)S(1)}, bf16[128,2048]{1,0:T(8,128)(2,1)S(1)}, u32[]{:S(2)}, u32[]{:S(2)}) %collective-permute-start.20) | collective-permute-done | bytes 524320 | tf_op jit(solution)/shard_map/ppermute | solution.py:39
  498.7 3.8 maximum_bitcast_fusion
  502.6 8.8 copy.141
  515.1 2.5 convolution_add_fusion.1
  520.4 4.3 convolution_convert_fusion.1
  524.7 2.3 copy.143
  527.7 7.8 convolution_convert_fusion
  536.3 3.0 fusion.87
  539.3 60.5 %reduce-scatter.10.cloned.1.call-done = bf16[1,4,128,1024]{3,2,1,0:T(8,128)(2,1)} async-done(((bf16[8,4,128,1024]{3,2,1,0:T(8,128)(2,1)}), bf16[1,4,128,1024]{3,2,1,0:T(8,128)(2,1)}) %reduce-scatter.10.cloned.1.call-update) | async-done | bytes 1048592 | tf_op jit(solution)/shard_map/reduce_scatter | solution.py:330
  601.1 2.1 fusion.51
  603.2 123.3 %all-reduce.3.cloned.1.call-done = f32[21504]{0:T(1024)} async-done(((f32[21504]{0:T(1024)}), f32[21504]{0:T(1024)}) %all-reduce.3.cloned.1.call-update) | async-done | bytes 86032 | tf_op jit(solution)/shard_map/psum | solution.py:392
  727.4 56.0 %reduce-scatter.18.cloned.1.call-done = bf16[1,4,32,2048]{3,2,1,0:T(8,128)(2,1)} async-done(((bf16[8,4,32,2048]{3,2,1,0:T(8,128)(2,1)}), bf16[1,4,32,2048]{3,2,1,0:T(8,128)(2,1)}) %reduce-scatter.18.cloned.1.call-update) | async-done | bytes 524304 | tf_op jit(solution)/shard_map/reduce_scatter | solution.py:285
  786.1 2.4 collective-permute-start.22
  792.2 45.8 %reduce-scatter.20.cloned.1.call-done = bf16[256,1024]{1,0:T(8,128)(2,1)} async-done(((bf16[2048,1024]{1,0:T(8,128)(2,1)}), bf16[256,1024]{1,0:T(8,128)(2,1)}) %reduce-scatter.20.cloned.1.call-update) | async-done | bytes 524304 | tf_op jit(solution)/shard_map/reduce_scatter | solution.py:288
  838.0 2.1 convert_element_type.444
  842.8 3.2 reshape.779
  846.0 21.6 %reduce-scatter.16.cloned.1.call-done = bf16[1,128,1024]{2,1,0:T(8,128)(2,1)} async-done(((bf16[4,128,1024]{2,1,0:T(8,128)(2,1)}), bf16[1,128,1024]{2,1,0:T(8,128)(2,1)}) %reduce-scatter.16.cloned.1.call-update) | async-done | bytes 262160 | tf_op jit(solution)/shard_map/reduce_scatter | solution.py:331
  870.1 25.5 %reduce-scatter.12.cloned.1.call-done = bf16[1,128,1024]{2,1,0:T(8,128)(2,1)} async-done(((bf16[4,128,1024]{2,1,0:T(8,128)(2,1)}), bf16[1,128,1024]{2,1,0:T(8,128)(2,1)}) %reduce-scatter.12.cloned.1.call-update) | async-done | bytes 262160 | tf_op jit(solution)/shard_map/reduce_scatter | solution.py:331
  (373 shorter events, 119.0 us)
Async XLA Ops:
  7.2 27.3 %copy-start = (f32[2,3,128,1024]{3,2,1,0:T(8,128)S(1)}, f32[2,3,128,1024]{3,2,1,0:T(8,128)}, u32[]{:S(2)}) copy-start(f32[2,3,128,1024]{3,2,1,0:T(8,128)} %param.20) | copy-start | bytes 9437188
  7.2 77.0 %all-gather.14.cloned.1.call-start = ((), (), s32[]{:S(2)}) async-start(), calls=%async_computation.18 | async-start | bytes 4718592 | tf_op jit(solution)/shard_map/all_gather | solution.py:191
  17.2 15.7 %copy-start.58 = (f32[1024]{0:T(1024)S(1)}, f32[1024]{0:T(1024)}, u32[]{:S(2)}) copy-start(f32[1024]{0:T(1024)} %param.25) | copy-start | bytes 12292
  17.3 15.7 %copy-start.59 = (f32[7,128]{1,0:T(8,128)S(1)}, f32[7,128]{1,0:T(8,128)}, u32[]{:S(2)}) copy-start(f32[7,128]{1,0:T(8,128)} %param.24) | copy-start | bytes 10756
  17.3 16.0 %copy-start.61 = (f32[3,128]{1,0:T(4,128)S(1)}, f32[3,128]{1,0:T(4,128)}, u32[]{:S(2)}) copy-start(f32[3,128]{1,0:T(4,128)} %param.26) | copy-start | bytes 4612
  17.3 16.2 %copy-start.62 = (f32[3,128]{1,0:T(4,128)S(1)}, f32[3,128]{1,0:T(4,128)}, u32[]{:S(2)}) copy-start(f32[3,128]{1,0:T(4,128)} %param.27) | copy-start | bytes 4612
  17.3 16.7 %copy-start.60 = (s32[1,128]{1,0:T(1,128)S(1)}, s32[1,128]{1,0:T(1,128)}, u32[]{:S(2)}) copy-start(s32[1,128]{1,0:T(1,128)} %param.17) | copy-start | bytes 1540
  17.3 16.9 %copy-start.65 = (s32[1,16]{1,0:T(1,128)S(1)}, s32[1,16]{1,0:T(1,128)}, u32[]{:S(2)}) copy-start(s32[1,16]{1,0:T(1,128)} %param.18) | copy-start | bytes 196
  17.3 6.9 collective-permute-start.6
  19.0 12.9 %collective-permute-start.7 = (bf16[32,2048]{1,0:T(8,128)(2,1)S(1)}, bf16[32,2048]{1,0:T(8,128)(2,1)S(1)}, u32[]{:S(2)}, u32[]{:S(2)}) collective-permute-start(bf16[32,2048]{1,0:T(8,128)(2,1)S(1)} %get-tuple-element.59), channel_id=1, source_target_pairs={{0,4},{2,6},{4,0},{6,2},{1,5},{3,7},{5,1},{7,3},{8,12},{10,14},{12... | collective-permute-start | bytes 393224 | tf_op jit(solution)/shard_map/ppermute | solution.py:39
  21.5 10.3 %collective-permute-start.8 = (bf16[32,2048]{1,0:T(8,128)(2,1)S(1)}, bf16[32,2048]{1,0:T(8,128)(2,1)S(1)}, u32[]{:S(2)}, u32[]{:S(2)}) collective-permute-start(bf16[32,2048]{1,0:T(8,128)(2,1)S(1)} %get-tuple-element.58), channel_id=1, source_target_pairs={{0,6},{2,4},{4,2},{6,0},{1,7},{3,5},{5,3},{7,1},{8,14},{10,12},{12... | collective-permute-start | bytes 393224 | tf_op jit(solution)/shard_map/ppermute | solution.py:39
  32.9 135.2 %all-gather.10.cloned.1.call-start = ((), (), s32[]{:S(2)}) async-start(), calls=%async_computation.16 | async-start | bytes 7569408 | tf_op jit(solution)/shard_map/all_gather | solution.py:139
  34.5 11.0 %copy-start.63 = (s32[8]{0:T(128)S(1)}, s32[8]{0:T(128)}, u32[]{:S(2)}) copy-start(s32[8]{0:T(128)} %param.19) | copy-start | bytes 100
  34.6 12.0 %copy-start.8 = (bf16[1,128,1024]{2,1,0:T(8,128)(2,1)S(1)}, bf16[1,128,1024]{2,1,0:T(8,128)(2,1)}, u32[]{:S(2)}) copy-start(bf16[1,128,1024]{2,1,0:T(8,128)(2,1)} %param.14) | copy-start | bytes 786436
  35.3 223.4 %all-gather.12.cloned.1.call-start = ((), (), s32[]{:S(2)}) async-start(), calls=%async_computation.17 | async-start | bytes 10813440 | tf_op jit(solution)/shard_map/all_gather | solution.py:140
  37.1 291.6 %all-gather.8.cloned.1.call-start = ((), (), s32[]{:S(2)}) async-start(), calls=%async_computation.7 | async-start | bytes 4718592 | tf_op jit(solution)/shard_map/all_gather | solution.py:172
  37.2 291.6 %collective-permute-start.13 = (bf16[128,1024]{1,0:T(8,128)(2,1)}, bf16[128,1024]{1,0:T(8,128)(2,1)}, u32[]{:S(2)}, u32[]{:S(2)}) collective-permute-start(bf16[128,1024]{1,0:T(8,128)(2,1)} %bitcast.85), channel_id=1, source_target_pairs={{0,2},{2,0},{4,6},{6,4},{1,3},{3,1},{5,7},{7,5},{8,10},{10,8},{12,... | collective-permute-start | bytes 786440 | tf_op jit(solution)/shard_map/ppermute | solution.py:39
  39.2 289.5 %collective-permute-start.14 = (bf16[128,1024]{1,0:T(8,128)(2,1)}, bf16[128,1024]{1,0:T(8,128)(2,1)}, u32[]{:S(2)}, u32[]{:S(2)}) collective-permute-start(bf16[128,1024]{1,0:T(8,128)(2,1)} %bitcast.85), channel_id=1, source_target_pairs={{0,4},{2,6},{4,0},{6,2},{1,5},{3,7},{5,1},{7,3},{8,12},{10,14},{12... | collective-permute-start | bytes 786440 | tf_op jit(solution)/shard_map/ppermute | solution.py:39
  41.7 33.2 %collective-permute-start.9 = (bf16[256,1024]{1,0:T(8,128)(2,1)S(1)}, bf16[256,1024]{1,0:T(8,128)(2,1)S(1)}, u32[]{:S(2)}, u32[]{:S(2)}) collective-permute-start(bf16[256,1024]{1,0:T(8,128)(2,1)S(1)} %dynamic-slice_convert_fusion), channel_id=1, source_target_pairs={{0,0},{1,4},{2,8},{3,12},{4,16},{5,20},{6,24},{7,28},{8,1},{9,5},{... | collective-permute-start | bytes 1572872 | tf_op jit(solution)/shard_map/ppermute | solution.py:167
  46.9 136.4 %copy-start.46 = (f32[128]{0:T(128)}, f32[128]{0:T(128)S(1)}, u32[]{:S(2)}) copy-start(f32[128]{0:T(128)S(1)} %add_rsqrt_fusion.2) | copy-start | bytes 1540
  75.7 350.1 %reduce-scatter.8.cloned.1.call-start = ((), (), s32[]{:S(2)}) async-start(), calls=%async_computation.8 | async-start | bytes 327680 | tf_op jit(solution)/shard_map/reduce_scatter | solution.py:318
  178.1 15.9 %collective-permute-start.1 = (bf16[128,2048]{1,0:T(8,128)(2,1)}, bf16[128,2048]{1,0:T(8,128)(2,1)}, u32[]{:S(2)}, u32[]{:S(2)}) collective-permute-start(bf16[128,2048]{1,0:T(8,128)(2,1)} %pad_maximum_fusion.5), channel_id=1, source_target_pairs={{0,16},{16,0},{1,17},{17,1},{2,18},{18,2},{3,19},{19,3},{4,20},{20... | collective-permute-start | bytes 1572872 | tf_op jit(solution)/shard_map/ppermute | solution.py:39
  178.7 15.9 %collective-permute-start = (bf16[128,2048]{1,0:T(8,128)(2,1)}, bf16[128,2048]{1,0:T(8,128)(2,1)}, u32[]{:S(2)}, u32[]{:S(2)}) collective-permute-start(bf16[128,2048]{1,0:T(8,128)(2,1)} %pad_maximum_fusion.5), channel_id=1, source_target_pairs={{0,8},{8,0},{1,9},{9,1},{2,10},{10,2},{3,11},{11,3},{4,12},{12,4},... | collective-permute-start | bytes 1572872 | tf_op jit(solution)/shard_map/ppermute | solution.py:39
  182.7 16.7 %copy-start.17 = (bf16[1,8,4,32,1024]{4,3,2,1,0:T(8,128)(2,1)}, bf16[1,8,4,32,1024]{4,3,2,1,0:T(8,128)(2,1)S(1)}, u32[]{:S(2)}) copy-start(bf16[1,8,4,32,1024]{4,3,2,1,0:T(8,128)(2,1)S(1)} %copy.117) | copy-start | bytes 6291460
  194.1 2.3 collective-permute-start.2
  194.3 9.6 %copy-start.35 = (bf16[128,1024]{0,1:T(8,128)(2,1)}, bf16[128,1024]{0,1:T(8,128)(2,1)S(1)}, u32[]{:S(2)}) copy-start(bf16[128,1024]{0,1:T(8,128)(2,1)S(1)} %copy.118) | copy-start | bytes 786436
  202.5 5.1 copy-start.27
  210.7 55.5 %copy-start.37 = (bf16[16,128,64]{1,2,0:T(8,128)(2,1)}, bf16[16,128,64]{1,2,0:T(8,128)(2,1)S(1)}, u32[]{:S(2)}) copy-start(bf16[16,128,64]{1,2,0:T(8,128)(2,1)S(1)} %convolution_convert_fusion.15) | copy-start | bytes 786436
  280.8 5.1 copy-start.34
  293.2 13.7 %collective-permute-start.3 = (bf16[128,1024]{1,0:T(8,128)(2,1)}, bf16[128,1024]{1,0:T(8,128)(2,1)}, u32[]{:S(2)}, u32[]{:S(2)}) collective-permute-start(bf16[128,1024]{1,0:T(8,128)(2,1)} %add_convert_fusion), channel_id=1, source_target_pairs={{0,2},{2,0},{4,6},{6,4},{1,3},{3,1},{5,7},{7,5},{8,10},{10,8},{12,... | collective-permute-start | bytes 786440 | tf_op jit(solution)/shard_map/ppermute | solution.py:39
  294.5 27.3 %collective-permute-start.4 = (bf16[128,1024]{1,0:T(8,128)(2,1)}, bf16[128,1024]{1,0:T(8,128)(2,1)}, u32[]{:S(2)}, u32[]{:S(2)}) collective-permute-start(bf16[128,1024]{1,0:T(8,128)(2,1)} %add_convert_fusion), channel_id=1, source_target_pairs={{0,4},{2,6},{4,0},{6,2},{1,5},{3,7},{5,1},{7,3},{8,12},{10,14},{12... | collective-permute-start | bytes 786440 | tf_op jit(solution)/shard_map/ppermute | solution.py:39
  295.7 26.2 %collective-permute-start.5 = (bf16[128,1024]{1,0:T(8,128)(2,1)}, bf16[128,1024]{1,0:T(8,128)(2,1)}, u32[]{:S(2)}, u32[]{:S(2)}) collective-permute-start(bf16[128,1024]{1,0:T(8,128)(2,1)} %add_convert_fusion), channel_id=1, source_target_pairs={{0,6},{2,4},{4,2},{6,0},{1,7},{3,5},{5,3},{7,1},{8,14},{10,12},{12... | collective-permute-start | bytes 786440 | tf_op jit(solution)/shard_map/ppermute | solution.py:39
  298.4 50.1 %copy-start.50 = (f32[4,1,512]{2,1,0:T(1,128)}, f32[4,1,512]{2,1,0:T(1,128)S(1)}, u32[]{:S(2)}) copy-start(f32[4,1,512]{2,1,0:T(1,128)S(1)} %constant_dynamic-slice_fusion.7) | copy-start | bytes 24580
  306.9 21.8 %collective-permute-start.15 = (bf16[128,1024]{1,0:T(8,128)(2,1)}, bf16[128,1024]{1,0:T(8,128)(2,1)}, u32[]{:S(2)}, u32[]{:S(2)}) collective-permute-start(bf16[128,1024]{1,0:T(8,128)(2,1)} %bitcast.85), channel_id=1, source_target_pairs={{0,6},{2,4},{4,2},{6,0},{1,7},{3,5},{5,3},{7,1},{8,14},{10,12},{12... | collective-permute-start | bytes 786440 | tf_op jit(solution)/shard_map/ppermute | solution.py:39
  328.8 8.5 copy-start.26
  337.3 11.2 %copy-start.64 = (bf16[2048,1024]{1,0:T(8,128)(2,1)S(1)}, bf16[2048,1024]{1,0:T(8,128)(2,1)}, u32[]{:S(2)}) copy-start(bf16[2048,1024]{1,0:T(8,128)(2,1)} %all-gather.8.cloned.1.call-done) | copy-start | bytes 12582916
  337.3 11.2 %copy-start.67 = (f32[512,2048]{1,0:T(8,128)S(1)}, f32[512,2048]{1,0:T(8,128)}, u32[]{:S(2)}) copy-start(f32[512,2048]{1,0:T(8,128)} %fusion.79) | copy-start | bytes 12582916
  339.7 17.7 %collective-permute-start.16 = (bf16[128,1024]{1,0:T(8,128)(2,1)S(1)}, bf16[128,1024]{1,0:T(8,128)(2,1)S(1)}, u32[]{:S(2)}, u32[]{:S(2)}) collective-permute-start(bf16[128,1024]{1,0:T(8,128)(2,1)S(1)} %get-tuple-element.38), channel_id=1, source_target_pairs={{0,2},{2,0},{4,6},{6,4},{1,3},{3,1},{5,7},{7,5},{8,10},{10,8},{12,... | collective-permute-start | bytes 786440 | tf_op jit(solution)/shard_map/ppermute | solution.py:39
  346.0 21.4 %collective-permute-start.17 = (bf16[128,1024]{1,0:T(8,128)(2,1)S(1)}, bf16[128,1024]{1,0:T(8,128)(2,1)S(1)}, u32[]{:S(2)}, u32[]{:S(2)}) collective-permute-start(bf16[128,1024]{1,0:T(8,128)(2,1)S(1)} %get-tuple-element.40), channel_id=1, source_target_pairs={{0,4},{2,6},{4,0},{6,2},{1,5},{3,7},{5,1},{7,3},{8,12},{10,14},{12... | collective-permute-start | bytes 786440 | tf_op jit(solution)/shard_map/ppermute | solution.py:39
  346.5 20.9 %copy-start.10 = (f32[128,1024]{1,0:T(8,128)S(1)}, f32[128,1024]{1,0:T(8,128)}, u32[]{:S(2)}) copy-start(f32[128,1024]{1,0:T(8,128)} %copy-done.9) | copy-start | bytes 1572868
  346.5 20.9 %copy-start.53 = (f32[128]{0:T(128)S(1)}, f32[128]{0:T(128)}, u32[]{:S(2)}) copy-start(f32[128]{0:T(128)} %copy-done.52) | copy-start | bytes 1540
  346.5 20.9 %copy-start.57 = (f32[128]{0:T(128)S(1)}, f32[128]{0:T(128)}, u32[]{:S(2)}) copy-start(f32[128]{0:T(128)} %copy-done.56) | copy-start | bytes 1540
  346.5 20.9 %collective-permute-start.18 = (bf16[128,1024]{1,0:T(8,128)(2,1)S(1)}, bf16[128,1024]{1,0:T(8,128)(2,1)S(1)}, u32[]{:S(2)}, u32[]{:S(2)}) collective-permute-start(bf16[128,1024]{1,0:T(8,128)(2,1)S(1)} %get-tuple-element.39), channel_id=1, source_target_pairs={{0,6},{2,4},{4,2},{6,0},{1,7},{3,5},{5,3},{7,1},{8,14},{10,12},{12... | collective-permute-start | bytes 786440 | tf_op jit(solution)/shard_map/ppermute | solution.py:39
  351.4 38.2 %copy-start.45 = (f32[1024]{0:T(1024)S(1)}, f32[1024]{0:T(1024)}, u32[]{:S(2)}) copy-start(f32[1024]{0:T(1024)} %get-tuple-element.70) | copy-start | bytes 12292
  351.5 18.1 %collective-permute-start.10 = (bf16[128,1024]{1,0:T(8,128)(2,1)S(1)}, bf16[128,1024]{1,0:T(8,128)(2,1)S(1)}, u32[]{:S(2)}, u32[]{:S(2)}) collective-permute-start(bf16[128,1024]{1,0:T(8,128)(2,1)S(1)} %get-tuple-element.41), channel_id=1, source_target_pairs={{0,2},{2,0},{4,6},{6,4},{1,3},{3,1},{5,7},{7,5},{8,10},{10,8},{12,... | collective-permute-start | bytes 786440 | tf_op jit(solution)/shard_map/ppermute | solution.py:39
  352.6 37.0 %collective-permute-start.11 = (bf16[128,1024]{1,0:T(8,128)(2,1)S(1)}, bf16[128,1024]{1,0:T(8,128)(2,1)S(1)}, u32[]{:S(2)}, u32[]{:S(2)}) collective-permute-start(bf16[128,1024]{1,0:T(8,128)(2,1)S(1)} %get-tuple-element.43), channel_id=1, source_target_pairs={{0,4},{2,6},{4,0},{6,2},{1,5},{3,7},{5,1},{7,3},{8,12},{10,14},{12... | collective-permute-start | bytes 786440 | tf_op jit(solution)/shard_map/ppermute | solution.py:39
  357.4 32.2 %collective-permute-start.12 = (bf16[128,1024]{1,0:T(8,128)(2,1)S(1)}, bf16[128,1024]{1,0:T(8,128)(2,1)S(1)}, u32[]{:S(2)}, u32[]{:S(2)}) collective-permute-start(bf16[128,1024]{1,0:T(8,128)(2,1)S(1)} %get-tuple-element.42), channel_id=1, source_target_pairs={{0,6},{2,4},{4,2},{6,0},{1,7},{3,5},{5,3},{7,1},{8,14},{10,12},{12... | collective-permute-start | bytes 786440 | tf_op jit(solution)/shard_map/ppermute | solution.py:39
  367.8 23.9 %copy-start.7 = (bf16[1,8,4,32,1024]{4,3,2,1,0:T(8,128)(2,1)S(1)}, bf16[1,8,4,32,1024]{4,3,2,1,0:T(8,128)(2,1)}, u32[]{:S(2)}) copy-start(bf16[1,8,4,32,1024]{4,3,2,1,0:T(8,128)(2,1)} %copy.130) | copy-start | bytes 6291460
  401.0 6.4 copy-start.49
  401.0 6.4 copy-start.55
  406.0 129.5 %reduce-scatter.14.cloned.1.call-start = ((), (), s32[]{:S(2)}) async-start(), calls=%async_computation.11 | async-start | bytes 9437184 | tf_op jit(solution)/shard_map/reduce_scatter | solution.py:330
  441.4 158.4 %reduce-scatter.10.cloned.1.call-start = ((), (), s32[]{:S(2)}) async-start(), calls=%async_computation.9 | async-start | bytes 9437184 | tf_op jit(solution)/shard_map/reduce_scatter | solution.py:330
  467.9 2.7 collective-permute-start.19
  471.0 25.9 %collective-permute-start.20 = (bf16[128,2048]{1,0:T(8,128)(2,1)S(1)}, bf16[128,2048]{1,0:T(8,128)(2,1)S(1)}, u32[]{:S(2)}, u32[]{:S(2)}) collective-permute-start(bf16[128,2048]{1,0:T(8,128)(2,1)S(1)} %fusion.60), channel_id=1, source_target_pairs={{0,16},{16,0},{1,17},{17,1},{2,18},{18,2},{3,19},{19,3},{4,20},{20... | collective-permute-start | bytes 1572872 | tf_op jit(solution)/shard_map/ppermute | solution.py:39
  511.4 215.0 %all-reduce.3.cloned.1.call-start = ((), (), s32[]{:S(2)}) async-start(), calls=%async_computation.15 | async-start | bytes 172032 | tf_op jit(solution)/shard_map/psum | solution.py:392
  520.1 263.3 %reduce-scatter.18.cloned.1.call-start = ((), (), s32[]{:S(2)}) async-start(), calls=%async_computation.13 | async-start | bytes 4718592 | tf_op jit(solution)/shard_map/reduce_scatter | solution.py:285
  527.0 311.0 %reduce-scatter.20.cloned.1.call-start = ((), (), s32[]{:S(2)}) async-start(), calls=%async_computation.14 | async-start | bytes 4718592 | tf_op jit(solution)/shard_map/reduce_scatter | solution.py:288
  535.5 332.1 %reduce-scatter.16.cloned.1.call-start = ((), (), s32[]{:S(2)}) async-start(), calls=%async_computation.12 | async-start | bytes 1310720 | tf_op jit(solution)/shard_map/reduce_scatter | solution.py:331
  535.6 64.2 %copy-start.3 = (bf16[1,8,4,32,1024]{4,3,2,1,0:T(8,128)(2,1)S(1)}, bf16[1,8,4,32,1024]{4,3,2,1,0:T(8,128)(2,1)}, u32[]{:S(2)}) copy-start(bf16[1,8,4,32,1024]{4,3,2,1,0:T(8,128)(2,1)} %copy-done.2) | copy-start | bytes 6291460
  536.2 359.3 %reduce-scatter.12.cloned.1.call-start = ((), (), s32[]{:S(2)}) async-start(), calls=%async_computation.10 | async-start | bytes 1310720 | tf_op jit(solution)/shard_map/reduce_scatter | solution.py:331
  784.5 55.6 %collective-permute-start.21 = (bf16[32,2048]{1,0:T(8,128)(2,1)S(1)}, bf16[32,2048]{1,0:T(8,128)(2,1)S(1)}, u32[]{:S(2)}, u32[]{:S(2)}) collective-permute-start(bf16[32,2048]{1,0:T(8,128)(2,1)S(1)} %get-tuple-element.51), channel_id=1, source_target_pairs={{0,2},{2,0},{4,6},{6,4},{1,3},{3,1},{5,7},{7,5},{8,10},{10,8},{12,... | collective-permute-start | bytes 393224 | tf_op jit(solution)/shard_map/ppermute | solution.py:39
  786.1 54.0 %collective-permute-start.22 = (bf16[32,2048]{1,0:T(8,128)(2,1)S(1)}, bf16[32,2048]{1,0:T(8,128)(2,1)S(1)}, u32[]{:S(2)}, u32[]{:S(2)}) collective-permute-start(bf16[32,2048]{1,0:T(8,128)(2,1)S(1)} %get-tuple-element.50), channel_id=1, source_target_pairs={{0,4},{2,6},{4,0},{6,2},{1,5},{3,7},{5,1},{7,3},{8,12},{10,14},{12... | collective-permute-start | bytes 393224 | tf_op jit(solution)/shard_map/ppermute | solution.py:39
  788.5 51.6 %collective-permute-start.23 = (bf16[32,2048]{1,0:T(8,128)(2,1)S(1)}, bf16[32,2048]{1,0:T(8,128)(2,1)S(1)}, u32[]{:S(2)}, u32[]{:S(2)}) collective-permute-start(bf16[32,2048]{1,0:T(8,128)(2,1)S(1)} %get-tuple-element.49), channel_id=1, source_target_pairs={{0,6},{2,4},{4,2},{6,0},{1,7},{3,5},{5,3},{7,1},{8,14},{10,12},{12... | collective-permute-start | bytes 393224 | tf_op jit(solution)/shard_map/ppermute | solution.py:39
  842.8 57.2 %copy-start.1 = (f32[2,3,128,1024]{3,2,1,0:T(8,128)S(1)}, f32[2,3,128,1024]{3,2,1,0:T(8,128)}, u32[]{:S(2)}) copy-start(f32[2,3,128,1024]{3,2,1,0:T(8,128)} %param.20) | copy-start | bytes 9437188
  (40 other events, 89.1 us)
Sparse Core Ops, SparseCore 0:
  33.0 51.0 all-gather.13
  87.6 80.4 all-gather.9
  171.6 87.0 all-gather.11
  260.5 35.1 all-gather.7
  406.2 19.5 reduce-scatter.7
  441.5 83.5 reduce-scatter.13
  528.5 71.2 reduce-scatter.9
  606.9 119.5 all-reduce.2
  730.2 53.1 reduce-scatter.17
  786.6 51.3 reduce-scatter.19
  840.4 27.1 reduce-scatter.15
  869.7 25.7 reduce-scatter.11

commit v2 on v1

v2 whole, which is shorter than its diff:
```python
import math

import jax
import jax.numpy as jnp
from jax import lax
from jax.sharding import Mesh
from jax.sharding import PartitionSpec as P

HEADS = 16
EPSILON = 1e-05
NEGATIVE = -1e30
GELU_IN = math.sqrt(2.0 / math.pi)
GELU_CUBE = 0.044715
SEQ = ("y", "core")
FSDP = ("z", "x")
PLANE = ("y", "core", "x")
ALL = ("y", "core", "z", "x")
BF = jnp.bfloat16
F32 = jnp.float32


def matmul(left, right):
    return jnp.dot(left, right, preferred_element_type=F32)


def contract_rows(left, right):
    return lax.dot_general(left, right, (((0,), (0,)), ((), ())), preferred_element_type=F32)


def times_transpose(left, right):
    return lax.dot_general(left, right, (((1,), (1,)), ((), ())), preferred_element_type=F32)


def column_sums(values):
    return jnp.sum(values.astype(F32), axis=0)


def swap(value, axis, step):
    return lax.ppermute(value, axis, [(i, i ^ step) for i in range(lax.axis_size(axis))])


def norm_parts(values):
    centred = values - jnp.mean(values, axis=-1, keepdims=True)
    scale = lax.rsqrt(jnp.mean(centred * centred, axis=-1, keepdims=True) + EPSILON)
    return centred * scale, scale


def norm_back(normed, scale, gain, grad):
    inner = grad * gain
    means = jnp.mean(inner, axis=-1, keepdims=True)
    along = jnp.mean(inner * normed, axis=-1, keepdims=True)
    return (
        scale * (inner - means - normed * along),
        jnp.sum(grad * normed, axis=0),
        jnp.sum(grad, axis=0),
    )


def heads_first(values, heads):
    return values.reshape(values.shape[0], heads, -1).transpose(1, 0, 2)


def heads_last(values):
    return values.transpose(1, 0, 2).reshape(values.shape[1], -1)


def batched(left, right, left_dim, right_dim):
    return lax.dot_general(
        left, right, (((left_dim,), (right_dim,)), ((0,), (0,))), preferred_element_type=F32
    )


def attend(queries, keys, values, allowed):
    score_scale = 1.0 / math.sqrt(queries.shape[2])
    scores = jnp.where(allowed[None], batched(queries, keys, 2, 2) * score_scale, NEGATIVE)
    top = jnp.max(scores, axis=-1, keepdims=True)
    raised = jnp.where(allowed[None], jnp.exp(scores - top), 0.0)
    chance = raised / jnp.maximum(jnp.sum(raised, axis=-1, keepdims=True), 1.0)
    return batched(chance.astype(BF), values, 2, 1), chance


def attend_back(queries, keys, values, chance, grad):
    score_scale = 1.0 / math.sqrt(queries.shape[2])
    chance_grad = batched(grad, values, 2, 2)
    delta = jnp.sum(chance * chance_grad, axis=-1, keepdims=True)
    score_grad = (chance * (chance_grad - delta)).astype(BF)
    return (
        batched(score_grad, keys, 2, 1) * score_scale,
        batched(score_grad, queries, 1, 1) * score_scale,
        batched(chance.astype(BF), grad, 1, 1),
    )


def gather_seq(value):
    lines = [value] + [swap(value, "y", k) for k in range(1, lax.axis_size("y"))]
    lines = jnp.concatenate(lines) if len(lines) > 1 else value
    return jnp.concatenate([lines, swap(lines, "core", 1)])


def scatter_seq(partial):
    line = partial[0].astype(F32) + swap(partial[1].astype(BF), "core", 1).astype(F32)
    total = line[0]
    for k in range(1, lax.axis_size("y")):
        total = total + swap(line[k].astype(BF), "y", k).astype(F32)
    return total


def exchange_seq(value):
    line = jnp.stack([value[0], swap(value[1], "core", 1)])
    lines = [line[:, 0]] + [swap(line[:, k], "y", k) for k in range(1, lax.axis_size("y"))]
    return jnp.stack(lines, axis=1)


def pick(value, at, axis=0):
    return lax.dynamic_index_in_dim(value, at, axis, keepdims=False)


def body(
    hidden_in,
    memory,
    out_grad,
    segment_ids,
    memory_segments,
    deal,
    attn_in,
    attn_out,
    fc1,
    fc2,
    proj_bias,
    fc1_bias,
    norm_gain,
    norm_bias,
):
    y_size, z_size, x_size = lax.axis_size("y"), lax.axis_size("z"), lax.axis_size("x")
    s_size, f_size = y_size * 2, z_size * x_size
    y_place, core_place = lax.axis_index("y"), lax.axis_index("core")
    z_place, x_place = lax.axis_index("z"), lax.axis_index("x")
    s_place = y_place * 2 + core_place
    f_place = z_place * x_size + x_place
    place = s_place * f_size + f_place
    count = s_size * f_size
    tokens, width = hidden_in.shape[1:]
    sources_len = memory.shape[1]
    held = attn_in.shape[2]
    share = held // s_size
    lane = width // f_size
    cut = width // s_size
    row_len = s_size * tokens
    blocks = [(c, k) for c in range(2) for k in range(y_size)]
    block_of = [((j % 2) ^ core_place) * y_size + ((j // 2) ^ y_place) for j in range(s_size)]
    owners = jnp.stack([(y_place ^ k) * 2 + (core_place ^ c) for c, k in blocks])

    def cut_cols(value, at):
        return lax.dynamic_slice_in_dim(value, at * cut, cut, value.ndim - 1)

    small = jnp.concatenate(
        [
            proj_bias.reshape(-1).astype(BF),
            norm_gain.reshape(-1).astype(BF),
            norm_bias.reshape(-1).astype(BF),
            fc1_bias.astype(BF),
        ]
    )
    small_len = small.shape[0]
    small_rows = -(-small_len // (16 * cut)) * 16
    small = jnp.pad(small, (0, small_rows * cut - small_len)).reshape(small_rows, cut)
    early = jnp.concatenate([cut_cols(attn_in[0], s_place).astype(BF).reshape(3 * held, cut), small])
    early = jnp.stack([early] + [swap(early, "x", k) for k in range(1, x_size)])
    early = jnp.stack([early] + [swap(early, "z", k) for k in range(1, z_size)])
    early = early.reshape((f_size,) + early.shape[2:])
    early = jnp.stack(
        [
            pick(early, ((j // x_size) ^ z_place) * x_size + ((j % x_size) ^ x_place))
            for j in range(f_size)
        ]
    )
    w_self = early[:, : 3 * held].reshape(f_size, 3, held, cut).transpose(1, 0, 2, 3)
    w_self = w_self.reshape(3, width, cut)
    by_fsdp = early[:, 3 * held :].reshape(f_size, small_rows * cut)

    def columns(start, number):
        part = by_fsdp[:, start : start + number * lane].reshape(f_size, number, lane)
        return part.transpose(1, 0, 2).reshape(number, width).astype(F32)

    biases = columns(0, 7)
    gains = columns(7 * lane, 3)
    shifts = columns(10 * lane, 3)
    up_bias = by_fsdp[:, 13 * lane : small_len].reshape(-1).astype(F32)

    wi_share = lax.dynamic_slice_in_dim(attn_in[1], s_place * share, share, 1).astype(BF)
    wo_share = lax.dynamic_slice_in_dim(attn_out, s_place * share, share, 1).astype(BF)
    rest = jnp.concatenate([wi_share.reshape(3 * share, width), wo_share.reshape(2 * share, width)])
    rest = lax.all_gather(rest, ALL)
    w_rest = rest.reshape(s_size, f_size, 5, share, width).transpose(2, 1, 0, 3, 4)
    w_rest = w_rest.reshape(5, width, width)

    unit = fc2.shape[0] // s_size
    hidden = s_size * x_size * unit
    down_share = lax.dynamic_slice_in_dim(fc2, s_place * unit, unit, 0).astype(BF)
    down_share = lax.ppermute(
        down_share,
        ALL,
        [(s * f_size + f, f * s_size + s) for s in range(s_size) for f in range(f_size)],
    )
    up_share = lax.dynamic_slice_in_dim(fc1, s_place * share, share, 0).astype(BF)
    up_share = up_share.reshape(share, s_size, z_size, x_size, unit).transpose(2, 0, 1, 3, 4)
    up_share = up_share.reshape(z_size, share, hidden)
    up_parts = jnp.stack(
        [swap(pick(up_share, z_place ^ k), "z", k) if k else pick(up_share, z_place) for k in range(z_size)]
    )
    up_parts = jnp.stack([pick(up_parts, z_place ^ j) for j in range(z_size)])
    mlp_share = jnp.concatenate(
        [up_parts.reshape(z_size * share, hidden), down_share.reshape(-1, hidden)]
    )
    mlp_share, _ = lax.optimization_barrier((mlp_share, rest))
    w_mlp = lax.all_gather(mlp_share, PLANE)
    w_up = w_mlp[:, : z_size * share].reshape(s_size, x_size, z_size, share, hidden)
    w_up = w_up.transpose(2, 1, 0, 3, 4).reshape(width, hidden)
    w_down = w_mlp[:, z_size * share :].reshape(hidden, width)
    up_bias = pick(up_bias.reshape(s_size, z_size, x_size * unit), z_place, 1).reshape(hidden)

    down_grad = out_grad[0]
    down_all = jnp.concatenate([down_grad] + [swap(down_grad, "z", k) for k in range(1, z_size)])

    labels = jnp.concatenate([segment_ids[0], memory_segments[0]]).astype(BF)
    label_rows = -(-labels.shape[0] // (16 * width)) * 16
    labels = jnp.pad(labels, (0, label_rows * width - labels.shape[0])).reshape(label_rows, width)
    row = gather_seq(jnp.concatenate([hidden_in[0], memory[0], labels]))
    row = row.reshape(s_size, tokens + sources_len + label_rows, width)
    row_inputs = row[:, :tokens].reshape(row_len, width).astype(F32)
    labels = row[:, tokens + sources_len :].reshape(s_size, label_rows * width).astype(jnp.int32)
    row_seg = labels[:, :tokens].reshape(-1)
    row_sources = jnp.concatenate(
        [pick(row, block_of[j])[tokens : tokens + sources_len] for j in range(s_size)]
    )
    source_seg = jnp.concatenate(
        [pick(labels, block_of[j])[tokens : tokens + sources_len] for j in range(s_size)]
    )
    half_rows = tokens // 2
    offsets = jnp.arange(half_rows, dtype=jnp.int32)
    row_pos = (deal.reshape(s_size, 2)[owners][:, :, None] * half_rows + offsets).reshape(-1)
    real = row_seg[:, None] != 0
    self_allowed = (row_seg[:, None] == row_seg[None]) & real & (row_pos[None] <= row_pos[:, None])
    cross_allowed = (segment_ids[0][:, None] == source_seg[None]) & (segment_ids[0][:, None] != 0)

    heads = HEADS // s_size
    unit_row, _ = norm_parts(row_inputs)
    normed_row = (unit_row * gains[0] + shifts[0]).astype(BF)
    query_self = (matmul(normed_row, w_self[0]) + cut_cols(biases[0], s_place)).astype(BF)
    key_self = matmul(normed_row, w_self[1]).astype(BF)
    value_self = (matmul(normed_row, w_self[2]) + cut_cols(biases[1], s_place)).astype(BF)
    query_heads = heads_first(query_self, heads)
    key_heads = heads_first(key_self, heads)
    value_heads = heads_first(value_self, heads)
    self_mixed, self_chance = attend(query_heads, key_heads, value_heads, self_allowed)
    self_cut = heads_last(self_mixed).astype(BF)
    self_out = exchange_seq(self_cut.reshape(2, y_size, tokens, cut)).reshape(s_size, tokens, cut)
    self_out = jnp.concatenate([pick(self_out, block_of[j]) for j in range(s_size)], axis=1)
    inputs = hidden_in[0].astype(F32)
    after_self = inputs + matmul(self_out, w_rest[3]) + biases[2]

    source_key = matmul(row_sources, cut_cols(w_rest[1], s_place)).astype(BF)
    source_value = matmul(row_sources, cut_cols(w_rest[2], s_place)) + cut_cols(biases[4], s_place)
    source_pair = jnp.stack([source_key, source_value.astype(BF)])
    sources_row = s_size * sources_len
    source_all = gather_seq(source_pair[None]).reshape(s_size, 2, sources_row, cut)
    source_all = jnp.stack([pick(source_all, block_of[j]) for j in range(s_size)])
    source_all = source_all.reshape(s_size, 2, sources_row, heads, cut // heads)
    source_all = source_all.transpose(1, 0, 3, 2, 4).reshape(2, HEADS, sources_row, cut // heads)
    source_key_heads, source_value_heads = source_all[0], source_all[1]
    unit_two, scale_two = norm_parts(after_self)
    normed_two = (unit_two * gains[1] + shifts[1]).astype(BF)
    query_cross = (matmul(normed_two, w_rest[0]) + biases[3]).astype(BF)
    query_cross_heads = heads_first(query_cross, HEADS)
    cross_mixed, cross_chance = attend(
        query_cross_heads, source_key_heads, source_value_heads, cross_allowed
    )
    cross_out = heads_last(cross_mixed).astype(BF)
    after_cross = after_self + matmul(cross_out, w_rest[4]) + biases[5]

    unit_three, scale_three = norm_parts(after_cross)
    normed_three = (unit_three * gains[2] + shifts[2]).astype(BF)
    normed_all = jnp.concatenate(
        [normed_three] + [swap(normed_three, "z", k) for k in range(1, z_size)]
    )
    pre_act = matmul(normed_all, w_up) + up_bias
    bent = jnp.tanh(GELU_IN * (pre_act + GELU_CUBE * pre_act * pre_act * pre_act))
    activated = (0.5 * pre_act * (1.0 + bent)).astype(BF)
    slope = 0.5 * (1.0 + bent) + 0.5 * pre_act * (1.0 - bent * bent) * GELU_IN * (
        1.0 + 3.0 * GELU_CUBE * pre_act * pre_act
    )
    pre_grad = (times_transpose(down_all, w_down) * slope).astype(BF)

    def to_owners(partial):
        parts = partial.reshape(z_size, tokens, width)
        total = parts[0]
        for k in range(1, z_size):
            total = total + swap(parts[k].astype(BF), "z", k).astype(F32)
        return total

    normed_grad_three = to_owners(times_transpose(pre_grad, w_up))
    result = after_cross + to_owners(matmul(activated, w_down)) + biases[6]
    grad_up = contract_rows(normed_all, pre_grad).astype(BF)
    grad_down = contract_rows(activated, down_all).astype(BF)
    up_rows = width // count
    grad_up = grad_up.reshape(s_size, z_size, x_size, up_rows, hidden).transpose(0, 2, 1, 3, 4)
    grad_up = lax.psum_scatter(
        grad_up.reshape(s_size * x_size, z_size, up_rows, hidden), PLANE, scatter_dimension=0
    )
    grad_down = lax.psum_scatter(grad_down, PLANE, scatter_dimension=0, tiled=True).astype(F32)
    grad_up = jnp.stack(
        [swap(pick(grad_up, z_place ^ k), "z", k) if k else pick(grad_up, z_place) for k in range(z_size)]
    )
    grad_up = jnp.stack([pick(grad_up, z_place ^ j) for j in range(z_size)])
    grad_up = grad_up.reshape(z_size, up_rows, s_size, x_size, unit).transpose(1, 2, 0, 3, 4)
    grad_up = grad_up.reshape(up_rows, -1).astype(F32)
    grad_up_bias = column_sums(pre_grad)

    result_grad = down_grad.astype(F32)
    moved, gain_three, shift_three = norm_back(unit_three, scale_three, gains[2], normed_grad_three)
    after_grad = result_grad + moved
    cross_branch = after_grad.astype(BF)
    cross_head_grad = times_transpose(cross_branch, w_rest[4]).astype(BF)
    query_cross_grad, source_key_grad, source_value_grad = attend_back(
        query_cross_heads,
        source_key_heads,
        source_value_heads,
        cross_chance,
        heads_first(cross_head_grad, HEADS),
    )
    query_cross_grad = heads_last(query_cross_grad).astype(BF)
    normed_grad_two = times_transpose(query_cross_grad, w_rest[0])
    moved, gain_two, shift_two = norm_back(unit_two, scale_two, gains[1], normed_grad_two)
    self_grad = after_grad + moved

    self_branch = self_grad.astype(BF)
    branch_row = gather_seq(self_branch)
    wo_rows = lax.dynamic_slice_in_dim(w_rest[3], s_place * cut, cut, 0)
    self_head_grad = times_transpose(branch_row, wo_rows).astype(BF)
    query_grad, key_grad, value_grad = attend_back(
        query_heads, key_heads, value_heads, self_chance, heads_first(self_head_grad, heads)
    )
    query_grad = heads_last(query_grad).astype(BF)
    key_grad = heads_last(key_grad).astype(BF)
    value_grad = heads_last(value_grad).astype(BF)
    normed_grad_one = (
        times_transpose(query_grad, w_self[0])
        + times_transpose(key_grad, w_self[1])
        + times_transpose(value_grad, w_self[2])
    )
    normed_grad_one = scatter_seq(normed_grad_one.reshape(2, y_size, tokens, width))
    unit_one, scale_one = norm_parts(inputs)
    moved, gain_one, shift_one = norm_back(unit_one, scale_one, gains[0], normed_grad_one)
    grad_hidden = self_grad + moved

    source_grad = jnp.concatenate([source_key_grad, source_value_grad], axis=2).astype(BF)
    source_grad = source_grad.reshape(s_size, heads, sources_row, 2, cut // heads)
    source_grad = source_grad.transpose(0, 3, 2, 1, 4).reshape(s_size, 2, sources_row, cut)
    source_grad = jnp.stack([pick(source_grad, owners[j]) for j in range(s_size)])
    source_grad = scatter_seq(source_grad.reshape(2, y_size, 2, sources_row, cut)).astype(BF)
    grad_memory = times_transpose(source_grad[0], cut_cols(w_rest[1], s_place)) + times_transpose(
        source_grad[1], cut_cols(w_rest[2], s_place)
    )
    grad_memory = grad_memory.reshape(s_size, sources_len, width)
    grad_memory = jnp.stack([pick(grad_memory, owners[j]) for j in range(s_size)])
    grad_memory = scatter_seq(grad_memory.reshape(2, y_size, sources_len, width))

    def row_sum(grads):
        parts = jnp.stack([g.astype(BF).reshape(y_size, 2, cut, width) for g in grads])
        kept = pick(parts, core_place, 2).astype(F32)
        kept = kept + swap(pick(parts, core_place ^ 1, 2), "core", 1).astype(F32)
        total = pick(kept, y_place, 1)
        for k in range(1, y_size):
            total = total + swap(pick(kept, y_place ^ k, 1).astype(BF), "y", k).astype(F32)
        return total.astype(BF)

    def by_rows(grad):
        grad = grad.astype(BF).reshape(s_size, f_size, up_rows, -1)
        return grad.transpose(1, 0, 2, 3).reshape(f_size, -1, width)

    cross_pair = row_sum(
        [contract_rows(normed_two, query_cross_grad), contract_rows(cross_out, cross_branch)]
    )
    first = jnp.concatenate(
        [
            cross_pair[0].reshape(f_size, up_rows, width),
            cross_pair[1].reshape(f_size, up_rows, width),
            contract_rows(self_cut, branch_row).astype(BF).reshape(f_size, up_rows, width),
            by_rows(contract_rows(row_sources, source_grad[0])),
            by_rows(contract_rows(row_sources, source_grad[1])),
        ],
        axis=1,
    )
    first = lax.psum_scatter(first, FSDP, scatter_dimension=0)
    second = jnp.concatenate(
        [by_rows(contract_rows(normed_row, g)) for g in (query_grad, key_grad, value_grad)], axis=1
    )
    second = lax.psum_scatter(second, FSDP, scatter_dimension=0)

    def to_rows(grads, number):
        grads = grads.reshape(number, s_size, up_rows, cut).transpose(1, 0, 2, 3)
        grads = lax.all_to_all(grads, SEQ, 0, 0)
        return grads.transpose(1, 2, 0, 3).reshape(number, up_rows, width)

    by_cut = to_rows(jnp.concatenate([second, first[3 * up_rows :]]), 5).astype(F32)
    first = first[: 3 * up_rows].reshape(3, up_rows, width).astype(F32)

    def spread_cut(values):
        return lax.dynamic_update_slice_in_dim(jnp.zeros(width, F32), values, s_place * cut, 0)

    rows = [
        spread_cut(column_sums(query_grad)),
        spread_cut(column_sums(value_grad)),
        column_sums(self_branch),
        column_sums(query_cross_grad),
        spread_cut(column_sums(source_grad[1])),
        column_sums(cross_branch),
        column_sums(down_grad),
        gain_one,
        gain_two,
        gain_three,
        shift_one,
        shift_two,
        shift_three,
    ]
    spread = jnp.zeros((s_size, z_size, x_size * unit), F32)
    spread = lax.dynamic_update_slice_in_dim(
        spread, grad_up_bias.reshape(s_size, 1, x_size * unit), z_place, 1
    )
    table = jnp.stack(rows).reshape(len(rows), count, up_rows).transpose(1, 0, 2).reshape(count, -1)
    table = jnp.concatenate([table, spread.reshape(count, unit)], axis=1)
    table = jnp.sum(lax.all_to_all(table, ALL, 0, 0), axis=0)
    grad_up_bias = table[len(rows) * up_rows :]
    table = table[: len(rows) * up_rows].reshape(len(rows), up_rows)
    return (
        result.astype(BF)[None],
        grad_hidden[None],
        grad_memory[None],
        jnp.stack([by_cut[:3], jnp.stack([first[0], by_cut[3], by_cut[4]])]),
        jnp.stack([first[2], first[1]]),
        grad_up,
        grad_down,
        table[:7],
        grad_up_bias,
        table[7:10],
        table[10:13],
    )


def solution(mesh):
    seq, fsdp = mesh.shape["seq"], mesh.shape["fsdp"]
    split = Mesh(mesh.devices.reshape(seq // 2, 2, 4, fsdp // 4), ALL)
    placed = (
        P(FSDP, SEQ, None),
        P(FSDP, SEQ, None),
        P(FSDP, SEQ, None),
        P(FSDP, SEQ),
        P(FSDP, SEQ),
        P(),
        P(None, None, FSDP, None),
        P(None, FSDP, None),
        P(FSDP, None),
        P(FSDP, None),
        P(None, FSDP),
        P(FSDP),
        P(None, FSDP),
        P(None, FSDP),
    )
    return jax.shard_map(
        body,
        mesh=split,
        in_specs=placed,
        out_specs=(
            P(FSDP, SEQ, None),
            P(FSDP, SEQ, None),
            P(FSDP, SEQ, None),
            P(None, None, ALL, None),
            P(None, ALL, None),
            P(ALL, None),
            P(ALL, None),
            P(None, ALL),
            P(ALL),
            P(None, ALL),
            P(None, ALL),
        ),
        check_vma=False,
    )
```

time: 917 us -> 598 us (0.65)
  the two profiles are of different devices: /device:TPU:4 before, /device:TPU:0 now
where the time goes in v2:
time: 598 us; the launch traced here: 588 us
  waiting for transfers between devices  208 us (35%)
  starting transfers between devices  125 us (21%)
  local copies, waits for them, and re-layouts  109 us (18%)
  matrix products  81.9 us (14%)
  other arithmetic  46.7 us (8%)
  between operations  16.8 us (3%)
    ppermute x38, waiting for transfers between devices, swap(): lax.ppermute(value, axis, [(i, i ^ step) for i in range(lax.axis_size(axi...  125 us
    ppermute x38, starting transfers between devices, swap(): lax.ppermute(value, axis, [(i, i ^ step) for i in range(lax.axis_size(axi...  113 us
    reduce_scatter x1, waiting for transfers between devices, body(): second = lax.psum_scatter(second, FSDP, scatter_dimension=0)  65.2 us
    dot_general x10, matrix products, contract_rows(): lax.dot_general(left, right, (((0,), (0,)), ((), ())), preferred_element_...  20.8 us
    dot_general x10, matrix products, matmul(): return jnp.dot(left, right, preferred_element_type=F32)  20.1 us
    dot_general x10, matrix products, times_transpose(): lax.dot_general(left, right, (((1,), (1,)), ((), ())), preferred_element_...  19.2 us
    dot_general x11, matrix products, batched(): lax.dot_general(left, right, (((left_dim,), (right_dim,)), ((0,), (0,))),...  16.5 us
    unnamed x229, local copies, waits for them, and re-layouts  13.8 us
  transfers between devices with their start and end apart: 47, of which 19 were waited for; matrix products, arithmetic and copies ran while one was open for 36% of the time, Pallas kernels for 0%

profile of v2, /device:TPU:0, one launch (start us, length us, event | category | flops | bytes accessed | tf_op | source)
XLA Modules:
  0.0 588.2 jit_solution(5468823689850948556)
XLA Ops:
  7.3 2.2 fusion.125
  11.3 2.9 collective-permute-start.2
  19.8 2.6 collective-permute-start.14
  26.0 11.4 %collective-permute-done.14 = bf16[32,2048]{1,0:T(8,128)(2,1)S(1)} collective-permute-done((bf16[32,2048]{1,0:T(8,128)(2,1)S(1)}, bf16[32,2048]{1,0:T(8,128)(2,1)S(1)}, u32[]{:S(2)}, u32[]{:S(2)}) %collective-permute-start.14) | collective-permute-done | bytes 131104 | tf_op jit(solution)/shard_map/ppermute | solution.py:39
  38.1 3.4 collective-permute-start.20
  46.6 44.2 %collective-permute-start.3 = (bf16[2,400,256]{2,1,0:T(8,128)(2,1)}, bf16[2,400,256]{2,1,0:T(8,128)(2,1)}, u32[]{:S(2)}, u32[]{:S(2)}) collective-permute-start(bf16[2,400,256]{2,1,0:T(8,128)(2,1)} %get-tuple-element.75), channel_id=1, source_target_pairs={{0,2},{2,0},{4,6},{6,4},{1,3},{3,1},{5,7},{7,5},{8,10},{10,8},{12,... | collective-permute-start | bytes 1228808 | tf_op jit(solution)/shard_map/ppermute | solution.py:39
  90.8 2.4 collective-permute-start.5
  95.9 18.2 %collective-permute-done.3 = bf16[2,400,256]{2,1,0:T(8,128)(2,1)} collective-permute-done((bf16[2,400,256]{2,1,0:T(8,128)(2,1)}, bf16[2,400,256]{2,1,0:T(8,128)(2,1)}, u32[]{:S(2)}, u32[]{:S(2)}) %collective-permute-start.3) | collective-permute-done | bytes 409632 | tf_op jit(solution)/shard_map/ppermute | solution.py:39
  114.1 9.6 %collective-permute-start.1 = (bf16[320,1024]{1,0:T(8,128)(2,1)S(1)}, bf16[320,1024]{1,0:T(8,128)(2,1)}, u32[]{:S(2)}, u32[]{:S(2)}) collective-permute-start(bf16[320,1024]{1,0:T(8,128)(2,1)S(1)} %pad_maximum_fusion.7), channel_id=1, source_target_pairs={{0,8},{8,0},{1,9},{9,1},{2,10},{10,2},{3,11},{11,3},{4,12},{12,4},... | collective-permute-start | bytes 1966088 | tf_op jit(solution)/shard_map/ppermute | solution.py:39
  123.6 25.8 %collective-permute-done.4 = bf16[2,400,256]{2,1,0:T(8,128)(2,1)} collective-permute-done((bf16[2,400,256]{2,1,0:T(8,128)(2,1)}, bf16[2,400,256]{2,1,0:T(8,128)(2,1)}, u32[]{:S(2)}, u32[]{:S(2)}) %collective-permute-start.4) | collective-permute-done | bytes 409632 | tf_op jit(solution)/shard_map/ppermute | solution.py:39
  155.5 2.5 fusion.126
  163.7 5.1 fusion.134
  169.3 3.2 convolution_convert_fusion.11
  175.0 8.2 %collective-permute-done.7 = bf16[2,128,256]{2,1,0:T(8,128)(2,1)S(1)} collective-permute-done((bf16[2,128,256]{2,1,0:T(8,128)(2,1)S(1)}, bf16[2,128,256]{2,1,0:T(8,128)(2,1)S(1)}, u32[]{:S(2)}, u32[]{:S(2)}) %collective-permute-start.7) | collective-permute-done | bytes 131104 | tf_op jit(solution)/shard_map/ppermute | solution.py:39
  183.3 5.9 fusion.123
  193.5 4.2 collective-permute-done.8
  201.5 3.2 copy.100
  206.4 2.0 reshape.971
  208.4 1.9 fusion.130
  215.8 2.3 convolution_convert_fusion.10
  218.1 2.3 fusion.137
  222.1 12.9 %collective-permute-start.10 = (bf16[128,1024]{1,0:T(8,128)(2,1)}, bf16[128,1024]{1,0:T(8,128)(2,1)}, u32[]{:S(2)}, u32[]{:S(2)}) collective-permute-start(bf16[128,1024]{1,0:T(8,128)(2,1)} %add_convert_fusion), channel_id=1, source_target_pairs={{0,2},{2,0},{4,6},{6,4},{1,3},{3,1},{5,7},{7,5},{8,10},{10,8},{12,... | collective-permute-start | bytes 786440 | tf_op jit(solution)/shard_map/ppermute | solution.py:39
  235.0 2.4 collective-permute-start.12
  237.4 5.3 fusion.124
  242.7 2.4 copy.102
  245.1 7.3 %reshape.978 = bf16[2048,1024]{1,0:T(8,128)(2,1)} reshape(bf16[8,128,2048]{2,1,0:T(8,128)(2,1)} %get-tuple-element.37) | data formatting | bytes 8388608 | tf_op jit(solution)/shard_map/reshape | solution.py:219
  253.9 2.7 collective-permute-done.11
  256.7 5.0 fusion.80
  262.6 6.3 %convert_reduce_fusion = (f32[2048]{0:T(1024)S(1)}, bf16[512,2048]{1,0:T(8,128)(2,1)S(1)}) fusion(f32[512,2048]{1,0:T(8,128)S(1)} %fusion.80, f32[2048]{0:T(1024)S(1)} %bitcast.529, bf16[2048,1024]{1,0:T(8,128)(2,1)S(1)} %copy-done.20, bf16[128,1024]{1,0:T(8,128)(2,1)S(1)} %collective-permute-done.22, bf16[128,1024]{1,0:T(8,128)(2,1)} %collective-permute-done.21, ...), kind=kOutput, calls=%fused_computation.17 | convolution fusion | flops 2174744576 | bytes 11550720 | tf_op jit(solution)/shard_map/dot_general | solution.py:31
  268.9 4.3 convolution_convert_fusion.1
  273.3 2.3 copy.118
  277.0 7.7 %fusion.139 = (bf16[512,1024]{1,0:T(8,128)(2,1)S(1)}, f32[512,1024]{1,0:T(8,128)}) fusion(bf16[2048,1024]{1,0:T(8,128)(2,1)} %reshape.978, f32[512,2048]{1,0:T(8,128)} %copy-done.103, f32[2048]{0:T(1024)S(1)} %bitcast.530), kind=kOutput, calls=%fused_computation.392 | convolution fusion | flops 2158493696 | bytes 11542528 | tf_op jit(solution)/shard_map/dot_general | solution.py:23
  285.6 11.2 %collective-permute-start.17 = (bf16[128,1024]{1,0:T(8,128)(2,1)}, bf16[128,1024]{1,0:T(8,128)(2,1)}, u32[]{:S(2)}, u32[]{:S(2)}) collective-permute-start(bf16[128,1024]{1,0:T(8,128)(2,1)} %get-tuple-element.52), channel_id=1, source_target_pairs={{0,2},{2,0},{4,6},{6,4},{1,3},{3,1},{5,7},{7,5},{8,10},{10,8},{12,... | collective-permute-start | bytes 786440 | tf_op jit(solution)/shard_map/ppermute | solution.py:39
  296.9 3.7 fusion.138
  302.1 2.3 collective-permute-start.24
  305.9 6.7 %convolution_convert_fusion = bf16[2048,1024]{1,0:T(8,128)(2,1)} fusion(bf16[128,1024]{1,0:T(8,128)(2,1)S(1)} %copy-done.97, bf16[128,1024]{1,0:T(8,128)(2,1)} %collective-permute-done.21, bf16[128,1024]{1,0:T(8,128)(2,1)} %collective-permute-done.20, bf16[128,1024]{1,0:T(8,128)(2,1)} %bitcast.111, f32[512,2048]{1,0:T(8,128)S(1)} %copy-done.104, ...), kind=kOutput, calls=%fused_computation.23 | convolution fusion | flops 2164260864 | bytes 9445376 | tf_op jit(solution)/shard_map/dot_general | solution.py:27
  313.5 3.5 collective-permute-done.23
  317.0 2.1 collective-permute-start.19
  319.0 15.8 %collective-permute-done.24 = bf16[128,1024]{1,0:T(8,128)(2,1)} collective-permute-done((bf16[128,1024]{1,0:T(8,128)(2,1)}, bf16[128,1024]{1,0:T(8,128)(2,1)}, u32[]{:S(2)}, u32[]{:S(2)}) %collective-permute-start.24) | collective-permute-done | bytes 262176 | tf_op jit(solution)/shard_map/ppermute | solution.py:39
  334.9 2.4 multiply_reduce_fusion.1
  337.3 3.1 convert_reduce_fusion.4
  342.7 1.8 copy.103
  344.5 2.3 convolution_convert_fusion.12
  350.5 2.0 convert_element_type.493
  352.5 2.3 copy.142
  354.8 2.2 reshape.981
  358.0 2.1 convert_reduce_fusion.5
  360.1 1.9 convolution_convert_fusion.2
  383.2 1.9 convolution_convert_fusion.9
  385.2 2.7 convert_add_fusion
  387.9 2.1 copy-done.11
  399.5 19.0 %collective-permute-done.35 = bf16[2,256,1024]{2,1,0:T(8,128)(2,1)} collective-permute-done((bf16[2,256,1024]{2,1,0:T(8,128)(2,1)}, bf16[2,256,1024]{2,1,0:T(8,128)(2,1)}, u32[]{:S(2)}, u32[]{:S(2)}) %collective-permute-start.35) | collective-permute-done | bytes 1048608 | tf_op jit(solution)/shard_map/ppermute | solution.py:39
  428.8 2.0 convolution_convert_fusion.14
  451.4 4.2 collective-permute-done.29
  457.5 7.1 %all-to-all-start.1 = ((f32[32,1,672]{2,1,0:T(1,128)}), f32[32,1,672]{2,1,0:T(1,128)S(1)}, u32[]{:S(2)}, u32[]{:S(2)}) async-start(f32[32,1,672]{2,1,0:T(1,128)} %copy.120), calls=%async_computation.5 | async-start | bytes 196608 | tf_op jit(solution)/shard_map/all_to_all | solution.py:432
  465.7 6.5 %all-to-all-done.1 = f32[32,1,672]{2,1,0:T(1,128)S(1)} async-done(((f32[32,1,672]{2,1,0:T(1,128)}), f32[32,1,672]{2,1,0:T(1,128)S(1)}, u32[]{:S(2)}, u32[]{:S(2)}) %all-to-all-start.1) | async-done | bytes 86048 | tf_op jit(solution)/shard_map/all_to_all | solution.py:432
  476.3 2.8 collective-permute-start.38
  480.5 2.1 convert_element_type.527
  482.7 9.7 %collective-permute-done.37 = bf16[32,2048]{1,0:T(8,128)(2,1)S(1)} collective-permute-done((bf16[32,2048]{1,0:T(8,128)(2,1)S(1)}, bf16[32,2048]{1,0:T(8,128)(2,1)S(1)}, u32[]{:S(2)}, u32[]{:S(2)}) %collective-permute-start.37) | collective-permute-done | bytes 131104 | tf_op jit(solution)/shard_map/ppermute | solution.py:39
  494.1 1.8 reshape.1003
  495.9 5.2 reduce-scatter.7.cloned.1.call-done
  502.0 65.2 %reduce-scatter.5.cloned.1.call-done = bf16[1,96,1024]{2,1,0:T(8,128)(2,1)} async-done(((bf16[8,96,1024]{2,1,0:T(8,128)(2,1)}), bf16[1,96,1024]{2,1,0:T(8,128)(2,1)}) %reduce-scatter.5.cloned.1.call-update) | async-done | bytes 196624 | tf_op jit(solution)/shard_map/reduce_scatter | solution.py:398
  569.1 3.5 all-to-all-start
  573.4 5.9 %all-to-all-done = bf16[4,5,32,256]{3,2,1,0:T(8,128)(2,1)S(1)} async-done(((bf16[4,5,32,256]{3,2,1,0:T(8,128)(2,1)}), bf16[4,5,32,256]{3,2,1,0:T(8,128)(2,1)S(1)}, u32[]{:S(2)}, u32[]{:S(2)}) %all-to-all-start) | async-done | bytes 327712 | tf_op jit(solution)/shard_map/all_to_all | solution.py:402
  (532 shorter events, 142.4 us)
Async XLA Ops:
  7.2 176.1 %all-gather.5.cloned.1.call-start = ((), (), s32[]{:S(2)}) async-start(), calls=%async_computation.10 | async-start | bytes 10813440 | tf_op jit(solution)/shard_map/all_gather | solution.py:193
  10.4 227.0 %all-gather.7.cloned.1.call-start = ((), (), s32[]{:S(2)}) async-start(), calls=%async_computation.11 | async-start | bytes 9437184 | tf_op jit(solution)/shard_map/all_gather | solution.py:216
  11.3 33.6 %collective-permute-start.2 = (bf16[400,256]{1,0:T(8,128)(2,1)}, bf16[400,256]{1,0:T(8,128)(2,1)}, u32[]{:S(2)}, u32[]{:S(2)}) collective-permute-start(bf16[400,256]{1,0:T(8,128)(2,1)} %get-tuple-element.105), channel_id=1, source_target_pairs={{0,1},{1,0},{2,3},{3,2},{4,5},{5,4},{6,7},{7,6},{8,9},{9,8},{10,11... | collective-permute-start | bytes 614408 | tf_op jit(solution)/shard_map/ppermute | solution.py:39
  15.1 78.2 %collective-permute-start = (bf16[160,1024]{1,0:T(8,128)(2,1)}, bf16[160,1024]{1,0:T(8,128)(2,1)}, u32[]{:S(2)}, u32[]{:S(2)}) collective-permute-start(bf16[160,1024]{1,0:T(8,128)(2,1)} %pad_maximum_fusion.15), channel_id=1, source_target_pairs={{0,16},{16,0},{1,17},{17,1},{2,18},{18,2},{3,19},{19,3},{4,20},{20... | collective-permute-start | bytes 983048 | tf_op jit(solution)/shard_map/ppermute | solution.py:39
  19.8 17.7 %collective-permute-start.14 = (bf16[32,2048]{1,0:T(8,128)(2,1)S(1)}, bf16[32,2048]{1,0:T(8,128)(2,1)S(1)}, u32[]{:S(2)}, u32[]{:S(2)}) collective-permute-start(bf16[32,2048]{1,0:T(8,128)(2,1)S(1)} %get-tuple-element.70), channel_id=1, source_target_pairs={{0,4},{2,6},{4,0},{6,2},{1,5},{3,7},{5,1},{7,3},{8,12},{10,14},{12... | collective-permute-start | bytes 393224 | tf_op jit(solution)/shard_map/ppermute | solution.py:39
  22.3 15.8 %collective-permute-start.15 = (bf16[32,2048]{1,0:T(8,128)(2,1)}, bf16[32,2048]{1,0:T(8,128)(2,1)S(1)}, u32[]{:S(2)}, u32[]{:S(2)}) collective-permute-start(bf16[32,2048]{1,0:T(8,128)(2,1)} %get-tuple-element.69), channel_id=1, source_target_pairs={{0,6},{2,4},{4,2},{6,0},{1,7},{3,5},{5,3},{7,1},{8,14},{10,12},{12... | collective-permute-start | bytes 393224 | tf_op jit(solution)/shard_map/ppermute | solution.py:39
  23.7 17.8 %collective-permute-start.13 = (bf16[32,2048]{1,0:T(8,128)(2,1)S(1)}, bf16[32,2048]{1,0:T(8,128)(2,1)S(1)}, u32[]{:S(2)}, u32[]{:S(2)}) collective-permute-start(bf16[32,2048]{1,0:T(8,128)(2,1)S(1)} %get-tuple-element.71), channel_id=1, source_target_pairs={{0,2},{2,0},{4,6},{6,4},{1,3},{3,1},{5,7},{7,5},{8,10},{10,8},{12,... | collective-permute-start | bytes 393224 | tf_op jit(solution)/shard_map/ppermute | solution.py:39
  37.4 6.0 %collective-permute-start.16 = (bf16[256,1024]{1,0:T(8,128)(2,1)S(1)}, bf16[256,1024]{1,0:T(8,128)(2,1)S(1)}, u32[]{:S(2)}, u32[]{:S(2)}) collective-permute-start(bf16[256,1024]{1,0:T(8,128)(2,1)S(1)} %dynamic-slice_convert_fusion.1), channel_id=1, source_target_pairs={{0,0},{1,4},{2,8},{3,12},{4,16},{5,20},{6,24},{7,28},{8,1},{9,5},{... | collective-permute-start | bytes 1572872 | tf_op jit(solution)/shard_map/ppermute | solution.py:200
  38.1 223.5 %collective-permute-start.20 = (bf16[128,1024]{1,0:T(8,128)(2,1)}, bf16[128,1024]{1,0:T(8,128)(2,1)}, u32[]{:S(2)}, u32[]{:S(2)}) collective-permute-start(bf16[128,1024]{1,0:T(8,128)(2,1)} %bitcast.111), channel_id=1, source_target_pairs={{0,2},{2,0},{4,6},{6,4},{1,3},{3,1},{5,7},{7,5},{8,10},{10,8},{12,... | collective-permute-start | bytes 786440 | tf_op jit(solution)/shard_map/ppermute | solution.py:39
  44.7 428.8 %reduce-scatter.9.cloned.1.call-start = ((), (), s32[]{:S(2)}) async-start(), calls=%async_computation.8 | async-start | bytes 4718592 | tf_op jit(solution)/shard_map/reduce_scatter | solution.py:307
  46.6 67.4 %collective-permute-start.3 = (bf16[2,400,256]{2,1,0:T(8,128)(2,1)}, bf16[2,400,256]{2,1,0:T(8,128)(2,1)}, u32[]{:S(2)}, u32[]{:S(2)}) collective-permute-start(bf16[2,400,256]{2,1,0:T(8,128)(2,1)} %get-tuple-element.75), channel_id=1, source_target_pairs={{0,2},{2,0},{4,6},{6,4},{1,3},{3,1},{5,7},{7,5},{8,10},{10,8},{12,... | collective-permute-start | bytes 1228808 | tf_op jit(solution)/shard_map/ppermute | solution.py:39
  90.8 58.7 %collective-permute-start.4 = (bf16[2,400,256]{2,1,0:T(8,128)(2,1)}, bf16[2,400,256]{2,1,0:T(8,128)(2,1)}, u32[]{:S(2)}, u32[]{:S(2)}) collective-permute-start(bf16[2,400,256]{2,1,0:T(8,128)(2,1)} %get-tuple-element.75), channel_id=1, source_target_pairs={{0,4},{2,6},{4,0},{6,2},{1,5},{3,7},{5,1},{7,3},{8,12},{10,14},{12... | collective-permute-start | bytes 1228808 | tf_op jit(solution)/shard_map/ppermute | solution.py:39
  90.8 58.7 %collective-permute-start.5 = (bf16[2,400,256]{2,1,0:T(8,128)(2,1)}, bf16[2,400,256]{2,1,0:T(8,128)(2,1)}, u32[]{:S(2)}, u32[]{:S(2)}) collective-permute-start(bf16[2,400,256]{2,1,0:T(8,128)(2,1)} %get-tuple-element.75), channel_id=1, source_target_pairs={{0,6},{2,4},{4,2},{6,0},{1,7},{3,5},{5,3},{7,1},{8,14},{10,12},{12... | collective-permute-start | bytes 1228808 | tf_op jit(solution)/shard_map/ppermute | solution.py:39
  93.2 168.5 %collective-permute-start.21 = (bf16[128,1024]{1,0:T(8,128)(2,1)}, bf16[128,1024]{1,0:T(8,128)(2,1)}, u32[]{:S(2)}, u32[]{:S(2)}) collective-permute-start(bf16[128,1024]{1,0:T(8,128)(2,1)} %bitcast.111), channel_id=1, source_target_pairs={{0,4},{2,6},{4,0},{6,2},{1,5},{3,7},{5,1},{7,3},{8,12},{10,14},{12... | collective-permute-start | bytes 786440 | tf_op jit(solution)/shard_map/ppermute | solution.py:39
  114.1 44.0 %collective-permute-start.1 = (bf16[320,1024]{1,0:T(8,128)(2,1)S(1)}, bf16[320,1024]{1,0:T(8,128)(2,1)}, u32[]{:S(2)}, u32[]{:S(2)}) collective-permute-start(bf16[320,1024]{1,0:T(8,128)(2,1)S(1)} %pad_maximum_fusion.7), channel_id=1, source_target_pairs={{0,8},{8,0},{1,9},{9,1},{2,10},{10,2},{3,11},{11,3},{4,12},{12,4},... | collective-permute-start | bytes 1966088 | tf_op jit(solution)/shard_map/ppermute | solution.py:39
  172.6 16.6 %copy-start.48 = (bf16[4,512,64]{1,2,0:T(8,128)(2,1)}, bf16[4,512,64]{1,2,0:T(8,128)(2,1)S(1)}, u32[]{:S(2)}) copy-start(bf16[4,512,64]{1,2,0:T(8,128)(2,1)S(1)} %convolution_convert_fusion.11) | copy-start | bytes 786436
  172.8 1.4 collective-permute-start.6
  174.2 9.0 %collective-permute-start.7 = (bf16[2,128,256]{2,1,0:T(8,128)(2,1)S(1)}, bf16[2,128,256]{2,1,0:T(8,128)(2,1)S(1)}, u32[]{:S(2)}, u32[]{:S(2)}) collective-permute-start(bf16[2,128,256]{2,1,0:T(8,128)(2,1)S(1)} %get-tuple-element.101), channel_id=1, source_target_pairs={{0,16},{16,0},{1,17},{17,1},{2,18},{18,2},{3,19},{19,3},{4,20},{20... | collective-permute-start | bytes 393224 | tf_op jit(solution)/shard_map/ppermute | solution.py:39
  175.0 15.1 %copy-start.70 = (bf16[16,1024]{1,0:T(8,128)(2,1)}, bf16[16,1024]{1,0:T(8,128)(2,1)S(1)}, u32[]{:S(2)}) copy-start(bf16[16,1024]{1,0:T(8,128)(2,1)S(1)} %get-tuple-element.45) | copy-start | bytes 98308
  175.0 15.8 %copy-start.68 = (bf16[16,1024]{1,0:T(8,128)(2,1)}, bf16[16,1024]{1,0:T(8,128)(2,1)S(1)}, u32[]{:S(2)}) copy-start(bf16[16,1024]{1,0:T(8,128)(2,1)S(1)} %get-tuple-element.43) | copy-start | bytes 98308
  175.0 15.8 %copy-start.69 = (bf16[16,1024]{1,0:T(8,128)(2,1)}, bf16[16,1024]{1,0:T(8,128)(2,1)S(1)}, u32[]{:S(2)}) copy-start(bf16[16,1024]{1,0:T(8,128)(2,1)S(1)} %get-tuple-element.44) | copy-start | bytes 98308
  192.3 5.4 collective-permute-start.8
  198.4 6.2 %collective-permute-start.9 = (bf16[2,2,64,256]{3,2,1,0:T(8,128)(2,1)}, bf16[2,2,64,256]{3,2,1,0:T(8,128)(2,1)}, u32[]{:S(2)}, u32[]{:S(2)}) collective-permute-start(bf16[2,2,64,256]{3,2,1,0:T(8,128)(2,1)} %pad_maximum_fusion.30), channel_id=1, source_target_pairs={{0,8},{8,0},{1,9},{9,1},{2,10},{10,2},{3,11},{11,3},{4,12},{12,4},... | collective-permute-start | bytes 393224 | tf_op jit(solution)/shard_map/ppermute | solution.py:39
  222.1 30.3 %collective-permute-start.10 = (bf16[128,1024]{1,0:T(8,128)(2,1)}, bf16[128,1024]{1,0:T(8,128)(2,1)}, u32[]{:S(2)}, u32[]{:S(2)}) collective-permute-start(bf16[128,1024]{1,0:T(8,128)(2,1)} %add_convert_fusion), channel_id=1, source_target_pairs={{0,2},{2,0},{4,6},{6,4},{1,3},{3,1},{5,7},{7,5},{8,10},{10,8},{12,... | collective-permute-start | bytes 786440 | tf_op jit(solution)/shard_map/ppermute | solution.py:39
  235.0 21.7 %collective-permute-start.11 = (bf16[128,1024]{1,0:T(8,128)(2,1)}, bf16[128,1024]{1,0:T(8,128)(2,1)}, u32[]{:S(2)}, u32[]{:S(2)}) collective-permute-start(bf16[128,1024]{1,0:T(8,128)(2,1)} %add_convert_fusion), channel_id=1, source_target_pairs={{0,4},{2,6},{4,0},{6,2},{1,5},{3,7},{5,1},{7,3},{8,12},{10,14},{12... | collective-permute-start | bytes 786440 | tf_op jit(solution)/shard_map/ppermute | solution.py:39
  235.0 21.7 %collective-permute-start.12 = (bf16[128,1024]{1,0:T(8,128)(2,1)}, bf16[128,1024]{1,0:T(8,128)(2,1)}, u32[]{:S(2)}, u32[]{:S(2)}) collective-permute-start(bf16[128,1024]{1,0:T(8,128)(2,1)} %add_convert_fusion), channel_id=1, source_target_pairs={{0,6},{2,4},{4,2},{6,0},{1,7},{3,5},{5,3},{7,1},{8,14},{10,12},{12... | collective-permute-start | bytes 786440 | tf_op jit(solution)/shard_map/ppermute | solution.py:39
  252.4 10.2 %collective-permute-start.22 = (bf16[128,1024]{1,0:T(8,128)(2,1)}, bf16[128,1024]{1,0:T(8,128)(2,1)S(1)}, u32[]{:S(2)}, u32[]{:S(2)}) collective-permute-start(bf16[128,1024]{1,0:T(8,128)(2,1)} %bitcast.111), channel_id=1, source_target_pairs={{0,6},{2,4},{4,2},{6,0},{1,7},{3,5},{5,3},{7,1},{8,14},{10,12},{12... | collective-permute-start | bytes 786440 | tf_op jit(solution)/shard_map/ppermute | solution.py:39
  275.6 205.0 %reduce-scatter.11.cloned.1.call-start = ((), (), s32[]{:S(2)}) async-start(), calls=%async_computation.9 | async-start | bytes 4718592 | tf_op jit(solution)/shard_map/reduce_scatter | solution.py:310
  277.0 19.9 %copy-start.19 = (bf16[4,2,4,32,2048]{4,3,2,1,0:T(8,128)(2,1)S(1)}, bf16[4,2,4,32,2048]{4,3,2,1,0:T(8,128)(2,1)}, u32[]{:S(2)}) copy-start(bf16[4,2,4,32,2048]{4,3,2,1,0:T(8,128)(2,1)} %copy.102) | copy-start | bytes 12582916
  277.0 19.9 %copy-start.102 = (bf16[512,2048]{1,0:T(8,128)(2,1)S(1)}, bf16[512,2048]{1,0:T(8,128)(2,1)}, u32[]{:S(2)}) copy-start(bf16[512,2048]{1,0:T(8,128)(2,1)} %copy-done.101) | copy-start | bytes 6291460
  285.6 51.7 %collective-permute-start.17 = (bf16[128,1024]{1,0:T(8,128)(2,1)}, bf16[128,1024]{1,0:T(8,128)(2,1)}, u32[]{:S(2)}, u32[]{:S(2)}) collective-permute-start(bf16[128,1024]{1,0:T(8,128)(2,1)} %get-tuple-element.52), channel_id=1, source_target_pairs={{0,2},{2,0},{4,6},{6,4},{1,3},{3,1},{5,7},{7,5},{8,10},{10,8},{12,... | collective-permute-start | bytes 786440 | tf_op jit(solution)/shard_map/ppermute | solution.py:39
  296.9 40.4 %collective-permute-start.18 = (bf16[128,1024]{1,0:T(8,128)(2,1)}, bf16[128,1024]{1,0:T(8,128)(2,1)}, u32[]{:S(2)}, u32[]{:S(2)}) collective-permute-start(bf16[128,1024]{1,0:T(8,128)(2,1)} %get-tuple-element.54), channel_id=1, source_target_pairs={{0,4},{2,6},{4,0},{6,2},{1,5},{3,7},{5,1},{7,3},{8,12},{10,14},{12... | collective-permute-start | bytes 786440 | tf_op jit(solution)/shard_map/ppermute | solution.py:39
  301.5 15.5 %collective-permute-start.23 = (bf16[128,1024]{1,0:T(8,128)(2,1)}, bf16[128,1024]{1,0:T(8,128)(2,1)}, u32[]{:S(2)}, u32[]{:S(2)}) collective-permute-start(bf16[128,1024]{1,0:T(8,128)(2,1)} %get-tuple-element.49), channel_id=1, source_target_pairs={{0,2},{2,0},{4,6},{6,4},{1,3},{3,1},{5,7},{7,5},{8,10},{10,8},{12,... | collective-permute-start | bytes 786440 | tf_op jit(solution)/shard_map/ppermute | solution.py:39
  302.1 32.7 %collective-permute-start.24 = (bf16[128,1024]{1,0:T(8,128)(2,1)}, bf16[128,1024]{1,0:T(8,128)(2,1)}, u32[]{:S(2)}, u32[]{:S(2)}) collective-permute-start(bf16[128,1024]{1,0:T(8,128)(2,1)} %get-tuple-element.51), channel_id=1, source_target_pairs={{0,4},{2,6},{4,0},{6,2},{1,5},{3,7},{5,1},{7,3},{8,12},{10,14},{12... | collective-permute-start | bytes 786440 | tf_op jit(solution)/shard_map/ppermute | solution.py:39
  304.4 30.4 %collective-permute-start.25 = (bf16[128,1024]{1,0:T(8,128)(2,1)}, bf16[128,1024]{1,0:T(8,128)(2,1)}, u32[]{:S(2)}, u32[]{:S(2)}) collective-permute-start(bf16[128,1024]{1,0:T(8,128)(2,1)} %get-tuple-element.50), channel_id=1, source_target_pairs={{0,6},{2,4},{4,2},{6,0},{1,7},{3,5},{5,3},{7,1},{8,14},{10,12},{12... | collective-permute-start | bytes 786440 | tf_op jit(solution)/shard_map/ppermute | solution.py:39
  313.2 24.1 %copy-start.72 = (f32[1024]{0:T(1024)S(1)}, f32[1024]{0:T(1024)}, u32[]{:S(2)}) copy-start(f32[1024]{0:T(1024)} %get-tuple-element.108) | copy-start | bytes 12292
  313.2 187.8 %reduce-scatter.7.cloned.1.call-start = ((), (), s32[]{:S(2)}) async-start(), calls=%async_computation.7 | async-start | bytes 2949120 | tf_op jit(solution)/shard_map/reduce_scatter | solution.py:394
  313.4 23.9 %copy-start.9 = (f32[128,1024]{1,0:T(8,128)S(1)}, f32[128,1024]{1,0:T(8,128)}, u32[]{:S(2)}) copy-start(f32[128,1024]{1,0:T(8,128)} %copy-done.8) | copy-start | bytes 1572868
  317.0 20.3 %collective-permute-start.19 = (bf16[128,1024]{1,0:T(8,128)(2,1)}, bf16[128,1024]{1,0:T(8,128)(2,1)S(1)}, u32[]{:S(2)}, u32[]{:S(2)}) collective-permute-start(bf16[128,1024]{1,0:T(8,128)(2,1)} %get-tuple-element.53), channel_id=1, source_target_pairs={{0,6},{2,4},{4,2},{6,0},{1,7},{3,5},{5,3},{7,1},{8,14},{10,12},{12... | collective-permute-start | bytes 786440 | tf_op jit(solution)/shard_map/ppermute | solution.py:39
  357.9 9.1 %collective-permute-start.30 = (bf16[2,2,64,256]{3,2,1,0:T(8,128)(2,1)S(1)}, bf16[2,2,64,256]{3,2,1,0:T(8,128)(2,1)S(1)}, u32[]{:S(2)}, u32[]{:S(2)}) collective-permute-start(bf16[2,2,64,256]{3,2,1,0:T(8,128)(2,1)S(1)} %pad_maximum_fusion.31), channel_id=1, source_target_pairs={{0,8},{8,0},{1,9},{9,1},{2,10},{10,2},{3,11},{11,3},{4,12},{12,4},... | collective-permute-start | bytes 393224 | tf_op jit(solution)/shard_map/ppermute | solution.py:39
  365.0 20.2 %collective-permute-start.34 = (bf16[2,2,256,1024]{3,2,1,0:T(8,128)(2,1)}, bf16[2,2,256,1024]{3,2,1,0:T(8,128)(2,1)}, u32[]{:S(2)}, u32[]{:S(2)}) collective-permute-start(bf16[2,2,256,1024]{3,2,1,0:T(8,128)(2,1)} %fusion.17), channel_id=1, source_target_pairs={{0,8},{8,0},{1,9},{9,1},{2,10},{10,2},{3,11},{11,3},{4,12},{12,4},... | collective-permute-start | bytes 6291464 | tf_op jit(solution)/shard_map/ppermute | solution.py:39
  367.1 14.1 %collective-permute-start.31 = (bf16[2,64,256]{2,1,0:T(8,128)(2,1)S(1)}, bf16[2,64,256]{2,1,0:T(8,128)(2,1)S(1)}, u32[]{:S(2)}, u32[]{:S(2)}) collective-permute-start(bf16[2,64,256]{2,1,0:T(8,128)(2,1)S(1)} %fusion.87), channel_id=1, source_target_pairs={{0,16},{16,0},{1,17},{17,1},{2,18},{18,2},{3,19},{19,3},{4,20},{20... | collective-permute-start | bytes 196616 | tf_op jit(solution)/shard_map/ppermute | solution.py:39
  367.6 17.6 %copy-start.4 = (bf16[1024,1024]{1,0:T(8,128)(2,1)S(1)}, bf16[1024,1024]{1,0:T(8,128)(2,1)}, u32[]{:S(2)}) copy-start(bf16[1024,1024]{1,0:T(8,128)(2,1)} %copy-done.3) | copy-start | bytes 6291460
  369.3 25.4 %collective-permute-start.26 = (bf16[128,1024]{1,0:T(8,128)(2,1)}, bf16[128,1024]{1,0:T(8,128)(2,1)}, u32[]{:S(2)}, u32[]{:S(2)}) collective-permute-start(bf16[128,1024]{1,0:T(8,128)(2,1)} %get-tuple-element.28), channel_id=1, source_target_pairs={{0,16},{16,0},{1,17},{17,1},{2,18},{18,2},{3,19},{19,3},{4,20},{20... | collective-permute-start | bytes 786440 | tf_op jit(solution)/shard_map/ppermute | solution.py:39
  391.2 27.3 %collective-permute-start.35 = (bf16[2,256,1024]{2,1,0:T(8,128)(2,1)}, bf16[2,256,1024]{2,1,0:T(8,128)(2,1)}, u32[]{:S(2)}, u32[]{:S(2)}) collective-permute-start(bf16[2,256,1024]{2,1,0:T(8,128)(2,1)} %fusion.40), channel_id=1, source_target_pairs={{0,16},{16,0},{1,17},{17,1},{2,18},{18,2},{3,19},{19,3},{4,20},{20... | collective-permute-start | bytes 3145736 | tf_op jit(solution)/shard_map/ppermute | solution.py:39
  395.8 2.0 collective-permute-start.27
  395.8 22.6 %copy-start.12 = (f32[2,2,256,1024]{3,2,1,0:T(8,128)S(1)}, f32[2,2,256,1024]{3,2,1,0:T(8,128)}, u32[]{:S(2)}) copy-start(f32[2,2,256,1024]{3,2,1,0:T(8,128)} %copy-done.11) | copy-start | bytes 12582916
  397.3 21.1 %copy-start.40 = (f32[64,1024]{1,0:T(8,128)}, f32[64,1024]{1,0:T(8,128)S(1)}, u32[]{:S(2)}) copy-start(f32[64,1024]{1,0:T(8,128)S(1)} %convolution_add_fusion.5) | copy-start | bytes 786436
  424.4 142.8 %reduce-scatter.5.cloned.1.call-start = ((), (), s32[]{:S(2)}) async-start(), calls=%async_computation.6 | async-start | bytes 1769472 | tf_op jit(solution)/shard_map/reduce_scatter | solution.py:398
  426.6 1.3 collective-permute-start.32
  428.5 19.8 %collective-permute-start.33 = (bf16[16,1024]{1,0:T(8,128)(2,1)}, bf16[16,1024]{1,0:T(8,128)(2,1)}, u32[]{:S(2)}, u32[]{:S(2)}) collective-permute-start(bf16[16,1024]{1,0:T(8,128)(2,1)} %fusion.93), channel_id=1, source_target_pairs={{0,16},{16,0},{1,17},{17,1},{2,18},{18,2},{3,19},{19,3},{4,20},{20... | collective-permute-start | bytes 98312 | tf_op jit(solution)/shard_map/ppermute | solution.py:39
  438.9 6.4 %collective-permute-start.28 = (bf16[2,128,1024]{2,1,0:T(8,128)(2,1)}, bf16[2,128,1024]{2,1,0:T(8,128)(2,1)}, u32[]{:S(2)}, u32[]{:S(2)}) collective-permute-start(bf16[2,128,1024]{2,1,0:T(8,128)(2,1)} %bitcast.133), channel_id=1, source_target_pairs={{0,8},{8,0},{1,9},{9,1},{2,10},{10,2},{3,11},{11,3},{4,12},{12,4},... | collective-permute-start | bytes 1572872 | tf_op jit(solution)/shard_map/ppermute | solution.py:39
  445.4 10.7 %copy-start.58 = (f32[1,32,32]{2,0,1:T(1,128)S(1)}, f32[1,32,32]{2,0,1:T(1,128)}, u32[]{:S(2)}) copy-start(f32[1,32,32]{2,0,1:T(1,128)} %stack.257) | copy-start | bytes 12292
  445.4 10.7 %copy-start.59 = (f32[1,32,32]{2,0,1:T(1,128)S(1)}, f32[1,32,32]{2,0,1:T(1,128)}, u32[]{:S(2)}) copy-start(f32[1,32,32]{2,0,1:T(1,128)} %stack.260) | copy-start | bytes 12292
  445.5 10.7 %copy-start.60 = (f32[1,32,32]{2,0,1:T(1,128)S(1)}, f32[1,32,32]{2,0,1:T(1,128)}, u32[]{:S(2)}) copy-start(f32[1,32,32]{2,0,1:T(1,128)} %stack.263) | copy-start | bytes 12292
  445.5 11.2 %copy-start.49 = (f32[32,256]{1,0:T(8,128)S(1)}, f32[32,256]{1,0:T(8,128)}, u32[]{:S(2)}) copy-start(f32[32,256]{1,0:T(8,128)} %reshape.999) | copy-start | bytes 98308
  446.8 17.9 %copy-start.31 = (f32[128,1024]{1,0:T(8,128)S(1)}, f32[128,1024]{1,0:T(8,128)}, u32[]{:S(2)}) copy-start(f32[128,1024]{1,0:T(8,128)} %get-tuple-element.29) | copy-start | bytes 1572868
  446.8 8.8 %collective-permute-start.29 = (bf16[128,1024]{1,0:T(8,128)(2,1)S(1)}, bf16[128,1024]{1,0:T(8,128)(2,1)S(1)}, u32[]{:S(2)}, u32[]{:S(2)}) collective-permute-start(bf16[128,1024]{1,0:T(8,128)(2,1)S(1)} %fusion.72), channel_id=1, source_target_pairs={{0,16},{16,0},{1,17},{17,1},{2,18},{18,2},{3,19},{19,3},{4,20},{20... | collective-permute-start | bytes 786440 | tf_op jit(solution)/shard_map/ppermute | solution.py:39
  457.5 14.7 %all-to-all-start.1 = ((f32[32,1,672]{2,1,0:T(1,128)}), f32[32,1,672]{2,1,0:T(1,128)S(1)}, u32[]{:S(2)}, u32[]{:S(2)}) async-start(f32[32,1,672]{2,1,0:T(1,128)} %copy.120), calls=%async_computation.5 | async-start | bytes 196608 | tf_op jit(solution)/shard_map/all_to_all | solution.py:432
  474.7 8.0 %collective-permute-start.36 = (bf16[32,2048]{1,0:T(8,128)(2,1)S(1)}, bf16[32,2048]{1,0:T(8,128)(2,1)S(1)}, u32[]{:S(2)}, u32[]{:S(2)}) collective-permute-start(bf16[32,2048]{1,0:T(8,128)(2,1)S(1)} %get-tuple-element.62), channel_id=1, source_target_pairs={{0,2},{2,0},{4,6},{6,4},{1,3},{3,1},{5,7},{7,5},{8,10},{10,8},{12,... | collective-permute-start | bytes 393224 | tf_op jit(solution)/shard_map/ppermute | solution.py:39
  475.4 16.9 %collective-permute-start.37 = (bf16[32,2048]{1,0:T(8,128)(2,1)S(1)}, bf16[32,2048]{1,0:T(8,128)(2,1)S(1)}, u32[]{:S(2)}, u32[]{:S(2)}) collective-permute-start(bf16[32,2048]{1,0:T(8,128)(2,1)S(1)} %get-tuple-element.61), channel_id=1, source_target_pairs={{0,4},{2,6},{4,0},{6,2},{1,5},{3,7},{5,1},{7,3},{8,12},{10,14},{12... | collective-permute-start | bytes 393224 | tf_op jit(solution)/shard_map/ppermute | solution.py:39
  476.3 16.0 %collective-permute-start.38 = (bf16[32,2048]{1,0:T(8,128)(2,1)S(1)}, bf16[32,2048]{1,0:T(8,128)(2,1)S(1)}, u32[]{:S(2)}, u32[]{:S(2)}) collective-permute-start(bf16[32,2048]{1,0:T(8,128)(2,1)S(1)} %get-tuple-element.60), channel_id=1, source_target_pairs={{0,6},{2,4},{4,2},{6,0},{1,7},{3,5},{5,3},{7,1},{8,14},{10,12},{12... | collective-permute-start | bytes 393224 | tf_op jit(solution)/shard_map/ppermute | solution.py:39
  501.0 71.5 %copy-start.42 = (bf16[1,160,1024]{2,1,0:T(8,128)(2,1)S(1)}, bf16[1,160,1024]{2,1,0:T(8,128)(2,1)}, u32[]{:S(2)}) copy-start(bf16[1,160,1024]{2,1,0:T(8,128)(2,1)} %reduce-scatter.7.cloned.1.call-done) | copy-start | bytes 983044
  569.1 10.2 %all-to-all-start = ((bf16[4,5,32,256]{3,2,1,0:T(8,128)(2,1)}), bf16[4,5,32,256]{3,2,1,0:T(8,128)(2,1)S(1)}, u32[]{:S(2)}, u32[]{:S(2)}) async-start(bf16[4,5,32,256]{3,2,1,0:T(8,128)(2,1)} %copy.115), calls=%async_computation.2 | async-start | bytes 655360 | tf_op jit(solution)/shard_map/all_to_all | solution.py:402
  (89 other events, 362.7 us)
Sparse Core Ops, SparseCore 0:
  11.5 150.4 all-gather.4
  164.5 56.0 all-gather.6
  275.7 59.4 reduce-scatter.8
  338.8 60.4 reduce-scatter.10
  424.5 76.4 reduce-scatter.6
  504.3 62.8 reduce-scatter.4

commit v3 on v2

v3 whole, which is shorter than its diff:
```python
import functools
import math

import jax
import jax.numpy as jnp
from jax import lax
from jax.experimental import pallas as pl
from jax.experimental.pallas import tpu as pltpu
from jax.sharding import Mesh
from jax.sharding import PartitionSpec as P

HEADS = 16
EPSILON = 1e-05
NEGATIVE = -1e30
GELU_IN = math.sqrt(2.0 / math.pi)
GELU_CUBE = 0.044715
SEQ = ("y", "core")
FSDP = ("z", "x")
PLANE = ("x", "y", "core")
ALL = ("y", "core", "z", "x")
BF = jnp.bfloat16
F32 = jnp.float32
VMEM_LIMIT = 52 * 1024 * 1024


def matmul(left, right):
    return jnp.dot(left, right, preferred_element_type=F32)


def swap(value, axis, step):
    return lax.ppermute(value, axis, [(i, i ^ step) for i in range(lax.axis_size(axis))])


def norm_parts(values):
    centred = values - jnp.mean(values, axis=-1, keepdims=True)
    scale = lax.rsqrt(jnp.mean(centred * centred, axis=-1, keepdims=True) + EPSILON)
    return centred * scale, scale


def norm_back(normed, scale, gain, grad):
    inner = grad * gain
    means = jnp.mean(inner, axis=-1, keepdims=True)
    along = jnp.mean(inner * normed, axis=-1, keepdims=True)
    return (
        scale * (inner - means - normed * along),
        jnp.sum(grad * normed, axis=0, keepdims=True),
        jnp.sum(grad, axis=0, keepdims=True),
    )


def nt(left, right):
    return lax.dot_general(left, right, (((1,), (1,)), ((), ())), preferred_element_type=F32)


def tn(left, right):
    return lax.dot_general(left, right, (((0,), (0,)), ((), ())), preferred_element_type=F32)


def total_rows(values):
    return jnp.sum(values, axis=0, keepdims=True)


def call(kernel, outs, scratch, scalars, *operands, flops=0):
    vmem = pl.BlockSpec(memory_space=pltpu.VMEM)
    moved = sum(o.size * o.dtype.itemsize for o in operands)
    return pl.pallas_call(
        kernel,
        out_shape=[jax.ShapeDtypeStruct(shape, kind) for shape, kind in outs],
        in_specs=[pl.BlockSpec(memory_space=pltpu.SMEM)] + [vmem] * len(operands),
        out_specs=[vmem] * len(outs),
        scratch_shapes=[pltpu.VMEM(shape, kind) for shape, kind in scratch],
        compiler_params=pltpu.CompilerParams(vmem_limit_bytes=VMEM_LIMIT),
        cost_estimate=pl.CostEstimate(flops=flops, bytes_accessed=moved, transcendentals=0),
    )(scalars, *operands)


def softmax_rows(scores, bias):
    scores = scores + bias
    top = jnp.max(scores, axis=1, keepdims=True)
    raised = jnp.exp(scores - top)
    whole = jnp.maximum(jnp.sum(raised, axis=1, keepdims=True), 1.0)
    scale = jnp.where(top > 0.5 * NEGATIVE, 1.0 / whole, 0.0)
    return raised * scale, top, scale


def softmax_again(scores, bias, top, scale):
    return jnp.exp(scores + bias - top) * scale


def softmax_back(chance, chance_grad):
    return chance * (chance_grad - jnp.sum(chance * chance_grad, axis=1, keepdims=True))


def bias_of(query_seg, key_seg, query_pos=None, key_pos=None):
    allowed = (query_seg == key_seg) & (query_seg != 0)
    if query_pos is not None:
        allowed = allowed & (key_pos <= query_pos)
    return jnp.where(allowed, 0.0, NEGATIVE)


def self_forward(
    z_size, x_size, held, lane, heads, at, lines, row, seg, seg_line, pos, pos_line,
    weights, params, up_bias, normed, query, key, value, stats, mixed,
):
    z_place, x_place = at[0], at[1]
    width = row.shape[1]
    cut = query.shape[1]
    row_len = row.shape[0]
    block = min(row_len, 512)
    for j in range(z_size * x_size):
        kx, kz = (j % x_size) ^ x_place, (j // x_size) ^ z_place
        for m in range(3):
            weights[m, j * held : (j + 1) * held, :] = lines[kx, kz, m * held : (m + 1) * held, :]
        small = lines[kx, kz, 3 * held :, :].astype(F32)
        for r in range(13):
            o, c = divmod(r * lane, cut)
            params[r : r + 1, j * lane : (j + 1) * lane] = small[o : o + 1, c : c + lane]
    part = up_bias.shape[1] // x_size
    for xx in range(x_size):
        small = lines[xx ^ x_place, 0, 3 * held :, :].astype(F32)
        for r in range(part // lane):
            o, c = divmod((13 + r) * lane, cut)
            first = xx * part + r * lane
            up_bias[:, first : first + lane] = small[o : o + 1, c : c + lane]
    gain, shift = params[7:8, :], params[10:11, :]
    both = jnp.zeros((2, cut), F32)
    for j in range(width // cut):
        both = jnp.where(at[2] == j, params[0:2, j * cut : (j + 1) * cut], both)
    query_bias, value_bias = both[0:1], both[1:2]
    for b in range(row_len // block):
        rows = slice(b * block, (b + 1) * block)
        unit, _ = norm_parts(row[rows, :].astype(F32))
        h = (unit * gain + shift).astype(BF)
        normed[rows, :] = h
        query[rows, :] = (matmul(h, weights[0]) + query_bias).astype(BF)
        key[rows, :] = matmul(h, weights[1]).astype(BF)
        value[rows, :] = (matmul(h, weights[2]) + value_bias).astype(BF)
    size = cut // heads
    score_scale = 1.0 / math.sqrt(size)
    for b in range(row_len // block):
        rows = slice(b * block, (b + 1) * block)
        bias = bias_of(seg[rows, :], seg_line[...], pos[rows, :], pos_line[...])
        for h in range(heads):
            cols = slice(h * size, (h + 1) * size)
            scores = nt(query[rows, cols], key[:, cols]) * score_scale
            chance, top, scale = softmax_rows(scores, bias)
            stats[rows, h : h + 1] = top
            stats[rows, 64 + h : 65 + h] = scale
            mixed[rows, cols] = matmul(chance.astype(BF), value[:, cols]).astype(BF)


def matrix(rest, m):
    values = rest[:, m]
    return values.reshape(values.shape[0] * values.shape[1], values.shape[2])


def middle_forward(
    s_size, at, parts, inputs, rest, params, sources, seg, source_seg,
    after_self, after_cross, left, query, stats, keys, normed,
):
    width = inputs.shape[1]
    cut = width // s_size
    for j in range(s_size):
        left[:, 2 * width + j * cut : 2 * width + (j + 1) * cut] = parts[at[j]]
        for n in range(2):
            keys[n, :, j * cut : (j + 1) * cut] = sources[at[j], n]
    x1 = (
        inputs[...].astype(F32)
        + matmul(left[:, 2 * width :], matrix(rest, 1))
        + params[2:3, :]
    )
    after_self[...] = x1
    unit, _ = norm_parts(x1)
    left[:, :width] = (unit * params[8:9, :] + params[11:12, :]).astype(BF)
    query[...] = (matmul(left[:, :width], matrix(rest, 0)) + params[3:4, :]).astype(BF)
    bias = bias_of(seg[...], source_seg[...])
    size = width // HEADS
    score_scale = 1.0 / math.sqrt(size)
    for h in range(HEADS):
        cols = slice(h * size, (h + 1) * size)
        scores = nt(query[:, cols], keys[0, :, cols]) * score_scale
        chance, top, scale = softmax_rows(scores, bias)
        stats[:, h : h + 1] = top
        stats[:, 64 + h : 65 + h] = scale
        left[:, width + h * size : width + (h + 1) * size] = matmul(
            chance.astype(BF), keys[1, :, cols]
        ).astype(BF)
    x2 = x1 + matmul(left[:, width : 2 * width], matrix(rest, 2)) + params[5:6, :]
    after_cross[...] = x2
    unit, _ = norm_parts(x2)
    normed[...] = (unit * params[9:10, :] + params[12:13, :]).astype(BF)


def middle_backward(
    s_size, at, terms, out_grad, after_self, after_cross, rest, params, query,
    keys, stats, seg, source_seg,
    branch, self_grad, pair, sums,
):
    tokens, width = out_grad.shape
    cut = width // s_size
    size = width // HEADS
    score_scale = 1.0 / math.sqrt(size)
    down = out_grad[...].astype(F32)
    grad = terms[...].astype(F32)
    unit, scale = norm_parts(after_cross[...])
    moved, gain, shift = norm_back(unit, scale, params[9:10, :], grad)
    sums[2:3, :] = gain
    sums[5:6, :] = shift
    x2_grad = down + moved
    d2 = x2_grad.astype(BF)
    sums[6:7, :] = total_rows(d2.astype(F32))
    sums[7:8, :] = total_rows(down)
    for j in range(s_size):
        pair[at[j], :tokens, cut:] = d2[:, j * cut : (j + 1) * cut]
    head_grad = nt(d2, matrix(rest, 2)).astype(BF)
    bias = bias_of(seg[...], source_seg[...])
    per = HEADS // s_size
    grads = []
    for h in range(HEADS):
        cols = slice(h * size, (h + 1) * size)
        q, do = query[:, cols], head_grad[:, cols]
        k, v = keys[0, :, cols], keys[1, :, cols]
        scores = nt(q, k) * score_scale
        chance = softmax_again(scores, bias, stats[:, h : h + 1], stats[:, 64 + h : 65 + h])
        score_grad = softmax_back(chance, nt(do, v)).astype(BF)
        grads.append((matmul(score_grad, k) * score_scale).astype(BF))
        to = slice((h % per) * size, (h % per + 1) * size)
        pair[at[h // per], tokens:, to] = (tn(score_grad, q) * score_scale).astype(BF)
        to = slice(cut + to.start, cut + to.stop)
        pair[at[h // per], tokens:, to] = tn(chance.astype(BF), do).astype(BF)
    query_grad = jnp.concatenate(grads, axis=1)
    sums[8:9, :] = total_rows(query_grad.astype(F32))
    for j in range(s_size):
        pair[at[j], :tokens, :cut] = query_grad[:, j * cut : (j + 1) * cut]
    unit, scale = norm_parts(after_self[...])
    moved, gain, shift = norm_back(unit, scale, params[8:9, :], nt(query_grad, matrix(rest, 0)))
    sums[1:2, :] = gain
    sums[4:5, :] = shift
    x1_grad = x2_grad + moved
    self_grad[...] = x1_grad
    d1 = x1_grad.astype(BF)
    branch[...] = d1
    sums[9:10, :] = total_rows(d1.astype(F32))


def feed_forward(
    steps, normed, down, w_up, w_down, up_bias,
    activated, pre_grad, partial, bias_grad,
    held, total,
):
    step = pl.program_id(0)
    groups, z_size, share, columns = w_up.shape
    per = groups * share
    for z in range(z_size):
        held[z * per : (z + 1) * per, :] = w_up[:, z].reshape(per, columns)
    u = matmul(normed[...], held[...]) + up_bias[...]
    square = u * u
    bent = jnp.tanh(GELU_IN * (u + GELU_CUBE * square * u))
    half = 0.5 * (1.0 + bent)
    activated[...] = (u * half).astype(BF)
    slope = half + 0.5 * u * (1.0 - bent * bent) * (GELU_IN + 3.0 * GELU_IN * GELU_CUBE * square)
    du = (nt(down[...], w_down[...]) * slope).astype(BF)
    pre_grad[...] = du
    bias_grad[...] = total_rows(du.astype(F32))
    term = nt(du, held[...])

    @pl.when(step == 0)
    def _():
        total[...] = term

    @pl.when(step > 0)
    def _():
        total[...] += term

    @pl.when(step == steps - 1)
    def _():
        partial[...] = total[...].astype(BF)


def feed_forward_gradients(
    s_size, z_size, x_size, up_rows, at, normed, pre_grad, activated, down, w_down,
    out, mixed,
):
    width = normed.shape[1]
    half = pre_grad.shape[1] // 2
    places = z_size * x_size
    unit = out.shape[1] - 2 * z_size * up_rows
    for b in range(x_size * s_size):
        term = tn(activated[:, b * unit : (b + 1) * unit], down[...])
        out[b, 2 * z_size * up_rows :, :] = term.astype(BF)
    for t in range(width // 256):
        cols = slice(t * 256, (t + 1) * 256)
        mixed[:, cols] = matmul(activated[...], w_down[:, cols]).astype(BF)
    tile = places * up_rows
    for s in range(s_size):
        for i in range(2):
            term = tn(normed[:, s * tile : (s + 1) * tile], pre_grad[:, i * half : (i + 1) * half])
            term = term.astype(BF)
            for f in range(places):
                z, x = divmod(f, x_size)
                first = (i * z_size + z) * up_rows
                out[x * s_size + s, first : first + up_rows, :] = term[f * up_rows : (f + 1) * up_rows]


def self_backward(
    heads, at, branch, w_out, query, key, value, stats, seg, seg_line, pos, pos_line, weights, normed,
    cuts, partial, sums,
    grads, key_total, value_total,
):
    row_len, cut = query.shape
    block = min(row_len, 512)
    size = cut // heads
    score_scale = 1.0 / math.sqrt(size)
    for b in range(row_len // block):
        rows = slice(b * block, (b + 1) * block)
        head_grad = nt(branch[rows, :], w_out[...]).astype(BF)
        bias = bias_of(seg[rows, :], seg_line[...], pos[rows, :], pos_line[...])
        for h in range(heads):
            cols = slice(h * size, (h + 1) * size)
            q, do, k, v = query[rows, cols], head_grad[:, cols], key[:, cols], value[:, cols]
            chance = softmax_again(
                nt(q, k) * score_scale, bias, stats[rows, h : h + 1], stats[rows, 64 + h : 65 + h]
            )
            score_grad = softmax_back(chance, nt(do, v)).astype(BF)
            grads[rows, cols] = (matmul(score_grad, k) * score_scale).astype(BF)
            key_term = tn(score_grad, q) * score_scale
            value_term = tn(chance.astype(BF), do)
            if b == 0:
                key_total[:, cols] = key_term
                value_total[:, cols] = value_term
            else:
                key_total[:, cols] += key_term
                value_total[:, cols] += value_term
    grads[:, cut : 2 * cut] = key_total[...].astype(BF)
    grads[:, 2 * cut :] = value_total[...].astype(BF)
    sums[0:1, :] = total_rows(grads[:, :cut].astype(F32))
    sums[1:2, :] = total_rows(grads[:, 2 * cut :].astype(F32))
    tile = min(256, normed.shape[1])
    for t in range(normed.shape[1] // tile):
        rows = slice(t * tile, (t + 1) * tile)
        cuts[rows, :] = tn(normed[:, rows], grads[...]).astype(BF)
    for b in range(row_len // block):
        rows = slice(b * block, (b + 1) * block)
        grad = nt(grads[rows, :cut], weights[0]) + nt(grads[rows, cut : 2 * cut], weights[1])
        partial[rows, :] = (grad + nt(grads[rows, 2 * cut :], weights[2])).astype(BF)


def group_gradients(at, own, swapped, pair, branch_cut, sources, source_grad, out):
    rows, cut = own.shape[0], branch_cut.shape[1]
    width = sources.shape[1]
    tile = min(256, width)
    for t in range(width // tile):
        to = slice(t * tile, (t + 1) * tile)
        for n in range(3):
            cols = slice(n * width + t * tile, n * width + (t + 1) * tile)
            right = branch_cut if n == 2 else pair
            first = n * cut if n < 2 else 0
            term = tn(own[:, cols], right[:rows, first : first + cut])
            term = term + tn(swapped[:, cols], right[rows:, first : first + cut])
            out[to, n * cut : (n + 1) * cut] = term.astype(BF)
        for n in range(2):
            out[to, (3 + n) * cut : (4 + n) * cut] = tn(sources[:, to], source_grad[n]).astype(BF)


def last_step(at, line, others, inputs, params, self_grad, sums, cut_sums, up_bias_grad, grad_hidden, table, rows):
    count, _, lanes = table.shape
    width = inputs.shape[1]
    unit, scale = norm_parts(inputs[...].astype(F32))
    grad = line[...] + jnp.sum(others[...].astype(F32), axis=0)
    moved, gain, shift = norm_back(unit, scale, params[7:8, :], grad)
    grad_hidden[...] = self_grad[...] + moved
    rows[...] = jnp.zeros(rows.shape, F32)
    rows[0:2, :] = cut_sums[0:2, :]
    rows[2:3, :] = sums[9:10, :]
    rows[3:4, :] = sums[8:9, :]
    rows[4:5, :] = cut_sums[2:3, :]
    rows[5:7, :] = sums[6:8, :]
    rows[7:8, :] = gain
    rows[8:10, :] = sums[1:3, :]
    rows[10:11, :] = shift
    rows[11:13, :] = sums[4:6, :]
    for j in range(count):
        table[j, 0:16, :] = rows[:, j * lanes : (j + 1) * lanes]
    table[:, 16:24, :] = jnp.zeros((count, 8, lanes), F32)
    mine = up_bias_grad.shape[1] // (8 * lanes)
    for j in range(mine):
        for r in range(8):
            first = (j * 8 + r) * lanes
            table[at[0] * mine + j, 16 + r : 17 + r, :] = up_bias_grad[:, first : first + lanes]


def gather_pair(value):
    lines = [value] + [swap(value, "y", k) for k in range(1, lax.axis_size("y"))]
    lines = jnp.concatenate(lines) if len(lines) > 1 else value
    return lines, swap(lines, "core", 1)


def gather_seq(value):
    return jnp.concatenate(gather_pair(value))


def scatter_seq(partial):
    line = partial[0].astype(F32) + swap(partial[1].astype(BF), "core", 1).astype(F32)
    total = line[0]
    for k in range(1, lax.axis_size("y")):
        total = total + swap(line[k].astype(BF), "y", k).astype(F32)
    return total


def exchange_seq(value):
    line = jnp.stack([value[0], swap(value[1], "core", 1)])
    lines = [line[:, 0]] + [swap(line[:, k], "y", k) for k in range(1, lax.axis_size("y"))]
    return jnp.stack(lines, axis=1)


def trade_z(parts):
    return lax.all_to_all(parts, "z", 0, 0)


def gather_z(value):
    return trade_z(jnp.broadcast_to(value, (lax.axis_size("z"),) + value.shape))


def behind(value, other):
    last = other[(-1,) * other.ndim].astype(F32) * 0.0
    return value + last.astype(value.dtype)


def pick(value, at, axis=0):
    return lax.dynamic_index_in_dim(value, at, axis, keepdims=False)


def body(
    hidden_in,
    memory,
    out_grad,
    segment_ids,
    memory_segments,
    deal,
    attn_in,
    attn_out,
    fc1,
    fc2,
    proj_bias,
    fc1_bias,
    norm_gain,
    norm_bias,
):
    y_size, z_size, x_size = lax.axis_size("y"), lax.axis_size("z"), lax.axis_size("x")
    s_size, f_size = y_size * 2, z_size * x_size
    y_place, core_place = lax.axis_index("y"), lax.axis_index("core")
    z_place, x_place = lax.axis_index("z"), lax.axis_index("x")
    s_place = y_place * 2 + core_place
    f_place = z_place * x_size + x_place
    place = s_place * f_size + f_place
    count = s_size * f_size
    tokens, width = hidden_in.shape[1:]
    sources_len = memory.shape[1]
    held = attn_in.shape[2]
    share = held // s_size
    lane = width // f_size
    cut = width // s_size
    row_len = s_size * tokens
    blocks = [(c, k) for c in range(2) for k in range(y_size)]
    block_of = [((j % 2) ^ core_place) * y_size + ((j // 2) ^ y_place) for j in range(s_size)]
    owners = jnp.stack([(y_place ^ k) * 2 + (core_place ^ c) for c, k in blocks])

    def cut_cols(value, at):
        return lax.dynamic_slice_in_dim(value, at * cut, cut, value.ndim - 1)

    here = jnp.stack([z_place, x_place, s_place]).astype(jnp.int32)
    block_list = jnp.stack(block_of).astype(jnp.int32)

    small = jnp.concatenate(
        [
            proj_bias.reshape(-1).astype(BF),
            norm_gain.reshape(-1).astype(BF),
            norm_bias.reshape(-1).astype(BF),
            fc1_bias.astype(BF),
        ]
    )
    small_len = small.shape[0]
    small_rows = -(-small_len // (16 * cut)) * 16
    small = jnp.pad(small, (0, small_rows * cut - small_len)).reshape(small_rows, cut)
    early = jnp.concatenate([cut_cols(attn_in[0], s_place).astype(BF).reshape(3 * held, cut), small])

    rest = jnp.concatenate(
        [
            lax.dynamic_slice_in_dim(attn_in[1, 0], s_place * share, share, 0),
            lax.dynamic_slice_in_dim(attn_out, s_place * share, share, 1).reshape(-1, width),
        ]
    ).astype(BF)
    labels = jnp.concatenate([segment_ids[0], memory_segments[0]]).astype(BF)
    label_rows = -(-labels.shape[0] // (16 * width)) * 16
    labels = jnp.pad(labels, (0, label_rows * width - labels.shape[0])).reshape(label_rows, width)
    row = jnp.concatenate([hidden_in[0], memory[0], labels])
    row_lines = [row] + [swap(row, "y", k) for k in range(1, y_size)]
    row_lines = jnp.concatenate(row_lines)
    row = jnp.concatenate([row_lines, swap(row_lines, "core", 1)])
    early_lines = [early] + [swap(early, "z", k) for k in range(1, z_size)]
    early_lines = jnp.stack(early_lines)
    unit = fc2.shape[0] // s_size
    hidden = x_size * fc2.shape[0]
    down_share = lax.dynamic_slice_in_dim(fc2, s_place * unit, unit, 0).astype(BF)
    down_lines = [swap(down_share, "x", k) for k in range(1, x_size)]
    send = behind(early_lines, down_lines[-1])

    up_share = lax.dynamic_slice_in_dim(fc1, s_place * share, share, 0).astype(BF)
    up_share = up_share.reshape(share, z_size, hidden).transpose(1, 0, 2).reshape(z_size, -1, width)
    memory_cuts = cut_cols(attn_in[1, 1:], s_place).astype(BF).reshape(1, -1, width)
    memory_cuts = jnp.broadcast_to(memory_cuts, (z_size,) + memory_cuts.shape[1:])
    over_z = trade_z(jnp.concatenate([up_share, memory_cuts], axis=1))

    rest = lax.all_gather(rest, FSDP + SEQ).reshape(count, 3, share, width)
    if share % 16:
        rest = rest.transpose(1, 0, 2, 3).reshape(1, 3, width, width)
    early = jnp.stack([early_lines] + [swap(send, "x", k) for k in range(1, x_size)])

    row = row.reshape(s_size, tokens + sources_len + label_rows, width)
    row_inputs = row[:, :tokens].reshape(row_len, width)
    labels = row[:, tokens + sources_len :].reshape(s_size, label_rows * width).astype(jnp.int32)
    row_seg = labels[:, :tokens].reshape(-1)
    row_sources = jnp.concatenate(
        [pick(row, block_of[j])[tokens : tokens + sources_len] for j in range(s_size)]
    )
    source_seg = jnp.concatenate(
        [pick(labels, block_of[j])[tokens : tokens + sources_len] for j in range(s_size)]
    )
    half_rows = tokens // 2
    offsets = jnp.arange(half_rows, dtype=jnp.int32)
    row_pos = (deal.reshape(s_size, 2)[owners][:, :, None] * half_rows + offsets).reshape(-1)
    row_places = (row_seg[:, None], row_seg[None], row_pos[:, None], row_pos[None])
    places = (segment_ids[0][:, None], source_seg[None])

    heads = HEADS // s_size
    weights, params, up_bias, normed_row, query, key, value, stats, self_cut = call(
        functools.partial(self_forward, z_size, x_size, held, lane, heads),
        [
            ((3, width, cut), BF),
            ((16, width), F32),
            ((1, hidden), F32),
            ((row_len, width), BF),
            ((row_len, cut), BF),
            ((row_len, cut), BF),
            ((row_len, cut), BF),
            ((row_len, 128), F32),
            ((row_len, cut), BF),
        ],
        [],
        here,
        early,
        row_inputs,
        *row_places,
        flops=2 * row_len * cut * (3 * width + 2 * row_len),
    )
    parts = exchange_seq(self_cut.reshape(2, y_size, tokens, cut)).reshape(s_size, tokens, cut)

    late_z = behind(over_z, self_cut)
    up_parts = late_z[:, : up_share.shape[1]].reshape(z_size, share, hidden)
    memory_lines = late_z[:, up_share.shape[1] :].reshape(z_size, 2, held, cut)
    memory_lines = jnp.stack([memory_lines] + [swap(memory_lines, "x", k) for k in range(1, x_size)])
    w_memory = jnp.stack([pick(memory_lines, j ^ x_place) for j in range(x_size)])
    w_memory = w_memory.transpose(2, 1, 0, 3, 4).reshape(2, width, cut)
    source_key = matmul(row_sources, w_memory[0]).astype(BF)
    value_bias = cut_cols(params[4], s_place)
    source_value = (matmul(row_sources, w_memory[1]) + value_bias).astype(BF)
    sources_row = s_size * sources_len
    source_all = gather_seq(jnp.stack([source_key, source_value])[None])

    down_grad = out_grad[0]
    down_all = gather_z(behind(down_grad, late_z)).reshape(z_size * tokens, width)

    after_self, after_cross, left, query_cross, cross_stats, source_keys, normed_three = call(
        functools.partial(middle_forward, s_size),
        [
            ((tokens, width), F32),
            ((tokens, width), F32),
            ((tokens, 3 * width), BF),
            ((tokens, width), BF),
            ((tokens, 128), F32),
            ((2, sources_row, width), BF),
            ((tokens, width), BF),
        ],
        [],
        behind(block_list, down_all),
        parts,
        hidden_in[0],
        rest,
        params,
        source_all,
        *places,
        flops=2 * tokens * width * (3 * width + 2 * sources_row),
    )

    w_up = lax.all_gather(up_parts, PLANE).reshape(s_size * x_size, z_size, share, hidden)
    if share % 16:
        w_up = w_up.transpose(1, 0, 2, 3).reshape(1, 1, width, hidden)
    down_lines = [behind(line, normed_three) for line in down_lines]
    down_lines = [gather_seq(line).reshape(s_size, unit, width) for line in down_lines]
    down_lines = [
        jnp.concatenate([pick(line, block_of[j]) for j in range(s_size)]) for line in down_lines
    ]
    down_lines = jnp.stack([fc2.astype(BF)] + down_lines)
    w_down = jnp.concatenate([pick(down_lines, j ^ x_place) for j in range(x_size)])

    normed_all = gather_z(normed_three).reshape(z_size * tokens, width)
    group = z_size * tokens
    columns = 512
    activated, pre_grad, partial, grad_up_bias = pl.pallas_call(
        functools.partial(feed_forward, hidden // columns),
        grid=(hidden // columns,),
        out_shape=[
            jax.ShapeDtypeStruct((group, hidden), BF),
            jax.ShapeDtypeStruct((group, hidden), BF),
            jax.ShapeDtypeStruct((group, width), BF),
            jax.ShapeDtypeStruct((1, hidden), F32),
        ],
        in_specs=[
            pl.BlockSpec((group, width), lambda i: (0, 0)),
            pl.BlockSpec((group, width), lambda i: (0, 0)),
            pl.BlockSpec(w_up.shape[:3] + (columns,), lambda i: (0, 0, 0, i)),
            pl.BlockSpec((columns, width), lambda i: (i, 0)),
            pl.BlockSpec((1, columns), lambda i: (0, i)),
        ],
        out_specs=[
            pl.BlockSpec((group, columns), lambda i: (0, i)),
            pl.BlockSpec((group, columns), lambda i: (0, i)),
            pl.BlockSpec((group, width), lambda i: (0, 0)),
            pl.BlockSpec((1, columns), lambda i: (0, i)),
        ],
        scratch_shapes=[pltpu.VMEM((width, columns), BF), pltpu.VMEM((group, width), F32)],
        compiler_params=pltpu.CompilerParams(vmem_limit_bytes=VMEM_LIMIT),
        cost_estimate=pl.CostEstimate(
            flops=6 * group * width * hidden, bytes_accessed=12 << 20, transcendentals=group * hidden
        ),
    )(normed_all, down_all, w_up, w_down, up_bias)
    terms = lax.psum_scatter(partial.reshape(z_size, tokens, width), "z", scatter_dimension=0)
    up_rows = width // count
    half = hidden // 2
    first_rows = 2 * z_size * up_rows
    if up_rows % 16:
        late = behind(activated, partial)
        grad_down = tn(late, down_all).astype(BF)
        grad_up = [tn(normed_all, pre_grad[:, i * half : (i + 1) * half]) for i in range(2)]
        grad_up = jnp.stack(grad_up).astype(BF)
        grad_up = grad_up.reshape(2, s_size, z_size, x_size, up_rows, half)
        grad_up = grad_up.transpose(3, 1, 0, 2, 4, 5).reshape(x_size * s_size, -1, width)
        grad_down = grad_down.reshape(x_size * s_size, unit, width)
        grad_mlp = jnp.concatenate([grad_up, grad_down], axis=1)
        mixed_down = matmul(activated, w_down).astype(BF)
    else:
        grad_mlp, mixed_down = call(
            functools.partial(feed_forward_gradients, s_size, z_size, x_size, up_rows),
            [((x_size * s_size, first_rows + unit, width), BF), ((group, width), BF)],
            [],
            behind(here, partial),
            normed_all,
            pre_grad,
            activated,
            down_all,
            w_down,
            flops=6 * group * width * hidden,
        )
    terms = behind(terms, mixed_down)
    grad_mlp = lax.psum_scatter(grad_mlp, PLANE, scatter_dimension=0)
    grad_up = grad_mlp[:-unit].reshape(2, z_size, up_rows, half)
    grad_down = lax.ppermute(
        grad_mlp[-unit:],
        ALL,
        [(s * f_size + f, f * s_size + s) for s in range(s_size) for f in range(f_size)],
    ).astype(F32)
    grad_up = jnp.stack(
        [
            swap(pick(grad_up, z_place ^ k, 1), "z", k) if k else pick(grad_up, z_place, 1)
            for k in range(z_size)
        ]
    )
    grad_up = jnp.stack([pick(grad_up, z_place ^ j) for j in range(z_size)])
    grad_up = grad_up.transpose(2, 0, 1, 3).reshape(up_rows, -1).astype(F32)

    branch, self_grad, pair, sums = call(
        functools.partial(middle_backward, s_size),
        [
            ((tokens, width), BF),
            ((tokens, width), F32),
            ((s_size, tokens + sources_row, 2 * cut), BF),
            ((16, width), F32),
        ],
        [],
        block_list,
        terms,
        down_grad,
        after_self,
        after_cross,
        rest,
        params,
        query_cross,
        source_keys,
        cross_stats,
        *places,
        flops=2 * tokens * width * (2 * width + 5 * sources_row),
    )

    results = trade_z(behind(mixed_down, terms).reshape(z_size, tokens, width))

    branch_row = gather_seq(branch)
    left_own, left_swapped = gather_pair(behind(left, branch_row))
    pair = behind(pair, branch_row)
    pair = exchange_seq(pair.reshape((2, y_size) + pair.shape[1:])).reshape(pair.shape)
    source_grad = jnp.sum(pair[:, tokens:].astype(F32), axis=0).astype(BF)
    source_grad = jnp.stack([source_grad[:, :cut], source_grad[:, cut:]])
    pair = pair[:, :tokens].reshape(row_len, 2 * cut)
    w_out = rest[:, 1].reshape(width, width)
    w_out = lax.dynamic_slice_in_dim(w_out, s_place * cut, cut, 0)
    self_cuts, partial, cut_sums = call(
        functools.partial(self_backward, heads),
        [((width, 3 * cut), BF), ((row_len, width), BF), ((8, cut), F32)],
        [((row_len, 3 * cut), BF), ((row_len, cut), F32), ((row_len, cut), F32)],
        behind(here, results),
        branch_row,
        w_out,
        query,
        key,
        value,
        stats,
        *row_places,
        weights,
        normed_row,
        flops=2 * row_len * cut * (7 * width + 5 * row_len),
    )

    result = after_cross + jnp.sum(results.astype(F32), axis=0) + params[6]

    (group_cuts,) = call(
        group_gradients,
        [((width, 5 * cut), BF)],
        [],
        here,
        left_own,
        left_swapped,
        pair,
        cut_cols(branch_row, s_place),
        row_sources,
        source_grad,
        flops=2 * row_len * cut * 3 * width,
    )
    group_cuts = group_cuts.reshape(s_size * z_size, x_size, up_rows, 5 * cut)
    kept = pick(group_cuts, x_place, 1).astype(F32)
    for k in range(1, x_size):
        kept = kept + swap(pick(group_cuts, x_place ^ k, 1), "x", k).astype(F32)

    def whole_columns(grads, number):
        grads = jnp.sum(grads.astype(F32), axis=1).reshape(s_size, up_rows, number, cut)
        return grads.transpose(2, 1, 0, 3).reshape(number, up_rows, width)

    grad_memory = nt(source_grad[0], w_memory[0]) + nt(source_grad[1], w_memory[1])
    grad_memory = grad_memory.reshape(s_size, sources_len, width)
    grad_memory = jnp.stack([pick(grad_memory, owners[j]) for j in range(s_size)])
    grad_memory = scatter_seq(grad_memory.reshape(2, y_size, sources_len, width))

    partial = partial.reshape(2, y_size, tokens, width)
    line = partial[0].astype(F32) + swap(partial[1], "core", 1).astype(F32)
    others = jnp.stack([swap(line[k].astype(BF), "y", k) for k in range(1, y_size)])
    cut_sums = jnp.concatenate([cut_sums[:2], jnp.sum(source_grad[1].astype(F32), axis=0)[None]])
    cut_sums = lax.dynamic_update_slice(
        jnp.zeros((3, width), F32), cut_sums, (jnp.int32(0), (s_place * cut).astype(jnp.int32))
    )
    grad_hidden, table = call(
        last_step,
        [((tokens, width), F32), ((count, 24, up_rows), F32)],
        [((16, width), F32)],
        here,
        line[0],
        others,
        hidden_in[0],
        params,
        self_grad,
        sums,
        cut_sums,
        grad_up_bias,
    )

    self_cuts = self_cuts.reshape(count, up_rows, 3 * cut)
    self_cuts = lax.all_to_all(self_cuts, ALL, 0, 0).reshape(s_size, f_size, up_rows, 3 * cut)
    table = behind(behind(table, self_cuts), grad_memory)
    table = jnp.sum(lax.all_to_all(table, ALL, 0, 0), axis=0)
    kept = behind(kept, table)
    kept = lax.all_to_all(kept.astype(BF), ("y", "core", "z"), 0, 0)
    group_cuts = whole_columns(kept.reshape(s_size, z_size, up_rows, 5 * cut), 5)
    self_cuts = whole_columns(self_cuts, 3)
    return (
        result.astype(BF)[None],
        grad_hidden[None],
        grad_memory[None],
        jnp.stack([self_cuts, jnp.concatenate([group_cuts[:1], group_cuts[3:]])]),
        jnp.stack([group_cuts[2], group_cuts[1]]),
        grad_up,
        grad_down,
        table[:7],
        table[16:].reshape(-1),
        table[7:10],
        table[10:13],
    )


def solution(mesh):
    seq, fsdp = mesh.shape["seq"], mesh.shape["fsdp"]
    split = Mesh(mesh.devices.reshape(seq // 2, 2, 4, fsdp // 4), ALL)
    placed = (
        P(FSDP, SEQ, None),
        P(FSDP, SEQ, None),
        P(FSDP, SEQ, None),
        P(FSDP, SEQ),
        P(FSDP, SEQ),
        P(),
        P(None, None, FSDP, None),
        P(None, FSDP, None),
        P(FSDP, None),
        P(FSDP, None),
        P(None, FSDP),
        P(FSDP),
        P(None, FSDP),
        P(None, FSDP),
    )
    return jax.shard_map(
        body,
        mesh=split,
        in_specs=placed,
        out_specs=(
            P(FSDP, SEQ, None),
            P(FSDP, SEQ, None),
            P(FSDP, SEQ, None),
            P(None, None, ALL, None),
            P(None, ALL, None),
            P(ALL, None),
            P(ALL, None),
            P(None, ALL),
            P(ALL),
            P(None, ALL),
            P(None, ALL),
        ),
        check_vma=False,
    )
```

time: 598 us -> 467 us (0.78)
  the two profiles are of different devices: /device:TPU:0 before, /device:TPU:1 now
where the time goes in v3:
time: 467 us; the launch traced here: 458 us
  waiting for transfers between devices  166 us (36%)
  starting transfers between devices  86.7 us (19%)
  Pallas kernels  68.1 us (15%)
  local copies, waits for them, and re-layouts  52.1 us (11%)
  other arithmetic  39.7 us (9%)
  between operations  24 us (5%)
  blocking collectives  19.4 us (4%)
    ppermute x28, waiting for transfers between devices, swap(): lax.ppermute(value, axis, [(i, i ^ step) for i in range(lax.axis_size(axi...  103 us
    pallas_call x7, Pallas kernels, call(): pl.pallas_call(kernel, out_shape=[jax.ShapeDtypeStruct(shape, kind) for s...  55.8 us
    ppermute x28, starting transfers between devices, swap(): lax.ppermute(value, axis, [(i, i ^ step) for i in range(lax.axis_size(axi...  51.6 us
    all_to_all x1, waiting for transfers between devices, body(): kept = lax.all_to_all(kept.astype(BF), ('y', 'core', 'z'), 0, 0)  26.9 us
    all_to_all x4, waiting for transfers between devices, trade_z(): return lax.all_to_all(parts, 'z', 0, 0)  23.4 us
    all_to_all x1, blocking collectives, body(): table = jnp.sum(lax.all_to_all(table, ALL, 0, 0), axis=0)  19.4 us
    all_to_all x4, starting transfers between devices, trade_z(): return lax.all_to_all(parts, 'z', 0, 0)  18.6 us
    pallas_call x1, Pallas kernels, body(): pl.pallas_call(functools.partial(feed_forward, hidden // columns), grid=(...  12.3 us
  transfers between devices with their start and end apart: 39, of which 17 were waited for; matrix products, arithmetic and copies ran while one was open for 18% of the time, Pallas kernels for 12%

profile of v3, /device:TPU:1, one launch (start us, length us, event | category | flops | bytes accessed | tf_op | source)
XLA Modules:
  0.0 458.0 jit_solution(18386499611594702033)
XLA Ops:
  9.3 1.5 slice.253
  11.7 2.1 collective-permute-start
  13.8 2.3 collective-permute-start.1
  16.3 1.3 collective-permute-start.5
  17.6 2.1 dynamic-slice_convert_fusion
  20.9 1.3 slice.252
  22.3 1.3 dynamic-slice_convert_fusion.1
  25.6 4.5 all-to-all-start
  31.3 2.4 collective-permute-start.6
  35.8 2.4 fusion.16
  38.2 1.3 collective-permute-start.4
  41.1 15.2 %collective-permute-done.4 = bf16[4,400,256]{2,1,0:T(8,128)(2,1)} collective-permute-done((bf16[4,400,256]{2,1,0:T(8,128)(2,1)}, bf16[4,400,256]{2,1,0:T(8,128)(2,1)}, u32[]{:S(2)}, u32[]{:S(2)}) %collective-permute-start.4) | collective-permute-done | bytes 819232 | tf_op jit(solution)/shard_map/ppermute | solution.py:31
  56.4 2.8 pad_maximum_fusion.2.lines
  59.2 7.3 %shard_map.221 = (bf16[3,1024,256]{2,1,0:T(8,128)(2,1)}, f32[16,1024]{1,0:T(8,128)S(1)}, f32[1,2048]{1,0:T(1,128)S(1)}, bf16[512,1024]{1,0:T(8,128)(2,1)}, bf16[...) custom-call(s32[3]{0:T(128)S(1)} %pad_add_fusion.1.at, ...), custom_call_target="tpu_custom_call" | custom-call | flops 1073741824 | bytes 2695168 | tf_op jit(solution)/shard_map/pallas_call | solution.py:66
  75.9 1.3 slice.336
  79.0 5.1 %all-to-all-start.1 = ((bf16[4,128,1024]{2,1,0:T(8,128)(2,1)}), bf16[4,128,1024]{2,1,0:T(8,128)(2,1)S(1)}, u32[]{:S(2)}, u32[]{:S(2)}) async-start(bf16[4,128,1024]{2,1,0:T(8,128)(2,1)} %broadcast_in_dim.37), calls=%async_computation.1 | async-start | bytes 2097152 | tf_op jit(solution)/shard_map/all_to_all | solution.py:417
  84.2 15.5 %collective-permute-start.7 = (bf16[2,128,256]{2,1,0:T(8,128)(2,1)}, bf16[2,128,256]{2,1,0:T(8,128)(2,1)}, u32[]{:S(2)}, u32[]{:S(2)}) collective-permute-start(bf16[2,128,256]{2,1,0:T(8,128)(2,1)} %bitcast.39), channel_id=1, source_target_pairs={{0,8},{8,0},{1,9},{9,1},{2,10},{10,2},{3,11},{11,3},{4,12},{12,4},... | collective-permute-start | bytes 393224 | tf_op jit(solution)/shard_map/ppermute | solution.py:31
  100.0 1.5 fusion.10
  105.9 1.7 collective-permute-start.11
  107.7 1.6 collective-permute-done.8
  109.4 4.6 %all-to-all-done.1 = bf16[4,128,1024]{2,1,0:T(8,128)(2,1)S(1)} async-done(((bf16[4,128,1024]{2,1,0:T(8,128)(2,1)}), bf16[4,128,1024]{2,1,0:T(8,128)(2,1)S(1)}, u32[]{:S(2)}, u32[]{:S(2)}) %all-to-all-start.1) | async-done | bytes 1048608 | tf_op jit(solution)/shard_map/all_to_all | solution.py:417
  115.4 6.4 %shard_map.222 = (f32[128,1024]{1,0:T(8,128)}, f32[128,1024]{1,0:T(8,128)}, bf16[128,3072]{1,0:T(8,128)(2,1)}, bf16[128,1024]{1,0:T(8,128)(2,1)S(1)}, f32[128,12...) custom-call(s32[4]{0:T(128)S(1)} %get-tuple-element.73.at, ...), custom_call_target="tpu_custom_call" | custom-call | flops 838860800 | bytes 7144192 | tf_op jit(solution)/shard_map/pallas_call | solution.py:66
  124.8 15.2 %collective-permute-done.12 = bf16[256,1024]{1,0:T(8,128)(2,1)S(1)} collective-permute-done((bf16[256,1024]{1,0:T(8,128)(2,1)S(1)}, bf16[256,1024]{1,0:T(8,128)(2,1)S(1)}, u32[]{:S(2)}, u32[]{:S(2)}) %collective-permute-start.12) | collective-permute-done | bytes 524320 | tf_op jit(solution)/shard_map/ppermute | solution.py:31
  141.1 4.1 collective-permute-start.13
  146.2 4.4 all-to-all-start.2
  150.6 2.5 convert_bitcast_fusion
  153.2 1.4 pad_maximum_fusion.1
  154.9 1.6 fusion.5
  156.5 2.4 pad_maximum_fusion.w_down
  159.3 17.0 %all-to-all-done.2 = bf16[4,128,1024]{2,1,0:T(8,128)(2,1)} async-done(((bf16[4,128,1024]{2,1,0:T(8,128)(2,1)}), bf16[4,128,1024]{2,1,0:T(8,128)(2,1)}, u32[]{:S(2)}, u32[]{:S(2)}) %all-to-all-start.2) | async-done | bytes 1048608 | tf_op jit(solution)/shard_map/all_to_all | solution.py:417
  176.3 12.3 %shard_map.223 = (bf16[512,2048]{1,0:T(8,128)(2,1)}, bf16[512,2048]{1,0:T(8,128)(2,1)}, bf16[512,1024]{1,0:T(8,128)(2,1)}, f32[1,2048]{1,0:T(1,128)S(1)}) custom-call(bf16[512,1024]{1,0:T(8,128)(2,1)} %bitcast.66.normed, bf16[512,1024]{1,0:T(8,128)(2,1)} %bitcast.247, bf16[8,4,32,2048]{3,2,1,0:T(8,128)(2,1)} %all-gather.5.cloned.1.call-done.w_up, ...), custom_call_target="tpu_custom_call" | custom-call | flops 6442450944 | bytes 12582912 | tf_op jit(solution)/shard_map/pallas_call | solution.py:609
  191.2 14.1 %shard_map.224 = (bf16[8,512,1024]{2,1,0:T(8,128)(2,1)}, bf16[512,1024]{1,0:T(8,128)(2,1)S(1)}) custom-call(s32[3]{0:T(128)S(1)} %broadcast_add_fusion.8.at, bf16[512,1024]{1,0:T(8,128)(2,1)} %bitcast.66.normed, bf16[512,2048]{1,0:T(8,128)(2,1)} %get-tuple-element.48.pre_grad, bf16[512,2048]{1,0:T(8,128)(2,1)} %get-tuple-element.49.activated, ...), custom_call_target="tpu_custom_call" | custom-call | flops 6442450944 | bytes 10485760 | tf_op jit(solution)/shard_map/pallas_call | solution.py:66
  206.6 9.3 %reduce-scatter.3.cloned.1.call-done = bf16[1,128,1024]{2,1,0:T(8,128)(2,1)} async-done(((bf16[4,128,1024]{2,1,0:T(8,128)(2,1)}), bf16[1,128,1024]{2,1,0:T(8,128)(2,1)}) %reduce-scatter.3.cloned.1.call-update) | async-done | bytes 262160 | tf_op jit(solution)/shard_map/reduce_scatter | solution.py:637
  216.9 11.1 %shard_map.225 = (bf16[128,1024]{1,0:T(8,128)(2,1)S(1)}, f32[128,1024]{1,0:T(8,128)}, bf16[4,192,512]{2,1,0:T(8,128)(2,1)}, f32[16,1024]{1,0:T(8,128)S(1)}) custom-call(s32[4]{0:T(128)S(1)} %get-tuple-element.74.at, bf16[128,1024]{1,0:T(8,128)(2,1)S(1)} %add_bitcast_fusion.terms, bf16[128,1024]{1,0:T(8,128)(2,1)S(1)} %bitcast.215, ...), custom_call_target="tpu_custom_call" | custom-call | flops 620756992 | bytes 8520448 | tf_op jit(solution)/shard_map/pallas_call | solution.py:66
  229.1 5.8 %collective-permute-done.14 = bf16[128,1024]{1,0:T(8,128)(2,1)S(1)} collective-permute-done((bf16[128,1024]{1,0:T(8,128)(2,1)S(1)}, bf16[128,1024]{1,0:T(8,128)(2,1)S(1)}, u32[]{:S(2)}, u32[]{:S(2)}) %collective-permute-start.14) | collective-permute-done | bytes 262176 | tf_op jit(solution)/shard_map/ppermute | solution.py:31
  235.8 1.7 collective-permute-start.15
  238.3 3.3 slice.346
  246.2 4.6 all-to-all-start.3
  250.7 2.0 constant_dynamic-slice_fusion.7.w_out
  256.5 16.7 %collective-permute-done.19 = bf16[2,192,512]{2,1,0:T(8,128)(2,1)S(1)} collective-permute-done((bf16[2,192,512]{2,1,0:T(8,128)(2,1)S(1)}, bf16[2,192,512]{2,1,0:T(8,128)(2,1)S(1)}, u32[]{:S(2)}, u32[]{:S(2)}) %collective-permute-start.19) | collective-permute-done | bytes 393248 | tf_op jit(solution)/shard_map/ppermute | solution.py:31
  274.3 1.8 all-to-all-done.3
  278.1 9.8 %shard_map.226 = (bf16[1024,768]{1,0:T(8,128)(2,1)}, bf16[512,1024]{1,0:T(8,128)(2,1)}, f32[8,256]{1,0:T(8,128)S(1)}) custom-call(s32[3]{0:T(128)S(1)} %broadcast_add_fusion.7.at, bf16[512,1024]{1,0:T(8,128)(2,1)} %copy-done.31, bf16[256,1024]{1,0:T(8,128)(2,1)} %constant_dynamic-slice_fusion.7.w_out, bf16[512,256]{1,0:T(8,128)(2,1)S(1)} %copy-done.5, ...), custom_call_target="tpu_custom_call" | custom-call | flops 2550136832 | bytes 5251072 | tf_op jit(solution)/shard_map/pallas_call | solution.py:66
  288.0 5.6 %all-to-all-start.4 = ((bf16[32,32,768]{2,1,0:T(8,128)(2,1)}), bf16[32,32,768]{2,1,0:T(8,128)(2,1)S(1)}, u32[]{:S(2)}, u32[]{:S(2)}) async-start(bf16[32,32,768]{2,1,0:T(8,128)(2,1)} %bitcast.245), calls=%async_computation.5 | async-start | bytes 3145728 | tf_op jit(solution)/shard_map/all_to_all | solution.py:784
  294.6 1.3 fusion.26
  296.0 3.3 collective-permute-done.22
  299.3 1.5 pad_maximum_fusion.3.own
  301.1 5.8 %collective-permute-start.23 = (bf16[256,3072]{1,0:T(8,128)(2,1)S(1)}, bf16[256,3072]{1,0:T(8,128)(2,1)S(1)}, u32[]{:S(2)}, u32[]{:S(2)}) collective-permute-start(bf16[256,3072]{1,0:T(8,128)(2,1)S(1)} %pad_maximum_fusion.3.own), channel_id=1, source_target_pairs={{0,8},{8,0},{1,9},{9,1},{2,10},{10,2},{3,11},{11,3},{4,12},{12,4},... | collective-permute-start | bytes 4718600 | tf_op jit(solution)/shard_map/ppermute | solution.py:31
  307.8 2.3 collective-permute-done.20
  311.3 4.8 %shard_map.228 = bf16[1024,1280]{1,0:T(8,128)(2,1)} custom-call(s32[3]{0:T(128)S(1)} %pad_add_fusion.1.at, bf16[256,3072]{1,0:T(8,128)(2,1)} %copy-done.12, bf16[256,3072]{1,0:T(8,128)(2,1)} %copy-done.20, bf16[512,512]{1,0:T(8,128)(2,1)S(1)} %bitcast.214, bf16[512,256]{1,0:T(8,128)(2,1)S(1)} %constant_dynamic-slice_fusion.4.branch_cut, ...), custom_call_target="tpu_custom_call" | custom-call | flops 805306368 | bytes 4128768 | tf_op jit(solution)/shard_map/pallas_call | solution.py:66
  316.1 2.5 dynamic-slice_bitcast_fusion
  319.0 1.5 collective-permute-start.17
  321.8 4.6 %collective-permute-done.17 = bf16[128,1024]{1,0:T(8,128)(2,1)S(1)} collective-permute-done((bf16[128,1024]{1,0:T(8,128)(2,1)S(1)}, bf16[128,1024]{1,0:T(8,128)(2,1)S(1)}, u32[]{:S(2)}, u32[]{:S(2)}) %collective-permute-start.17) | collective-permute-done | bytes 262176 | tf_op jit(solution)/shard_map/ppermute | solution.py:31
  326.4 2.3 shard_map.227
  328.8 3.1 all-to-all-done.4
  333.3 19.4 %all_to_all.35 = f32[32,1,768]{2,1,0:T(1,128)S(1)} all-to-all(f32[32,1,768]{2,1,0:T(1,128)S(1)} %reshape.503), channel_id=1, replica_groups=mesh['y'=2,'core'=2,'z'=4,'x'=2] {'y','core','z','x'}, dimensions={0} | all-to-all | bytes 196608 | tf_op jit(solution)/shard_map/all_to_all | solution.py:786
  355.6 3.2 fusion.1
  358.8 4.9 %all-to-all-start.6 = ((bf16[16,32,1280]{2,1,0:T(8,128)(2,1)}), bf16[16,32,1280]{2,1,0:T(8,128)(2,1)S(1)}, u32[]{:S(2)}, u32[]{:S(2)}) async-start(bf16[16,32,1280]{2,1,0:T(8,128)(2,1)} %fusion.1), calls=%async_computation.7 | async-start | bytes 2621440 | tf_op jit(solution)/shard_map/all_to_all | solution.py:788
  363.7 1.5 convert_reduce_fusion.2
  368.7 26.9 %all-to-all-done.6 = bf16[16,32,1280]{2,1,0:T(8,128)(2,1)S(1)} async-done(((bf16[16,32,1280]{2,1,0:T(8,128)(2,1)}), bf16[16,32,1280]{2,1,0:T(8,128)(2,1)S(1)}, u32[]{:S(2)}, u32[]{:S(2)}) %all-to-all-start.6) | async-done | bytes 1310752 | tf_op jit(solution)/shard_map/all_to_all | solution.py:788
  398.0 2.1 slice_bitcast_fusion
  400.0 5.5 %collective-permute-start.28 = (bf16[256,1024]{1,0:T(8,128)(2,1)}, bf16[256,1024]{1,0:T(8,128)(2,1)S(1)}, u32[]{:S(2)}, u32[]{:S(2)}) collective-permute-start(bf16[256,1024]{1,0:T(8,128)(2,1)} %get-tuple-element.85), channel_id=1, source_target_pairs={{0,0},{1,4},{2,8},{3,12},{4,16},{5,20},{6,24},{7,28},{8,1},{9,5},{... | collective-permute-start | bytes 1572872 | tf_op jit(solution)/shard_map/ppermute | solution.py:667
  406.1 2.7 collective-permute-start.26
  410.1 37.1 %collective-permute-done.25 = bf16[2,32,1024]{2,1,0:T(8,128)(2,1)S(1)} collective-permute-done((bf16[2,32,1024]{2,1,0:T(8,128)(2,1)S(1)}, bf16[2,32,1024]{2,1,0:T(8,128)(2,1)S(1)}, u32[]{:S(2)}, u32[]{:S(2)}) %collective-permute-start.25) | collective-permute-done | bytes 131104 | tf_op jit(solution)/shard_map/ppermute | solution.py:31
  448.3 1.9 reshape.494
  (287 shorter events, 63.8 us)
Async XLA Ops:
  7.2 8.9 %copy-start.40 = (s32[1,16]{1,0:T(1,128)S(1)}, s32[1,16]{1,0:T(1,128)}, u32[]{:S(2)}) copy-start(s32[1,16]{1,0:T(1,128)} %param.18) | copy-start | bytes 196
  7.2 8.9 %copy-start.38 = (s32[1,128]{1,0:T(1,128)S(1)}, s32[1,128]{1,0:T(1,128)}, u32[]{:S(2)}) copy-start(s32[1,128]{1,0:T(1,128)} %param.17) | copy-start | bytes 1540
  7.3 108.1 %all-gather.3.cloned.1.call-start = ((), (), s32[]{:S(2)}) async-start(), calls=%async_computation.9 | async-start | bytes 6488064 | tf_op jit(solution)/shard_map/all_gather | solution.py:514
  7.3 8.9 %copy-start.2 = (bf16[1,128,1024]{2,1,0:T(8,128)(2,1)S(1)}, bf16[1,128,1024]{2,1,0:T(8,128)(2,1)}, u32[]{:S(2)}) copy-start(bf16[1,128,1024]{2,1,0:T(8,128)(2,1)} %param.14) | copy-start | bytes 786436
  7.3 8.9 %copy-start.30 = (bf16[1,16,1024]{2,1,0:T(8,128)(2,1)S(1)}, bf16[1,16,1024]{2,1,0:T(8,128)(2,1)}, u32[]{:S(2)}) copy-start(bf16[1,16,1024]{2,1,0:T(8,128)(2,1)} %param.15) | copy-start | bytes 98308
  11.7 24.0 %collective-permute-start = (bf16[400,256]{1,0:T(8,128)(2,1)}, bf16[400,256]{1,0:T(8,128)(2,1)}, u32[]{:S(2)}, u32[]{:S(2)}) collective-permute-start(bf16[400,256]{1,0:T(8,128)(2,1)} %get-tuple-element.125), channel_id=1, source_target_pairs={{0,2},{2,0},{4,6},{6,4},{1,3},{3,1},{5,7},{7,5},{8,10},{10,8},{12,... | collective-permute-start | bytes 614408 | tf_op jit(solution)/shard_map/ppermute | solution.py:31
  13.8 21.9 %collective-permute-start.1 = (bf16[400,256]{1,0:T(8,128)(2,1)}, bf16[400,256]{1,0:T(8,128)(2,1)}, u32[]{:S(2)}, u32[]{:S(2)}) collective-permute-start(bf16[400,256]{1,0:T(8,128)(2,1)} %get-tuple-element.125), channel_id=1, source_target_pairs={{0,4},{2,6},{4,0},{6,2},{1,5},{3,7},{5,1},{7,3},{8,12},{10,14},{12... | collective-permute-start | bytes 614408 | tf_op jit(solution)/shard_map/ppermute | solution.py:31
  16.1 19.6 %collective-permute-start.2 = (bf16[400,256]{1,0:T(8,128)(2,1)}, bf16[400,256]{1,0:T(8,128)(2,1)}, u32[]{:S(2)}, u32[]{:S(2)}) collective-permute-start(bf16[400,256]{1,0:T(8,128)(2,1)} %get-tuple-element.125), channel_id=1, source_target_pairs={{0,6},{2,4},{4,2},{6,0},{1,7},{3,5},{5,3},{7,1},{8,14},{10,12},{12... | collective-permute-start | bytes 614408 | tf_op jit(solution)/shard_map/ppermute | solution.py:31
  16.3 15.0 %collective-permute-start.5 = (bf16[160,1024]{1,0:T(8,128)(2,1)S(1)}, bf16[160,1024]{1,0:T(8,128)(2,1)S(1)}, u32[]{:S(2)}, u32[]{:S(2)}) collective-permute-start(bf16[160,1024]{1,0:T(8,128)(2,1)S(1)} %pad_maximum_fusion.13), channel_id=1, source_target_pairs={{0,16},{16,0},{1,17},{17,1},{2,18},{18,2},{3,19},{19,3},{4,20},{20... | collective-permute-start | bytes 983048 | tf_op jit(solution)/shard_map/ppermute | solution.py:31
  19.7 14.2 %collective-permute-start.3 = (bf16[256,1024]{1,0:T(8,128)(2,1)}, bf16[256,1024]{1,0:T(8,128)(2,1)}, u32[]{:S(2)}, u32[]{:S(2)}) collective-permute-start(bf16[256,1024]{1,0:T(8,128)(2,1)} %dynamic-slice_convert_fusion), channel_id=1, source_target_pairs={{0,1},{1,0},{2,3},{3,2},{4,5},{5,4},{6,7},{7,6},{8,9},{9,8},{10,11... | collective-permute-start | bytes 1572872 | tf_op jit(solution)/shard_map/ppermute | solution.py:31
  24.6 5.6 %copy-start.39 = (s32[8]{0:T(128)S(1)}, s32[8]{0:T(128)}, u32[]{:S(2)}) copy-start(s32[8]{0:T(128)} %param.19) | copy-start | bytes 100
  25.6 44.3 %all-to-all-start = ((bf16[4,128,1024]{2,1,0:T(8,128)(2,1)}), bf16[4,128,1024]{2,1,0:T(8,128)(2,1)S(1)}, u32[]{:S(2)}, u32[]{:S(2)}) async-start(bf16[4,128,1024]{2,1,0:T(8,128)(2,1)} %pad_maximum_fusion.4), calls=%async_computation | async-start | bytes 2097152 | tf_op jit(solution)/shard_map/all_to_all | solution.py:417
  30.1 129.2 %all-gather.5.cloned.1.call-start = ((), (), s32[]{:S(2)}) async-start(), calls=%async_computation.10 | async-start | bytes 4718592 | tf_op jit(solution)/shard_map/all_gather | solution.py:595
  31.3 8.2 %collective-permute-start.6 = (bf16[320,1024]{1,0:T(8,128)(2,1)S(1)}, bf16[320,1024]{1,0:T(8,128)(2,1)S(1)}, u32[]{:S(2)}, u32[]{:S(2)}) collective-permute-start(bf16[320,1024]{1,0:T(8,128)(2,1)S(1)} %pad_maximum_fusion.9), channel_id=1, source_target_pairs={{0,8},{8,0},{1,9},{9,1},{2,10},{10,2},{3,11},{11,3},{4,12},{12,4},... | collective-permute-start | bytes 1966088 | tf_op jit(solution)/shard_map/ppermute | solution.py:31
  38.2 18.2 %collective-permute-start.4 = (bf16[4,400,256]{2,1,0:T(8,128)(2,1)}, bf16[4,400,256]{2,1,0:T(8,128)(2,1)}, u32[]{:S(2)}, u32[]{:S(2)}) collective-permute-start(bf16[4,400,256]{2,1,0:T(8,128)(2,1)} %get-tuple-element.99), channel_id=1, source_target_pairs={{0,1},{1,0},{2,3},{3,2},{4,5},{5,4},{6,7},{7,6},{8,9},{9,8},{10,11... | collective-permute-start | bytes 2457608 | tf_op jit(solution)/shard_map/ppermute | solution.py:31
  71.1 6.8 %copy-start.3 = (bf16[1,128,1024]{2,1,0:T(8,128)(2,1)S(1)}, bf16[1,128,1024]{2,1,0:T(8,128)(2,1)}, u32[]{:S(2)}) copy-start(bf16[1,128,1024]{2,1,0:T(8,128)(2,1)} %param.16) | copy-start | bytes 786436
  73.2 28.8 %copy-start.32 = (bf16[16,1024]{1,0:T(8,128)(2,1)}, bf16[16,1024]{1,0:T(8,128)(2,1)S(1)}, u32[]{:S(2)}) copy-start(bf16[16,1024]{1,0:T(8,128)(2,1)S(1)} %get-tuple-element.84) | copy-start | bytes 98308
  75.0 25.0 %collective-permute-start.9 = (bf16[4,2,128,256]{3,2,1,0:T(8,128)(2,1)}, bf16[4,2,128,256]{3,2,1,0:T(8,128)(2,1)}, u32[]{:S(2)}, u32[]{:S(2)}) collective-permute-start(bf16[4,2,128,256]{3,2,1,0:T(8,128)(2,1)} %reshape.475), channel_id=1, source_target_pairs={{0,1},{1,0},{2,3},{3,2},{4,5},{5,4},{6,7},{7,6},{8,9},{9,8},{10,11... | collective-permute-start | bytes 1572872 | tf_op jit(solution)/shard_map/ppermute | solution.py:31
  79.0 34.9 %all-to-all-start.1 = ((bf16[4,128,1024]{2,1,0:T(8,128)(2,1)}), bf16[4,128,1024]{2,1,0:T(8,128)(2,1)S(1)}, u32[]{:S(2)}, u32[]{:S(2)}) async-start(bf16[4,128,1024]{2,1,0:T(8,128)(2,1)} %broadcast_in_dim.37), calls=%async_computation.1 | async-start | bytes 2097152 | tf_op jit(solution)/shard_map/all_to_all | solution.py:417
  84.2 19.4 %collective-permute-start.7 = (bf16[2,128,256]{2,1,0:T(8,128)(2,1)}, bf16[2,128,256]{2,1,0:T(8,128)(2,1)}, u32[]{:S(2)}, u32[]{:S(2)}) collective-permute-start(bf16[2,128,256]{2,1,0:T(8,128)(2,1)} %bitcast.39), channel_id=1, source_target_pairs={{0,8},{8,0},{1,9},{9,1},{2,10},{10,2},{3,11},{11,3},{4,12},{12,4},... | collective-permute-start | bytes 393224 | tf_op jit(solution)/shard_map/ppermute | solution.py:31
  101.7 7.6 %copy-start.18 = (bf16[1,4,2,128,256]{4,3,2,1,0:T(8,128)(2,1)}, bf16[1,4,2,128,256]{4,3,2,1,0:T(8,128)(2,1)S(1)}, u32[]{:S(2)}) copy-start(bf16[1,4,2,128,256]{4,3,2,1,0:T(8,128)(2,1)S(1)} %copy.74) | copy-start | bytes 1572868
  101.8 7.5 %copy-start.16 = (bf16[1,4,2,128,256]{4,3,2,1,0:T(8,128)(2,1)}, bf16[1,4,2,128,256]{4,3,2,1,0:T(8,128)(2,1)S(1)}, u32[]{:S(2)}) copy-start(bf16[1,4,2,128,256]{4,3,2,1,0:T(8,128)(2,1)S(1)} %copy.75) | copy-start | bytes 1572868
  102.3 3.6 collective-permute-start.10
  104.4 4.9 %collective-permute-start.8 = (bf16[2,128,256]{2,1,0:T(8,128)(2,1)S(1)}, bf16[2,128,256]{2,1,0:T(8,128)(2,1)S(1)}, u32[]{:S(2)}, u32[]{:S(2)}) collective-permute-start(bf16[2,128,256]{2,1,0:T(8,128)(2,1)S(1)} %get-tuple-element.121), channel_id=1, source_target_pairs={{0,16},{16,0},{1,17},{17,1},{2,18},{18,2},{3,19},{19,3},{4,20},{20... | collective-permute-start | bytes 393224 | tf_op jit(solution)/shard_map/ppermute | solution.py:31
  105.9 3.5 collective-permute-start.11
  114.0 7.8 %copy-start.21 = (bf16[4,128,1024]{2,1,0:T(8,128)(2,1)}, bf16[4,128,1024]{2,1,0:T(8,128)(2,1)S(1)}, u32[]{:S(2)}) copy-start(bf16[4,128,1024]{2,1,0:T(8,128)(2,1)S(1)} %all-to-all-done.1) | copy-start | bytes 3145732
  124.1 16.0 %collective-permute-start.12 = (bf16[256,1024]{1,0:T(8,128)(2,1)S(1)}, bf16[256,1024]{1,0:T(8,128)(2,1)S(1)}, u32[]{:S(2)}, u32[]{:S(2)}) collective-permute-start(bf16[256,1024]{1,0:T(8,128)(2,1)S(1)} %broadcast_add_fusion.5), channel_id=1, source_target_pairs={{0,16},{16,0},{1,17},{17,1},{2,18},{18,2},{3,19},{19,3},{4,20},{20... | collective-permute-start | bytes 1572872 | tf_op jit(solution)/shard_map/ppermute | solution.py:31
  141.1 12.1 %collective-permute-start.13 = (bf16[512,1024]{1,0:T(8,128)(2,1)}, bf16[512,1024]{1,0:T(8,128)(2,1)}, u32[]{:S(2)}, u32[]{:S(2)}) collective-permute-start(bf16[512,1024]{1,0:T(8,128)(2,1)} %pad_maximum_fusion.5), channel_id=1, source_target_pairs={{0,8},{8,0},{1,9},{9,1},{2,10},{10,2},{3,11},{11,3},{4,12},{12,4},... | collective-permute-start | bytes 3145736 | tf_op jit(solution)/shard_map/ppermute | solution.py:31
  146.2 30.1 %all-to-all-start.2 = ((bf16[4,128,1024]{2,1,0:T(8,128)(2,1)}), bf16[4,128,1024]{2,1,0:T(8,128)(2,1)}, u32[]{:S(2)}, u32[]{:S(2)}) async-start(bf16[4,128,1024]{2,1,0:T(8,128)(2,1)} %broadcast_in_dim.40), calls=%async_computation.2 | async-start | bytes 2097152 | tf_op jit(solution)/shard_map/all_to_all | solution.py:417
  150.6 65.3 %reduce-scatter.3.cloned.1.call-start = ((), (), s32[]{:S(2)}) async-start(), calls=%async_computation.11 | async-start | bytes 1310720 | tf_op jit(solution)/shard_map/reduce_scatter | solution.py:637
  188.6 209.3 %reduce-scatter.5.cloned.1.call-start = ((), (), s32[]{:S(2)}) async-start(), calls=%async_computation.12 | async-start | bytes 9437184 | tf_op jit(solution)/shard_map/reduce_scatter | solution.py:665
  227.9 7.0 %collective-permute-start.14 = (bf16[128,1024]{1,0:T(8,128)(2,1)S(1)}, bf16[128,1024]{1,0:T(8,128)(2,1)S(1)}, u32[]{:S(2)}, u32[]{:S(2)}) collective-permute-start(bf16[128,1024]{1,0:T(8,128)(2,1)S(1)} %get-tuple-element.55), channel_id=1, source_target_pairs={{0,16},{16,0},{1,17},{17,1},{2,18},{18,2},{3,19},{19,3},{4,20},{20... | collective-permute-start | bytes 786440 | tf_op jit(solution)/shard_map/ppermute | solution.py:31
  235.8 7.1 %collective-permute-start.15 = (bf16[256,1024]{1,0:T(8,128)(2,1)}, bf16[256,1024]{1,0:T(8,128)(2,1)S(1)}, u32[]{:S(2)}, u32[]{:S(2)}) collective-permute-start(bf16[256,1024]{1,0:T(8,128)(2,1)} %pad_maximum_fusion.10), channel_id=1, source_target_pairs={{0,8},{8,0},{1,9},{9,1},{2,10},{10,2},{3,11},{11,3},{4,12},{12,4},... | collective-permute-start | bytes 1572872 | tf_op jit(solution)/shard_map/ppermute | solution.py:31
  238.3 5.9 %copy-start.26 = (bf16[4,192,512]{2,1,0:T(8,128)(2,1)S(1)}, bf16[4,192,512]{2,1,0:T(8,128)(2,1)}, u32[]{:S(2)}) copy-start(bf16[4,192,512]{2,1,0:T(8,128)(2,1)} %get-tuple-element.66) | copy-start | bytes 2359300
  245.1 7.6 %collective-permute-start.18 = (bf16[2,192,512]{2,1,0:T(8,128)(2,1)}, bf16[2,192,512]{2,1,0:T(8,128)(2,1)}, u32[]{:S(2)}, u32[]{:S(2)}) collective-permute-start(bf16[2,192,512]{2,1,0:T(8,128)(2,1)} %get-tuple-element.103), channel_id=1, source_target_pairs={{0,8},{8,0},{1,9},{9,1},{2,10},{10,2},{3,11},{11,3},{4,12},{12,4},... | collective-permute-start | bytes 1179656 | tf_op jit(solution)/shard_map/ppermute | solution.py:31
  246.2 6.6 %copy-start.24 = (bf16[128,1024]{1,0:T(8,128)(2,1)S(1)}, bf16[128,1024]{1,0:T(8,128)(2,1)}, u32[]{:S(2)}) copy-start(bf16[128,1024]{1,0:T(8,128)(2,1)} %copy-done.23) | copy-start | bytes 786436
  246.2 30.0 %all-to-all-start.3 = ((bf16[4,128,1024]{2,1,0:T(8,128)(2,1)}), bf16[4,128,1024]{2,1,0:T(8,128)(2,1)}, u32[]{:S(2)}, u32[]{:S(2)}) async-start(bf16[4,128,1024]{2,1,0:T(8,128)(2,1)} %bitcast.228), calls=%async_computation.4 | async-start | bytes 2097152 | tf_op jit(solution)/shard_map/all_to_all | solution.py:417
  250.7 4.4 copy-start.25
  253.9 19.3 %collective-permute-start.19 = (bf16[2,192,512]{2,1,0:T(8,128)(2,1)S(1)}, bf16[2,192,512]{2,1,0:T(8,128)(2,1)S(1)}, u32[]{:S(2)}, u32[]{:S(2)}) collective-permute-start(bf16[2,192,512]{2,1,0:T(8,128)(2,1)S(1)} %get-tuple-element.101), channel_id=1, source_target_pairs={{0,16},{16,0},{1,17},{17,1},{2,18},{18,2},{3,19},{19,3},{4,20},{20... | collective-permute-start | bytes 1179656 | tf_op jit(solution)/shard_map/ppermute | solution.py:31
  256.1 43.1 %collective-permute-start.22 = (bf16[128,3072]{1,0:T(8,128)(2,1)}, bf16[128,3072]{1,0:T(8,128)(2,1)}, u32[]{:S(2)}, u32[]{:S(2)}) collective-permute-start(bf16[128,3072]{1,0:T(8,128)(2,1)} %broadcast_add_fusion.3), channel_id=1, source_target_pairs={{0,16},{16,0},{1,17},{17,1},{2,18},{18,2},{3,19},{19,3},{4,20},{20... | collective-permute-start | bytes 2359304 | tf_op jit(solution)/shard_map/ppermute | solution.py:31
  256.4 16.9 %copy-start.31 = (bf16[512,1024]{1,0:T(8,128)(2,1)}, bf16[512,1024]{1,0:T(8,128)(2,1)S(1)}, u32[]{:S(2)}) copy-start(bf16[512,1024]{1,0:T(8,128)(2,1)S(1)} %constant_dynamic-update-slice_fusion.5.branch) | copy-start | bytes 3145732
  256.5 21.6 %copy-start.5 = (bf16[512,256]{1,0:T(8,128)(2,1)S(1)}, bf16[512,256]{1,0:T(8,128)(2,1)}, u32[]{:S(2)}) copy-start(bf16[512,256]{1,0:T(8,128)(2,1)} %copy-done.4) | copy-start | bytes 786436
  256.5 21.6 %copy-start.7 = (bf16[512,256]{1,0:T(8,128)(2,1)S(1)}, bf16[512,256]{1,0:T(8,128)(2,1)}, u32[]{:S(2)}) copy-start(bf16[512,256]{1,0:T(8,128)(2,1)} %copy-done.6) | copy-start | bytes 786436
  256.5 21.6 %copy-start.9 = (bf16[512,256]{1,0:T(8,128)(2,1)S(1)}, bf16[512,256]{1,0:T(8,128)(2,1)}, u32[]{:S(2)}) copy-start(bf16[512,256]{1,0:T(8,128)(2,1)} %copy-done.8) | copy-start | bytes 786436
  256.5 21.6 %copy-start.11 = (f32[512,128]{1,0:T(8,128)S(1)}, f32[512,128]{1,0:T(8,128)}, u32[]{:S(2)}) copy-start(f32[512,128]{1,0:T(8,128)} %copy-done.10) | copy-start | bytes 786436
  288.0 43.9 %all-to-all-start.4 = ((bf16[32,32,768]{2,1,0:T(8,128)(2,1)}), bf16[32,32,768]{2,1,0:T(8,128)(2,1)S(1)}, u32[]{:S(2)}, u32[]{:S(2)}) async-start(bf16[32,32,768]{2,1,0:T(8,128)(2,1)} %bitcast.245), calls=%async_computation.5 | async-start | bytes 3145728 | tf_op jit(solution)/shard_map/all_to_all | solution.py:784
  293.6 7.2 %copy-start.17 = (bf16[1,4,2,128,256]{4,3,2,1,0:T(8,128)(2,1)S(1)}, bf16[1,4,2,128,256]{4,3,2,1,0:T(8,128)(2,1)}, u32[]{:S(2)}) copy-start(bf16[1,4,2,128,256]{4,3,2,1,0:T(8,128)(2,1)} %copy-done.16) | copy-start | bytes 1572868
  296.0 5.1 %copy-start.14 = (bf16[2,2,192,512]{3,2,1,0:T(8,128)(2,1)S(1)}, bf16[2,2,192,512]{3,2,1,0:T(8,128)(2,1)}, u32[]{:S(2)}) copy-start(bf16[2,2,192,512]{3,2,1,0:T(8,128)(2,1)} %copy.81) | copy-start | bytes 2359300
  296.0 11.0 %copy-start.22 = (bf16[512,1024]{1,0:T(8,128)(2,1)S(1)}, bf16[512,1024]{1,0:T(8,128)(2,1)}, u32[]{:S(2)}) copy-start(bf16[512,1024]{1,0:T(8,128)(2,1)} %get-tuple-element.62) | copy-start | bytes 3145732
  300.7 6.4 %copy-start.12 = (bf16[256,3072]{1,0:T(8,128)(2,1)}, bf16[256,3072]{1,0:T(8,128)(2,1)S(1)}, u32[]{:S(2)}) copy-start(bf16[256,3072]{1,0:T(8,128)(2,1)S(1)} %pad_maximum_fusion.3.own) | copy-start | bytes 4718596
  301.1 9.1 %collective-permute-start.23 = (bf16[256,3072]{1,0:T(8,128)(2,1)S(1)}, bf16[256,3072]{1,0:T(8,128)(2,1)S(1)}, u32[]{:S(2)}, u32[]{:S(2)}) collective-permute-start(bf16[256,3072]{1,0:T(8,128)(2,1)S(1)} %pad_maximum_fusion.3.own), channel_id=1, source_target_pairs={{0,8},{8,0},{1,9},{9,1},{2,10},{10,2},{3,11},{11,3},{4,12},{12,4},... | collective-permute-start | bytes 4718600 | tf_op jit(solution)/shard_map/ppermute | solution.py:31
  306.9 3.1 collective-permute-start.20
  307.1 11.6 %collective-permute-start.16 = (bf16[2,128,1024]{2,1,0:T(8,128)(2,1)S(1)}, bf16[2,128,1024]{2,1,0:T(8,128)(2,1)S(1)}, u32[]{:S(2)}, u32[]{:S(2)}) collective-permute-start(bf16[2,128,1024]{2,1,0:T(8,128)(2,1)S(1)} %bitcast.254), channel_id=1, source_target_pairs={{0,8},{8,0},{1,9},{9,1},{2,10},{10,2},{3,11},{11,3},{4,12},{12,4},... | collective-permute-start | bytes 1572872 | tf_op jit(solution)/shard_map/ppermute | solution.py:31
  310.1 10.4 %collective-permute-start.21 = (bf16[16,1024]{1,0:T(8,128)(2,1)S(1)}, bf16[16,1024]{1,0:T(8,128)(2,1)S(1)}, u32[]{:S(2)}, u32[]{:S(2)}) collective-permute-start(bf16[16,1024]{1,0:T(8,128)(2,1)S(1)} %fusion.25), channel_id=1, source_target_pairs={{0,16},{16,0},{1,17},{17,1},{2,18},{18,2},{3,19},{19,3},{4,20},{20... | collective-permute-start | bytes 98312 | tf_op jit(solution)/shard_map/ppermute | solution.py:31
  318.5 37.0 %collective-permute-start.24 = (bf16[16,32,1280]{2,1,0:T(8,128)(2,1)}, bf16[16,32,1280]{2,1,0:T(8,128)(2,1)}, u32[]{:S(2)}, u32[]{:S(2)}) collective-permute-start(bf16[16,32,1280]{2,1,0:T(8,128)(2,1)} %dynamic-slice_bitcast_fusion), channel_id=1, source_target_pairs={{0,1},{1,0},{2,3},{3,2},{4,5},{5,4},{6,7},{7,6},{8,9},{9,8},{10,11... | collective-permute-start | bytes 3932168 | tf_op jit(solution)/shard_map/ppermute | solution.py:31
  319.0 7.5 %collective-permute-start.17 = (bf16[128,1024]{1,0:T(8,128)(2,1)S(1)}, bf16[128,1024]{1,0:T(8,128)(2,1)S(1)}, u32[]{:S(2)}, u32[]{:S(2)}) collective-permute-start(bf16[128,1024]{1,0:T(8,128)(2,1)S(1)} %fusion.15), channel_id=1, source_target_pairs={{0,16},{16,0},{1,17},{17,1},{2,18},{18,2},{3,19},{19,3},{4,20},{20... | collective-permute-start | bytes 786440 | tf_op jit(solution)/shard_map/ppermute | solution.py:31
  320.5 32.2 %copy-start.33 = (f32[16,1024]{1,0:T(8,128)}, f32[16,1024]{1,0:T(8,128)S(1)}, u32[]{:S(2)}) copy-start(f32[16,1024]{1,0:T(8,128)S(1)} %fusion.21) | copy-start | bytes 196612
  358.8 6.3 %copy-start.15 = (f32[128,1024]{1,0:T(8,128)S(1)}, f32[128,1024]{1,0:T(8,128)}, u32[]{:S(2)}) copy-start(f32[128,1024]{1,0:T(8,128)} %get-tuple-element.44.after_cross) | copy-start | bytes 1572868
  358.8 36.7 %all-to-all-start.6 = ((bf16[16,32,1280]{2,1,0:T(8,128)(2,1)}), bf16[16,32,1280]{2,1,0:T(8,128)(2,1)S(1)}, u32[]{:S(2)}, u32[]{:S(2)}) async-start(bf16[16,32,1280]{2,1,0:T(8,128)(2,1)} %fusion.1), calls=%async_computation.7 | async-start | bytes 2621440 | tf_op jit(solution)/shard_map/all_to_all | solution.py:788
  400.0 50.2 %collective-permute-start.28 = (bf16[256,1024]{1,0:T(8,128)(2,1)}, bf16[256,1024]{1,0:T(8,128)(2,1)S(1)}, u32[]{:S(2)}, u32[]{:S(2)}) collective-permute-start(bf16[256,1024]{1,0:T(8,128)(2,1)} %get-tuple-element.85), channel_id=1, source_target_pairs={{0,0},{1,4},{2,8},{3,12},{4,16},{5,20},{6,24},{7,28},{8,1},{9,5},{... | collective-permute-start | bytes 1572872 | tf_op jit(solution)/shard_map/ppermute | solution.py:667
  405.6 41.7 %collective-permute-start.25 = (bf16[2,32,1024]{2,1,0:T(8,128)(2,1)S(1)}, bf16[2,32,1024]{2,1,0:T(8,128)(2,1)S(1)}, u32[]{:S(2)}, u32[]{:S(2)}) collective-permute-start(bf16[2,32,1024]{2,1,0:T(8,128)(2,1)S(1)} %get-tuple-element.110), channel_id=1, source_target_pairs={{0,2},{2,0},{4,6},{6,4},{1,3},{3,1},{5,7},{7,5},{8,10},{10,8},{12,... | collective-permute-start | bytes 393224 | tf_op jit(solution)/shard_map/ppermute | solution.py:31
  406.1 41.2 %collective-permute-start.26 = (bf16[2,32,1024]{2,1,0:T(8,128)(2,1)S(1)}, bf16[2,32,1024]{2,1,0:T(8,128)(2,1)S(1)}, u32[]{:S(2)}, u32[]{:S(2)}) collective-permute-start(bf16[2,32,1024]{2,1,0:T(8,128)(2,1)S(1)} %get-tuple-element.109), channel_id=1, source_target_pairs={{0,4},{2,6},{4,0},{6,2},{1,5},{3,7},{5,1},{7,3},{8,12},{10,14},{12... | collective-permute-start | bytes 393224 | tf_op jit(solution)/shard_map/ppermute | solution.py:31
  408.8 38.4 %collective-permute-start.27 = (bf16[2,32,1024]{2,1,0:T(8,128)(2,1)S(1)}, bf16[2,32,1024]{2,1,0:T(8,128)(2,1)S(1)}, u32[]{:S(2)}, u32[]{:S(2)}) collective-permute-start(bf16[2,32,1024]{2,1,0:T(8,128)(2,1)S(1)} %get-tuple-element.111), channel_id=1, source_target_pairs={{0,6},{2,4},{4,2},{6,0},{1,7},{3,5},{5,3},{7,1},{8,14},{10,12},{12... | collective-permute-start | bytes 393224 | tf_op jit(solution)/shard_map/ppermute | solution.py:31
  447.5 3.8 copy-start.1
  (16 other events, 33.6 us)
Sparse Core Ops, SparseCore 0:
  11.6 99.5 all-gather.2
  113.0 46.2 all-gather.4
  188.8 27.1 reduce-scatter.2
  219.6 103.3 reduce-scatter.4

commit v4 on v3

--- a/solution.py
+++ b/solution.py
@@ -362,9 +362,10 @@
             out[to, (3 + n) * cut : (4 + n) * cut] = tn(sources[:, to], source_grad[n]).astype(BF)
 
 
-def last_step(at, line, others, inputs, params, self_grad, sums, cut_sums, up_bias_grad, grad_hidden, table, rows):
-    count, _, lanes = table.shape
-    width = inputs.shape[1]
+def last_step(
+    lanes, at, line, others, inputs, params, self_grad, sums, cut_sums, up_bias_grad,
+    grad_hidden, table, rows,
+):
     unit, scale = norm_parts(inputs[...].astype(F32))
     grad = line[...] + jnp.sum(others[...].astype(F32), axis=0)
     moved, gain, shift = norm_back(unit, scale, params[7:8, :], grad)
@@ -379,14 +380,15 @@
     rows[8:10, :] = sums[1:3, :]
     rows[10:11, :] = shift
     rows[11:13, :] = sums[4:6, :]
-    for j in range(count):
-        table[j, 0:16, :] = rows[:, j * lanes : (j + 1) * lanes]
-    table[:, 16:24, :] = jnp.zeros((count, 8, lanes), F32)
-    mine = up_bias_grad.shape[1] // (8 * lanes)
-    for j in range(mine):
-        for r in range(8):
-            first = (j * 8 + r) * lanes
-            table[at[0] * mine + j, 16 + r : 17 + r, :] = up_bias_grad[:, first : first + lanes]
+    mine = up_bias_grad.shape[1] // 8
+    at_lane = pl.ds(pl.multiple_of(at[0] * mine, mine), mine)
+    for k in range(8):
+        parts = [
+            up_bias_grad[:, first : first + lanes]
+            for first in range(k * lanes, up_bias_grad.shape[1], 8 * lanes)
+        ]
+        rows[16 + k : 17 + k, at_lane] = jnp.concatenate(parts, axis=1)
+    table[...] = rows[...].T.astype(BF)
 
 
 def gather_pair(value):
@@ -468,7 +470,7 @@
     def cut_cols(value, at):
         return lax.dynamic_slice_in_dim(value, at * cut, cut, value.ndim - 1)
 
-    here = jnp.stack([z_place, x_place, s_place]).astype(jnp.int32)
+    here = jnp.stack([z_place, x_place, s_place, core_place]).astype(jnp.int32)
     block_list = jnp.stack(block_of).astype(jnp.int32)
 
     small = jnp.concatenate(
@@ -504,12 +506,18 @@
     down_share = lax.dynamic_slice_in_dim(fc2, s_place * unit, unit, 0).astype(BF)
     down_lines = [swap(down_share, "x", k) for k in range(1, x_size)]
     send = behind(early_lines, down_lines[-1])
+    down_lines = [behind(line, early_lines) for line in down_lines]
+    down_lines = [[line] + [swap(line, "y", k) for k in range(1, y_size)] for line in down_lines]
 
     up_share = lax.dynamic_slice_in_dim(fc1, s_place * share, share, 0).astype(BF)
     up_share = up_share.reshape(share, z_size, hidden).transpose(1, 0, 2).reshape(z_size, -1, width)
     memory_cuts = cut_cols(attn_in[1, 1:], s_place).astype(BF).reshape(1, -1, width)
     memory_cuts = jnp.broadcast_to(memory_cuts, (z_size,) + memory_cuts.shape[1:])
-    over_z = trade_z(jnp.concatenate([up_share, memory_cuts], axis=1))
+    down_grad = out_grad[0]
+    down_copies = jnp.broadcast_to(down_grad, (z_size,) + down_grad.shape)
+    over_z = trade_z(jnp.concatenate([up_share, memory_cuts, down_copies], axis=1))
+    down_all = over_z[:, -tokens:].reshape(z_size * tokens, width)
+    over_z = over_z[:, :-tokens]
 
     rest = lax.all_gather(rest, FSDP + SEQ).reshape(count, 3, share, width)
     if share % 16:
@@ -547,7 +555,7 @@
             ((row_len, cut), BF),
         ],
         [],
-        here,
+        behind(here, down_lines[-1][-1]),
         early,
         row_inputs,
         *row_places,
@@ -556,7 +564,6 @@
     parts = exchange_seq(self_cut.reshape(2, y_size, tokens, cut)).reshape(s_size, tokens, cut)
 
     late_z = behind(over_z, self_cut)
-    up_parts = late_z[:, : up_share.shape[1]].reshape(z_size, share, hidden)
     memory_lines = late_z[:, up_share.shape[1] :].reshape(z_size, 2, held, cut)
     memory_lines = jnp.stack([memory_lines] + [swap(memory_lines, "x", k) for k in range(1, x_size)])
     w_memory = jnp.stack([pick(memory_lines, j ^ x_place) for j in range(x_size)])
@@ -567,8 +574,9 @@
     sources_row = s_size * sources_len
     source_all = gather_seq(jnp.stack([source_key, source_value])[None])
 
-    down_grad = out_grad[0]
-    down_all = gather_z(behind(down_grad, late_z)).reshape(z_size * tokens, width)
+    up_parts = behind(late_z[:, : up_share.shape[1]], source_all)
+    up_parts = behind(behind(up_parts, parts), rest)
+    up_parts = up_parts.reshape(z_size, share, hidden)
 
     after_self, after_cross, left, query_cross, cross_stats, source_keys, normed_three = call(
         functools.partial(middle_forward, s_size),
@@ -582,7 +590,7 @@
             ((tokens, width), BF),
         ],
         [],
-        behind(block_list, down_all),
+        block_list,
         parts,
         hidden_in[0],
         rest,
@@ -595,8 +603,9 @@
     w_up = lax.all_gather(up_parts, PLANE).reshape(s_size * x_size, z_size, share, hidden)
     if share % 16:
         w_up = w_up.transpose(1, 0, 2, 3).reshape(1, 1, width, hidden)
-    down_lines = [behind(line, normed_three) for line in down_lines]
-    down_lines = [gather_seq(line).reshape(s_size, unit, width) for line in down_lines]
+    down_lines = [behind(jnp.concatenate(lines), parts) for lines in down_lines]
+    down_lines = [jnp.concatenate([lines, swap(lines, "core", 1)]) for lines in down_lines]
+    down_lines = [line.reshape(s_size, unit, width) for line in down_lines]
     down_lines = [
         jnp.concatenate([pick(line, block_of[j]) for j in range(s_size)]) for line in down_lines
     ]
@@ -661,7 +670,9 @@
             w_down,
             flops=6 * group * width * hidden,
         )
-    terms = behind(terms, mixed_down)
+    left_own = behind(left, partial)
+    left_own = jnp.concatenate([left_own] + [swap(left_own, "y", k) for k in range(1, y_size)])
+    terms = behind(behind(terms, mixed_down), left_own)
     grad_mlp = lax.psum_scatter(grad_mlp, PLANE, scatter_dimension=0)
     grad_up = grad_mlp[:-unit].reshape(2, z_size, up_rows, half)
     grad_down = lax.ppermute(
@@ -701,22 +712,15 @@
         flops=2 * tokens * width * (2 * width + 5 * sources_row),
     )
 
-    results = trade_z(behind(mixed_down, terms).reshape(z_size, tokens, width))
-
     branch_row = gather_seq(branch)
-    left_own, left_swapped = gather_pair(behind(left, branch_row))
-    pair = behind(pair, branch_row)
-    pair = exchange_seq(pair.reshape((2, y_size) + pair.shape[1:])).reshape(pair.shape)
-    source_grad = jnp.sum(pair[:, tokens:].astype(F32), axis=0).astype(BF)
-    source_grad = jnp.stack([source_grad[:, :cut], source_grad[:, cut:]])
-    pair = pair[:, :tokens].reshape(row_len, 2 * cut)
+    left_swapped = swap(behind(left_own, terms), "core", 1)
     w_out = rest[:, 1].reshape(width, width)
     w_out = lax.dynamic_slice_in_dim(w_out, s_place * cut, cut, 0)
     self_cuts, partial, cut_sums = call(
         functools.partial(self_backward, heads),
         [((width, 3 * cut), BF), ((row_len, width), BF), ((8, cut), F32)],
         [((row_len, 3 * cut), BF), ((row_len, cut), F32), ((row_len, cut), F32)],
-        behind(here, results),
+        here,
         branch_row,
         w_out,
         query,
@@ -729,7 +733,44 @@
         flops=2 * row_len * cut * (7 * width + 5 * row_len),
     )
 
+    pair = exchange_seq(pair.reshape((2, y_size) + pair.shape[1:])).reshape(pair.shape)
+    pair = behind(pair, self_cuts)
+    source_grad = jnp.sum(pair[:, tokens:].astype(F32), axis=0).astype(BF)
+    source_grad = jnp.stack([source_grad[:, :cut], source_grad[:, cut:]])
+    pair = pair[:, :tokens].reshape(row_len, 2 * cut)
+
+    results = trade_z(behind(mixed_down, branch).reshape(z_size, tokens, width))
     result = after_cross + jnp.sum(results.astype(F32), axis=0) + params[6]
+    def whole_columns(grads, number):
+        grads = jnp.sum(grads.astype(F32), axis=1).reshape(s_size, up_rows, number, cut)
+        return grads.transpose(2, 1, 0, 3).reshape(number, up_rows, width)
+
+    grad_memory = nt(source_grad[0], w_memory[0]) + nt(source_grad[1], w_memory[1])
+    grad_memory = grad_memory.reshape(s_size, sources_len, width)
+    grad_memory = jnp.stack([pick(grad_memory, owners[j]) for j in range(s_size)])
+    grad_memory = scatter_seq(grad_memory.reshape(2, y_size, sources_len, width))
+
+    partial = partial.reshape(2, y_size, tokens, width)
+    line = partial[0].astype(F32) + swap(partial[1], "core", 1).astype(F32)
+    others = jnp.stack([swap(line[k].astype(BF), "y", k) for k in range(1, y_size)])
+    cut_sums = jnp.concatenate([cut_sums[:2], jnp.sum(source_grad[1].astype(F32), axis=0)[None]])
+    cut_sums = lax.dynamic_update_slice(
+        jnp.zeros((3, width), F32), cut_sums, (jnp.int32(0), (s_place * cut).astype(jnp.int32))
+    )
+    grad_hidden, table = call(
+        functools.partial(last_step, up_rows),
+        [((tokens, width), F32), ((width, 128), BF)],
+        [((128, width), F32)],
+        here,
+        line[0],
+        others,
+        hidden_in[0],
+        params,
+        self_grad,
+        sums,
+        cut_sums,
+        grad_up_bias,
+    )
 
     (group_cuts,) = call(
         group_gradients,
@@ -749,41 +790,12 @@
     for k in range(1, x_size):
         kept = kept + swap(pick(group_cuts, x_place ^ k, 1), "x", k).astype(F32)
 
-    def whole_columns(grads, number):
-        grads = jnp.sum(grads.astype(F32), axis=1).reshape(s_size, up_rows, number, cut)
-        return grads.transpose(2, 1, 0, 3).reshape(number, up_rows, width)
-
-    grad_memory = nt(source_grad[0], w_memory[0]) + nt(source_grad[1], w_memory[1])
-    grad_memory = grad_memory.reshape(s_size, sources_len, width)
-    grad_memory = jnp.stack([pick(grad_memory, owners[j]) for j in range(s_size)])
-    grad_memory = scatter_seq(grad_memory.reshape(2, y_size, sources_len, width))
-
-    partial = partial.reshape(2, y_size, tokens, width)
-    line = partial[0].astype(F32) + swap(partial[1], "core", 1).astype(F32)
-    others = jnp.stack([swap(line[k].astype(BF), "y", k) for k in range(1, y_size)])
-    cut_sums = jnp.concatenate([cut_sums[:2], jnp.sum(source_grad[1].astype(F32), axis=0)[None]])
-    cut_sums = lax.dynamic_update_slice(
-        jnp.zeros((3, width), F32), cut_sums, (jnp.int32(0), (s_place * cut).astype(jnp.int32))
-    )
-    grad_hidden, table = call(
-        last_step,
-        [((tokens, width), F32), ((count, 24, up_rows), F32)],
-        [((16, width), F32)],
-        here,
-        line[0],
-        others,
-        hidden_in[0],
-        params,
-        self_grad,
-        sums,
-        cut_sums,
-        grad_up_bias,
-    )
-
-    self_cuts = self_cuts.reshape(count, up_rows, 3 * cut)
+    self_cuts = behind(self_cuts, results).reshape(count, up_rows, 3 * cut)
     self_cuts = lax.all_to_all(self_cuts, ALL, 0, 0).reshape(s_size, f_size, up_rows, 3 * cut)
-    table = behind(behind(table, self_cuts), grad_memory)
-    table = jnp.sum(lax.all_to_all(table, ALL, 0, 0), axis=0)
+    kept = behind(behind(behind(behind(kept, self_cuts), grad_memory), grad_down), grad_up)
+    table = behind(table, self_cuts)
+    table = lax.all_to_all(table.reshape(count, up_rows, 128), ALL, 0, 0)
+    table = jnp.sum(table.astype(F32), axis=0).T
     kept = behind(kept, table)
     kept = lax.all_to_all(kept.astype(BF), ("y", "core", "z"), 0, 0)
     group_cuts = whole_columns(kept.reshape(s_size, z_size, up_rows, 5 * cut), 5)
@@ -797,7 +809,7 @@
         grad_up,
         grad_down,
         table[:7],
-        table[16:].reshape(-1),
+        table[16:24].reshape(-1),
         table[7:10],
         table[10:13],
     )

time: 467 us -> 435 us (0.931)
  the two profiles are of different devices: /device:TPU:1 before, /device:TPU:4 now
where the time goes in v4:
time: 435 us; the launch traced here: 428 us
  waiting for transfers between devices  159 us (37%)
  Pallas kernels  68.9 us (16%)
  starting transfers between devices  62.6 us (14%)
  local copies, waits for them, and re-layouts  61.8 us (14%)
  other arithmetic  47 us (11%)
  between operations  27.9 us (6%)
    ppermute x28, waiting for transfers between devices, swap(): lax.ppermute(value, axis, [(i, i ^ step) for i in range(lax.axis_size(axi...  102 us
    pallas_call x7, Pallas kernels, call(): pl.pallas_call(kernel, out_shape=[jax.ShapeDtypeStruct(shape, kind) for s...  56.5 us
    ppermute x28, starting transfers between devices, swap(): lax.ppermute(value, axis, [(i, i ^ step) for i in range(lax.axis_size(axi...  24.1 us
    all_to_all x1, waiting for transfers between devices, body(): kept = lax.all_to_all(kept.astype(BF), ('y', 'core', 'z'), 0, 0)  23.1 us
    all_to_all x3, waiting for transfers between devices, trade_z(): return lax.all_to_all(parts, 'z', 0, 0)  20.3 us
    slice x19, local copies, waits for them, and re-layouts, behind(): last = other[(-1,) * other.ndim].astype(F32) * 0.0  16 us
    all_to_all x3, starting transfers between devices, trade_z(): return lax.all_to_all(parts, 'z', 0, 0)  13.7 us
    all_to_all x1, starting transfers between devices, body(): kept = lax.all_to_all(kept.astype(BF), ('y', 'core', 'z'), 0, 0)  13.4 us
  transfers between devices with their start and end apart: 39, of which 18 were waited for; matrix products, arithmetic and copies ran while one was open for 21% of the time, Pallas kernels for 13%

profile of v4, /device:TPU:4, one launch (start us, length us, event | category | flops | bytes accessed | tf_op | source)
XLA Modules:
  0.0 427.9 jit_solution(14184185917072157284)
XLA Ops:
  9.3 1.5 slice.278
  11.0 3.7 collective-permute-start.1
  16.8 1.6 collective-permute-start
  22.2 1.6 pad_maximum_fusion.1
  23.8 5.0 %all-to-all-start = ((bf16[4,256,1024]{2,1,0:T(8,128)(2,1)}), bf16[4,256,1024]{2,1,0:T(8,128)(2,1)}, u32[]{:S(2)}, u32[]{:S(2)}) async-start(bf16[4,256,1024]{2,1,0:T(8,128)(2,1)} %pad_maximum_fusion.1), calls=%async_computation | async-start | bytes 4194304 | tf_op jit(solution)/shard_map/all_to_all | solution.py:419
  31.9 5.5 %collective-permute-done.6 = bf16[160,1024]{1,0:T(8,128)(2,1)S(1)} collective-permute-done((bf16[160,1024]{1,0:T(8,128)(2,1)S(1)}, bf16[160,1024]{1,0:T(8,128)(2,1)S(1)}, u32[]{:S(2)}, u32[]{:S(2)}) %collective-permute-start.6) | collective-permute-done | bytes 327712 | tf_op jit(solution)/shard_map/ppermute | solution.py:31
  39.2 1.4 slice.366
  42.5 6.1 %collective-permute-done.4 = bf16[400,256]{1,0:T(8,128)(2,1)} collective-permute-done((bf16[400,256]{1,0:T(8,128)(2,1)S(1)}, bf16[400,256]{1,0:T(8,128)(2,1)}, u32[]{:S(2)}, u32[]{:S(2)}) %collective-permute-start.4) | collective-permute-done | bytes 204832 | tf_op jit(solution)/shard_map/ppermute | solution.py:31
  48.6 2.2 fusion.22
  50.8 1.5 collective-permute-start.5
  56.5 9.6 %collective-permute-done.2 = bf16[256,1024]{1,0:T(8,128)(2,1)S(1)} collective-permute-done((bf16[256,1024]{1,0:T(8,128)(2,1)S(1)}, bf16[256,1024]{1,0:T(8,128)(2,1)S(1)}, u32[]{:S(2)}, u32[]{:S(2)}) %collective-permute-start.2) | collective-permute-done | bytes 524320 | tf_op jit(solution)/shard_map/ppermute | solution.py:31
  67.5 7.2 %collective-permute-done.5 = bf16[4,400,256]{2,1,0:T(8,128)(2,1)} collective-permute-done((bf16[4,400,256]{2,1,0:T(8,128)(2,1)}, bf16[4,400,256]{2,1,0:T(8,128)(2,1)}, u32[]{:S(2)}, u32[]{:S(2)}) %collective-permute-start.5) | collective-permute-done | bytes 819232 | tf_op jit(solution)/shard_map/ppermute | solution.py:31
  74.8 2.5 pad_maximum_fusion.3.lines
  77.3 7.3 %shard_map.221 = (bf16[3,1024,256]{2,1,0:T(8,128)(2,1)}, f32[16,1024]{1,0:T(8,128)S(1)}, f32[1,2048]{1,0:T(1,128)S(1)}, bf16[512,1024]{1,0:T(8,128)(2,1)}, bf16[...) custom-call(s32[4]{0:T(128)S(1)} %get-tuple-element.73.at, ...), custom_call_target="tpu_custom_call" | custom-call | flops 1073741824 | bytes 2695168 | tf_op jit(solution)/shard_map/pallas_call | solution.py:66
  87.9 2.4 all-to-all-done
  90.3 2.6 fusion.44
  94.1 1.5 collective-permute-start.10
  97.4 13.6 %collective-permute-done.10 = bf16[4,2,128,256]{3,2,1,0:T(8,128)(2,1)} collective-permute-done((bf16[4,2,128,256]{3,2,1,0:T(8,128)(2,1)}, bf16[4,2,128,256]{3,2,1,0:T(8,128)(2,1)}, u32[]{:S(2)}, u32[]{:S(2)}) %collective-permute-start.10) | collective-permute-done | bytes 524320 | tf_op jit(solution)/shard_map/ppermute | solution.py:31
  111.1 1.6 fusion.14
  114.6 1.6 collective-permute-start.9
  116.1 2.7 collective-permute-done.11
  125.6 2.0 all_gather_reshape.3
  130.2 6.4 %shard_map.222 = (f32[128,1024]{1,0:T(8,128)}, f32[128,1024]{1,0:T(8,128)}, bf16[128,3072]{1,0:T(8,128)(2,1)}, bf16[128,1024]{1,0:T(8,128)(2,1)S(1)}, f32[128,12...) custom-call(s32[4]{0:T(128)S(1)} %pad_add_fusion.at, ...), custom_call_target="tpu_custom_call" | custom-call | flops 838860800 | bytes 7144192 | tf_op jit(solution)/shard_map/pallas_call | solution.py:66
  137.7 4.3 all-to-all-start.1
  142.5 2.5 convert_bitcast_fusion
  145.0 1.4 pad_maximum_fusion.2
  146.8 1.6 fusion.9
  148.3 2.4 pad_maximum_fusion.w_down
  150.7 17.9 %all-to-all-done.1 = bf16[4,128,1024]{2,1,0:T(8,128)(2,1)} async-done(((bf16[4,128,1024]{2,1,0:T(8,128)(2,1)}), bf16[4,128,1024]{2,1,0:T(8,128)(2,1)}, u32[]{:S(2)}, u32[]{:S(2)}) %all-to-all-start.1) | async-done | bytes 1048608 | tf_op jit(solution)/shard_map/all_to_all | solution.py:419
  168.7 12.4 %shard_map.223 = (bf16[512,2048]{1,0:T(8,128)(2,1)}, bf16[512,2048]{1,0:T(8,128)(2,1)}, bf16[512,1024]{1,0:T(8,128)(2,1)}, f32[1,2048]{1,0:T(1,128)S(1)}) custom-call(bf16[512,1024]{1,0:T(8,128)(2,1)} %bitcast.66.normed, bf16[512,1024]{1,0:T(8,128)(2,1)} %bitcast.254, bf16[8,4,32,2048]{3,2,1,0:T(8,128)(2,1)} %all-gather.5.cloned.1.call-done.w_up, ...), custom_call_target="tpu_custom_call" | custom-call | flops 6442450944 | bytes 12582912 | tf_op jit(solution)/shard_map/pallas_call | solution.py:618
  183.0 14.4 %shard_map.224 = (bf16[8,512,1024]{2,1,0:T(8,128)(2,1)}, bf16[512,1024]{1,0:T(8,128)(2,1)S(1)}) custom-call(s32[4]{0:T(128)S(1)} %broadcast_add_fusion.7.at, bf16[512,1024]{1,0:T(8,128)(2,1)} %bitcast.66.normed, bf16[512,2048]{1,0:T(8,128)(2,1)} %get-tuple-element.48.pre_grad, bf16[512,2048]{1,0:T(8,128)(2,1)} %get-tuple-element.49.activated, ...), custom_call_target="tpu_custom_call" | custom-call | flops 6442450944 | bytes 10485760 | tf_op jit(solution)/shard_map/pallas_call | solution.py:66
  197.4 2.1 broadcast_add_fusion.4
  200.7 1.8 slice.384
  204.5 14.4 %collective-permute-done.14 = bf16[128,3072]{1,0:T(8,128)(2,1)} collective-permute-done((bf16[128,3072]{1,0:T(8,128)(2,1)}, bf16[128,3072]{1,0:T(8,128)(2,1)}, u32[]{:S(2)}, u32[]{:S(2)}) %collective-permute-start.14) | collective-permute-done | bytes 786464 | tf_op jit(solution)/shard_map/ppermute | solution.py:31
  222.0 11.9 %shard_map.225 = (bf16[128,1024]{1,0:T(8,128)(2,1)S(1)}, f32[128,1024]{1,0:T(8,128)}, bf16[4,192,512]{2,1,0:T(8,128)(2,1)}, f32[16,1024]{1,0:T(8,128)S(1)}) custom-call(s32[4]{0:T(128)S(1)} %pad_add_fusion.at, bf16[128,1024]{1,0:T(8,128)(2,1)S(1)} %add_bitcast_fusion.terms, bf16[128,1024]{1,0:T(8,128)(2,1)S(1)} %bitcast.221, ...), custom_call_target="tpu_custom_call" | custom-call | flops 620756992 | bytes 8520448 | tf_op jit(solution)/shard_map/pallas_call | solution.py:66
  237.7 4.4 %all-to-all-start.2 = ((bf16[4,128,1024]{2,1,0:T(8,128)(2,1)}), bf16[4,128,1024]{2,1,0:T(8,128)(2,1)}, u32[]{:S(2)}, u32[]{:S(2)}) async-start(bf16[4,128,1024]{2,1,0:T(8,128)(2,1)} %bitcast.237), calls=%async_computation.3 | async-start | bytes 2097152 | tf_op jit(solution)/shard_map/all_to_all | solution.py:419
  242.9 5.1 %collective-permute-done.15 = bf16[128,1024]{1,0:T(8,128)(2,1)S(1)} collective-permute-done((bf16[128,1024]{1,0:T(8,128)(2,1)S(1)}, bf16[128,1024]{1,0:T(8,128)(2,1)S(1)}, u32[]{:S(2)}, u32[]{:S(2)}) %collective-permute-start.15) | collective-permute-done | bytes 262176 | tf_op jit(solution)/shard_map/ppermute | solution.py:31
  248.7 3.5 broadcast_add_fusion
  254.3 9.9 %shard_map.226 = (bf16[1024,768]{1,0:T(8,128)(2,1)}, bf16[512,1024]{1,0:T(8,128)(2,1)}, f32[8,256]{1,0:T(8,128)S(1)}) custom-call(s32[4]{0:T(128)S(1)} %get-tuple-element.74.at, bf16[512,1024]{1,0:T(8,128)(2,1)} %copy-done.33, bf16[256,1024]{1,0:T(8,128)(2,1)} %constant_dynamic-slice_fusion.11.w_out, bf16[512,256]{1,0:T(8,128)(2,1)S(1)} %copy-done.6, ...), custom_call_target="tpu_custom_call" | custom-call | flops 2550136832 | bytes 5251072 | tf_op jit(solution)/shard_map/pallas_call | solution.py:66
  266.2 5.2 %collective-permute-done.20 = bf16[2,192,512]{2,1,0:T(8,128)(2,1)S(1)} collective-permute-done((bf16[2,192,512]{2,1,0:T(8,128)(2,1)S(1)}, bf16[2,192,512]{2,1,0:T(8,128)(2,1)S(1)}, u32[]{:S(2)}, u32[]{:S(2)}) %collective-permute-start.20) | collective-permute-done | bytes 393248 | tf_op jit(solution)/shard_map/ppermute | solution.py:31
  276.0 4.1 all-to-all-start.3
  284.1 1.7 collective-permute-start.18
  285.9 4.7 %shard_map.228 = bf16[1024,1280]{1,0:T(8,128)(2,1)} custom-call(s32[4]{0:T(128)S(1)} %get-tuple-element.74.at, bf16[256,3072]{1,0:T(8,128)(2,1)} %get-tuple-element.84.own, bf16[256,3072]{1,0:T(8,128)(2,1)} %collective-permute-done.23.swapped, bf16[512,512]{1,0:T(8,128)(2,1)S(1)} %bitcast.219, bf16[512,256]{1,0:T(8,128)(2,1)S(1)} %constant_dynamic-slice_fusion.8.branch_cut, ...), custom_call_target="tpu_custom_call" | custom-call | flops 805306368 | bytes 4128768 | tf_op jit(solution)/shard_map/pallas_call | solution.py:66
  290.6 2.5 dynamic-slice_bitcast_fusion
  293.1 1.5 collective-permute-start.24
  294.6 17.0 %collective-permute-done.18 = bf16[128,1024]{1,0:T(8,128)(2,1)S(1)} collective-permute-done((bf16[128,1024]{1,0:T(8,128)(2,1)S(1)}, bf16[128,1024]{1,0:T(8,128)(2,1)S(1)}, u32[]{:S(2)}, u32[]{:S(2)}) %collective-permute-start.18) | collective-permute-done | bytes 262176 | tf_op jit(solution)/shard_map/ppermute | solution.py:31
  311.6 1.9 shard_map.227
  313.5 4.5 %all-to-all-done.3 = bf16[32,32,768]{2,1,0:T(8,128)(2,1)S(1)} async-done(((bf16[32,32,768]{2,1,0:T(8,128)(2,1)}), bf16[32,32,768]{2,1,0:T(8,128)(2,1)S(1)}, u32[]{:S(2)}, u32[]{:S(2)}) %all-to-all-start.3) | async-done | bytes 1572896 | tf_op jit(solution)/shard_map/all_to_all | solution.py:794
  319.9 4.0 all-to-all-start.4
  324.0 2.1 slice_bitcast_fusion
  326.2 1.6 collective-permute-start.26
  328.0 2.6 collective-permute-start.27
  332.4 2.5 collective-permute-start.25
  334.9 3.0 all-to-all-done.4
  339.4 13.7 %collective-permute-done.27 = bf16[2,32,1024]{2,0,1:T(2,128)(2,1)S(1)} collective-permute-done((bf16[2,32,1024]{2,0,1:T(2,128)(2,1)S(1)}, bf16[2,32,1024]{2,0,1:T(2,128)(2,1)S(1)}, u32[]{:S(2)}, u32[]{:S(2)}) %collective-permute-start.27) | collective-permute-done | bytes 131104 | tf_op jit(solution)/shard_map/ppermute | solution.py:31
  353.9 1.8 pad_maximum_fusion.9
  356.9 1.9 reshape.519
  360.6 6.2 %collective-permute-done.25 = bf16[256,1024]{1,0:T(8,128)(2,1)S(1)} collective-permute-done((bf16[256,1024]{1,0:T(8,128)(2,1)}, bf16[256,1024]{1,0:T(8,128)(2,1)S(1)}, u32[]{:S(2)}, u32[]{:S(2)}) %collective-permute-start.25) | collective-permute-done | bytes 524320 | tf_op jit(solution)/shard_map/ppermute | solution.py:678
  368.1 3.5 fusion.5
  371.6 13.4 %all-to-all-start.5 = ((bf16[16,32,1280]{2,1,0:T(8,128)(2,1)}), bf16[16,32,1280]{2,1,0:T(8,128)(2,1)}, u32[]{:S(2)}, u32[]{:S(2)}) async-start(bf16[16,32,1280]{2,1,0:T(8,128)(2,1)} %fusion.5), calls=%async_computation.7 | async-start | bytes 2621440 | tf_op jit(solution)/shard_map/all_to_all | solution.py:800
  385.1 1.5 convert_reduce_fusion.2
  390.8 1.4 fusion.49
  393.3 23.1 %all-to-all-done.5 = bf16[16,32,1280]{2,1,0:T(8,128)(2,1)} async-done(((bf16[16,32,1280]{2,1,0:T(8,128)(2,1)}), bf16[16,32,1280]{2,1,0:T(8,128)(2,1)}, u32[]{:S(2)}, u32[]{:S(2)}) %all-to-all-start.5) | async-done | bytes 1310752 | tf_op jit(solution)/shard_map/all_to_all | solution.py:800
  416.4 1.6 convert_reduce_fusion.1
  (313 shorter events, 72.2 us)
Async XLA Ops:
  7.2 3.7 copy-start.48
  7.2 3.7 copy-start.47
  7.2 115.6 %all-gather.3.cloned.1.call-start = ((), (), s32[]{:S(2)}) async-start(), calls=%async_computation.8 | async-start | bytes 6488064 | tf_op jit(solution)/shard_map/all_gather | solution.py:522
  11.0 28.2 %collective-permute-start.1 = (bf16[400,256]{1,0:T(8,128)(2,1)S(1)}, bf16[400,256]{1,0:T(8,128)(2,1)}, u32[]{:S(2)}, u32[]{:S(2)}) collective-permute-start(bf16[400,256]{1,0:T(8,128)(2,1)S(1)} %get-tuple-element.127), channel_id=1, source_target_pairs={{0,6},{2,4},{4,2},{6,0},{1,7},{3,5},{5,3},{7,1},{8,14},{10,12},{12... | collective-permute-start | bytes 614408 | tf_op jit(solution)/shard_map/ppermute | solution.py:31
  14.7 27.8 %collective-permute-start.3 = (bf16[400,256]{1,0:T(8,128)(2,1)S(1)}, bf16[400,256]{1,0:T(8,128)(2,1)}, u32[]{:S(2)}, u32[]{:S(2)}) collective-permute-start(bf16[400,256]{1,0:T(8,128)(2,1)S(1)} %get-tuple-element.127), channel_id=1, source_target_pairs={{0,2},{2,0},{4,6},{6,4},{1,3},{3,1},{5,7},{7,5},{8,10},{10,8},{12,... | collective-permute-start | bytes 614408 | tf_op jit(solution)/shard_map/ppermute | solution.py:31
  14.7 33.9 %collective-permute-start.4 = (bf16[400,256]{1,0:T(8,128)(2,1)S(1)}, bf16[400,256]{1,0:T(8,128)(2,1)}, u32[]{:S(2)}, u32[]{:S(2)}) collective-permute-start(bf16[400,256]{1,0:T(8,128)(2,1)S(1)} %get-tuple-element.127), channel_id=1, source_target_pairs={{0,4},{2,6},{4,0},{6,2},{1,5},{3,7},{5,1},{7,3},{8,12},{10,14},{12... | collective-permute-start | bytes 614408 | tf_op jit(solution)/shard_map/ppermute | solution.py:31
  16.8 24.5 %collective-permute-start = (bf16[256,1024]{1,0:T(8,128)(2,1)S(1)}, bf16[256,1024]{1,0:T(8,128)(2,1)S(1)}, u32[]{:S(2)}, u32[]{:S(2)}) collective-permute-start(bf16[256,1024]{1,0:T(8,128)(2,1)S(1)} %dynamic-slice_convert_fusion.1), channel_id=1, source_target_pairs={{0,1},{1,0},{2,3},{3,2},{4,5},{5,4},{6,7},{7,6},{8,9},{9,8},{10,11... | collective-permute-start | bytes 1572872 | tf_op jit(solution)/shard_map/ppermute | solution.py:31
  23.8 5.3 %copy-start.51 = (s32[1,16]{1,0:T(1,128)S(1)}, s32[1,16]{1,0:T(1,128)}, u32[]{:S(2)}) copy-start(s32[1,16]{1,0:T(1,128)} %param.18) | copy-start | bytes 196
  23.8 5.3 %copy-start.49 = (s32[1,128]{1,0:T(1,128)S(1)}, s32[1,128]{1,0:T(1,128)}, u32[]{:S(2)}) copy-start(s32[1,128]{1,0:T(1,128)} %param.17) | copy-start | bytes 1540
  23.8 5.3 %copy-start.2 = (bf16[1,128,1024]{2,1,0:T(8,128)(2,1)S(1)}, bf16[1,128,1024]{2,1,0:T(8,128)(2,1)}, u32[]{:S(2)}) copy-start(bf16[1,128,1024]{2,1,0:T(8,128)(2,1)} %param.14) | copy-start | bytes 786436
  23.8 5.4 %copy-start.31 = (bf16[1,16,1024]{2,1,0:T(8,128)(2,1)S(1)}, bf16[1,16,1024]{2,1,0:T(8,128)(2,1)}, u32[]{:S(2)}) copy-start(bf16[1,16,1024]{2,1,0:T(8,128)(2,1)} %param.15) | copy-start | bytes 98308
  23.8 6.0 %copy-start.50 = (s32[8]{0:T(128)S(1)}, s32[8]{0:T(128)}, u32[]{:S(2)}) copy-start(s32[8]{0:T(128)} %param.19) | copy-start | bytes 100
  23.8 66.5 %all-to-all-start = ((bf16[4,256,1024]{2,1,0:T(8,128)(2,1)}), bf16[4,256,1024]{2,1,0:T(8,128)(2,1)}, u32[]{:S(2)}, u32[]{:S(2)}) async-start(bf16[4,256,1024]{2,1,0:T(8,128)(2,1)} %pad_maximum_fusion.1), calls=%async_computation | async-start | bytes 4194304 | tf_op jit(solution)/shard_map/all_to_all | solution.py:419
  28.9 139.8 %all-gather.5.cloned.1.call-start = ((), (), s32[]{:S(2)}) async-start(), calls=%async_computation.9 | async-start | bytes 4718592 | tf_op jit(solution)/shard_map/all_gather | solution.py:603
  29.2 8.1 %collective-permute-start.6 = (bf16[160,1024]{1,0:T(8,128)(2,1)S(1)}, bf16[160,1024]{1,0:T(8,128)(2,1)S(1)}, u32[]{:S(2)}, u32[]{:S(2)}) collective-permute-start(bf16[160,1024]{1,0:T(8,128)(2,1)S(1)} %pad_maximum_fusion.11), channel_id=1, source_target_pairs={{0,16},{16,0},{1,17},{17,1},{2,18},{18,2},{3,19},{19,3},{4,20},{20... | collective-permute-start | bytes 983048 | tf_op jit(solution)/shard_map/ppermute | solution.py:31
  38.2 14.7 %collective-permute-start.7 = (bf16[320,1024]{1,0:T(8,128)(2,1)}, bf16[320,1024]{1,0:T(8,128)(2,1)}, u32[]{:S(2)}, u32[]{:S(2)}) collective-permute-start(bf16[320,1024]{1,0:T(8,128)(2,1)} %pad_maximum_fusion.7), channel_id=1, source_target_pairs={{0,8},{8,0},{1,9},{9,1},{2,10},{10,2},{3,11},{11,3},{4,12},{12,4},... | collective-permute-start | bytes 1966088 | tf_op jit(solution)/shard_map/ppermute | solution.py:31
  39.2 13.6 %copy-start.23 = (bf16[640,1024]{1,0:T(8,128)(2,1)S(1)}, bf16[640,1024]{1,0:T(8,128)(2,1)}, u32[]{:S(2)}) copy-start(bf16[640,1024]{1,0:T(8,128)(2,1)} %constant_dynamic-update-slice_fusion.2) | copy-start | bytes 3932164
  50.8 24.0 %collective-permute-start.5 = (bf16[4,400,256]{2,1,0:T(8,128)(2,1)}, bf16[4,400,256]{2,1,0:T(8,128)(2,1)}, u32[]{:S(2)}, u32[]{:S(2)}) collective-permute-start(bf16[4,400,256]{2,1,0:T(8,128)(2,1)} %get-tuple-element.101), channel_id=1, source_target_pairs={{0,1},{1,0},{2,3},{3,2},{4,5},{5,4},{6,7},{7,6},{8,9},{9,8},{10,11... | collective-permute-start | bytes 2457608 | tf_op jit(solution)/shard_map/ppermute | solution.py:31
  52.3 13.8 %collective-permute-start.2 = (bf16[256,1024]{1,0:T(8,128)(2,1)S(1)}, bf16[256,1024]{1,0:T(8,128)(2,1)S(1)}, u32[]{:S(2)}, u32[]{:S(2)}) collective-permute-start(bf16[256,1024]{1,0:T(8,128)(2,1)S(1)} %broadcast_add_fusion.5), channel_id=1, source_target_pairs={{0,16},{16,0},{1,17},{17,1},{2,18},{18,2},{3,19},{19,3},{4,20},{20... | collective-permute-start | bytes 1572872 | tf_op jit(solution)/shard_map/ppermute | solution.py:31
  55.4 29.1 %copy-start.32 = (s32[1,4,16,1024]{3,1,2,0:T(4,128)}, s32[1,4,16,1024]{3,1,2,0:T(4,128)S(1)}, u32[]{:S(2)}) copy-start(s32[1,4,16,1024]{3,1,2,0:T(4,128)S(1)} %copy.96) | copy-start | bytes 786436
  56.5 56.7 %copy-start.37 = (bf16[16,1024]{1,0:T(8,128)(2,1)}, bf16[16,1024]{1,0:T(8,128)(2,1)S(1)}, u32[]{:S(2)}) copy-start(bf16[16,1024]{1,0:T(8,128)(2,1)S(1)} %get-tuple-element.86) | copy-start | bytes 98308
  56.5 56.7 %copy-start.39 = (bf16[16,1024]{1,0:T(8,128)(2,1)}, bf16[16,1024]{1,0:T(8,128)(2,1)S(1)}, u32[]{:S(2)}) copy-start(bf16[16,1024]{1,0:T(8,128)(2,1)S(1)} %get-tuple-element.87) | copy-start | bytes 98308
  56.5 56.7 %copy-start.41 = (bf16[16,1024]{1,0:T(8,128)(2,1)}, bf16[16,1024]{1,0:T(8,128)(2,1)S(1)}, u32[]{:S(2)}) copy-start(bf16[16,1024]{1,0:T(8,128)(2,1)S(1)} %get-tuple-element.88) | copy-start | bytes 98308
  66.1 18.4 %copy-start.30 = (bf16[256,1024]{1,0:T(8,128)(2,1)}, bf16[256,1024]{1,0:T(8,128)(2,1)S(1)}, u32[]{:S(2)}) copy-start(bf16[256,1024]{1,0:T(8,128)(2,1)S(1)} %collective-permute-done.2) | copy-start | bytes 1572868
  86.7 6.3 %copy-start.11 = (f32[512,128]{1,0:T(8,128)}, f32[512,128]{1,0:T(8,128)S(1)}, u32[]{:S(2)}) copy-start(f32[512,128]{1,0:T(8,128)S(1)} %get-tuple-element.60.stats) | copy-start | bytes 786436
  94.1 17.0 %collective-permute-start.10 = (bf16[4,2,128,256]{3,2,1,0:T(8,128)(2,1)}, bf16[4,2,128,256]{3,2,1,0:T(8,128)(2,1)}, u32[]{:S(2)}, u32[]{:S(2)}) collective-permute-start(bf16[4,2,128,256]{3,2,1,0:T(8,128)(2,1)} %reshape.500), channel_id=1, source_target_pairs={{0,1},{1,0},{2,3},{3,2},{4,5},{5,4},{6,7},{7,6},{8,9},{9,8},{10,11... | collective-permute-start | bytes 1572872 | tf_op jit(solution)/shard_map/ppermute | solution.py:31
  96.3 18.2 %collective-permute-start.8 = (bf16[2,128,256]{2,1,0:T(8,128)(2,1)}, bf16[2,128,256]{2,1,0:T(8,128)(2,1)S(1)}, u32[]{:S(2)}, u32[]{:S(2)}) collective-permute-start(bf16[2,128,256]{2,1,0:T(8,128)(2,1)} %bitcast.36), channel_id=1, source_target_pairs={{0,8},{8,0},{1,9},{9,1},{2,10},{10,2},{3,11},{11,3},{4,12},{12,4},... | collective-permute-start | bytes 393224 | tf_op jit(solution)/shard_map/ppermute | solution.py:31
  113.0 7.3 %copy-start.20 = (bf16[1,4,2,128,256]{4,3,2,1,0:T(8,128)(2,1)}, bf16[1,4,2,128,256]{4,3,2,1,0:T(8,128)(2,1)S(1)}, u32[]{:S(2)}) copy-start(bf16[1,4,2,128,256]{4,3,2,1,0:T(8,128)(2,1)S(1)} %copy.78) | copy-start | bytes 1572868
  113.9 13.7 %copy-start.17 = (bf16[256,1024]{1,0:T(8,128)(2,1)S(1)}, bf16[256,1024]{1,0:T(8,128)(2,1)}, u32[]{:S(2)}) copy-start(bf16[256,1024]{1,0:T(8,128)(2,1)} %copy-done.16) | copy-start | bytes 1572868
  114.0 4.9 %collective-permute-start.11 = (bf16[1,2,64,256]{3,2,1,0:T(8,128)(2,1)S(1)}, bf16[1,2,64,256]{3,2,1,0:T(8,128)(2,1)S(1)}, u32[]{:S(2)}, u32[]{:S(2)}) collective-permute-start(bf16[1,2,64,256]{3,2,1,0:T(8,128)(2,1)S(1)} %maximum_bitcast_fusion.3), channel_id=1, source_target_pairs={{0,16},{16,0},{1,17},{17,1},{2,18},{18,2},{3,19},{19,3},{4,20},{20... | collective-permute-start | bytes 196616 | tf_op jit(solution)/shard_map/ppermute | solution.py:31
  114.6 5.7 %collective-permute-start.9 = (bf16[2,128,256]{2,1,0:T(8,128)(2,1)S(1)}, bf16[2,128,256]{2,1,0:T(8,128)(2,1)S(1)}, u32[]{:S(2)}, u32[]{:S(2)}) collective-permute-start(bf16[2,128,256]{2,1,0:T(8,128)(2,1)S(1)} %get-tuple-element.123), channel_id=1, source_target_pairs={{0,16},{16,0},{1,17},{17,1},{2,18},{18,2},{3,19},{19,3},{4,20},{20... | collective-permute-start | bytes 393224 | tf_op jit(solution)/shard_map/ppermute | solution.py:31
  118.9 2.7 collective-permute-start.12
  128.9 16.1 %collective-permute-start.13 = (bf16[512,1024]{1,0:T(8,128)(2,1)S(1)}, bf16[512,1024]{1,0:T(8,128)(2,1)}, u32[]{:S(2)}, u32[]{:S(2)}) collective-permute-start(bf16[512,1024]{1,0:T(8,128)(2,1)S(1)} %maximum_add_fusion), channel_id=1, source_target_pairs={{0,8},{8,0},{1,9},{9,1},{2,10},{10,2},{3,11},{11,3},{4,12},{12,4},... | collective-permute-start | bytes 3145736 | tf_op jit(solution)/shard_map/ppermute | solution.py:31
  137.7 31.0 %all-to-all-start.1 = ((bf16[4,128,1024]{2,1,0:T(8,128)(2,1)}), bf16[4,128,1024]{2,1,0:T(8,128)(2,1)}, u32[]{:S(2)}, u32[]{:S(2)}) async-start(bf16[4,128,1024]{2,1,0:T(8,128)(2,1)} %broadcast_in_dim.40), calls=%async_computation.1 | async-start | bytes 2097152 | tf_op jit(solution)/shard_map/all_to_all | solution.py:419
  141.9 79.0 %reduce-scatter.3.cloned.1.call-start = ((), (), s32[]{:S(2)}) async-start(), calls=%async_computation.10 | async-start | bytes 1310720 | tf_op jit(solution)/shard_map/reduce_scatter | solution.py:646
  181.1 142.9 %reduce-scatter.5.cloned.1.call-start = ((), (), s32[]{:S(2)}) async-start(), calls=%async_computation.11 | async-start | bytes 9437184 | tf_op jit(solution)/shard_map/reduce_scatter | solution.py:676
  199.5 19.5 %collective-permute-start.14 = (bf16[128,3072]{1,0:T(8,128)(2,1)}, bf16[128,3072]{1,0:T(8,128)(2,1)}, u32[]{:S(2)}, u32[]{:S(2)}) collective-permute-start(bf16[128,3072]{1,0:T(8,128)(2,1)} %broadcast_add_fusion.4), channel_id=1, source_target_pairs={{0,16},{16,0},{1,17},{17,1},{2,18},{18,2},{3,19},{19,3},{4,20},{20... | collective-permute-start | bytes 2359304 | tf_op jit(solution)/shard_map/ppermute | solution.py:31
  233.9 14.0 %collective-permute-start.15 = (bf16[128,1024]{1,0:T(8,128)(2,1)S(1)}, bf16[128,1024]{1,0:T(8,128)(2,1)S(1)}, u32[]{:S(2)}, u32[]{:S(2)}) collective-permute-start(bf16[128,1024]{1,0:T(8,128)(2,1)S(1)} %get-tuple-element.56), channel_id=1, source_target_pairs={{0,16},{16,0},{1,17},{17,1},{2,18},{18,2},{3,19},{19,3},{4,20},{20... | collective-permute-start | bytes 786440 | tf_op jit(solution)/shard_map/ppermute | solution.py:31
  237.1 5.0 %copy-start.29 = (bf16[4,192,512]{2,1,0:T(8,128)(2,1)S(1)}, bf16[4,192,512]{2,1,0:T(8,128)(2,1)}, u32[]{:S(2)}) copy-start(bf16[4,192,512]{2,1,0:T(8,128)(2,1)} %get-tuple-element.67) | copy-start | bytes 2359300
  237.7 35.2 %all-to-all-start.2 = ((bf16[4,128,1024]{2,1,0:T(8,128)(2,1)}), bf16[4,128,1024]{2,1,0:T(8,128)(2,1)}, u32[]{:S(2)}, u32[]{:S(2)}) async-start(bf16[4,128,1024]{2,1,0:T(8,128)(2,1)} %bitcast.237), calls=%async_computation.3 | async-start | bytes 2097152 | tf_op jit(solution)/shard_map/all_to_all | solution.py:419
  242.2 10.1 %collective-permute-start.19 = (bf16[2,192,512]{2,1,0:T(8,128)(2,1)S(1)}, bf16[2,192,512]{2,1,0:T(8,128)(2,1)S(1)}, u32[]{:S(2)}, u32[]{:S(2)}) collective-permute-start(bf16[2,192,512]{2,1,0:T(8,128)(2,1)S(1)} %get-tuple-element.105), channel_id=1, source_target_pairs={{0,8},{8,0},{1,9},{9,1},{2,10},{10,2},{3,11},{11,3},{4,12},{12,4},... | collective-permute-start | bytes 1179656 | tf_op jit(solution)/shard_map/ppermute | solution.py:31
  248.0 5.3 %collective-permute-start.16 = (bf16[256,1024]{1,0:T(8,128)(2,1)S(1)}, bf16[256,1024]{1,0:T(8,128)(2,1)S(1)}, u32[]{:S(2)}, u32[]{:S(2)}) collective-permute-start(bf16[256,1024]{1,0:T(8,128)(2,1)S(1)} %pad_maximum_fusion.8), channel_id=1, source_target_pairs={{0,8},{8,0},{1,9},{9,1},{2,10},{10,2},{3,11},{11,3},{4,12},{12,4},... | collective-permute-start | bytes 1572872 | tf_op jit(solution)/shard_map/ppermute | solution.py:31
  252.1 33.7 %collective-permute-start.23 = (bf16[256,3072]{1,0:T(8,128)(2,1)}, bf16[256,3072]{1,0:T(8,128)(2,1)}, u32[]{:S(2)}, u32[]{:S(2)}) collective-permute-start(bf16[256,3072]{1,0:T(8,128)(2,1)} %get-tuple-element.83), channel_id=1, source_target_pairs={{0,8},{8,0},{1,9},{9,1},{2,10},{10,2},{3,11},{11,3},{4,12},{12,4},... | collective-permute-start | bytes 4718600 | tf_op jit(solution)/shard_map/ppermute | solution.py:31
  252.3 19.1 %collective-permute-start.20 = (bf16[2,192,512]{2,1,0:T(8,128)(2,1)S(1)}, bf16[2,192,512]{2,1,0:T(8,128)(2,1)S(1)}, u32[]{:S(2)}, u32[]{:S(2)}) collective-permute-start(bf16[2,192,512]{2,1,0:T(8,128)(2,1)S(1)} %get-tuple-element.103), channel_id=1, source_target_pairs={{0,16},{16,0},{1,17},{17,1},{2,18},{18,2},{3,19},{19,3},{4,20},{20... | collective-permute-start | bytes 1179656 | tf_op jit(solution)/shard_map/ppermute | solution.py:31
  264.2 7.4 %copy-start.26 = (bf16[512,1024]{1,0:T(8,128)(2,1)S(1)}, bf16[512,1024]{1,0:T(8,128)(2,1)}, u32[]{:S(2)}) copy-start(bf16[512,1024]{1,0:T(8,128)(2,1)} %get-tuple-element.63) | copy-start | bytes 3145732
  272.6 10.2 %collective-permute-start.17 = (bf16[2,128,1024]{2,1,0:T(8,128)(2,1)}, bf16[2,128,1024]{2,1,0:T(8,128)(2,1)}, u32[]{:S(2)}, u32[]{:S(2)}) collective-permute-start(bf16[2,128,1024]{2,1,0:T(8,128)(2,1)} %bitcast.92), channel_id=1, source_target_pairs={{0,8},{8,0},{1,9},{9,1},{2,10},{10,2},{3,11},{11,3},{4,12},{12,4},... | collective-permute-start | bytes 1572872 | tf_op jit(solution)/shard_map/ppermute | solution.py:31
  276.0 4.1 copy-start.19
  276.0 4.4 %copy-start.21 = (bf16[1,4,2,128,256]{4,3,2,1,0:T(8,128)(2,1)S(1)}, bf16[1,4,2,128,256]{4,3,2,1,0:T(8,128)(2,1)}, u32[]{:S(2)}) copy-start(bf16[1,4,2,128,256]{4,3,2,1,0:T(8,128)(2,1)} %copy-done.20) | copy-start | bytes 1572868
  276.0 41.9 %all-to-all-start.3 = ((bf16[32,32,768]{2,1,0:T(8,128)(2,1)}), bf16[32,32,768]{2,1,0:T(8,128)(2,1)S(1)}, u32[]{:S(2)}, u32[]{:S(2)}) async-start(bf16[32,32,768]{2,1,0:T(8,128)(2,1)} %bitcast.236), calls=%async_computation.4 | async-start | bytes 3145728 | tf_op jit(solution)/shard_map/all_to_all | solution.py:794
  280.7 1.6 collective-permute-start.21
  282.4 48.7 %collective-permute-start.22 = (bf16[16,1024]{1,0:T(8,128)(2,1)S(1)}, bf16[16,1024]{1,0:T(8,128)(2,1)S(1)}, u32[]{:S(2)}, u32[]{:S(2)}) collective-permute-start(bf16[16,1024]{1,0:T(8,128)(2,1)S(1)} %fusion.31), channel_id=1, source_target_pairs={{0,16},{16,0},{1,17},{17,1},{2,18},{18,2},{3,19},{19,3},{4,20},{20... | collective-permute-start | bytes 98312 | tf_op jit(solution)/shard_map/ppermute | solution.py:31
  284.1 27.5 %collective-permute-start.18 = (bf16[128,1024]{1,0:T(8,128)(2,1)S(1)}, bf16[128,1024]{1,0:T(8,128)(2,1)S(1)}, u32[]{:S(2)}, u32[]{:S(2)}) collective-permute-start(bf16[128,1024]{1,0:T(8,128)(2,1)S(1)} %fusion.21), channel_id=1, source_target_pairs={{0,16},{16,0},{1,17},{17,1},{2,18},{18,2},{3,19},{19,3},{4,20},{20... | collective-permute-start | bytes 786440 | tf_op jit(solution)/shard_map/ppermute | solution.py:31
  290.6 21.0 %copy-start.4 = (f32[128,1024]{1,0:T(8,128)S(1)}, f32[128,1024]{1,0:T(8,128)}, u32[]{:S(2)}) copy-start(f32[128,1024]{1,0:T(8,128)} %get-tuple-element.64.self_grad) | copy-start | bytes 1572868
  293.1 74.9 %collective-permute-start.24 = (bf16[16,32,1280]{2,1,0:T(8,128)(2,1)}, bf16[16,32,1280]{2,1,0:T(8,128)(2,1)}, u32[]{:S(2)}, u32[]{:S(2)}) collective-permute-start(bf16[16,32,1280]{2,1,0:T(8,128)(2,1)} %dynamic-slice_bitcast_fusion), channel_id=1, source_target_pairs={{0,1},{1,0},{2,3},{3,2},{4,5},{5,4},{6,7},{7,6},{8,9},{9,8},{10,11... | collective-permute-start | bytes 3932168 | tf_op jit(solution)/shard_map/ppermute | solution.py:31
  319.9 18.0 %all-to-all-start.4 = ((bf16[32,32,128]{2,1,0:T(8,128)(2,1)}), bf16[32,32,128]{2,1,0:T(8,128)(2,1)S(1)}, u32[]{:S(2)}, u32[]{:S(2)}) async-start(bf16[32,32,128]{2,1,0:T(8,128)(2,1)} %bitcast.133), calls=%async_computation.6 | async-start | bytes 524288 | tf_op jit(solution)/shard_map/all_to_all | solution.py:797
  326.2 13.2 %collective-permute-start.26 = (bf16[2,32,1024]{2,0,1:T(2,128)(2,1)S(1)}, bf16[2,32,1024]{2,0,1:T(2,128)(2,1)S(1)}, u32[]{:S(2)}, u32[]{:S(2)}) collective-permute-start(bf16[2,32,1024]{2,0,1:T(2,128)(2,1)S(1)} %bitcast.269), channel_id=1, source_target_pairs={{0,2},{2,0},{4,6},{6,4},{1,3},{3,1},{5,7},{7,5},{8,10},{10,8},{12,... | collective-permute-start | bytes 393224 | tf_op jit(solution)/shard_map/ppermute | solution.py:31
  328.0 25.2 %collective-permute-start.27 = (bf16[2,32,1024]{2,0,1:T(2,128)(2,1)S(1)}, bf16[2,32,1024]{2,0,1:T(2,128)(2,1)S(1)}, u32[]{:S(2)}, u32[]{:S(2)}) collective-permute-start(bf16[2,32,1024]{2,0,1:T(2,128)(2,1)S(1)} %bitcast.270), channel_id=1, source_target_pairs={{0,4},{2,6},{4,0},{6,2},{1,5},{3,7},{5,1},{7,3},{8,12},{10,14},{12... | collective-permute-start | bytes 393224 | tf_op jit(solution)/shard_map/ppermute | solution.py:31
  330.7 22.5 %collective-permute-start.28 = (bf16[2,32,1024]{2,0,1:T(2,128)(2,1)S(1)}, bf16[2,32,1024]{2,0,1:T(2,128)(2,1)S(1)}, u32[]{:S(2)}, u32[]{:S(2)}) collective-permute-start(bf16[2,32,1024]{2,0,1:T(2,128)(2,1)S(1)} %bitcast.271), channel_id=1, source_target_pairs={{0,6},{2,4},{4,2},{6,0},{1,7},{3,5},{5,3},{7,1},{8,14},{10,12},{12... | collective-permute-start | bytes 393224 | tf_op jit(solution)/shard_map/ppermute | solution.py:31
  331.1 6.8 %copy-start.44 = (f32[16,1024]{1,0:T(8,128)}, f32[16,1024]{1,0:T(8,128)S(1)}, u32[]{:S(2)}) copy-start(f32[16,1024]{1,0:T(8,128)S(1)} %fusion.27) | copy-start | bytes 196612
  332.4 34.5 %collective-permute-start.25 = (bf16[256,1024]{1,0:T(8,128)(2,1)}, bf16[256,1024]{1,0:T(8,128)(2,1)S(1)}, u32[]{:S(2)}, u32[]{:S(2)}) collective-permute-start(bf16[256,1024]{1,0:T(8,128)(2,1)} %get-tuple-element.92), channel_id=1, source_target_pairs={{0,0},{1,4},{2,8},{3,12},{4,16},{5,20},{6,24},{7,28},{8,1},{9,5},{... | collective-permute-start | bytes 1572872 | tf_op jit(solution)/shard_map/ppermute | solution.py:678
  338.0 15.2 %copy-start.43 = (f32[32,128]{0,1:T(8,128)}, f32[32,128]{0,1:T(8,128)S(1)}, u32[]{:S(2)}) copy-start(f32[32,128]{0,1:T(8,128)S(1)} %copy.90) | copy-start | bytes 49156
  339.4 13.8 %copy-start.34 = (bf16[2,32,1024]{2,0,1:T(2,128)(2,1)}, bf16[2,32,1024]{2,0,1:T(2,128)(2,1)S(1)}, u32[]{:S(2)}) copy-start(bf16[2,32,1024]{2,0,1:T(2,128)(2,1)S(1)} %collective-permute-done.26) | copy-start | bytes 393220
  371.6 14.9 %copy-start.15 = (f32[128,1024]{1,0:T(8,128)S(1)}, f32[128,1024]{1,0:T(8,128)}, u32[]{:S(2)}) copy-start(f32[128,1024]{1,0:T(8,128)} %get-tuple-element.44.after_cross) | copy-start | bytes 1572868
  371.6 44.8 %all-to-all-start.5 = ((bf16[16,32,1280]{2,1,0:T(8,128)(2,1)}), bf16[16,32,1280]{2,1,0:T(8,128)(2,1)}, u32[]{:S(2)}, u32[]{:S(2)}) async-start(bf16[16,32,1280]{2,1,0:T(8,128)(2,1)} %fusion.5), calls=%async_computation.7 | async-start | bytes 2621440 | tf_op jit(solution)/shard_map/all_to_all | solution.py:800
  (27 other events, 50.1 us)
Sparse Core Ops, SparseCore 0:
  11.0 104.2 all-gather.2
  127.7 36.0 all-gather.4
  181.2 25.2 reduce-scatter.2
  210.2 101.7 reduce-scatter.4

commit v5 on v4

--- a/solution.py
+++ b/solution.py
@@ -201,7 +201,7 @@
     size = width // HEADS
     score_scale = 1.0 / math.sqrt(size)
     down = out_grad[...].astype(F32)
-    grad = terms[...].astype(F32)
+    grad = terms[...]
     unit, scale = norm_parts(after_cross[...])
     moved, gain, shift = norm_back(unit, scale, params[9:10, :], grad)
     sums[2:3, :] = gain
@@ -299,7 +299,8 @@
             for f in range(places):
                 z, x = divmod(f, x_size)
                 first = (i * z_size + z) * up_rows
-                out[x * s_size + s, first : first + up_rows, :] = term[f * up_rows : (f + 1) * up_rows]
+                b = ((s % 2) * (s_size // 2) + s // 2) * x_size + x
+                out[b, first : first + up_rows, :] = term[f * up_rows : (f + 1) * up_rows]
 
 
 def self_backward(
@@ -346,7 +347,8 @@
 
 
 def group_gradients(at, own, swapped, pair, branch_cut, sources, source_grad, out):
-    rows, cut = own.shape[0], branch_cut.shape[1]
+    (y_size, rows, _), cut = own.shape, branch_cut.shape[1]
+    y_place = lax.div(at[2], 2)
     width = sources.shape[1]
     tile = min(256, width)
     for t in range(width // tile):
@@ -355,8 +357,12 @@
             cols = slice(n * width + t * tile, n * width + (t + 1) * tile)
             right = branch_cut if n == 2 else pair
             first = n * cut if n < 2 else 0
-            term = tn(own[:, cols], right[:rows, first : first + cut])
-            term = term + tn(swapped[:, cols], right[rows:, first : first + cut])
+            term = jnp.zeros((tile, cut), F32)
+            for k in range(y_size):
+                near = slice(k * rows, (k + 1) * rows)
+                far = slice((y_size + k) * rows, (y_size + k + 1) * rows)
+                term = term + tn(own[y_place ^ k, :, cols], right[near, first : first + cut])
+                term = term + tn(swapped[y_place ^ k, :, cols], right[far, first : first + cut])
             out[to, n * cut : (n + 1) * cut] = term.astype(BF)
         for n in range(2):
             out[to, (3 + n) * cut : (4 + n) * cut] = tn(sources[:, to], source_grad[n]).astype(BF)
@@ -643,7 +649,9 @@
             flops=6 * group * width * hidden, bytes_accessed=12 << 20, transcendentals=group * hidden
         ),
     )(normed_all, down_all, w_up, w_down, up_bias)
-    terms = lax.psum_scatter(partial.reshape(z_size, tokens, width), "z", scatter_dimension=0)
+    terms = partial.reshape(z_size, tokens, width)
+    terms = [swap(pick(terms, z_place ^ k), "z", k) if k else pick(terms, z_place) for k in range(z_size)]
+    terms = sum(term.astype(F32) for term in terms)
     up_rows = width // count
     half = hidden // 2
     first_rows = 2 * z_size * up_rows
@@ -652,8 +660,8 @@
         grad_down = tn(late, down_all).astype(BF)
         grad_up = [tn(normed_all, pre_grad[:, i * half : (i + 1) * half]) for i in range(2)]
         grad_up = jnp.stack(grad_up).astype(BF)
-        grad_up = grad_up.reshape(2, s_size, z_size, x_size, up_rows, half)
-        grad_up = grad_up.transpose(3, 1, 0, 2, 4, 5).reshape(x_size * s_size, -1, width)
+        grad_up = grad_up.reshape(2, y_size, 2, z_size, x_size, up_rows, half)
+        grad_up = grad_up.transpose(2, 1, 4, 0, 3, 5, 6).reshape(x_size * s_size, -1, width)
         grad_down = grad_down.reshape(x_size * s_size, unit, width)
         grad_mlp = jnp.concatenate([grad_up, grad_down], axis=1)
         mixed_down = matmul(activated, w_down).astype(BF)
@@ -670,16 +678,18 @@
             w_down,
             flops=6 * group * width * hidden,
         )
-    left_own = behind(left, partial)
-    left_own = jnp.concatenate([left_own] + [swap(left_own, "y", k) for k in range(1, y_size)])
+    left_own = lax.all_gather(left, "y")
     terms = behind(behind(terms, mixed_down), left_own)
-    grad_mlp = lax.psum_scatter(grad_mlp, PLANE, scatter_dimension=0)
+    grad_mlp = lax.psum_scatter(grad_mlp, ("core", "y", "x"), scatter_dimension=0)
     grad_up = grad_mlp[:-unit].reshape(2, z_size, up_rows, half)
-    grad_down = lax.ppermute(
-        grad_mlp[-unit:],
-        ALL,
-        [(s * f_size + f, f * s_size + s) for s in range(s_size) for f in range(f_size)],
-    ).astype(F32)
+    owner = [
+        (((y * 2 + c) * z_size + z) * x_size + x, ((z * 2 + c) * y_size + y) * x_size + x)
+        for y in range(y_size)
+        for c in range(2)
+        for z in range(z_size)
+        for x in range(x_size)
+    ]
+    grad_down = lax.ppermute(grad_mlp[-unit:], ALL, owner).astype(F32)
     grad_up = jnp.stack(
         [
             swap(pick(grad_up, z_place ^ k, 1), "z", k) if k else pick(grad_up, z_place, 1)
@@ -792,12 +802,13 @@
 
     self_cuts = behind(self_cuts, results).reshape(count, up_rows, 3 * cut)
     self_cuts = lax.all_to_all(self_cuts, ALL, 0, 0).reshape(s_size, f_size, up_rows, 3 * cut)
-    kept = behind(behind(behind(behind(kept, self_cuts), grad_memory), grad_down), grad_up)
-    table = behind(table, self_cuts)
+    kept = behind(behind(behind(kept, self_cuts), grad_memory), grad_up)
+    table = behind(behind(table, self_cuts), grad_up)
     table = lax.all_to_all(table.reshape(count, up_rows, 128), ALL, 0, 0)
     table = jnp.sum(table.astype(F32), axis=0).T
     kept = behind(kept, table)
     kept = lax.all_to_all(kept.astype(BF), ("y", "core", "z"), 0, 0)
+    kept = behind(kept, grad_down)
     group_cuts = whole_columns(kept.reshape(s_size, z_size, up_rows, 5 * cut), 5)
     self_cuts = whole_columns(self_cuts, 3)
     return (

time: 435 us -> 417 us (0.959)
  waiting for transfers between devices: 159 us -> 141 us
    ppermute x28 -> x30, waiting for transfers between devices: 102 us -> 63 us  [swap(): lax.ppermute(value, axis, [(i, i ^ step) for i in range(lax.axis_size(axi...]
    ppermute x1, waiting for transfers between devices: 6.21 us -> 36.2 us  [body(): grad_down = lax.ppermute(grad_mlp[-unit:], ALL, owner).astype(F32)]
    all_to_all x1, waiting for transfers between devices: 23.1 us -> 0.01 us  [body(): kept = lax.all_to_all(kept.astype(BF), ('y', 'core', 'z'), 0, 0)]
    all_to_all x1, waiting for transfers between devices: 4.46 us -> 18.9 us  [body(): lax.all_to_all(self_cuts, ALL, 0, 0)]
    all_to_all x1, starting transfers between devices: 13.4 us -> 5.17 us  [body(): kept = lax.all_to_all(kept.astype(BF), ('y', 'core', 'z'), 0, 0)]
    ppermute x28 -> x30, starting transfers between devices: 24.1 us -> 26.3 us  [swap(): lax.ppermute(value, axis, [(i, i ^ step) for i in range(lax.axis_size(axi...]
    add x12 -> x11, other arithmetic: 11.9 us -> 11 us  [behind(): return value + last.astype(value.dtype)]
  transfers between devices with their start and end apart: 39 -> 41, of which waited for: 18 -> 18; matrix products, arithmetic and copies ran while one was open for 21% -> 23% of each run, Pallas kernels for 13% -> 17%
where the time goes in v5:
time: 417 us; the launch traced here: 412 us
  waiting for transfers between devices  141 us (34%)
  Pallas kernels  68.2 us (16%)
  local copies, waits for them, and re-layouts  62.2 us (15%)
  starting transfers between devices  62.2 us (15%)
  other arithmetic  49.2 us (12%)
  between operations  27.9 us (7%)
    ppermute x30, waiting for transfers between devices, swap(): lax.ppermute(value, axis, [(i, i ^ step) for i in range(lax.axis_size(axi...  63 us
    pallas_call x7, Pallas kernels, call(): pl.pallas_call(kernel, out_shape=[jax.ShapeDtypeStruct(shape, kind) for s...  56.1 us
    ppermute x1, waiting for transfers between devices, body(): grad_down = lax.ppermute(grad_mlp[-unit:], ALL, owner).astype(F32)  36.2 us
    ppermute x30, starting transfers between devices, swap(): lax.ppermute(value, axis, [(i, i ^ step) for i in range(lax.axis_size(axi...  26.3 us
    all_to_all x3, waiting for transfers between devices, trade_z(): return lax.all_to_all(parts, 'z', 0, 0)  19.7 us
    all_to_all x1, waiting for transfers between devices, body(): lax.all_to_all(self_cuts, ALL, 0, 0)  18.9 us
    all_to_all x3, starting transfers between devices, trade_z(): return lax.all_to_all(parts, 'z', 0, 0)  15.7 us
    slice x19, local copies, waits for them, and re-layouts, behind(): last = other[(-1,) * other.ndim].astype(F32) * 0.0  15.6 us
  transfers between devices with their start and end apart: 41, of which 18 were waited for; matrix products, arithmetic and copies ran while one was open for 23% of the time, Pallas kernels for 17%

profile of v5, /device:TPU:4, one launch (start us, length us, event | category | flops | bytes accessed | tf_op | source)
XLA Modules:
  0.0 411.8 jit_solution(1185959751451640584)
XLA Ops:
  9.3 1.5 slice.278
  11.0 3.7 collective-permute-start.1
  16.8 1.6 collective-permute-start
  19.8 1.3 dynamic-slice_convert_fusion
  22.2 1.6 pad_maximum_fusion.1
  23.8 5.0 %all-to-all-start = ((bf16[4,256,1024]{2,1,0:T(8,128)(2,1)}), bf16[4,256,1024]{2,1,0:T(8,128)(2,1)}, u32[]{:S(2)}, u32[]{:S(2)}) async-start(bf16[4,256,1024]{2,1,0:T(8,128)(2,1)} %pad_maximum_fusion.1), calls=%async_computation | async-start | bytes 4194304 | tf_op jit(solution)/shard_map/all_to_all | solution.py:425
  31.8 5.5 %collective-permute-done.6 = bf16[160,1024]{1,0:T(8,128)(2,1)S(1)} collective-permute-done((bf16[160,1024]{1,0:T(8,128)(2,1)S(1)}, bf16[160,1024]{1,0:T(8,128)(2,1)S(1)}, u32[]{:S(2)}, u32[]{:S(2)}) %collective-permute-start.6) | collective-permute-done | bytes 327712 | tf_op jit(solution)/shard_map/ppermute | solution.py:31
  39.2 1.3 slice.366
  42.4 6.2 %collective-permute-done.4 = bf16[400,256]{1,0:T(8,128)(2,1)} collective-permute-done((bf16[400,256]{1,0:T(8,128)(2,1)S(1)}, bf16[400,256]{1,0:T(8,128)(2,1)}, u32[]{:S(2)}, u32[]{:S(2)}) %collective-permute-start.4) | collective-permute-done | bytes 204832 | tf_op jit(solution)/shard_map/ppermute | solution.py:31
  48.6 2.2 fusion.25
  50.8 1.5 collective-permute-start.5
  56.8 1.5 dynamic-slice_bitcast_fusion.15
  58.3 8.6 %collective-permute-done.2 = bf16[256,1024]{1,0:T(8,128)(2,1)S(1)} collective-permute-done((bf16[256,1024]{1,0:T(8,128)(2,1)S(1)}, bf16[256,1024]{1,0:T(8,128)(2,1)S(1)}, u32[]{:S(2)}, u32[]{:S(2)}) %collective-permute-start.2) | collective-permute-done | bytes 524320 | tf_op jit(solution)/shard_map/ppermute | solution.py:31
  68.3 6.4 %collective-permute-done.5 = bf16[4,400,256]{2,1,0:T(8,128)(2,1)} collective-permute-done((bf16[4,400,256]{2,1,0:T(8,128)(2,1)}, bf16[4,400,256]{2,1,0:T(8,128)(2,1)}, u32[]{:S(2)}, u32[]{:S(2)}) %collective-permute-start.5) | collective-permute-done | bytes 819232 | tf_op jit(solution)/shard_map/ppermute | solution.py:31
  74.8 2.5 pad_maximum_fusion.3.lines
  77.3 7.3 %shard_map.221 = (bf16[3,1024,256]{2,1,0:T(8,128)(2,1)}, f32[16,1024]{1,0:T(8,128)S(1)}, f32[1,2048]{1,0:T(1,128)S(1)}, bf16[512,1024]{1,0:T(8,128)(2,1)}, bf16[...) custom-call(s32[4]{0:T(128)S(1)} %get-tuple-element.73.at, ...), custom_call_target="tpu_custom_call" | custom-call | flops 1073741824 | bytes 2695168 | tf_op jit(solution)/shard_map/pallas_call | solution.py:66
  88.7 1.6 all-to-all-done
  90.3 2.6 fusion.47
  94.1 1.5 collective-permute-start.10
  96.6 14.4 %collective-permute-done.10 = bf16[4,2,128,256]{3,2,1,0:T(8,128)(2,1)} collective-permute-done((bf16[4,2,128,256]{3,2,1,0:T(8,128)(2,1)}, bf16[4,2,128,256]{3,2,1,0:T(8,128)(2,1)}, u32[]{:S(2)}, u32[]{:S(2)}) %collective-permute-start.10) | collective-permute-done | bytes 524320 | tf_op jit(solution)/shard_map/ppermute | solution.py:31
  111.0 1.4 fusion.13
  114.5 1.5 collective-permute-start.9
  116.0 2.8 collective-permute-done.11
  125.5 2.0 all_gather_reshape.3
  127.6 2.3 maximum_add_fusion
  131.1 6.4 %shard_map.222 = (f32[128,1024]{1,0:T(8,128)}, f32[128,1024]{1,0:T(8,128)}, bf16[128,3072]{1,0:T(8,128)(2,1)}, bf16[128,1024]{1,0:T(8,128)(2,1)S(1)}, f32[128,12...) custom-call(s32[4]{0:T(128)S(1)} %pad_add_fusion.at, ...), custom_call_target="tpu_custom_call" | custom-call | flops 838860800 | bytes 7144192 | tf_op jit(solution)/shard_map/pallas_call | solution.py:66
  138.6 4.2 %all-to-all-start.1 = ((bf16[4,128,1024]{2,1,0:T(8,128)(2,1)}), bf16[4,128,1024]{2,1,0:T(8,128)(2,1)}, u32[]{:S(2)}, u32[]{:S(2)}) async-start(bf16[4,128,1024]{2,1,0:T(8,128)(2,1)} %broadcast_in_dim.40), calls=%async_computation.1 | async-start | bytes 2097152 | tf_op jit(solution)/shard_map/all_to_all | solution.py:425
  143.3 2.5 convert_bitcast_fusion
  145.8 1.7 pad_maximum_fusion.2
  147.9 2.9 fusion.8
  150.8 4.6 %pad_maximum_fusion.w_down = bf16[2048,1024]{1,0:T(8,128)(2,1)} fusion(bf16[1024,1024]{1,0:T(8,128)(2,1)} %get-tuple-element.76, bf16[1024,1024]{1,0:T(8,128)(2,1)} %get-tuple-element.75), kind=kLoop, calls=%fused_computation.5 | loop fusion | flops 8388608 | bytes 8388608 | tf_op jit(solution)/shard_map/concatenate | solution.py:619
  155.5 14.2 %all-to-all-done.1 = bf16[4,128,1024]{2,1,0:T(8,128)(2,1)} async-done(((bf16[4,128,1024]{2,1,0:T(8,128)(2,1)}), bf16[4,128,1024]{2,1,0:T(8,128)(2,1)}, u32[]{:S(2)}, u32[]{:S(2)}) %all-to-all-start.1) | async-done | bytes 1048608 | tf_op jit(solution)/shard_map/all_to_all | solution.py:425
  169.6 12.0 %shard_map.223 = (bf16[512,2048]{1,0:T(8,128)(2,1)}, bf16[512,2048]{1,0:T(8,128)(2,1)}, bf16[512,1024]{1,0:T(8,128)(2,1)S(1)}, f32[1,2048]{1,0:T(1,128)S(1)}) custom-call(bf16[512,1024]{1,0:T(8,128)(2,1)} %bitcast.66.normed, bf16[512,1024]{1,0:T(8,128)(2,1)} %bitcast.268, bf16[8,4,32,2048]{3,2,1,0:T(8,128)(2,1)} %all-gather.7.cloned.1.call-done.w_up, ...), custom_call_target="tpu_custom_call" | custom-call | flops 6442450944 | bytes 12582912 | tf_op jit(solution)/shard_map/pallas_call | solution.py:624
  182.9 14.1 %shard_map.224 = (bf16[8,512,1024]{2,1,0:T(8,128)(2,1)}, bf16[512,1024]{1,0:T(8,128)(2,1)S(1)}) custom-call(s32[4]{0:T(128)S(1)} %broadcast_add_fusion.6.at, bf16[512,1024]{1,0:T(8,128)(2,1)} %bitcast.66.normed, bf16[512,2048]{1,0:T(8,128)(2,1)} %get-tuple-element.48.pre_grad, bf16[512,2048]{1,0:T(8,128)(2,1)} %get-tuple-element.49.activated, ...), custom_call_target="tpu_custom_call" | custom-call | flops 6442450944 | bytes 10485760 | tf_op jit(solution)/shard_map/pallas_call | solution.py:66
  198.0 2.0 collective-permute-start.15
  200.0 2.4 collective-permute-start.16
  203.2 1.9 slice.384
  209.1 1.7 collective-permute-done.14
  210.8 8.9 %collective-permute-done.15 = bf16[128,1024]{1,0:T(8,128)(2,1)} collective-permute-done((bf16[128,1024]{1,0:T(8,128)(2,1)}, bf16[128,1024]{1,0:T(8,128)(2,1)}, u32[]{:S(2)}, u32[]{:S(2)}) %collective-permute-start.15) | collective-permute-done | bytes 262176 | tf_op jit(solution)/shard_map/ppermute | solution.py:31
  219.7 2.1 fusion.19.terms
  223.0 11.0 %shard_map.225 = (bf16[128,1024]{1,0:T(8,128)(2,1)S(1)}, f32[128,1024]{1,0:T(8,128)S(1)}, bf16[4,192,512]{2,1,0:T(8,128)(2,1)}, f32[16,1024]{1,0:T(8,128)S(1)}) custom-call(s32[4]{0:T(128)S(1)} %copy-done.9, f32[128,1024]{1,0:T(8,128)} %fusion.19.terms, bf16[128,1024]{1,0:T(8,128)(2,1)S(1)} %bitcast.232, f32[128,1024]{1,0:T(8,128)} %get-tuple-element.52.after_self, ...), custom_call_target="tpu_custom_call" | custom-call | flops 620756992 | bytes 8782592 | tf_op jit(solution)/shard_map/pallas_call | solution.py:66
  234.0 1.6 collective-permute-start.17
  239.2 6.5 %all-to-all-start.2 = ((bf16[4,128,1024]{2,1,0:T(8,128)(2,1)}), bf16[4,128,1024]{2,1,0:T(8,128)(2,1)S(1)}, u32[]{:S(2)}, u32[]{:S(2)}) async-start(bf16[4,128,1024]{2,1,0:T(8,128)(2,1)} %bitcast.251), calls=%async_computation.2 | async-start | bytes 2097152 | tf_op jit(solution)/shard_map/all_to_all | solution.py:425
  249.8 1.5 collective-permute-start.22
  252.4 9.9 %shard_map.226 = (bf16[1024,768]{1,0:T(8,128)(2,1)}, bf16[512,1024]{1,0:T(8,128)(2,1)}, f32[8,256]{1,0:T(8,128)S(1)}) custom-call(s32[4]{0:T(128)S(1)} %get-tuple-element.74.at, bf16[512,1024]{1,0:T(8,128)(2,1)} %copy-done.41, bf16[256,1024]{1,0:T(8,128)(2,1)} %constant_dynamic-slice_fusion.7.w_out, bf16[512,256]{1,0:T(8,128)(2,1)S(1)} %copy-done.15, ...), custom_call_target="tpu_custom_call" | custom-call | flops 2550136832 | bytes 5251072 | tf_op jit(solution)/shard_map/pallas_call | solution.py:66
  262.3 1.4 slice.335
  266.4 3.9 all-to-all-done.2
  271.6 2.7 broadcast_add_fusion.1
  274.3 5.3 %all-to-all-start.3 = ((bf16[32,32,768]{2,1,0:T(8,128)(2,1)}), bf16[32,32,768]{2,1,0:T(8,128)(2,1)}, u32[]{:S(2)}, u32[]{:S(2)}) async-start(bf16[32,32,768]{2,1,0:T(8,128)(2,1)} %bitcast.112), calls=%async_computation.3 | async-start | bytes 3145728 | tf_op jit(solution)/shard_map/all_to_all | solution.py:804
  285.1 5.5 %shard_map.228 = bf16[1024,1280]{1,0:T(8,128)(2,1)} custom-call(s32[4]{0:T(128)S(1)} %get-tuple-element.74.at, bf16[2,128,3072]{2,1,0:T(8,128)(2,1)} %bitcast.249, bf16[2,128,3072]{2,1,0:T(8,128)(2,1)} %collective-permute-done.25.swapped, bf16[512,512]{1,0:T(8,128)(2,1)S(1)} %bitcast.230, bf16[512,256]{1,0:T(8,128)(2,1)S(1)} %constant_dynamic-slice_fusion.4.branch_cut, ...), custom_call_target="tpu_custom_call" | custom-call | flops 805306368 | bytes 4128768 | tf_op jit(solution)/shard_map/pallas_call | solution.py:66
  290.7 2.2 slice_bitcast_fusion
  293.6 2.1 collective-permute-start.27
  295.7 2.2 collective-permute-start.28
  299.2 2.7 collective-permute-done.20
  302.0 1.9 shard_map.227
  303.9 18.9 %all-to-all-done.3 = bf16[32,32,768]{2,1,0:T(8,128)(2,1)} async-done(((bf16[32,32,768]{2,1,0:T(8,128)(2,1)}), bf16[32,32,768]{2,1,0:T(8,128)(2,1)}, u32[]{:S(2)}, u32[]{:S(2)}) %all-to-all-start.3) | async-done | bytes 1572896 | tf_op jit(solution)/shard_map/all_to_all | solution.py:804
  329.4 5.7 %all-to-all-start.4 = ((bf16[32,32,128]{2,1,0:T(8,128)(2,1)}), bf16[32,32,128]{2,1,0:T(8,128)(2,1)S(1)}, u32[]{:S(2)}, u32[]{:S(2)}) async-start(bf16[32,32,128]{2,1,0:T(8,128)(2,1)} %bitcast.134), calls=%async_computation.5 | async-start | bytes 524288 | tf_op jit(solution)/shard_map/all_to_all | solution.py:807
  336.3 3.7 collective-permute-done.24
  341.3 3.2 all-to-all-done.4
  346.0 3.4 fusion.4
  349.4 5.2 %all-to-all-start.5 = ((bf16[16,32,1280]{2,1,0:T(8,128)(2,1)}), bf16[16,32,1280]{2,1,0:T(8,128)(2,1)S(1)}, u32[]{:S(2)}, u32[]{:S(2)}) async-start(bf16[16,32,1280]{2,1,0:T(8,128)(2,1)} %fusion.4), calls=%async_computation.6 | async-start | bytes 2621440 | tf_op jit(solution)/shard_map/all_to_all | solution.py:810
  354.6 3.3 collective-permute-start.30
  358.9 1.7 convert_reduce_fusion
  361.3 36.2 %collective-permute-done.30 = bf16[256,1024]{1,0:T(8,128)(2,1)S(1)} collective-permute-done((bf16[256,1024]{1,0:T(8,128)(2,1)}, bf16[256,1024]{1,0:T(8,128)(2,1)S(1)}, u32[]{:S(2)}, u32[]{:S(2)}) %collective-permute-start.30) | collective-permute-done | bytes 524320 | tf_op jit(solution)/shard_map/ppermute | solution.py:692
  (326 shorter events, 72.8 us)
Async XLA Ops:
  7.2 115.5 %all-gather.5.cloned.1.call-start = ((), (), s32[]{:S(2)}) async-start(), calls=%async_computation.7 | async-start | bytes 6488064 | tf_op jit(solution)/shard_map/all_gather | solution.py:528
  11.0 28.1 %collective-permute-start.1 = (bf16[400,256]{1,0:T(8,128)(2,1)S(1)}, bf16[400,256]{1,0:T(8,128)(2,1)}, u32[]{:S(2)}, u32[]{:S(2)}) collective-permute-start(bf16[400,256]{1,0:T(8,128)(2,1)S(1)} %get-tuple-element.128), channel_id=1, source_target_pairs={{0,6},{2,4},{4,2},{6,0},{1,7},{3,5},{5,3},{7,1},{8,14},{10,12},{12... | collective-permute-start | bytes 614408 | tf_op jit(solution)/shard_map/ppermute | solution.py:31
  14.7 27.7 %collective-permute-start.3 = (bf16[400,256]{1,0:T(8,128)(2,1)S(1)}, bf16[400,256]{1,0:T(8,128)(2,1)}, u32[]{:S(2)}, u32[]{:S(2)}) collective-permute-start(bf16[400,256]{1,0:T(8,128)(2,1)S(1)} %get-tuple-element.128), channel_id=1, source_target_pairs={{0,2},{2,0},{4,6},{6,4},{1,3},{3,1},{5,7},{7,5},{8,10},{10,8},{12,... | collective-permute-start | bytes 614408 | tf_op jit(solution)/shard_map/ppermute | solution.py:31
  14.7 33.9 %collective-permute-start.4 = (bf16[400,256]{1,0:T(8,128)(2,1)S(1)}, bf16[400,256]{1,0:T(8,128)(2,1)}, u32[]{:S(2)}, u32[]{:S(2)}) collective-permute-start(bf16[400,256]{1,0:T(8,128)(2,1)S(1)} %get-tuple-element.128), channel_id=1, source_target_pairs={{0,4},{2,6},{4,0},{6,2},{1,5},{3,7},{5,1},{7,3},{8,12},{10,14},{12... | collective-permute-start | bytes 614408 | tf_op jit(solution)/shard_map/ppermute | solution.py:31
  16.8 24.4 %collective-permute-start = (bf16[256,1024]{1,0:T(8,128)(2,1)S(1)}, bf16[256,1024]{1,0:T(8,128)(2,1)S(1)}, u32[]{:S(2)}, u32[]{:S(2)}) collective-permute-start(bf16[256,1024]{1,0:T(8,128)(2,1)S(1)} %dynamic-slice_convert_fusion.1), channel_id=1, source_target_pairs={{0,1},{1,0},{2,3},{3,2},{4,5},{5,4},{6,7},{7,6},{8,9},{9,8},{10,11... | collective-permute-start | bytes 1572872 | tf_op jit(solution)/shard_map/ppermute | solution.py:31
  23.7 5.3 %copy-start.39 = (bf16[1,16,1024]{2,1,0:T(8,128)(2,1)S(1)}, bf16[1,16,1024]{2,1,0:T(8,128)(2,1)}, u32[]{:S(2)}) copy-start(bf16[1,16,1024]{2,1,0:T(8,128)(2,1)} %param.15) | copy-start | bytes 98308
  23.7 5.9 %copy-start.56 = (s32[8]{0:T(128)S(1)}, s32[8]{0:T(128)}, u32[]{:S(2)}) copy-start(s32[8]{0:T(128)} %param.19) | copy-start | bytes 100
  23.8 66.5 %all-to-all-start = ((bf16[4,256,1024]{2,1,0:T(8,128)(2,1)}), bf16[4,256,1024]{2,1,0:T(8,128)(2,1)}, u32[]{:S(2)}, u32[]{:S(2)}) async-start(bf16[4,256,1024]{2,1,0:T(8,128)(2,1)} %pad_maximum_fusion.1), calls=%async_computation | async-start | bytes 4194304 | tf_op jit(solution)/shard_map/all_to_all | solution.py:425
  28.8 140.9 %all-gather.7.cloned.1.call-start = ((), (), s32[]{:S(2)}) async-start(), calls=%async_computation.8 | async-start | bytes 4718592 | tf_op jit(solution)/shard_map/all_gather | solution.py:609
  29.1 8.1 %collective-permute-start.6 = (bf16[160,1024]{1,0:T(8,128)(2,1)S(1)}, bf16[160,1024]{1,0:T(8,128)(2,1)S(1)}, u32[]{:S(2)}, u32[]{:S(2)}) collective-permute-start(bf16[160,1024]{1,0:T(8,128)(2,1)S(1)} %pad_maximum_fusion.10), channel_id=1, source_target_pairs={{0,16},{16,0},{1,17},{17,1},{2,18},{18,2},{3,19},{19,3},{4,20},{20... | collective-permute-start | bytes 983048 | tf_op jit(solution)/shard_map/ppermute | solution.py:31
  38.1 14.8 %collective-permute-start.7 = (bf16[320,1024]{1,0:T(8,128)(2,1)}, bf16[320,1024]{1,0:T(8,128)(2,1)}, u32[]{:S(2)}, u32[]{:S(2)}) collective-permute-start(bf16[320,1024]{1,0:T(8,128)(2,1)} %pad_maximum_fusion.6), channel_id=1, source_target_pairs={{0,8},{8,0},{1,9},{9,1},{2,10},{10,2},{3,11},{11,3},{4,12},{12,4},... | collective-permute-start | bytes 1966088 | tf_op jit(solution)/shard_map/ppermute | solution.py:31
  38.4 38.8 %copy-start.4 = (s32[512,1]{1,0:T(8,128)}, s32[512,1]{1,0:T(8,128)S(1)}, u32[]{:S(2)}) copy-start(s32[512,1]{1,0:T(8,128)S(1)} %add.432.pos) | copy-start | bytes 6148
  38.5 38.7 %copy-start.12 = (s32[1,512]{1,0:T(1,128)}, s32[1,512]{1,0:T(1,128)S(1)}, u32[]{:S(2)}) copy-start(s32[1,512]{1,0:T(1,128)S(1)} %add.362.pos_line) | copy-start | bytes 6148
  39.2 13.7 %copy-start.34 = (bf16[640,1024]{1,0:T(8,128)(2,1)S(1)}, bf16[640,1024]{1,0:T(8,128)(2,1)}, u32[]{:S(2)}) copy-start(bf16[640,1024]{1,0:T(8,128)(2,1)} %constant_dynamic-update-slice_fusion.2) | copy-start | bytes 3932164
  50.8 24.0 %collective-permute-start.5 = (bf16[4,400,256]{2,1,0:T(8,128)(2,1)}, bf16[4,400,256]{2,1,0:T(8,128)(2,1)}, u32[]{:S(2)}, u32[]{:S(2)}) collective-permute-start(bf16[4,400,256]{2,1,0:T(8,128)(2,1)} %get-tuple-element.102), channel_id=1, source_target_pairs={{0,1},{1,0},{2,3},{3,2},{4,5},{5,4},{6,7},{7,6},{8,9},{9,8},{10,11... | collective-permute-start | bytes 2457608 | tf_op jit(solution)/shard_map/ppermute | solution.py:31
  52.3 14.6 %collective-permute-start.2 = (bf16[256,1024]{1,0:T(8,128)(2,1)S(1)}, bf16[256,1024]{1,0:T(8,128)(2,1)S(1)}, u32[]{:S(2)}, u32[]{:S(2)}) collective-permute-start(bf16[256,1024]{1,0:T(8,128)(2,1)S(1)} %broadcast_add_fusion.5), channel_id=1, source_target_pairs={{0,16},{16,0},{1,17},{17,1},{2,18},{18,2},{3,19},{19,3},{4,20},{20... | collective-permute-start | bytes 1572872 | tf_op jit(solution)/shard_map/ppermute | solution.py:31
  56.6 20.7 %copy-start.40 = (s32[1,4,16,1024]{3,1,2,0:T(4,128)}, s32[1,4,16,1024]{3,1,2,0:T(4,128)S(1)}, u32[]{:S(2)}) copy-start(s32[1,4,16,1024]{3,1,2,0:T(4,128)S(1)} %copy.99) | copy-start | bytes 786436
  56.8 27.8 %copy-start.6 = (s32[512,1]{1,0:T(8,128)}, s32[512,1]{1,0:T(8,128)S(1)}, u32[]{:S(2)}) copy-start(s32[512,1]{1,0:T(8,128)S(1)} %copy.70.seg) | copy-start | bytes 6148
  58.3 55.3 %copy-start.42 = (bf16[16,1024]{1,0:T(8,128)(2,1)}, bf16[16,1024]{1,0:T(8,128)(2,1)S(1)}, u32[]{:S(2)}) copy-start(bf16[16,1024]{1,0:T(8,128)(2,1)S(1)} %get-tuple-element.83) | copy-start | bytes 98308
  66.9 17.7 %copy-start.38 = (bf16[256,1024]{1,0:T(8,128)(2,1)}, bf16[256,1024]{1,0:T(8,128)(2,1)S(1)}, u32[]{:S(2)}) copy-start(bf16[256,1024]{1,0:T(8,128)(2,1)S(1)} %collective-permute-done.2) | copy-start | bytes 1572868
  94.1 17.0 %collective-permute-start.10 = (bf16[4,2,128,256]{3,2,1,0:T(8,128)(2,1)}, bf16[4,2,128,256]{3,2,1,0:T(8,128)(2,1)}, u32[]{:S(2)}, u32[]{:S(2)}) collective-permute-start(bf16[4,2,128,256]{3,2,1,0:T(8,128)(2,1)} %reshape.495), channel_id=1, source_target_pairs={{0,1},{1,0},{2,3},{3,2},{4,5},{5,4},{6,7},{7,6},{8,9},{9,8},{10,11... | collective-permute-start | bytes 1572872 | tf_op jit(solution)/shard_map/ppermute | solution.py:31
  95.6 18.9 %collective-permute-start.8 = (bf16[2,128,256]{2,1,0:T(8,128)(2,1)S(1)}, bf16[2,128,256]{2,1,0:T(8,128)(2,1)S(1)}, u32[]{:S(2)}, u32[]{:S(2)}) collective-permute-start(bf16[2,128,256]{2,1,0:T(8,128)(2,1)S(1)} %bitcast.284), channel_id=1, source_target_pairs={{0,8},{8,0},{1,9},{9,1},{2,10},{10,2},{3,11},{11,3},{4,12},{12,4},... | collective-permute-start | bytes 393224 | tf_op jit(solution)/shard_map/ppermute | solution.py:31
  112.8 12.7 %copy-start.31 = (bf16[1,4,2,128,256]{4,3,2,1,0:T(8,128)(2,1)}, bf16[1,4,2,128,256]{4,3,2,1,0:T(8,128)(2,1)S(1)}, u32[]{:S(2)}) copy-start(bf16[1,4,2,128,256]{4,3,2,1,0:T(8,128)(2,1)S(1)} %copy.76) | copy-start | bytes 1572868
  113.8 13.8 %copy-start.28 = (bf16[256,1024]{1,0:T(8,128)(2,1)S(1)}, bf16[256,1024]{1,0:T(8,128)(2,1)}, u32[]{:S(2)}) copy-start(bf16[256,1024]{1,0:T(8,128)(2,1)} %copy-done.27) | copy-start | bytes 1572868
  113.8 4.9 %collective-permute-start.11 = (bf16[1,2,64,256]{3,2,1,0:T(8,128)(2,1)S(1)}, bf16[1,2,64,256]{3,2,1,0:T(8,128)(2,1)S(1)}, u32[]{:S(2)}, u32[]{:S(2)}) collective-permute-start(bf16[1,2,64,256]{3,2,1,0:T(8,128)(2,1)S(1)} %maximum_bitcast_fusion.3), channel_id=1, source_target_pairs={{0,16},{16,0},{1,17},{17,1},{2,18},{18,2},{3,19},{19,3},{4,20},{20... | collective-permute-start | bytes 196616 | tf_op jit(solution)/shard_map/ppermute | solution.py:31
  114.5 5.7 %collective-permute-start.9 = (bf16[2,128,256]{2,1,0:T(8,128)(2,1)S(1)}, bf16[2,128,256]{2,1,0:T(8,128)(2,1)S(1)}, u32[]{:S(2)}, u32[]{:S(2)}) collective-permute-start(bf16[2,128,256]{2,1,0:T(8,128)(2,1)S(1)} %get-tuple-element.124), channel_id=1, source_target_pairs={{0,16},{16,0},{1,17},{17,1},{2,18},{18,2},{3,19},{19,3},{4,20},{20... | collective-permute-start | bytes 393224 | tf_op jit(solution)/shard_map/ppermute | solution.py:31
  118.8 2.7 collective-permute-start.12
  129.9 15.9 %collective-permute-start.13 = (bf16[512,1024]{1,0:T(8,128)(2,1)}, bf16[512,1024]{1,0:T(8,128)(2,1)}, u32[]{:S(2)}, u32[]{:S(2)}) collective-permute-start(bf16[512,1024]{1,0:T(8,128)(2,1)} %maximum_add_fusion), channel_id=1, source_target_pairs={{0,8},{8,0},{1,9},{9,1},{2,10},{10,2},{3,11},{11,3},{4,12},{12,4},... | collective-permute-start | bytes 3145736 | tf_op jit(solution)/shard_map/ppermute | solution.py:31
  130.1 7.4 %copy-start.8 = (s32[4]{0:T(128)}, s32[4]{0:T(128)S(1)}, u32[]{:S(2)}) copy-start(s32[4]{0:T(128)S(1)} %pad_add_fusion.at) | copy-start | bytes 52
  131.0 6.4 %copy-start.10 = (s32[1,64]{1,0:T(1,128)}, s32[1,64]{1,0:T(1,128)S(1)}, u32[]{:S(2)}) copy-start(s32[1,64]{1,0:T(1,128)S(1)} %add_bitcast_fusion.source_seg) | copy-start | bytes 772
  138.6 31.0 %all-to-all-start.1 = ((bf16[4,128,1024]{2,1,0:T(8,128)(2,1)}), bf16[4,128,1024]{2,1,0:T(8,128)(2,1)}, u32[]{:S(2)}, u32[]{:S(2)}) async-start(bf16[4,128,1024]{2,1,0:T(8,128)(2,1)} %broadcast_in_dim.40), calls=%async_computation.1 | async-start | bytes 2097152 | tf_op jit(solution)/shard_map/all_to_all | solution.py:425
  142.8 63.1 %all-gather.9.cloned.1.call-start = ((), (), s32[]{:S(2)}) async-start(), calls=%async_computation.10 | async-start | bytes 2359296 | tf_op jit(solution)/shard_map/all_gather | solution.py:681
  150.8 139.9 %reduce-scatter.2.cloned.1.call-start = ((), (), s32[]{:S(2)}) async-start(), calls=%async_computation.9 | async-start | bytes 9437184 | tf_op jit(solution)/shard_map/reduce_scatter | solution.py:683
  197.1 5.3 %copy-start.43 = (bf16[16,1024]{1,0:T(8,128)(2,1)S(1)}, bf16[16,1024]{1,0:T(8,128)(2,1)}, u32[]{:S(2)}) copy-start(bf16[16,1024]{1,0:T(8,128)(2,1)} %copy-done.42) | copy-start | bytes 98308
  197.1 5.3 %copy-start.45 = (bf16[16,1024]{1,0:T(8,128)(2,1)S(1)}, bf16[16,1024]{1,0:T(8,128)(2,1)}, u32[]{:S(2)}) copy-start(bf16[16,1024]{1,0:T(8,128)(2,1)} %get-tuple-element.84) | copy-start | bytes 98308
  198.0 12.8 %collective-permute-start.14 = (bf16[128,1024]{1,0:T(8,128)(2,1)}, bf16[128,1024]{1,0:T(8,128)(2,1)}, u32[]{:S(2)}, u32[]{:S(2)}) collective-permute-start(bf16[128,1024]{1,0:T(8,128)(2,1)} %get-tuple-element.94), channel_id=1, source_target_pairs={{0,2},{2,0},{4,6},{6,4},{1,3},{3,1},{5,7},{7,5},{8,10},{10,8},{12,... | collective-permute-start | bytes 786440 | tf_op jit(solution)/shard_map/ppermute | solution.py:31
  198.0 21.7 %collective-permute-start.15 = (bf16[128,1024]{1,0:T(8,128)(2,1)}, bf16[128,1024]{1,0:T(8,128)(2,1)}, u32[]{:S(2)}, u32[]{:S(2)}) collective-permute-start(bf16[128,1024]{1,0:T(8,128)(2,1)} %get-tuple-element.96), channel_id=1, source_target_pairs={{0,4},{2,6},{4,0},{6,2},{1,5},{3,7},{5,1},{7,3},{8,12},{10,14},{12... | collective-permute-start | bytes 786440 | tf_op jit(solution)/shard_map/ppermute | solution.py:31
  200.0 19.6 %collective-permute-start.16 = (bf16[128,1024]{1,0:T(8,128)(2,1)}, bf16[128,1024]{1,0:T(8,128)(2,1)}, u32[]{:S(2)}, u32[]{:S(2)}) collective-permute-start(bf16[128,1024]{1,0:T(8,128)(2,1)} %get-tuple-element.95), channel_id=1, source_target_pairs={{0,6},{2,4},{4,2},{6,0},{1,7},{3,5},{5,3},{7,1},{8,14},{10,12},{12... | collective-permute-start | bytes 786440 | tf_op jit(solution)/shard_map/ppermute | solution.py:31
  234.0 13.7 %collective-permute-start.17 = (bf16[128,1024]{1,0:T(8,128)(2,1)S(1)}, bf16[128,1024]{1,0:T(8,128)(2,1)S(1)}, u32[]{:S(2)}, u32[]{:S(2)}) collective-permute-start(bf16[128,1024]{1,0:T(8,128)(2,1)S(1)} %get-tuple-element.56), channel_id=1, source_target_pairs={{0,16},{16,0},{1,17},{17,1},{2,18},{18,2},{3,19},{19,3},{4,20},{20... | collective-permute-start | bytes 786440 | tf_op jit(solution)/shard_map/ppermute | solution.py:31
  239.2 31.1 %all-to-all-start.2 = ((bf16[4,128,1024]{2,1,0:T(8,128)(2,1)}), bf16[4,128,1024]{2,1,0:T(8,128)(2,1)S(1)}, u32[]{:S(2)}, u32[]{:S(2)}) async-start(bf16[4,128,1024]{2,1,0:T(8,128)(2,1)} %bitcast.251), calls=%async_computation.2 | async-start | bytes 2097152 | tf_op jit(solution)/shard_map/all_to_all | solution.py:425
  247.0 2.8 collective-permute-start.21
  247.8 3.6 collective-permute-start.18
  249.6 35.5 %collective-permute-start.25 = (bf16[2,128,3072]{2,1,0:T(8,128)(2,1)}, bf16[2,128,3072]{2,1,0:T(8,128)(2,1)}, u32[]{:S(2)}, u32[]{:S(2)}) collective-permute-start(bf16[2,128,3072]{2,1,0:T(8,128)(2,1)} %broadcast_add_fusion), channel_id=1, source_target_pairs={{0,8},{8,0},{1,9},{9,1},{2,10},{10,2},{3,11},{11,3},{4,12},{12,4},... | collective-permute-start | bytes 4718600 | tf_op jit(solution)/shard_map/ppermute | solution.py:31
  249.8 14.5 %collective-permute-start.22 = (bf16[2,192,512]{2,1,0:T(8,128)(2,1)S(1)}, bf16[2,192,512]{2,1,0:T(8,128)(2,1)S(1)}, u32[]{:S(2)}, u32[]{:S(2)}) collective-permute-start(bf16[2,192,512]{2,1,0:T(8,128)(2,1)S(1)} %get-tuple-element.104), channel_id=1, source_target_pairs={{0,16},{16,0},{1,17},{17,1},{2,18},{18,2},{3,19},{19,3},{4,20},{20... | collective-permute-start | bytes 1179656 | tf_op jit(solution)/shard_map/ppermute | solution.py:31
  274.3 7.7 %copy-start.30 = (bf16[1,4,2,128,256]{4,3,2,1,0:T(8,128)(2,1)S(1)}, bf16[1,4,2,128,256]{4,3,2,1,0:T(8,128)(2,1)}, u32[]{:S(2)}) copy-start(bf16[1,4,2,128,256]{4,3,2,1,0:T(8,128)(2,1)} %copy-done.29) | copy-start | bytes 1572868
  274.3 7.9 %copy-start.32 = (bf16[1,4,2,128,256]{4,3,2,1,0:T(8,128)(2,1)S(1)}, bf16[1,4,2,128,256]{4,3,2,1,0:T(8,128)(2,1)}, u32[]{:S(2)}) copy-start(bf16[1,4,2,128,256]{4,3,2,1,0:T(8,128)(2,1)} %copy-done.31) | copy-start | bytes 1572868
  274.3 48.5 %all-to-all-start.3 = ((bf16[32,32,768]{2,1,0:T(8,128)(2,1)}), bf16[32,32,768]{2,1,0:T(8,128)(2,1)}, u32[]{:S(2)}, u32[]{:S(2)}) async-start(bf16[32,32,768]{2,1,0:T(8,128)(2,1)} %bitcast.112), calls=%async_computation.3 | async-start | bytes 3145728 | tf_op jit(solution)/shard_map/all_to_all | solution.py:804
  281.7 2.9 collective-permute-start.19
  283.2 52.0 %collective-permute-start.23 = (bf16[2,16,1024]{2,1,0:T(8,128)(2,1)}, bf16[2,16,1024]{2,1,0:T(8,128)(2,1)}, u32[]{:S(2)}, u32[]{:S(2)}) collective-permute-start(bf16[2,16,1024]{2,1,0:T(8,128)(2,1)} %pad_maximum_fusion.19), channel_id=1, source_target_pairs={{0,8},{8,0},{1,9},{9,1},{2,10},{10,2},{3,11},{11,3},{4,12},{12,4},... | collective-permute-start | bytes 196616 | tf_op jit(solution)/shard_map/ppermute | solution.py:31
  284.9 17.1 %collective-permute-start.20 = (bf16[128,1024]{1,0:T(8,128)(2,1)S(1)}, bf16[128,1024]{1,0:T(8,128)(2,1)S(1)}, u32[]{:S(2)}, u32[]{:S(2)}) collective-permute-start(bf16[128,1024]{1,0:T(8,128)(2,1)S(1)} %fusion.24), channel_id=1, source_target_pairs={{0,16},{16,0},{1,17},{17,1},{2,18},{18,2},{3,19},{19,3},{4,20},{20... | collective-permute-start | bytes 786440 | tf_op jit(solution)/shard_map/ppermute | solution.py:31
  290.7 7.4 %copy-start.22 = (bf16[1024,1280]{1,0:T(8,128)(2,1)S(1)}, bf16[1024,1280]{1,0:T(8,128)(2,1)}, u32[]{:S(2)}) copy-start(bf16[1024,1280]{1,0:T(8,128)(2,1)} %shard_map.228) | copy-start | bytes 7864324
  293.6 31.1 %collective-permute-start.27 = (bf16[2,32,1024]{2,1,0:T(8,128)(2,1)}, bf16[2,32,1024]{2,1,0:T(8,128)(2,1)S(1)}, u32[]{:S(2)}, u32[]{:S(2)}) collective-permute-start(bf16[2,32,1024]{2,1,0:T(8,128)(2,1)} %get-tuple-element.113), channel_id=1, source_target_pairs={{0,2},{2,0},{4,6},{6,4},{1,3},{3,1},{5,7},{7,5},{8,10},{10,8},{12,... | collective-permute-start | bytes 393224 | tf_op jit(solution)/shard_map/ppermute | solution.py:31
  295.7 29.7 %collective-permute-start.28 = (bf16[2,32,1024]{2,1,0:T(8,128)(2,1)S(1)}, bf16[2,32,1024]{2,1,0:T(8,128)(2,1)S(1)}, u32[]{:S(2)}, u32[]{:S(2)}) collective-permute-start(bf16[2,32,1024]{2,1,0:T(8,128)(2,1)S(1)} %get-tuple-element.112), channel_id=1, source_target_pairs={{0,4},{2,6},{4,0},{6,2},{1,5},{3,7},{5,1},{7,3},{8,12},{10,14},{12... | collective-permute-start | bytes 393224 | tf_op jit(solution)/shard_map/ppermute | solution.py:31
  297.9 27.5 %collective-permute-start.29 = (bf16[2,32,1024]{2,1,0:T(8,128)(2,1)S(1)}, bf16[2,32,1024]{2,1,0:T(8,128)(2,1)S(1)}, u32[]{:S(2)}, u32[]{:S(2)}) collective-permute-start(bf16[2,32,1024]{2,1,0:T(8,128)(2,1)S(1)} %get-tuple-element.114), channel_id=1, source_target_pairs={{0,6},{2,4},{4,2},{6,0},{1,7},{3,5},{5,3},{7,1},{8,14},{10,12},{12... | collective-permute-start | bytes 393224 | tf_op jit(solution)/shard_map/ppermute | solution.py:31
  302.0 44.0 %collective-permute-start.26 = (bf16[16,32,1280]{2,1,0:T(8,128)(2,1)}, bf16[16,32,1280]{2,1,0:T(8,128)(2,1)}, u32[]{:S(2)}, u32[]{:S(2)}) collective-permute-start(bf16[16,32,1280]{2,1,0:T(8,128)(2,1)} %dynamic-slice_bitcast_fusion), channel_id=1, source_target_pairs={{0,1},{1,0},{2,3},{3,2},{4,5},{5,4},{6,7},{7,6},{8,9},{9,8},{10,11... | collective-permute-start | bytes 3932168 | tf_op jit(solution)/shard_map/ppermute | solution.py:31
  327.4 18.6 %copy-start.36 = (f32[32,8192]{1,0:T(8,128)}, f32[32,8192]{1,0:T(8,128)S(1)}, u32[]{:S(2)}) copy-start(f32[32,8192]{1,0:T(8,128)S(1)} %reshape.515) | copy-start | bytes 3145732
  329.4 15.1 %all-to-all-start.4 = ((bf16[32,32,128]{2,1,0:T(8,128)(2,1)}), bf16[32,32,128]{2,1,0:T(8,128)(2,1)S(1)}, u32[]{:S(2)}, u32[]{:S(2)}) async-start(bf16[32,32,128]{2,1,0:T(8,128)(2,1)} %bitcast.134), calls=%async_computation.5 | async-start | bytes 524288 | tf_op jit(solution)/shard_map/all_to_all | solution.py:807
  336.0 4.1 collective-permute-start.24
  340.1 9.3 %copy-start.48 = (f32[16,1024]{1,0:T(8,128)}, f32[16,1024]{1,0:T(8,128)S(1)}, u32[]{:S(2)}) copy-start(f32[16,1024]{1,0:T(8,128)S(1)} %fusion.30) | copy-start | bytes 196612
  349.4 8.5 %copy-start.25 = (bf16[4,128,1024]{2,1,0:T(8,128)(2,1)S(1)}, bf16[4,128,1024]{2,1,0:T(8,128)(2,1)}, u32[]{:S(2)}) copy-start(bf16[4,128,1024]{2,1,0:T(8,128)(2,1)} %copy-done.24) | copy-start | bytes 3145732
  349.4 8.7 %copy-start.26 = (f32[128,1024]{1,0:T(8,128)S(1)}, f32[128,1024]{1,0:T(8,128)}, u32[]{:S(2)}) copy-start(f32[128,1024]{1,0:T(8,128)} %get-tuple-element.44.after_cross) | copy-start | bytes 1572868
  349.4 8.7 %copy-start.49 = (f32[1,1024]{1,0:T(1,128)S(1)}, f32[1,1024]{1,0:T(1,128)}, u32[]{:S(2)}) copy-start(f32[1,1024]{1,0:T(1,128)} %get-tuple-element.133) | copy-start | bytes 12292
  349.4 52.2 %all-to-all-start.5 = ((bf16[16,32,1280]{2,1,0:T(8,128)(2,1)}), bf16[16,32,1280]{2,1,0:T(8,128)(2,1)S(1)}, u32[]{:S(2)}, u32[]{:S(2)}) async-start(bf16[16,32,1280]{2,1,0:T(8,128)(2,1)} %fusion.4), calls=%async_computation.6 | async-start | bytes 2621440 | tf_op jit(solution)/shard_map/all_to_all | solution.py:810
  354.6 42.9 %collective-permute-start.30 = (bf16[256,1024]{1,0:T(8,128)(2,1)}, bf16[256,1024]{1,0:T(8,128)(2,1)S(1)}, u32[]{:S(2)}, u32[]{:S(2)}) collective-permute-start(bf16[256,1024]{1,0:T(8,128)(2,1)} %get-tuple-element.90), channel_id=1, source_target_pairs={{0,0},{1,1},{2,8},{3,9},{4,16},{5,17},{6,24},{7,25},{8,4},{9,5},{1... | collective-permute-start | bytes 1572872 | tf_op jit(solution)/shard_map/ppermute | solution.py:692
  (35 other events, 86.6 us)
Sparse Core Ops, SparseCore 0:
  11.5 103.7 all-gather.4
  127.7 36.0 all-gather.6
  165.9 26.1 all-gather.8
  197.2 76.8 reduce-scatter.1

commit v6 on v5

--- a/solution.py
+++ b/solution.py
@@ -670,7 +670,7 @@
             functools.partial(feed_forward_gradients, s_size, z_size, x_size, up_rows),
             [((x_size * s_size, first_rows + unit, width), BF), ((group, width), BF)],
             [],
-            behind(here, partial),
+            here,
             normed_all,
             pre_grad,
             activated,

time: 417 us -> 414 us (level)
    slice x19 -> x18, local copies, waits for them, and re-layouts: 15.6 us -> 15 us  [behind(): last = other[(-1,) * other.ndim].astype(F32) * 0.0]
    add x11 -> x10, other arithmetic: 11 us -> 11.1 us  [behind(): return value + last.astype(value.dtype)]
  transfers between devices with their start and end apart: 41 -> 41, of which waited for: 18 -> 18; matrix products, arithmetic and copies ran while one was open for 23% -> 22% of each run, Pallas kernels for 17% -> 17%
where the time goes in v6:
time: 414 us; the launch traced here: 410 us
  waiting for transfers between devices  141 us (34%)
  Pallas kernels  68.5 us (17%)
  local copies, waits for them, and re-layouts  61.8 us (15%)
  starting transfers between devices  61.6 us (15%)
  other arithmetic  48.2 us (12%)
  between operations  27.2 us (7%)
    ppermute x30, waiting for transfers between devices, swap(): lax.ppermute(value, axis, [(i, i ^ step) for i in range(lax.axis_size(axi...  62.3 us
    pallas_call x7, Pallas kernels, call(): pl.pallas_call(kernel, out_shape=[jax.ShapeDtypeStruct(shape, kind) for s...  56.4 us
    ppermute x1, waiting for transfers between devices, body(): grad_down = lax.ppermute(grad_mlp[-unit:], ALL, owner).astype(F32)  36.2 us
    ppermute x30, starting transfers between devices, swap(): lax.ppermute(value, axis, [(i, i ^ step) for i in range(lax.axis_size(axi...  26.6 us
    all_to_all x3, waiting for transfers between devices, trade_z(): return lax.all_to_all(parts, 'z', 0, 0)  20.7 us
    all_to_all x1, waiting for transfers between devices, body(): lax.all_to_all(self_cuts, ALL, 0, 0)  18.9 us
    all_to_all x3, starting transfers between devices, trade_z(): return lax.all_to_all(parts, 'z', 0, 0)  15.8 us
    slice x18, local copies, waits for them, and re-layouts, behind(): last = other[(-1,) * other.ndim].astype(F32) * 0.0  15 us
  transfers between devices with their start and end apart: 41, of which 18 were waited for; matrix products, arithmetic and copies ran while one was open for 22% of the time, Pallas kernels for 17%

profile of v6, /device:TPU:4, one launch (start us, length us, event | category | flops | bytes accessed | tf_op | source)
XLA Modules:
  0.0 409.7 jit_solution(13633968975220565330)
XLA Ops:
  9.3 1.5 slice.275
  11.0 3.7 collective-permute-start.1
  16.8 1.6 collective-permute-start
  22.2 1.6 pad_maximum_fusion.1
  23.8 5.0 %all-to-all-start = ((bf16[4,256,1024]{2,1,0:T(8,128)(2,1)}), bf16[4,256,1024]{2,1,0:T(8,128)(2,1)}, u32[]{:S(2)}, u32[]{:S(2)}) async-start(bf16[4,256,1024]{2,1,0:T(8,128)(2,1)} %pad_maximum_fusion.1), calls=%async_computation | async-start | bytes 4194304 | tf_op jit(solution)/shard_map/all_to_all | solution.py:425
  31.8 5.5 %collective-permute-done.6 = bf16[160,1024]{1,0:T(8,128)(2,1)S(1)} collective-permute-done((bf16[160,1024]{1,0:T(8,128)(2,1)S(1)}, bf16[160,1024]{1,0:T(8,128)(2,1)S(1)}, u32[]{:S(2)}, u32[]{:S(2)}) %collective-permute-start.6) | collective-permute-done | bytes 327712 | tf_op jit(solution)/shard_map/ppermute | solution.py:31
  39.2 1.3 slice.362
  42.4 6.2 %collective-permute-done.4 = bf16[400,256]{1,0:T(8,128)(2,1)} collective-permute-done((bf16[400,256]{1,0:T(8,128)(2,1)S(1)}, bf16[400,256]{1,0:T(8,128)(2,1)}, u32[]{:S(2)}, u32[]{:S(2)}) %collective-permute-start.4) | collective-permute-done | bytes 204832 | tf_op jit(solution)/shard_map/ppermute | solution.py:31
  48.6 2.2 fusion.25
  50.8 1.5 collective-permute-start.5
  56.8 1.5 dynamic-slice_bitcast_fusion.15
  58.3 8.6 %collective-permute-done.2 = bf16[256,1024]{1,0:T(8,128)(2,1)S(1)} collective-permute-done((bf16[256,1024]{1,0:T(8,128)(2,1)S(1)}, bf16[256,1024]{1,0:T(8,128)(2,1)S(1)}, u32[]{:S(2)}, u32[]{:S(2)}) %collective-permute-start.2) | collective-permute-done | bytes 524320 | tf_op jit(solution)/shard_map/ppermute | solution.py:31
  68.3 6.4 %collective-permute-done.5 = bf16[4,400,256]{2,1,0:T(8,128)(2,1)} collective-permute-done((bf16[4,400,256]{2,1,0:T(8,128)(2,1)}, bf16[4,400,256]{2,1,0:T(8,128)(2,1)}, u32[]{:S(2)}, u32[]{:S(2)}) %collective-permute-start.5) | collective-permute-done | bytes 819232 | tf_op jit(solution)/shard_map/ppermute | solution.py:31
  74.8 2.5 pad_maximum_fusion.3.lines
  77.3 7.3 %shard_map.221 = (bf16[3,1024,256]{2,1,0:T(8,128)(2,1)}, f32[16,1024]{1,0:T(8,128)S(1)}, f32[1,2048]{1,0:T(1,128)S(1)}, bf16[512,1024]{1,0:T(8,128)(2,1)}, bf16[...) custom-call(s32[4]{0:T(128)S(1)} %get-tuple-element.73.at, ...), custom_call_target="tpu_custom_call" | custom-call | flops 1073741824 | bytes 2695168 | tf_op jit(solution)/shard_map/pallas_call | solution.py:66
  88.7 1.6 all-to-all-done
  90.3 2.6 fusion.47
  94.1 1.5 collective-permute-start.10
  96.6 14.4 %collective-permute-done.10 = bf16[4,2,128,256]{3,2,1,0:T(8,128)(2,1)} collective-permute-done((bf16[4,2,128,256]{3,2,1,0:T(8,128)(2,1)}, bf16[4,2,128,256]{3,2,1,0:T(8,128)(2,1)}, u32[]{:S(2)}, u32[]{:S(2)}) %collective-permute-start.10) | collective-permute-done | bytes 524320 | tf_op jit(solution)/shard_map/ppermute | solution.py:31
  111.0 1.4 fusion.13
  114.5 1.5 collective-permute-start.9
  116.0 2.8 collective-permute-done.11
  125.5 2.0 all_gather_reshape.3
  127.6 2.3 maximum_add_fusion
  131.1 6.4 %shard_map.222 = (f32[128,1024]{1,0:T(8,128)}, f32[128,1024]{1,0:T(8,128)}, bf16[128,3072]{1,0:T(8,128)(2,1)}, bf16[128,1024]{1,0:T(8,128)(2,1)S(1)}, f32[128,12...) custom-call(s32[4]{0:T(128)S(1)} %pad_add_fusion.at, ...), custom_call_target="tpu_custom_call" | custom-call | flops 838860800 | bytes 7144192 | tf_op jit(solution)/shard_map/pallas_call | solution.py:66
  138.7 4.2 %all-to-all-start.1 = ((bf16[4,128,1024]{2,1,0:T(8,128)(2,1)}), bf16[4,128,1024]{2,1,0:T(8,128)(2,1)}, u32[]{:S(2)}, u32[]{:S(2)}) async-start(bf16[4,128,1024]{2,1,0:T(8,128)(2,1)} %broadcast_in_dim.40), calls=%async_computation.1 | async-start | bytes 2097152 | tf_op jit(solution)/shard_map/all_to_all | solution.py:425
  143.4 2.5 convert_bitcast_fusion
  145.9 1.7 pad_maximum_fusion.2
  147.8 1.5 maximum_bitcast_fusion
  149.4 2.8 fusion.8
  152.2 2.4 pad_maximum_fusion.w_down
  154.5 15.2 %all-to-all-done.1 = bf16[4,128,1024]{2,1,0:T(8,128)(2,1)} async-done(((bf16[4,128,1024]{2,1,0:T(8,128)(2,1)}), bf16[4,128,1024]{2,1,0:T(8,128)(2,1)}, u32[]{:S(2)}, u32[]{:S(2)}) %all-to-all-start.1) | async-done | bytes 1048608 | tf_op jit(solution)/shard_map/all_to_all | solution.py:425
  169.7 12.0 %shard_map.223 = (bf16[512,2048]{1,0:T(8,128)(2,1)}, bf16[512,2048]{1,0:T(8,128)(2,1)}, bf16[512,1024]{1,0:T(8,128)(2,1)S(1)}, f32[1,2048]{1,0:T(1,128)S(1)}) custom-call(bf16[512,1024]{1,0:T(8,128)(2,1)} %bitcast.66.normed, bf16[512,1024]{1,0:T(8,128)(2,1)} %bitcast.267, bf16[8,4,32,2048]{3,2,1,0:T(8,128)(2,1)} %all-gather.7.cloned.1.call-done.w_up, ...), custom_call_target="tpu_custom_call" | custom-call | flops 6442450944 | bytes 12582912 | tf_op jit(solution)/shard_map/pallas_call | solution.py:624
  181.7 14.1 %shard_map.224 = (bf16[8,512,1024]{2,1,0:T(8,128)(2,1)}, bf16[512,1024]{1,0:T(8,128)(2,1)S(1)}) custom-call(s32[4]{0:T(128)S(1)} %get-tuple-element.74.at, bf16[512,1024]{1,0:T(8,128)(2,1)} %bitcast.66.normed, bf16[512,2048]{1,0:T(8,128)(2,1)} %get-tuple-element.47.pre_grad, bf16[512,2048]{1,0:T(8,128)(2,1)} %get-tuple-element.48.activated, ...), custom_call_target="tpu_custom_call" | custom-call | flops 6442450944 | bytes 10485760 | tf_op jit(solution)/shard_map/pallas_call | solution.py:66
  196.8 2.0 collective-permute-start.15
  198.8 2.4 collective-permute-start.16
  202.0 1.9 slice.380
  208.0 1.6 collective-permute-done.14
  209.6 8.9 %collective-permute-done.15 = bf16[128,1024]{1,0:T(8,128)(2,1)} collective-permute-done((bf16[128,1024]{1,0:T(8,128)(2,1)}, bf16[128,1024]{1,0:T(8,128)(2,1)}, u32[]{:S(2)}, u32[]{:S(2)}) %collective-permute-start.15) | collective-permute-done | bytes 262176 | tf_op jit(solution)/shard_map/ppermute | solution.py:31
  218.5 2.1 fusion.19.terms
  221.8 11.2 %shard_map.225 = (bf16[128,1024]{1,0:T(8,128)(2,1)S(1)}, f32[128,1024]{1,0:T(8,128)S(1)}, bf16[4,192,512]{2,1,0:T(8,128)(2,1)}, f32[16,1024]{1,0:T(8,128)S(1)}) custom-call(s32[4]{0:T(128)S(1)} %copy-done.9, f32[128,1024]{1,0:T(8,128)} %fusion.19.terms, bf16[128,1024]{1,0:T(8,128)(2,1)S(1)} %bitcast.231, f32[128,1024]{1,0:T(8,128)} %get-tuple-element.52.after_self, ...), custom_call_target="tpu_custom_call" | custom-call | flops 620756992 | bytes 8782592 | tf_op jit(solution)/shard_map/pallas_call | solution.py:66
  233.0 1.4 collective-permute-start.17
  237.9 6.6 %all-to-all-start.2 = ((bf16[4,128,1024]{2,1,0:T(8,128)(2,1)}), bf16[4,128,1024]{2,1,0:T(8,128)(2,1)S(1)}, u32[]{:S(2)}, u32[]{:S(2)}) async-start(bf16[4,128,1024]{2,1,0:T(8,128)(2,1)} %bitcast.250), calls=%async_computation.2 | async-start | bytes 2097152 | tf_op jit(solution)/shard_map/all_to_all | solution.py:425
  248.7 1.4 collective-permute-start.22
  251.2 10.0 %shard_map.226 = (bf16[1024,768]{1,0:T(8,128)(2,1)}, bf16[512,1024]{1,0:T(8,128)(2,1)}, f32[8,256]{1,0:T(8,128)S(1)}) custom-call(s32[4]{0:T(128)S(1)} %get-tuple-element.74.at, bf16[512,1024]{1,0:T(8,128)(2,1)} %copy-done.41, bf16[256,1024]{1,0:T(8,128)(2,1)} %constant_dynamic-slice_fusion.7.w_out, bf16[512,256]{1,0:T(8,128)(2,1)S(1)} %copy-done.15, ...), custom_call_target="tpu_custom_call" | custom-call | flops 2550136832 | bytes 5251072 | tf_op jit(solution)/shard_map/pallas_call | solution.py:66
  261.1 1.4 slice.331
  265.2 3.9 all-to-all-done.2
  270.4 2.7 broadcast_add_fusion.1
  273.1 4.3 %all-to-all-start.3 = ((bf16[32,32,768]{2,1,0:T(8,128)(2,1)}), bf16[32,32,768]{2,1,0:T(8,128)(2,1)}, u32[]{:S(2)}, u32[]{:S(2)}) async-start(bf16[32,32,768]{2,1,0:T(8,128)(2,1)} %bitcast.111), calls=%async_computation.3 | async-start | bytes 3145728 | tf_op jit(solution)/shard_map/all_to_all | solution.py:804
  283.0 5.5 %shard_map.228 = bf16[1024,1280]{1,0:T(8,128)(2,1)} custom-call(s32[4]{0:T(128)S(1)} %get-tuple-element.74.at, bf16[2,128,3072]{2,1,0:T(8,128)(2,1)} %bitcast.248, bf16[2,128,3072]{2,1,0:T(8,128)(2,1)} %collective-permute-done.25.swapped, bf16[512,512]{1,0:T(8,128)(2,1)S(1)} %bitcast.229, bf16[512,256]{1,0:T(8,128)(2,1)S(1)} %constant_dynamic-slice_fusion.4.branch_cut, ...), custom_call_target="tpu_custom_call" | custom-call | flops 805306368 | bytes 4128768 | tf_op jit(solution)/shard_map/pallas_call | solution.py:66
  288.5 2.2 slice_bitcast_fusion
  291.5 2.8 collective-permute-start.27
  294.2 1.5 collective-permute-start.28
  297.8 2.1 collective-permute-done.20
  299.9 1.9 shard_map.227
  301.7 18.9 %all-to-all-done.3 = bf16[32,32,768]{2,1,0:T(8,128)(2,1)} async-done(((bf16[32,32,768]{2,1,0:T(8,128)(2,1)}), bf16[32,32,768]{2,1,0:T(8,128)(2,1)}, u32[]{:S(2)}, u32[]{:S(2)}) %all-to-all-start.3) | async-done | bytes 1572896 | tf_op jit(solution)/shard_map/all_to_all | solution.py:804
  327.3 5.7 %all-to-all-start.4 = ((bf16[32,32,128]{2,1,0:T(8,128)(2,1)}), bf16[32,32,128]{2,1,0:T(8,128)(2,1)S(1)}, u32[]{:S(2)}, u32[]{:S(2)}) async-start(bf16[32,32,128]{2,1,0:T(8,128)(2,1)} %bitcast.133), calls=%async_computation.5 | async-start | bytes 524288 | tf_op jit(solution)/shard_map/all_to_all | solution.py:807
  334.2 3.7 collective-permute-done.24
  339.2 3.2 all-to-all-done.4
  343.8 3.4 fusion.4
  347.3 5.2 %all-to-all-start.5 = ((bf16[16,32,1280]{2,1,0:T(8,128)(2,1)}), bf16[16,32,1280]{2,1,0:T(8,128)(2,1)S(1)}, u32[]{:S(2)}, u32[]{:S(2)}) async-start(bf16[16,32,1280]{2,1,0:T(8,128)(2,1)} %fusion.4), calls=%async_computation.6 | async-start | bytes 2621440 | tf_op jit(solution)/shard_map/all_to_all | solution.py:810
  352.4 3.3 collective-permute-start.30
  356.8 1.7 convert_reduce_fusion
  359.1 36.2 %collective-permute-done.30 = bf16[256,1024]{1,0:T(8,128)(2,1)S(1)} collective-permute-done((bf16[256,1024]{1,0:T(8,128)(2,1)}, bf16[256,1024]{1,0:T(8,128)(2,1)S(1)}, u32[]{:S(2)}, u32[]{:S(2)}) %collective-permute-start.30) | collective-permute-done | bytes 524320 | tf_op jit(solution)/shard_map/ppermute | solution.py:692
  (324 shorter events, 74.1 us)
Async XLA Ops:
  7.2 115.5 %all-gather.5.cloned.1.call-start = ((), (), s32[]{:S(2)}) async-start(), calls=%async_computation.7 | async-start | bytes 6488064 | tf_op jit(solution)/shard_map/all_gather | solution.py:528
  11.0 28.1 %collective-permute-start.1 = (bf16[400,256]{1,0:T(8,128)(2,1)S(1)}, bf16[400,256]{1,0:T(8,128)(2,1)}, u32[]{:S(2)}, u32[]{:S(2)}) collective-permute-start(bf16[400,256]{1,0:T(8,128)(2,1)S(1)} %get-tuple-element.128), channel_id=1, source_target_pairs={{0,6},{2,4},{4,2},{6,0},{1,7},{3,5},{5,3},{7,1},{8,14},{10,12},{12... | collective-permute-start | bytes 614408 | tf_op jit(solution)/shard_map/ppermute | solution.py:31
  14.7 27.7 %collective-permute-start.3 = (bf16[400,256]{1,0:T(8,128)(2,1)S(1)}, bf16[400,256]{1,0:T(8,128)(2,1)}, u32[]{:S(2)}, u32[]{:S(2)}) collective-permute-start(bf16[400,256]{1,0:T(8,128)(2,1)S(1)} %get-tuple-element.128), channel_id=1, source_target_pairs={{0,2},{2,0},{4,6},{6,4},{1,3},{3,1},{5,7},{7,5},{8,10},{10,8},{12,... | collective-permute-start | bytes 614408 | tf_op jit(solution)/shard_map/ppermute | solution.py:31
  14.7 33.9 %collective-permute-start.4 = (bf16[400,256]{1,0:T(8,128)(2,1)S(1)}, bf16[400,256]{1,0:T(8,128)(2,1)}, u32[]{:S(2)}, u32[]{:S(2)}) collective-permute-start(bf16[400,256]{1,0:T(8,128)(2,1)S(1)} %get-tuple-element.128), channel_id=1, source_target_pairs={{0,4},{2,6},{4,0},{6,2},{1,5},{3,7},{5,1},{7,3},{8,12},{10,14},{12... | collective-permute-start | bytes 614408 | tf_op jit(solution)/shard_map/ppermute | solution.py:31
  16.8 24.4 %collective-permute-start = (bf16[256,1024]{1,0:T(8,128)(2,1)S(1)}, bf16[256,1024]{1,0:T(8,128)(2,1)S(1)}, u32[]{:S(2)}, u32[]{:S(2)}) collective-permute-start(bf16[256,1024]{1,0:T(8,128)(2,1)S(1)} %dynamic-slice_convert_fusion.1), channel_id=1, source_target_pairs={{0,1},{1,0},{2,3},{3,2},{4,5},{5,4},{6,7},{7,6},{8,9},{9,8},{10,11... | collective-permute-start | bytes 1572872 | tf_op jit(solution)/shard_map/ppermute | solution.py:31
  23.7 5.3 %copy-start.39 = (bf16[1,16,1024]{2,1,0:T(8,128)(2,1)S(1)}, bf16[1,16,1024]{2,1,0:T(8,128)(2,1)}, u32[]{:S(2)}) copy-start(bf16[1,16,1024]{2,1,0:T(8,128)(2,1)} %param.15) | copy-start | bytes 98308
  23.7 5.9 %copy-start.56 = (s32[8]{0:T(128)S(1)}, s32[8]{0:T(128)}, u32[]{:S(2)}) copy-start(s32[8]{0:T(128)} %param.19) | copy-start | bytes 100
  23.8 66.5 %all-to-all-start = ((bf16[4,256,1024]{2,1,0:T(8,128)(2,1)}), bf16[4,256,1024]{2,1,0:T(8,128)(2,1)}, u32[]{:S(2)}, u32[]{:S(2)}) async-start(bf16[4,256,1024]{2,1,0:T(8,128)(2,1)} %pad_maximum_fusion.1), calls=%async_computation | async-start | bytes 4194304 | tf_op jit(solution)/shard_map/all_to_all | solution.py:425
  28.8 140.9 %all-gather.7.cloned.1.call-start = ((), (), s32[]{:S(2)}) async-start(), calls=%async_computation.8 | async-start | bytes 4718592 | tf_op jit(solution)/shard_map/all_gather | solution.py:609
  29.1 8.1 %collective-permute-start.6 = (bf16[160,1024]{1,0:T(8,128)(2,1)S(1)}, bf16[160,1024]{1,0:T(8,128)(2,1)S(1)}, u32[]{:S(2)}, u32[]{:S(2)}) collective-permute-start(bf16[160,1024]{1,0:T(8,128)(2,1)S(1)} %pad_maximum_fusion.10), channel_id=1, source_target_pairs={{0,16},{16,0},{1,17},{17,1},{2,18},{18,2},{3,19},{19,3},{4,20},{20... | collective-permute-start | bytes 983048 | tf_op jit(solution)/shard_map/ppermute | solution.py:31
  38.1 14.8 %collective-permute-start.7 = (bf16[320,1024]{1,0:T(8,128)(2,1)}, bf16[320,1024]{1,0:T(8,128)(2,1)}, u32[]{:S(2)}, u32[]{:S(2)}) collective-permute-start(bf16[320,1024]{1,0:T(8,128)(2,1)} %pad_maximum_fusion.6), channel_id=1, source_target_pairs={{0,8},{8,0},{1,9},{9,1},{2,10},{10,2},{3,11},{11,3},{4,12},{12,4},... | collective-permute-start | bytes 1966088 | tf_op jit(solution)/shard_map/ppermute | solution.py:31
  38.4 38.8 %copy-start.4 = (s32[512,1]{1,0:T(8,128)}, s32[512,1]{1,0:T(8,128)S(1)}, u32[]{:S(2)}) copy-start(s32[512,1]{1,0:T(8,128)S(1)} %add.424.pos) | copy-start | bytes 6148
  38.5 38.7 %copy-start.12 = (s32[1,512]{1,0:T(1,128)}, s32[1,512]{1,0:T(1,128)S(1)}, u32[]{:S(2)}) copy-start(s32[1,512]{1,0:T(1,128)S(1)} %add.356.pos_line) | copy-start | bytes 6148
  39.2 13.7 %copy-start.34 = (bf16[640,1024]{1,0:T(8,128)(2,1)S(1)}, bf16[640,1024]{1,0:T(8,128)(2,1)}, u32[]{:S(2)}) copy-start(bf16[640,1024]{1,0:T(8,128)(2,1)} %constant_dynamic-update-slice_fusion.2) | copy-start | bytes 3932164
  50.8 24.0 %collective-permute-start.5 = (bf16[4,400,256]{2,1,0:T(8,128)(2,1)}, bf16[4,400,256]{2,1,0:T(8,128)(2,1)}, u32[]{:S(2)}, u32[]{:S(2)}) collective-permute-start(bf16[4,400,256]{2,1,0:T(8,128)(2,1)} %get-tuple-element.102), channel_id=1, source_target_pairs={{0,1},{1,0},{2,3},{3,2},{4,5},{5,4},{6,7},{7,6},{8,9},{9,8},{10,11... | collective-permute-start | bytes 2457608 | tf_op jit(solution)/shard_map/ppermute | solution.py:31
  52.3 14.6 %collective-permute-start.2 = (bf16[256,1024]{1,0:T(8,128)(2,1)S(1)}, bf16[256,1024]{1,0:T(8,128)(2,1)S(1)}, u32[]{:S(2)}, u32[]{:S(2)}) collective-permute-start(bf16[256,1024]{1,0:T(8,128)(2,1)S(1)} %broadcast_add_fusion.5), channel_id=1, source_target_pairs={{0,16},{16,0},{1,17},{17,1},{2,18},{18,2},{3,19},{19,3},{4,20},{20... | collective-permute-start | bytes 1572872 | tf_op jit(solution)/shard_map/ppermute | solution.py:31
  56.6 20.7 %copy-start.40 = (s32[1,4,16,1024]{3,1,2,0:T(4,128)}, s32[1,4,16,1024]{3,1,2,0:T(4,128)S(1)}, u32[]{:S(2)}) copy-start(s32[1,4,16,1024]{3,1,2,0:T(4,128)S(1)} %copy.99) | copy-start | bytes 786436
  56.8 27.8 %copy-start.6 = (s32[512,1]{1,0:T(8,128)}, s32[512,1]{1,0:T(8,128)S(1)}, u32[]{:S(2)}) copy-start(s32[512,1]{1,0:T(8,128)S(1)} %copy.70.seg) | copy-start | bytes 6148
  58.3 55.3 %copy-start.42 = (bf16[16,1024]{1,0:T(8,128)(2,1)}, bf16[16,1024]{1,0:T(8,128)(2,1)S(1)}, u32[]{:S(2)}) copy-start(bf16[16,1024]{1,0:T(8,128)(2,1)S(1)} %get-tuple-element.83) | copy-start | bytes 98308
  66.9 17.7 %copy-start.38 = (bf16[256,1024]{1,0:T(8,128)(2,1)}, bf16[256,1024]{1,0:T(8,128)(2,1)S(1)}, u32[]{:S(2)}) copy-start(bf16[256,1024]{1,0:T(8,128)(2,1)S(1)} %collective-permute-done.2) | copy-start | bytes 1572868
  94.1 17.0 %collective-permute-start.10 = (bf16[4,2,128,256]{3,2,1,0:T(8,128)(2,1)}, bf16[4,2,128,256]{3,2,1,0:T(8,128)(2,1)}, u32[]{:S(2)}, u32[]{:S(2)}) collective-permute-start(bf16[4,2,128,256]{3,2,1,0:T(8,128)(2,1)} %reshape.491), channel_id=1, source_target_pairs={{0,1},{1,0},{2,3},{3,2},{4,5},{5,4},{6,7},{7,6},{8,9},{9,8},{10,11... | collective-permute-start | bytes 1572872 | tf_op jit(solution)/shard_map/ppermute | solution.py:31
  95.6 18.9 %collective-permute-start.8 = (bf16[2,128,256]{2,1,0:T(8,128)(2,1)S(1)}, bf16[2,128,256]{2,1,0:T(8,128)(2,1)S(1)}, u32[]{:S(2)}, u32[]{:S(2)}) collective-permute-start(bf16[2,128,256]{2,1,0:T(8,128)(2,1)S(1)} %bitcast.283), channel_id=1, source_target_pairs={{0,8},{8,0},{1,9},{9,1},{2,10},{10,2},{3,11},{11,3},{4,12},{12,4},... | collective-permute-start | bytes 393224 | tf_op jit(solution)/shard_map/ppermute | solution.py:31
  112.8 12.7 %copy-start.31 = (bf16[1,4,2,128,256]{4,3,2,1,0:T(8,128)(2,1)}, bf16[1,4,2,128,256]{4,3,2,1,0:T(8,128)(2,1)S(1)}, u32[]{:S(2)}) copy-start(bf16[1,4,2,128,256]{4,3,2,1,0:T(8,128)(2,1)S(1)} %copy.76) | copy-start | bytes 1572868
  113.8 13.8 %copy-start.28 = (bf16[256,1024]{1,0:T(8,128)(2,1)S(1)}, bf16[256,1024]{1,0:T(8,128)(2,1)}, u32[]{:S(2)}) copy-start(bf16[256,1024]{1,0:T(8,128)(2,1)} %copy-done.27) | copy-start | bytes 1572868
  113.8 4.9 %collective-permute-start.11 = (bf16[1,2,64,256]{3,2,1,0:T(8,128)(2,1)S(1)}, bf16[1,2,64,256]{3,2,1,0:T(8,128)(2,1)S(1)}, u32[]{:S(2)}, u32[]{:S(2)}) collective-permute-start(bf16[1,2,64,256]{3,2,1,0:T(8,128)(2,1)S(1)} %maximum_bitcast_fusion.3), channel_id=1, source_target_pairs={{0,16},{16,0},{1,17},{17,1},{2,18},{18,2},{3,19},{19,3},{4,20},{20... | collective-permute-start | bytes 196616 | tf_op jit(solution)/shard_map/ppermute | solution.py:31
  114.5 5.7 %collective-permute-start.9 = (bf16[2,128,256]{2,1,0:T(8,128)(2,1)S(1)}, bf16[2,128,256]{2,1,0:T(8,128)(2,1)S(1)}, u32[]{:S(2)}, u32[]{:S(2)}) collective-permute-start(bf16[2,128,256]{2,1,0:T(8,128)(2,1)S(1)} %get-tuple-element.124), channel_id=1, source_target_pairs={{0,16},{16,0},{1,17},{17,1},{2,18},{18,2},{3,19},{19,3},{4,20},{20... | collective-permute-start | bytes 393224 | tf_op jit(solution)/shard_map/ppermute | solution.py:31
  118.8 2.7 collective-permute-start.12
  129.9 16.0 %collective-permute-start.13 = (bf16[512,1024]{1,0:T(8,128)(2,1)}, bf16[512,1024]{1,0:T(8,128)(2,1)}, u32[]{:S(2)}, u32[]{:S(2)}) collective-permute-start(bf16[512,1024]{1,0:T(8,128)(2,1)} %maximum_add_fusion), channel_id=1, source_target_pairs={{0,8},{8,0},{1,9},{9,1},{2,10},{10,2},{3,11},{11,3},{4,12},{12,4},... | collective-permute-start | bytes 3145736 | tf_op jit(solution)/shard_map/ppermute | solution.py:31
  130.0 7.4 %copy-start.8 = (s32[4]{0:T(128)}, s32[4]{0:T(128)S(1)}, u32[]{:S(2)}) copy-start(s32[4]{0:T(128)S(1)} %pad_add_fusion.at) | copy-start | bytes 52
  131.0 6.4 %copy-start.10 = (s32[1,64]{1,0:T(1,128)}, s32[1,64]{1,0:T(1,128)S(1)}, u32[]{:S(2)}) copy-start(s32[1,64]{1,0:T(1,128)S(1)} %add_bitcast_fusion.source_seg) | copy-start | bytes 772
  138.7 31.0 %all-to-all-start.1 = ((bf16[4,128,1024]{2,1,0:T(8,128)(2,1)}), bf16[4,128,1024]{2,1,0:T(8,128)(2,1)}, u32[]{:S(2)}, u32[]{:S(2)}) async-start(bf16[4,128,1024]{2,1,0:T(8,128)(2,1)} %broadcast_in_dim.40), calls=%async_computation.1 | async-start | bytes 2097152 | tf_op jit(solution)/shard_map/all_to_all | solution.py:425
  142.9 61.9 %all-gather.9.cloned.1.call-start = ((), (), s32[]{:S(2)}) async-start(), calls=%async_computation.10 | async-start | bytes 2359296 | tf_op jit(solution)/shard_map/all_gather | solution.py:681
  149.3 139.2 %reduce-scatter.2.cloned.1.call-start = ((), (), s32[]{:S(2)}) async-start(), calls=%async_computation.9 | async-start | bytes 9437184 | tf_op jit(solution)/shard_map/reduce_scatter | solution.py:683
  195.9 5.3 %copy-start.43 = (bf16[16,1024]{1,0:T(8,128)(2,1)S(1)}, bf16[16,1024]{1,0:T(8,128)(2,1)}, u32[]{:S(2)}) copy-start(bf16[16,1024]{1,0:T(8,128)(2,1)} %copy-done.42) | copy-start | bytes 98308
  195.9 5.3 %copy-start.45 = (bf16[16,1024]{1,0:T(8,128)(2,1)S(1)}, bf16[16,1024]{1,0:T(8,128)(2,1)}, u32[]{:S(2)}) copy-start(bf16[16,1024]{1,0:T(8,128)(2,1)} %get-tuple-element.84) | copy-start | bytes 98308
  196.8 12.8 %collective-permute-start.14 = (bf16[128,1024]{1,0:T(8,128)(2,1)}, bf16[128,1024]{1,0:T(8,128)(2,1)}, u32[]{:S(2)}, u32[]{:S(2)}) collective-permute-start(bf16[128,1024]{1,0:T(8,128)(2,1)} %get-tuple-element.94), channel_id=1, source_target_pairs={{0,2},{2,0},{4,6},{6,4},{1,3},{3,1},{5,7},{7,5},{8,10},{10,8},{12,... | collective-permute-start | bytes 786440 | tf_op jit(solution)/shard_map/ppermute | solution.py:31
  196.8 21.7 %collective-permute-start.15 = (bf16[128,1024]{1,0:T(8,128)(2,1)}, bf16[128,1024]{1,0:T(8,128)(2,1)}, u32[]{:S(2)}, u32[]{:S(2)}) collective-permute-start(bf16[128,1024]{1,0:T(8,128)(2,1)} %get-tuple-element.96), channel_id=1, source_target_pairs={{0,4},{2,6},{4,0},{6,2},{1,5},{3,7},{5,1},{7,3},{8,12},{10,14},{12... | collective-permute-start | bytes 786440 | tf_op jit(solution)/shard_map/ppermute | solution.py:31
  198.8 19.6 %collective-permute-start.16 = (bf16[128,1024]{1,0:T(8,128)(2,1)}, bf16[128,1024]{1,0:T(8,128)(2,1)}, u32[]{:S(2)}, u32[]{:S(2)}) collective-permute-start(bf16[128,1024]{1,0:T(8,128)(2,1)} %get-tuple-element.95), channel_id=1, source_target_pairs={{0,6},{2,4},{4,2},{6,0},{1,7},{3,5},{5,3},{7,1},{8,14},{10,12},{12... | collective-permute-start | bytes 786440 | tf_op jit(solution)/shard_map/ppermute | solution.py:31
  233.0 13.5 %collective-permute-start.17 = (bf16[128,1024]{1,0:T(8,128)(2,1)S(1)}, bf16[128,1024]{1,0:T(8,128)(2,1)S(1)}, u32[]{:S(2)}, u32[]{:S(2)}) collective-permute-start(bf16[128,1024]{1,0:T(8,128)(2,1)S(1)} %get-tuple-element.56), channel_id=1, source_target_pairs={{0,16},{16,0},{1,17},{17,1},{2,18},{18,2},{3,19},{19,3},{4,20},{20... | collective-permute-start | bytes 786440 | tf_op jit(solution)/shard_map/ppermute | solution.py:31
  237.9 31.2 %all-to-all-start.2 = ((bf16[4,128,1024]{2,1,0:T(8,128)(2,1)}), bf16[4,128,1024]{2,1,0:T(8,128)(2,1)S(1)}, u32[]{:S(2)}, u32[]{:S(2)}) async-start(bf16[4,128,1024]{2,1,0:T(8,128)(2,1)} %bitcast.250), calls=%async_computation.2 | async-start | bytes 2097152 | tf_op jit(solution)/shard_map/all_to_all | solution.py:425
  245.8 2.8 collective-permute-start.21
  246.6 3.5 collective-permute-start.18
  248.5 34.5 %collective-permute-start.25 = (bf16[2,128,3072]{2,1,0:T(8,128)(2,1)}, bf16[2,128,3072]{2,1,0:T(8,128)(2,1)}, u32[]{:S(2)}, u32[]{:S(2)}) collective-permute-start(bf16[2,128,3072]{2,1,0:T(8,128)(2,1)} %broadcast_add_fusion), channel_id=1, source_target_pairs={{0,8},{8,0},{1,9},{9,1},{2,10},{10,2},{3,11},{11,3},{4,12},{12,4},... | collective-permute-start | bytes 4718600 | tf_op jit(solution)/shard_map/ppermute | solution.py:31
  248.7 14.5 %collective-permute-start.22 = (bf16[2,192,512]{2,1,0:T(8,128)(2,1)S(1)}, bf16[2,192,512]{2,1,0:T(8,128)(2,1)S(1)}, u32[]{:S(2)}, u32[]{:S(2)}) collective-permute-start(bf16[2,192,512]{2,1,0:T(8,128)(2,1)S(1)} %get-tuple-element.104), channel_id=1, source_target_pairs={{0,16},{16,0},{1,17},{17,1},{2,18},{18,2},{3,19},{19,3},{4,20},{20... | collective-permute-start | bytes 1179656 | tf_op jit(solution)/shard_map/ppermute | solution.py:31
  273.1 6.7 %copy-start.30 = (bf16[1,4,2,128,256]{4,3,2,1,0:T(8,128)(2,1)S(1)}, bf16[1,4,2,128,256]{4,3,2,1,0:T(8,128)(2,1)}, u32[]{:S(2)}) copy-start(bf16[1,4,2,128,256]{4,3,2,1,0:T(8,128)(2,1)} %copy-done.29) | copy-start | bytes 1572868
  273.1 7.0 %copy-start.32 = (bf16[1,4,2,128,256]{4,3,2,1,0:T(8,128)(2,1)S(1)}, bf16[1,4,2,128,256]{4,3,2,1,0:T(8,128)(2,1)}, u32[]{:S(2)}) copy-start(bf16[1,4,2,128,256]{4,3,2,1,0:T(8,128)(2,1)} %copy-done.31) | copy-start | bytes 1572868
  273.1 47.5 %all-to-all-start.3 = ((bf16[32,32,768]{2,1,0:T(8,128)(2,1)}), bf16[32,32,768]{2,1,0:T(8,128)(2,1)}, u32[]{:S(2)}, u32[]{:S(2)}) async-start(bf16[32,32,768]{2,1,0:T(8,128)(2,1)} %bitcast.111), calls=%async_computation.3 | async-start | bytes 3145728 | tf_op jit(solution)/shard_map/all_to_all | solution.py:804
  279.6 2.9 collective-permute-start.19
  281.0 52.0 %collective-permute-start.23 = (bf16[2,16,1024]{2,1,0:T(8,128)(2,1)}, bf16[2,16,1024]{2,1,0:T(8,128)(2,1)}, u32[]{:S(2)}, u32[]{:S(2)}) collective-permute-start(bf16[2,16,1024]{2,1,0:T(8,128)(2,1)} %pad_maximum_fusion.19), channel_id=1, source_target_pairs={{0,8},{8,0},{1,9},{9,1},{2,10},{10,2},{3,11},{11,3},{4,12},{12,4},... | collective-permute-start | bytes 196616 | tf_op jit(solution)/shard_map/ppermute | solution.py:31
  282.7 17.1 %collective-permute-start.20 = (bf16[128,1024]{1,0:T(8,128)(2,1)S(1)}, bf16[128,1024]{1,0:T(8,128)(2,1)S(1)}, u32[]{:S(2)}, u32[]{:S(2)}) collective-permute-start(bf16[128,1024]{1,0:T(8,128)(2,1)S(1)} %fusion.24), channel_id=1, source_target_pairs={{0,16},{16,0},{1,17},{17,1},{2,18},{18,2},{3,19},{19,3},{4,20},{20... | collective-permute-start | bytes 786440 | tf_op jit(solution)/shard_map/ppermute | solution.py:31
  288.5 8.1 %copy-start.22 = (bf16[1024,1280]{1,0:T(8,128)(2,1)S(1)}, bf16[1024,1280]{1,0:T(8,128)(2,1)}, u32[]{:S(2)}) copy-start(bf16[1024,1280]{1,0:T(8,128)(2,1)} %shard_map.228) | copy-start | bytes 7864324
  291.5 31.1 %collective-permute-start.27 = (bf16[2,32,1024]{2,1,0:T(8,128)(2,1)}, bf16[2,32,1024]{2,1,0:T(8,128)(2,1)S(1)}, u32[]{:S(2)}, u32[]{:S(2)}) collective-permute-start(bf16[2,32,1024]{2,1,0:T(8,128)(2,1)} %get-tuple-element.113), channel_id=1, source_target_pairs={{0,2},{2,0},{4,6},{6,4},{1,3},{3,1},{5,7},{7,5},{8,10},{10,8},{12,... | collective-permute-start | bytes 393224 | tf_op jit(solution)/shard_map/ppermute | solution.py:31
  294.2 29.0 %collective-permute-start.28 = (bf16[2,32,1024]{2,1,0:T(8,128)(2,1)S(1)}, bf16[2,32,1024]{2,1,0:T(8,128)(2,1)S(1)}, u32[]{:S(2)}, u32[]{:S(2)}) collective-permute-start(bf16[2,32,1024]{2,1,0:T(8,128)(2,1)S(1)} %get-tuple-element.112), channel_id=1, source_target_pairs={{0,4},{2,6},{4,0},{6,2},{1,5},{3,7},{5,1},{7,3},{8,12},{10,14},{12... | collective-permute-start | bytes 393224 | tf_op jit(solution)/shard_map/ppermute | solution.py:31
  295.7 27.5 %collective-permute-start.29 = (bf16[2,32,1024]{2,1,0:T(8,128)(2,1)S(1)}, bf16[2,32,1024]{2,1,0:T(8,128)(2,1)S(1)}, u32[]{:S(2)}, u32[]{:S(2)}) collective-permute-start(bf16[2,32,1024]{2,1,0:T(8,128)(2,1)S(1)} %get-tuple-element.114), channel_id=1, source_target_pairs={{0,6},{2,4},{4,2},{6,0},{1,7},{3,5},{5,3},{7,1},{8,14},{10,12},{12... | collective-permute-start | bytes 393224 | tf_op jit(solution)/shard_map/ppermute | solution.py:31
  299.8 44.0 %collective-permute-start.26 = (bf16[16,32,1280]{2,1,0:T(8,128)(2,1)}, bf16[16,32,1280]{2,1,0:T(8,128)(2,1)}, u32[]{:S(2)}, u32[]{:S(2)}) collective-permute-start(bf16[16,32,1280]{2,1,0:T(8,128)(2,1)} %dynamic-slice_bitcast_fusion), channel_id=1, source_target_pairs={{0,1},{1,0},{2,3},{3,2},{4,5},{5,4},{6,7},{7,6},{8,9},{9,8},{10,11... | collective-permute-start | bytes 3932168 | tf_op jit(solution)/shard_map/ppermute | solution.py:31
  325.2 18.6 %copy-start.36 = (f32[32,8192]{1,0:T(8,128)}, f32[32,8192]{1,0:T(8,128)S(1)}, u32[]{:S(2)}) copy-start(f32[32,8192]{1,0:T(8,128)S(1)} %reshape.511) | copy-start | bytes 3145732
  327.3 15.1 %all-to-all-start.4 = ((bf16[32,32,128]{2,1,0:T(8,128)(2,1)}), bf16[32,32,128]{2,1,0:T(8,128)(2,1)S(1)}, u32[]{:S(2)}, u32[]{:S(2)}) async-start(bf16[32,32,128]{2,1,0:T(8,128)(2,1)} %bitcast.133), calls=%async_computation.5 | async-start | bytes 524288 | tf_op jit(solution)/shard_map/all_to_all | solution.py:807
  333.9 4.1 collective-permute-start.24
  338.0 9.3 %copy-start.48 = (f32[16,1024]{1,0:T(8,128)}, f32[16,1024]{1,0:T(8,128)S(1)}, u32[]{:S(2)}) copy-start(f32[16,1024]{1,0:T(8,128)S(1)} %fusion.30) | copy-start | bytes 196612
  347.3 8.5 %copy-start.25 = (bf16[4,128,1024]{2,1,0:T(8,128)(2,1)S(1)}, bf16[4,128,1024]{2,1,0:T(8,128)(2,1)}, u32[]{:S(2)}) copy-start(bf16[4,128,1024]{2,1,0:T(8,128)(2,1)} %copy-done.24) | copy-start | bytes 3145732
  347.3 8.7 %copy-start.26 = (f32[128,1024]{1,0:T(8,128)S(1)}, f32[128,1024]{1,0:T(8,128)}, u32[]{:S(2)}) copy-start(f32[128,1024]{1,0:T(8,128)} %get-tuple-element.44.after_cross) | copy-start | bytes 1572868
  347.3 8.7 %copy-start.49 = (f32[1,1024]{1,0:T(1,128)S(1)}, f32[1,1024]{1,0:T(1,128)}, u32[]{:S(2)}) copy-start(f32[1,1024]{1,0:T(1,128)} %get-tuple-element.133) | copy-start | bytes 12292
  347.3 52.2 %all-to-all-start.5 = ((bf16[16,32,1280]{2,1,0:T(8,128)(2,1)}), bf16[16,32,1280]{2,1,0:T(8,128)(2,1)S(1)}, u32[]{:S(2)}, u32[]{:S(2)}) async-start(bf16[16,32,1280]{2,1,0:T(8,128)(2,1)} %fusion.4), calls=%async_computation.6 | async-start | bytes 2621440 | tf_op jit(solution)/shard_map/all_to_all | solution.py:810
  352.4 42.9 %collective-permute-start.30 = (bf16[256,1024]{1,0:T(8,128)(2,1)}, bf16[256,1024]{1,0:T(8,128)(2,1)S(1)}, u32[]{:S(2)}, u32[]{:S(2)}) collective-permute-start(bf16[256,1024]{1,0:T(8,128)(2,1)} %get-tuple-element.90), channel_id=1, source_target_pairs={{0,0},{1,1},{2,8},{3,9},{4,16},{5,17},{6,24},{7,25},{8,4},{9,5},{1... | collective-permute-start | bytes 1572872 | tf_op jit(solution)/shard_map/ppermute | solution.py:692
  (35 other events, 86.0 us)
Sparse Core Ops, SparseCore 0:
  11.5 103.7 all-gather.4
  127.7 36.0 all-gather.6
  165.9 26.1 all-gather.8
  196.0 78.1 reduce-scatter.1

commit v7 on v6

--- a/solution.py
+++ b/solution.py
@@ -802,7 +802,7 @@
 
     self_cuts = behind(self_cuts, results).reshape(count, up_rows, 3 * cut)
     self_cuts = lax.all_to_all(self_cuts, ALL, 0, 0).reshape(s_size, f_size, up_rows, 3 * cut)
-    kept = behind(behind(behind(kept, self_cuts), grad_memory), grad_up)
+    kept = behind(kept, grad_memory)
     table = behind(behind(table, self_cuts), grad_up)
     table = lax.all_to_all(table.reshape(count, up_rows, 128), ALL, 0, 0)
     table = jnp.sum(table.astype(F32), axis=0).T

time: 414 us -> 414 us (level)
  no operation moved by 1% of the time
where the time goes in v7:
time: 414 us; the launch traced here: 410 us
  waiting for transfers between devices  141 us (34%)
  Pallas kernels  68.5 us (17%)
  local copies, waits for them, and re-layouts  61.8 us (15%)
  starting transfers between devices  61.6 us (15%)
  other arithmetic  48.1 us (12%)
  between operations  27.2 us (7%)
    ppermute x30, waiting for transfers between devices, swap(): lax.ppermute(value, axis, [(i, i ^ step) for i in range(lax.axis_size(axi...  62.3 us
    pallas_call x7, Pallas kernels, call(): pl.pallas_call(kernel, out_shape=[jax.ShapeDtypeStruct(shape, kind) for s...  56.4 us
    ppermute x1, waiting for transfers between devices, body(): grad_down = lax.ppermute(grad_mlp[-unit:], ALL, owner).astype(F32)  36.2 us
    ppermute x30, starting transfers between devices, swap(): lax.ppermute(value, axis, [(i, i ^ step) for i in range(lax.axis_size(axi...  26.6 us
    all_to_all x3, waiting for transfers between devices, trade_z(): return lax.all_to_all(parts, 'z', 0, 0)  20.7 us
    all_to_all x1, waiting for transfers between devices, body(): lax.all_to_all(self_cuts, ALL, 0, 0)  18.9 us
    all_to_all x3, starting transfers between devices, trade_z(): return lax.all_to_all(parts, 'z', 0, 0)  15.8 us
    slice x18, local copies, waits for them, and re-layouts, behind(): last = other[(-1,) * other.ndim].astype(F32) * 0.0  15 us
  transfers between devices with their start and end apart: 41, of which 18 were waited for; matrix products, arithmetic and copies ran while one was open for 22% of the time, Pallas kernels for 17%

profile of v7, /device:TPU:4, one launch (start us, length us, event | category | flops | bytes accessed | tf_op | source)
XLA Modules:
  0.0 409.5 jit_solution(14152171291024886986)
XLA Ops:
  9.3 1.5 slice.273
  11.0 3.7 collective-permute-start.1
  16.8 1.6 collective-permute-start
  22.2 1.6 pad_maximum_fusion.1
  23.8 5.0 %all-to-all-start = ((bf16[4,256,1024]{2,1,0:T(8,128)(2,1)}), bf16[4,256,1024]{2,1,0:T(8,128)(2,1)}, u32[]{:S(2)}, u32[]{:S(2)}) async-start(bf16[4,256,1024]{2,1,0:T(8,128)(2,1)} %pad_maximum_fusion.1), calls=%async_computation | async-start | bytes 4194304 | tf_op jit(solution)/shard_map/all_to_all | solution.py:425
  31.8 5.5 %collective-permute-done.6 = bf16[160,1024]{1,0:T(8,128)(2,1)S(1)} collective-permute-done((bf16[160,1024]{1,0:T(8,128)(2,1)S(1)}, bf16[160,1024]{1,0:T(8,128)(2,1)S(1)}, u32[]{:S(2)}, u32[]{:S(2)}) %collective-permute-start.6) | collective-permute-done | bytes 327712 | tf_op jit(solution)/shard_map/ppermute | solution.py:31
  39.2 1.3 slice.360
  42.4 6.2 %collective-permute-done.4 = bf16[400,256]{1,0:T(8,128)(2,1)} collective-permute-done((bf16[400,256]{1,0:T(8,128)(2,1)S(1)}, bf16[400,256]{1,0:T(8,128)(2,1)}, u32[]{:S(2)}, u32[]{:S(2)}) %collective-permute-start.4) | collective-permute-done | bytes 204832 | tf_op jit(solution)/shard_map/ppermute | solution.py:31
  48.6 2.2 fusion.23
  50.8 1.5 collective-permute-start.5
  56.8 1.5 dynamic-slice_bitcast_fusion.15
  58.3 8.6 %collective-permute-done.2 = bf16[256,1024]{1,0:T(8,128)(2,1)S(1)} collective-permute-done((bf16[256,1024]{1,0:T(8,128)(2,1)S(1)}, bf16[256,1024]{1,0:T(8,128)(2,1)S(1)}, u32[]{:S(2)}, u32[]{:S(2)}) %collective-permute-start.2) | collective-permute-done | bytes 524320 | tf_op jit(solution)/shard_map/ppermute | solution.py:31
  68.3 6.4 %collective-permute-done.5 = bf16[4,400,256]{2,1,0:T(8,128)(2,1)} collective-permute-done((bf16[4,400,256]{2,1,0:T(8,128)(2,1)}, bf16[4,400,256]{2,1,0:T(8,128)(2,1)}, u32[]{:S(2)}, u32[]{:S(2)}) %collective-permute-start.5) | collective-permute-done | bytes 819232 | tf_op jit(solution)/shard_map/ppermute | solution.py:31
  74.8 2.5 pad_maximum_fusion.3.lines
  77.3 7.3 %shard_map.221 = (bf16[3,1024,256]{2,1,0:T(8,128)(2,1)}, f32[16,1024]{1,0:T(8,128)S(1)}, f32[1,2048]{1,0:T(1,128)S(1)}, bf16[512,1024]{1,0:T(8,128)(2,1)}, bf16[...) custom-call(s32[4]{0:T(128)S(1)} %get-tuple-element.73.at, ...), custom_call_target="tpu_custom_call" | custom-call | flops 1073741824 | bytes 2695168 | tf_op jit(solution)/shard_map/pallas_call | solution.py:66
  88.7 1.6 all-to-all-done
  90.3 2.6 fusion.45
  94.1 1.5 collective-permute-start.10
  96.6 14.4 %collective-permute-done.10 = bf16[4,2,128,256]{3,2,1,0:T(8,128)(2,1)} collective-permute-done((bf16[4,2,128,256]{3,2,1,0:T(8,128)(2,1)}, bf16[4,2,128,256]{3,2,1,0:T(8,128)(2,1)}, u32[]{:S(2)}, u32[]{:S(2)}) %collective-permute-start.10) | collective-permute-done | bytes 524320 | tf_op jit(solution)/shard_map/ppermute | solution.py:31
  111.0 1.4 fusion.11
  114.5 1.5 collective-permute-start.9
  116.0 2.8 collective-permute-done.11
  125.5 2.0 all_gather_reshape.3
  127.6 2.3 maximum_add_fusion
  131.1 6.4 %shard_map.222 = (f32[128,1024]{1,0:T(8,128)}, f32[128,1024]{1,0:T(8,128)}, bf16[128,3072]{1,0:T(8,128)(2,1)}, bf16[128,1024]{1,0:T(8,128)(2,1)S(1)}, f32[128,12...) custom-call(s32[4]{0:T(128)S(1)} %pad_add_fusion.at, ...), custom_call_target="tpu_custom_call" | custom-call | flops 838860800 | bytes 7144192 | tf_op jit(solution)/shard_map/pallas_call | solution.py:66
  138.7 4.2 %all-to-all-start.1 = ((bf16[4,128,1024]{2,1,0:T(8,128)(2,1)}), bf16[4,128,1024]{2,1,0:T(8,128)(2,1)}, u32[]{:S(2)}, u32[]{:S(2)}) async-start(bf16[4,128,1024]{2,1,0:T(8,128)(2,1)} %broadcast_in_dim.40), calls=%async_computation.1 | async-start | bytes 2097152 | tf_op jit(solution)/shard_map/all_to_all | solution.py:425
  143.4 2.5 convert_bitcast_fusion
  145.9 1.7 pad_maximum_fusion.2
  147.8 1.5 maximum_bitcast_fusion
  149.4 2.8 fusion.6
  152.2 2.4 pad_maximum_fusion.w_down
  154.5 15.2 %all-to-all-done.1 = bf16[4,128,1024]{2,1,0:T(8,128)(2,1)} async-done(((bf16[4,128,1024]{2,1,0:T(8,128)(2,1)}), bf16[4,128,1024]{2,1,0:T(8,128)(2,1)}, u32[]{:S(2)}, u32[]{:S(2)}) %all-to-all-start.1) | async-done | bytes 1048608 | tf_op jit(solution)/shard_map/all_to_all | solution.py:425
  169.7 12.0 %shard_map.223 = (bf16[512,2048]{1,0:T(8,128)(2,1)}, bf16[512,2048]{1,0:T(8,128)(2,1)}, bf16[512,1024]{1,0:T(8,128)(2,1)S(1)}, f32[1,2048]{1,0:T(1,128)S(1)}) custom-call(bf16[512,1024]{1,0:T(8,128)(2,1)} %bitcast.66.normed, bf16[512,1024]{1,0:T(8,128)(2,1)} %bitcast.267, bf16[8,4,32,2048]{3,2,1,0:T(8,128)(2,1)} %all-gather.7.cloned.1.call-done.w_up, ...), custom_call_target="tpu_custom_call" | custom-call | flops 6442450944 | bytes 12582912 | tf_op jit(solution)/shard_map/pallas_call | solution.py:624
  181.7 14.1 %shard_map.224 = (bf16[8,512,1024]{2,1,0:T(8,128)(2,1)}, bf16[512,1024]{1,0:T(8,128)(2,1)S(1)}) custom-call(s32[4]{0:T(128)S(1)} %get-tuple-element.74.at, bf16[512,1024]{1,0:T(8,128)(2,1)} %bitcast.66.normed, bf16[512,2048]{1,0:T(8,128)(2,1)} %get-tuple-element.47.pre_grad, bf16[512,2048]{1,0:T(8,128)(2,1)} %get-tuple-element.48.activated, ...), custom_call_target="tpu_custom_call" | custom-call | flops 6442450944 | bytes 10485760 | tf_op jit(solution)/shard_map/pallas_call | solution.py:66
  196.8 2.0 collective-permute-start.15
  198.8 2.4 collective-permute-start.16
  202.0 1.9 slice.378
  208.0 1.6 collective-permute-done.14
  209.6 8.9 %collective-permute-done.15 = bf16[128,1024]{1,0:T(8,128)(2,1)} collective-permute-done((bf16[128,1024]{1,0:T(8,128)(2,1)}, bf16[128,1024]{1,0:T(8,128)(2,1)}, u32[]{:S(2)}, u32[]{:S(2)}) %collective-permute-start.15) | collective-permute-done | bytes 262176 | tf_op jit(solution)/shard_map/ppermute | solution.py:31
  218.5 2.1 fusion.17.terms
  221.8 11.2 %shard_map.225 = (bf16[128,1024]{1,0:T(8,128)(2,1)S(1)}, f32[128,1024]{1,0:T(8,128)S(1)}, bf16[4,192,512]{2,1,0:T(8,128)(2,1)}, f32[16,1024]{1,0:T(8,128)S(1)}) custom-call(s32[4]{0:T(128)S(1)} %copy-done.9, f32[128,1024]{1,0:T(8,128)} %fusion.17.terms, bf16[128,1024]{1,0:T(8,128)(2,1)S(1)} %bitcast.231, f32[128,1024]{1,0:T(8,128)} %get-tuple-element.52.after_self, ...), custom_call_target="tpu_custom_call" | custom-call | flops 620756992 | bytes 8782592 | tf_op jit(solution)/shard_map/pallas_call | solution.py:66
  233.0 1.4 collective-permute-start.17
  237.9 6.6 %all-to-all-start.2 = ((bf16[4,128,1024]{2,1,0:T(8,128)(2,1)}), bf16[4,128,1024]{2,1,0:T(8,128)(2,1)S(1)}, u32[]{:S(2)}, u32[]{:S(2)}) async-start(bf16[4,128,1024]{2,1,0:T(8,128)(2,1)} %bitcast.250), calls=%async_computation.2 | async-start | bytes 2097152 | tf_op jit(solution)/shard_map/all_to_all | solution.py:425
  248.7 1.4 collective-permute-start.22
  251.2 10.0 %shard_map.226 = (bf16[1024,768]{1,0:T(8,128)(2,1)}, bf16[512,1024]{1,0:T(8,128)(2,1)}, f32[8,256]{1,0:T(8,128)S(1)}) custom-call(s32[4]{0:T(128)S(1)} %get-tuple-element.74.at, bf16[512,1024]{1,0:T(8,128)(2,1)} %copy-done.41, bf16[256,1024]{1,0:T(8,128)(2,1)} %constant_dynamic-slice_fusion.7.w_out, bf16[512,256]{1,0:T(8,128)(2,1)S(1)} %copy-done.15, ...), custom_call_target="tpu_custom_call" | custom-call | flops 2550136832 | bytes 5251072 | tf_op jit(solution)/shard_map/pallas_call | solution.py:66
  261.1 1.4 slice.329
  265.2 3.9 all-to-all-done.2
  270.4 2.7 broadcast_add_fusion.1
  273.1 4.3 %all-to-all-start.3 = ((bf16[32,32,768]{2,1,0:T(8,128)(2,1)}), bf16[32,32,768]{2,1,0:T(8,128)(2,1)}, u32[]{:S(2)}, u32[]{:S(2)}) async-start(bf16[32,32,768]{2,1,0:T(8,128)(2,1)} %bitcast.111), calls=%async_computation.3 | async-start | bytes 3145728 | tf_op jit(solution)/shard_map/all_to_all | solution.py:804
  283.0 5.5 %shard_map.228 = bf16[1024,1280]{1,0:T(8,128)(2,1)} custom-call(s32[4]{0:T(128)S(1)} %get-tuple-element.74.at, bf16[2,128,3072]{2,1,0:T(8,128)(2,1)} %bitcast.248, bf16[2,128,3072]{2,1,0:T(8,128)(2,1)} %collective-permute-done.25.swapped, bf16[512,512]{1,0:T(8,128)(2,1)S(1)} %bitcast.229, bf16[512,256]{1,0:T(8,128)(2,1)S(1)} %constant_dynamic-slice_fusion.4.branch_cut, ...), custom_call_target="tpu_custom_call" | custom-call | flops 805306368 | bytes 4128768 | tf_op jit(solution)/shard_map/pallas_call | solution.py:66
  288.5 2.2 slice_bitcast_fusion
  291.5 2.8 collective-permute-start.27
  294.2 1.5 collective-permute-start.28
  297.8 2.1 collective-permute-done.20
  299.9 1.9 shard_map.227
  301.7 18.9 %all-to-all-done.3 = bf16[32,32,768]{2,1,0:T(8,128)(2,1)} async-done(((bf16[32,32,768]{2,1,0:T(8,128)(2,1)}), bf16[32,32,768]{2,1,0:T(8,128)(2,1)}, u32[]{:S(2)}, u32[]{:S(2)}) %all-to-all-start.3) | async-done | bytes 1572896 | tf_op jit(solution)/shard_map/all_to_all | solution.py:804
  327.3 5.7 %all-to-all-start.4 = ((bf16[32,32,128]{2,1,0:T(8,128)(2,1)}), bf16[32,32,128]{2,1,0:T(8,128)(2,1)S(1)}, u32[]{:S(2)}, u32[]{:S(2)}) async-start(bf16[32,32,128]{2,1,0:T(8,128)(2,1)} %bitcast.133), calls=%async_computation.5 | async-start | bytes 524288 | tf_op jit(solution)/shard_map/all_to_all | solution.py:807
  334.2 3.7 collective-permute-done.24
  339.2 3.2 all-to-all-done.4
  343.8 3.3 fusion.2
  347.1 5.2 %all-to-all-start.5 = ((bf16[16,32,1280]{2,1,0:T(8,128)(2,1)}), bf16[16,32,1280]{2,1,0:T(8,128)(2,1)S(1)}, u32[]{:S(2)}, u32[]{:S(2)}) async-start(bf16[16,32,1280]{2,1,0:T(8,128)(2,1)} %fusion.2), calls=%async_computation.6 | async-start | bytes 2621440 | tf_op jit(solution)/shard_map/all_to_all | solution.py:810
  352.3 3.3 collective-permute-start.30
  356.6 1.7 convert_reduce_fusion
  359.0 36.2 %collective-permute-done.30 = bf16[256,1024]{1,0:T(8,128)(2,1)S(1)} collective-permute-done((bf16[256,1024]{1,0:T(8,128)(2,1)}, bf16[256,1024]{1,0:T(8,128)(2,1)S(1)}, u32[]{:S(2)}, u32[]{:S(2)}) %collective-permute-start.30) | collective-permute-done | bytes 524320 | tf_op jit(solution)/shard_map/ppermute | solution.py:692
  (324 shorter events, 74.1 us)
Async XLA Ops:
  7.2 115.5 %all-gather.5.cloned.1.call-start = ((), (), s32[]{:S(2)}) async-start(), calls=%async_computation.7 | async-start | bytes 6488064 | tf_op jit(solution)/shard_map/all_gather | solution.py:528
  11.0 28.1 %collective-permute-start.1 = (bf16[400,256]{1,0:T(8,128)(2,1)S(1)}, bf16[400,256]{1,0:T(8,128)(2,1)}, u32[]{:S(2)}, u32[]{:S(2)}) collective-permute-start(bf16[400,256]{1,0:T(8,128)(2,1)S(1)} %get-tuple-element.128), channel_id=1, source_target_pairs={{0,6},{2,4},{4,2},{6,0},{1,7},{3,5},{5,3},{7,1},{8,14},{10,12},{12... | collective-permute-start | bytes 614408 | tf_op jit(solution)/shard_map/ppermute | solution.py:31
  14.7 27.7 %collective-permute-start.3 = (bf16[400,256]{1,0:T(8,128)(2,1)S(1)}, bf16[400,256]{1,0:T(8,128)(2,1)}, u32[]{:S(2)}, u32[]{:S(2)}) collective-permute-start(bf16[400,256]{1,0:T(8,128)(2,1)S(1)} %get-tuple-element.128), channel_id=1, source_target_pairs={{0,2},{2,0},{4,6},{6,4},{1,3},{3,1},{5,7},{7,5},{8,10},{10,8},{12,... | collective-permute-start | bytes 614408 | tf_op jit(solution)/shard_map/ppermute | solution.py:31
  14.7 33.9 %collective-permute-start.4 = (bf16[400,256]{1,0:T(8,128)(2,1)S(1)}, bf16[400,256]{1,0:T(8,128)(2,1)}, u32[]{:S(2)}, u32[]{:S(2)}) collective-permute-start(bf16[400,256]{1,0:T(8,128)(2,1)S(1)} %get-tuple-element.128), channel_id=1, source_target_pairs={{0,4},{2,6},{4,0},{6,2},{1,5},{3,7},{5,1},{7,3},{8,12},{10,14},{12... | collective-permute-start | bytes 614408 | tf_op jit(solution)/shard_map/ppermute | solution.py:31
  16.8 24.4 %collective-permute-start = (bf16[256,1024]{1,0:T(8,128)(2,1)S(1)}, bf16[256,1024]{1,0:T(8,128)(2,1)S(1)}, u32[]{:S(2)}, u32[]{:S(2)}) collective-permute-start(bf16[256,1024]{1,0:T(8,128)(2,1)S(1)} %dynamic-slice_convert_fusion.1), channel_id=1, source_target_pairs={{0,1},{1,0},{2,3},{3,2},{4,5},{5,4},{6,7},{7,6},{8,9},{9,8},{10,11... | collective-permute-start | bytes 1572872 | tf_op jit(solution)/shard_map/ppermute | solution.py:31
  23.7 5.3 %copy-start.39 = (bf16[1,16,1024]{2,1,0:T(8,128)(2,1)S(1)}, bf16[1,16,1024]{2,1,0:T(8,128)(2,1)}, u32[]{:S(2)}) copy-start(bf16[1,16,1024]{2,1,0:T(8,128)(2,1)} %param.15) | copy-start | bytes 98308
  23.7 5.9 %copy-start.56 = (s32[8]{0:T(128)S(1)}, s32[8]{0:T(128)}, u32[]{:S(2)}) copy-start(s32[8]{0:T(128)} %param.19) | copy-start | bytes 100
  23.8 66.5 %all-to-all-start = ((bf16[4,256,1024]{2,1,0:T(8,128)(2,1)}), bf16[4,256,1024]{2,1,0:T(8,128)(2,1)}, u32[]{:S(2)}, u32[]{:S(2)}) async-start(bf16[4,256,1024]{2,1,0:T(8,128)(2,1)} %pad_maximum_fusion.1), calls=%async_computation | async-start | bytes 4194304 | tf_op jit(solution)/shard_map/all_to_all | solution.py:425
  28.8 140.9 %all-gather.7.cloned.1.call-start = ((), (), s32[]{:S(2)}) async-start(), calls=%async_computation.8 | async-start | bytes 4718592 | tf_op jit(solution)/shard_map/all_gather | solution.py:609
  29.1 8.1 %collective-permute-start.6 = (bf16[160,1024]{1,0:T(8,128)(2,1)S(1)}, bf16[160,1024]{1,0:T(8,128)(2,1)S(1)}, u32[]{:S(2)}, u32[]{:S(2)}) collective-permute-start(bf16[160,1024]{1,0:T(8,128)(2,1)S(1)} %pad_maximum_fusion.10), channel_id=1, source_target_pairs={{0,16},{16,0},{1,17},{17,1},{2,18},{18,2},{3,19},{19,3},{4,20},{20... | collective-permute-start | bytes 983048 | tf_op jit(solution)/shard_map/ppermute | solution.py:31
  38.1 14.8 %collective-permute-start.7 = (bf16[320,1024]{1,0:T(8,128)(2,1)}, bf16[320,1024]{1,0:T(8,128)(2,1)}, u32[]{:S(2)}, u32[]{:S(2)}) collective-permute-start(bf16[320,1024]{1,0:T(8,128)(2,1)} %pad_maximum_fusion.6), channel_id=1, source_target_pairs={{0,8},{8,0},{1,9},{9,1},{2,10},{10,2},{3,11},{11,3},{4,12},{12,4},... | collective-permute-start | bytes 1966088 | tf_op jit(solution)/shard_map/ppermute | solution.py:31
  38.4 38.8 %copy-start.4 = (s32[512,1]{1,0:T(8,128)}, s32[512,1]{1,0:T(8,128)S(1)}, u32[]{:S(2)}) copy-start(s32[512,1]{1,0:T(8,128)S(1)} %add.408.pos) | copy-start | bytes 6148
  38.5 38.7 %copy-start.12 = (s32[1,512]{1,0:T(1,128)}, s32[1,512]{1,0:T(1,128)S(1)}, u32[]{:S(2)}) copy-start(s32[1,512]{1,0:T(1,128)S(1)} %add.344.pos_line) | copy-start | bytes 6148
  39.2 13.7 %copy-start.34 = (bf16[640,1024]{1,0:T(8,128)(2,1)S(1)}, bf16[640,1024]{1,0:T(8,128)(2,1)}, u32[]{:S(2)}) copy-start(bf16[640,1024]{1,0:T(8,128)(2,1)} %constant_dynamic-update-slice_fusion.2) | copy-start | bytes 3932164
  50.8 24.0 %collective-permute-start.5 = (bf16[4,400,256]{2,1,0:T(8,128)(2,1)}, bf16[4,400,256]{2,1,0:T(8,128)(2,1)}, u32[]{:S(2)}, u32[]{:S(2)}) collective-permute-start(bf16[4,400,256]{2,1,0:T(8,128)(2,1)} %get-tuple-element.102), channel_id=1, source_target_pairs={{0,1},{1,0},{2,3},{3,2},{4,5},{5,4},{6,7},{7,6},{8,9},{9,8},{10,11... | collective-permute-start | bytes 2457608 | tf_op jit(solution)/shard_map/ppermute | solution.py:31
  52.3 14.6 %collective-permute-start.2 = (bf16[256,1024]{1,0:T(8,128)(2,1)S(1)}, bf16[256,1024]{1,0:T(8,128)(2,1)S(1)}, u32[]{:S(2)}, u32[]{:S(2)}) collective-permute-start(bf16[256,1024]{1,0:T(8,128)(2,1)S(1)} %broadcast_add_fusion.5), channel_id=1, source_target_pairs={{0,16},{16,0},{1,17},{17,1},{2,18},{18,2},{3,19},{19,3},{4,20},{20... | collective-permute-start | bytes 1572872 | tf_op jit(solution)/shard_map/ppermute | solution.py:31
  56.6 20.7 %copy-start.40 = (s32[1,4,16,1024]{3,1,2,0:T(4,128)}, s32[1,4,16,1024]{3,1,2,0:T(4,128)S(1)}, u32[]{:S(2)}) copy-start(s32[1,4,16,1024]{3,1,2,0:T(4,128)S(1)} %copy.99) | copy-start | bytes 786436
  56.8 27.8 %copy-start.6 = (s32[512,1]{1,0:T(8,128)}, s32[512,1]{1,0:T(8,128)S(1)}, u32[]{:S(2)}) copy-start(s32[512,1]{1,0:T(8,128)S(1)} %copy.70.seg) | copy-start | bytes 6148
  58.3 55.3 %copy-start.42 = (bf16[16,1024]{1,0:T(8,128)(2,1)}, bf16[16,1024]{1,0:T(8,128)(2,1)S(1)}, u32[]{:S(2)}) copy-start(bf16[16,1024]{1,0:T(8,128)(2,1)S(1)} %get-tuple-element.83) | copy-start | bytes 98308
  66.9 17.7 %copy-start.38 = (bf16[256,1024]{1,0:T(8,128)(2,1)}, bf16[256,1024]{1,0:T(8,128)(2,1)S(1)}, u32[]{:S(2)}) copy-start(bf16[256,1024]{1,0:T(8,128)(2,1)S(1)} %collective-permute-done.2) | copy-start | bytes 1572868
  94.1 17.0 %collective-permute-start.10 = (bf16[4,2,128,256]{3,2,1,0:T(8,128)(2,1)}, bf16[4,2,128,256]{3,2,1,0:T(8,128)(2,1)}, u32[]{:S(2)}, u32[]{:S(2)}) collective-permute-start(bf16[4,2,128,256]{3,2,1,0:T(8,128)(2,1)} %reshape.493), channel_id=1, source_target_pairs={{0,1},{1,0},{2,3},{3,2},{4,5},{5,4},{6,7},{7,6},{8,9},{9,8},{10,11... | collective-permute-start | bytes 1572872 | tf_op jit(solution)/shard_map/ppermute | solution.py:31
  95.6 18.9 %collective-permute-start.8 = (bf16[2,128,256]{2,1,0:T(8,128)(2,1)S(1)}, bf16[2,128,256]{2,1,0:T(8,128)(2,1)S(1)}, u32[]{:S(2)}, u32[]{:S(2)}) collective-permute-start(bf16[2,128,256]{2,1,0:T(8,128)(2,1)S(1)} %bitcast.283), channel_id=1, source_target_pairs={{0,8},{8,0},{1,9},{9,1},{2,10},{10,2},{3,11},{11,3},{4,12},{12,4},... | collective-permute-start | bytes 393224 | tf_op jit(solution)/shard_map/ppermute | solution.py:31
  112.8 12.7 %copy-start.31 = (bf16[1,4,2,128,256]{4,3,2,1,0:T(8,128)(2,1)}, bf16[1,4,2,128,256]{4,3,2,1,0:T(8,128)(2,1)S(1)}, u32[]{:S(2)}) copy-start(bf16[1,4,2,128,256]{4,3,2,1,0:T(8,128)(2,1)S(1)} %copy.76) | copy-start | bytes 1572868
  113.8 13.8 %copy-start.28 = (bf16[256,1024]{1,0:T(8,128)(2,1)S(1)}, bf16[256,1024]{1,0:T(8,128)(2,1)}, u32[]{:S(2)}) copy-start(bf16[256,1024]{1,0:T(8,128)(2,1)} %copy-done.27) | copy-start | bytes 1572868
  113.8 4.9 %collective-permute-start.11 = (bf16[1,2,64,256]{3,2,1,0:T(8,128)(2,1)S(1)}, bf16[1,2,64,256]{3,2,1,0:T(8,128)(2,1)S(1)}, u32[]{:S(2)}, u32[]{:S(2)}) collective-permute-start(bf16[1,2,64,256]{3,2,1,0:T(8,128)(2,1)S(1)} %maximum_bitcast_fusion.3), channel_id=1, source_target_pairs={{0,16},{16,0},{1,17},{17,1},{2,18},{18,2},{3,19},{19,3},{4,20},{20... | collective-permute-start | bytes 196616 | tf_op jit(solution)/shard_map/ppermute | solution.py:31
  114.5 5.7 %collective-permute-start.9 = (bf16[2,128,256]{2,1,0:T(8,128)(2,1)S(1)}, bf16[2,128,256]{2,1,0:T(8,128)(2,1)S(1)}, u32[]{:S(2)}, u32[]{:S(2)}) collective-permute-start(bf16[2,128,256]{2,1,0:T(8,128)(2,1)S(1)} %get-tuple-element.124), channel_id=1, source_target_pairs={{0,16},{16,0},{1,17},{17,1},{2,18},{18,2},{3,19},{19,3},{4,20},{20... | collective-permute-start | bytes 393224 | tf_op jit(solution)/shard_map/ppermute | solution.py:31
  118.8 2.7 collective-permute-start.12
  129.9 16.0 %collective-permute-start.13 = (bf16[512,1024]{1,0:T(8,128)(2,1)}, bf16[512,1024]{1,0:T(8,128)(2,1)}, u32[]{:S(2)}, u32[]{:S(2)}) collective-permute-start(bf16[512,1024]{1,0:T(8,128)(2,1)} %maximum_add_fusion), channel_id=1, source_target_pairs={{0,8},{8,0},{1,9},{9,1},{2,10},{10,2},{3,11},{11,3},{4,12},{12,4},... | collective-permute-start | bytes 3145736 | tf_op jit(solution)/shard_map/ppermute | solution.py:31
  130.0 7.4 %copy-start.8 = (s32[4]{0:T(128)}, s32[4]{0:T(128)S(1)}, u32[]{:S(2)}) copy-start(s32[4]{0:T(128)S(1)} %pad_add_fusion.at) | copy-start | bytes 52
  131.0 6.4 %copy-start.10 = (s32[1,64]{1,0:T(1,128)}, s32[1,64]{1,0:T(1,128)S(1)}, u32[]{:S(2)}) copy-start(s32[1,64]{1,0:T(1,128)S(1)} %add_bitcast_fusion.source_seg) | copy-start | bytes 772
  138.7 31.0 %all-to-all-start.1 = ((bf16[4,128,1024]{2,1,0:T(8,128)(2,1)}), bf16[4,128,1024]{2,1,0:T(8,128)(2,1)}, u32[]{:S(2)}, u32[]{:S(2)}) async-start(bf16[4,128,1024]{2,1,0:T(8,128)(2,1)} %broadcast_in_dim.40), calls=%async_computation.1 | async-start | bytes 2097152 | tf_op jit(solution)/shard_map/all_to_all | solution.py:425
  142.9 61.9 %all-gather.9.cloned.1.call-start = ((), (), s32[]{:S(2)}) async-start(), calls=%async_computation.10 | async-start | bytes 2359296 | tf_op jit(solution)/shard_map/all_gather | solution.py:681
  149.3 139.2 %reduce-scatter.2.cloned.1.call-start = ((), (), s32[]{:S(2)}) async-start(), calls=%async_computation.9 | async-start | bytes 9437184 | tf_op jit(solution)/shard_map/reduce_scatter | solution.py:683
  195.9 5.3 %copy-start.43 = (bf16[16,1024]{1,0:T(8,128)(2,1)S(1)}, bf16[16,1024]{1,0:T(8,128)(2,1)}, u32[]{:S(2)}) copy-start(bf16[16,1024]{1,0:T(8,128)(2,1)} %copy-done.42) | copy-start | bytes 98308
  195.9 5.3 %copy-start.45 = (bf16[16,1024]{1,0:T(8,128)(2,1)S(1)}, bf16[16,1024]{1,0:T(8,128)(2,1)}, u32[]{:S(2)}) copy-start(bf16[16,1024]{1,0:T(8,128)(2,1)} %get-tuple-element.84) | copy-start | bytes 98308
  196.8 12.8 %collective-permute-start.14 = (bf16[128,1024]{1,0:T(8,128)(2,1)}, bf16[128,1024]{1,0:T(8,128)(2,1)}, u32[]{:S(2)}, u32[]{:S(2)}) collective-permute-start(bf16[128,1024]{1,0:T(8,128)(2,1)} %get-tuple-element.94), channel_id=1, source_target_pairs={{0,2},{2,0},{4,6},{6,4},{1,3},{3,1},{5,7},{7,5},{8,10},{10,8},{12,... | collective-permute-start | bytes 786440 | tf_op jit(solution)/shard_map/ppermute | solution.py:31
  196.8 21.7 %collective-permute-start.15 = (bf16[128,1024]{1,0:T(8,128)(2,1)}, bf16[128,1024]{1,0:T(8,128)(2,1)}, u32[]{:S(2)}, u32[]{:S(2)}) collective-permute-start(bf16[128,1024]{1,0:T(8,128)(2,1)} %get-tuple-element.96), channel_id=1, source_target_pairs={{0,4},{2,6},{4,0},{6,2},{1,5},{3,7},{5,1},{7,3},{8,12},{10,14},{12... | collective-permute-start | bytes 786440 | tf_op jit(solution)/shard_map/ppermute | solution.py:31
  198.8 19.6 %collective-permute-start.16 = (bf16[128,1024]{1,0:T(8,128)(2,1)}, bf16[128,1024]{1,0:T(8,128)(2,1)}, u32[]{:S(2)}, u32[]{:S(2)}) collective-permute-start(bf16[128,1024]{1,0:T(8,128)(2,1)} %get-tuple-element.95), channel_id=1, source_target_pairs={{0,6},{2,4},{4,2},{6,0},{1,7},{3,5},{5,3},{7,1},{8,14},{10,12},{12... | collective-permute-start | bytes 786440 | tf_op jit(solution)/shard_map/ppermute | solution.py:31
  233.0 13.5 %collective-permute-start.17 = (bf16[128,1024]{1,0:T(8,128)(2,1)S(1)}, bf16[128,1024]{1,0:T(8,128)(2,1)S(1)}, u32[]{:S(2)}, u32[]{:S(2)}) collective-permute-start(bf16[128,1024]{1,0:T(8,128)(2,1)S(1)} %get-tuple-element.56), channel_id=1, source_target_pairs={{0,16},{16,0},{1,17},{17,1},{2,18},{18,2},{3,19},{19,3},{4,20},{20... | collective-permute-start | bytes 786440 | tf_op jit(solution)/shard_map/ppermute | solution.py:31
  237.9 31.2 %all-to-all-start.2 = ((bf16[4,128,1024]{2,1,0:T(8,128)(2,1)}), bf16[4,128,1024]{2,1,0:T(8,128)(2,1)S(1)}, u32[]{:S(2)}, u32[]{:S(2)}) async-start(bf16[4,128,1024]{2,1,0:T(8,128)(2,1)} %bitcast.250), calls=%async_computation.2 | async-start | bytes 2097152 | tf_op jit(solution)/shard_map/all_to_all | solution.py:425
  245.8 2.8 collective-permute-start.21
  246.6 3.5 collective-permute-start.18
  248.5 34.5 %collective-permute-start.25 = (bf16[2,128,3072]{2,1,0:T(8,128)(2,1)}, bf16[2,128,3072]{2,1,0:T(8,128)(2,1)}, u32[]{:S(2)}, u32[]{:S(2)}) collective-permute-start(bf16[2,128,3072]{2,1,0:T(8,128)(2,1)} %broadcast_add_fusion), channel_id=1, source_target_pairs={{0,8},{8,0},{1,9},{9,1},{2,10},{10,2},{3,11},{11,3},{4,12},{12,4},... | collective-permute-start | bytes 4718600 | tf_op jit(solution)/shard_map/ppermute | solution.py:31
  248.7 14.5 %collective-permute-start.22 = (bf16[2,192,512]{2,1,0:T(8,128)(2,1)S(1)}, bf16[2,192,512]{2,1,0:T(8,128)(2,1)S(1)}, u32[]{:S(2)}, u32[]{:S(2)}) collective-permute-start(bf16[2,192,512]{2,1,0:T(8,128)(2,1)S(1)} %get-tuple-element.104), channel_id=1, source_target_pairs={{0,16},{16,0},{1,17},{17,1},{2,18},{18,2},{3,19},{19,3},{4,20},{20... | collective-permute-start | bytes 1179656 | tf_op jit(solution)/shard_map/ppermute | solution.py:31
  273.1 6.7 %copy-start.30 = (bf16[1,4,2,128,256]{4,3,2,1,0:T(8,128)(2,1)S(1)}, bf16[1,4,2,128,256]{4,3,2,1,0:T(8,128)(2,1)}, u32[]{:S(2)}) copy-start(bf16[1,4,2,128,256]{4,3,2,1,0:T(8,128)(2,1)} %copy-done.29) | copy-start | bytes 1572868
  273.1 7.0 %copy-start.32 = (bf16[1,4,2,128,256]{4,3,2,1,0:T(8,128)(2,1)S(1)}, bf16[1,4,2,128,256]{4,3,2,1,0:T(8,128)(2,1)}, u32[]{:S(2)}) copy-start(bf16[1,4,2,128,256]{4,3,2,1,0:T(8,128)(2,1)} %copy-done.31) | copy-start | bytes 1572868
  273.1 47.5 %all-to-all-start.3 = ((bf16[32,32,768]{2,1,0:T(8,128)(2,1)}), bf16[32,32,768]{2,1,0:T(8,128)(2,1)}, u32[]{:S(2)}, u32[]{:S(2)}) async-start(bf16[32,32,768]{2,1,0:T(8,128)(2,1)} %bitcast.111), calls=%async_computation.3 | async-start | bytes 3145728 | tf_op jit(solution)/shard_map/all_to_all | solution.py:804
  279.6 2.9 collective-permute-start.19
  281.0 52.0 %collective-permute-start.23 = (bf16[2,16,1024]{2,1,0:T(8,128)(2,1)}, bf16[2,16,1024]{2,1,0:T(8,128)(2,1)}, u32[]{:S(2)}, u32[]{:S(2)}) collective-permute-start(bf16[2,16,1024]{2,1,0:T(8,128)(2,1)} %pad_maximum_fusion.19), channel_id=1, source_target_pairs={{0,8},{8,0},{1,9},{9,1},{2,10},{10,2},{3,11},{11,3},{4,12},{12,4},... | collective-permute-start | bytes 196616 | tf_op jit(solution)/shard_map/ppermute | solution.py:31
  282.7 17.1 %collective-permute-start.20 = (bf16[128,1024]{1,0:T(8,128)(2,1)S(1)}, bf16[128,1024]{1,0:T(8,128)(2,1)S(1)}, u32[]{:S(2)}, u32[]{:S(2)}) collective-permute-start(bf16[128,1024]{1,0:T(8,128)(2,1)S(1)} %fusion.22), channel_id=1, source_target_pairs={{0,16},{16,0},{1,17},{17,1},{2,18},{18,2},{3,19},{19,3},{4,20},{20... | collective-permute-start | bytes 786440 | tf_op jit(solution)/shard_map/ppermute | solution.py:31
  288.5 8.1 %copy-start.22 = (bf16[1024,1280]{1,0:T(8,128)(2,1)S(1)}, bf16[1024,1280]{1,0:T(8,128)(2,1)}, u32[]{:S(2)}) copy-start(bf16[1024,1280]{1,0:T(8,128)(2,1)} %shard_map.228) | copy-start | bytes 7864324
  291.5 31.1 %collective-permute-start.27 = (bf16[2,32,1024]{2,1,0:T(8,128)(2,1)}, bf16[2,32,1024]{2,1,0:T(8,128)(2,1)S(1)}, u32[]{:S(2)}, u32[]{:S(2)}) collective-permute-start(bf16[2,32,1024]{2,1,0:T(8,128)(2,1)} %get-tuple-element.113), channel_id=1, source_target_pairs={{0,2},{2,0},{4,6},{6,4},{1,3},{3,1},{5,7},{7,5},{8,10},{10,8},{12,... | collective-permute-start | bytes 393224 | tf_op jit(solution)/shard_map/ppermute | solution.py:31
  294.2 29.0 %collective-permute-start.28 = (bf16[2,32,1024]{2,1,0:T(8,128)(2,1)S(1)}, bf16[2,32,1024]{2,1,0:T(8,128)(2,1)S(1)}, u32[]{:S(2)}, u32[]{:S(2)}) collective-permute-start(bf16[2,32,1024]{2,1,0:T(8,128)(2,1)S(1)} %get-tuple-element.112), channel_id=1, source_target_pairs={{0,4},{2,6},{4,0},{6,2},{1,5},{3,7},{5,1},{7,3},{8,12},{10,14},{12... | collective-permute-start | bytes 393224 | tf_op jit(solution)/shard_map/ppermute | solution.py:31
  295.7 27.5 %collective-permute-start.29 = (bf16[2,32,1024]{2,1,0:T(8,128)(2,1)S(1)}, bf16[2,32,1024]{2,1,0:T(8,128)(2,1)S(1)}, u32[]{:S(2)}, u32[]{:S(2)}) collective-permute-start(bf16[2,32,1024]{2,1,0:T(8,128)(2,1)S(1)} %get-tuple-element.114), channel_id=1, source_target_pairs={{0,6},{2,4},{4,2},{6,0},{1,7},{3,5},{5,3},{7,1},{8,14},{10,12},{12... | collective-permute-start | bytes 393224 | tf_op jit(solution)/shard_map/ppermute | solution.py:31
  299.8 44.0 %collective-permute-start.26 = (bf16[16,32,1280]{2,1,0:T(8,128)(2,1)}, bf16[16,32,1280]{2,1,0:T(8,128)(2,1)}, u32[]{:S(2)}, u32[]{:S(2)}) collective-permute-start(bf16[16,32,1280]{2,1,0:T(8,128)(2,1)} %dynamic-slice_bitcast_fusion), channel_id=1, source_target_pairs={{0,1},{1,0},{2,3},{3,2},{4,5},{5,4},{6,7},{7,6},{8,9},{9,8},{10,11... | collective-permute-start | bytes 3932168 | tf_op jit(solution)/shard_map/ppermute | solution.py:31
  325.2 18.6 %copy-start.36 = (f32[32,8192]{1,0:T(8,128)}, f32[32,8192]{1,0:T(8,128)S(1)}, u32[]{:S(2)}) copy-start(f32[32,8192]{1,0:T(8,128)S(1)} %reshape.513) | copy-start | bytes 3145732
  327.3 15.1 %all-to-all-start.4 = ((bf16[32,32,128]{2,1,0:T(8,128)(2,1)}), bf16[32,32,128]{2,1,0:T(8,128)(2,1)S(1)}, u32[]{:S(2)}, u32[]{:S(2)}) async-start(bf16[32,32,128]{2,1,0:T(8,128)(2,1)} %bitcast.133), calls=%async_computation.5 | async-start | bytes 524288 | tf_op jit(solution)/shard_map/all_to_all | solution.py:807
  333.9 4.1 collective-permute-start.24
  338.0 9.1 %copy-start.48 = (f32[16,1024]{1,0:T(8,128)}, f32[16,1024]{1,0:T(8,128)S(1)}, u32[]{:S(2)}) copy-start(f32[16,1024]{1,0:T(8,128)S(1)} %fusion.28) | copy-start | bytes 196612
  347.1 8.5 %copy-start.25 = (bf16[4,128,1024]{2,1,0:T(8,128)(2,1)S(1)}, bf16[4,128,1024]{2,1,0:T(8,128)(2,1)}, u32[]{:S(2)}) copy-start(bf16[4,128,1024]{2,1,0:T(8,128)(2,1)} %copy-done.24) | copy-start | bytes 3145732
  347.1 8.7 %copy-start.26 = (f32[128,1024]{1,0:T(8,128)S(1)}, f32[128,1024]{1,0:T(8,128)}, u32[]{:S(2)}) copy-start(f32[128,1024]{1,0:T(8,128)} %get-tuple-element.44.after_cross) | copy-start | bytes 1572868
  347.1 8.7 %copy-start.49 = (f32[1,1024]{1,0:T(1,128)S(1)}, f32[1,1024]{1,0:T(1,128)}, u32[]{:S(2)}) copy-start(f32[1,1024]{1,0:T(1,128)} %get-tuple-element.133) | copy-start | bytes 12292
  347.1 52.2 %all-to-all-start.5 = ((bf16[16,32,1280]{2,1,0:T(8,128)(2,1)}), bf16[16,32,1280]{2,1,0:T(8,128)(2,1)S(1)}, u32[]{:S(2)}, u32[]{:S(2)}) async-start(bf16[16,32,1280]{2,1,0:T(8,128)(2,1)} %fusion.2), calls=%async_computation.6 | async-start | bytes 2621440 | tf_op jit(solution)/shard_map/all_to_all | solution.py:810
  352.3 42.9 %collective-permute-start.30 = (bf16[256,1024]{1,0:T(8,128)(2,1)}, bf16[256,1024]{1,0:T(8,128)(2,1)S(1)}, u32[]{:S(2)}, u32[]{:S(2)}) collective-permute-start(bf16[256,1024]{1,0:T(8,128)(2,1)} %get-tuple-element.90), channel_id=1, source_target_pairs={{0,0},{1,1},{2,8},{3,9},{4,16},{5,17},{6,24},{7,25},{8,4},{9,5},{1... | collective-permute-start | bytes 1572872 | tf_op jit(solution)/shard_map/ppermute | solution.py:692
  (35 other events, 86.0 us)
Sparse Core Ops, SparseCore 0:
  11.5 103.7 all-gather.4
  127.7 36.0 all-gather.6
  165.9 26.1 all-gather.8
  196.0 78.1 reduce-scatter.1
